TPU v7x, 128 devices: a whole 4x4x4 slice. The times are simulated.
128 devices in a mesh: grp: 8 (over y, core), sub: 8 (over x_hi, z), chip: 2 (over x_lo).
Axes of the slice: x: 4 (x_hi: 2, x_lo: 2; x = x_hi * 2 + x_lo), y: 4, z: 4, core: 2. Of those that a mesh axis runs over, the one named last changes fastest.
Arguments:
- right_side: float32 [64, 1048576], P(None, ('grp', 'sub', 'chip')), may hold values from -6 to 6
- diag_tiles: float32 [8192, 128, 128], P(('grp', 'sub', 'chip')), as said below
- remote_tiles: float32 [2048, 2, 128, 128], P(('grp', 'sub', 'chip')), as said below
- slot_counts: int32 [128, 16], P(('grp', 'sub', 'chip')), may hold values from 0 to 2, as said below
- slot_blocks: int32 [128, 16, 2], P(('grp', 'sub', 'chip')), may hold values from 0 to 63, as said below
- fine_map: int32 [1048576], P(('grp', 'sub', 'chip')), may hold values from 0 to 63, as said below
- coarse_map: int32 [8192], P('grp'), may hold values from 0 to 63, as said below
- level1_ops: float32 [8, 1024, 1024], P('grp'), as said below
- coarsest_inverse: float32 [512, 512], replicated, as said below
Outputs:
- solution: float32 [64, 1048576], P(None, ('grp', 'sub', 'chip'))
- residual: float32 [64, 1048576], P(None, ('grp', 'sub', 'chip'))
Inputs may be any that keep to these rules, and one draw needn't show every extreme that they name: slot_counts[d, q] equals slot_counts[e, i] for the devices d = g * 16 + i and e = g * 16 + q of one group; it is zero for q = i. `slot_blocks`: the 32 slots of one device name distinct tiles. remote_tiles[d * 16 + q, c] is the transpose of remote_tiles[e * 16 + i, c] for d = g * 16 + i and e = g * 16 + q; entries are nonnegative. `fine_map`: each aggregate holds the same number of vertices. `coarse_map`: each aggregate holds the same number of level-one vertices. `diag_tiles`: symmetric; each diagonal entry exceeds the sum of the magnitudes of the other entries of its row together with the live coupling weights of its vertex. `level1_ops`: symmetric, diagonally dominant by rows. `coarsest_inverse`: symmetric, diagonally dominant by rows.
All inputs are finite; a program needn't handle non-finite values.
Results may differ from a plain program's by a relative error of at most 0.0003.
Values sent between devices are 32-bit elements; how exact they have to be, the bound alone decides.
No kernel may reach another device: no remote copies, remote signals or barrier semaphores. Data moves between devices by JAX's collectives and lax.ppermute only.
A program may use at most 128 MiB of HBM per device.

v0:
```python
import jax
import jax.numpy as jnp
from jax import lax
from jax.sharding import PartitionSpec as P

CAP = 2
AGG_DEV = 64
AGG2 = 64
ITERS = 2


OMEGA = 0.6
HIGH = lax.Precision.HIGHEST


def couple_tiles(arrived, remote_tiles, live):
    product = jnp.einsum("kqcu,qcuv->kqcv", arrived, remote_tiles, precision=HIGH)
    return product * live[None, :, :, None]


def fine_apply(vector, diag_tiles, remote_tiles, live, slot_list):
    columns = vector.shape[0]
    blocks, tile = (diag_tiles.shape[0], diag_tiles.shape[1])
    peers, capacity = (remote_tiles.shape[0], remote_tiles.shape[1])
    shaped = vector.reshape(columns, blocks, tile)
    result = jnp.einsum("kbt,bts->kbs", shaped, diag_tiles, precision=HIGH)
    outgoing = jnp.take(shaped, slot_list, axis=1).reshape(columns, peers, capacity, tile)
    coupled = couple_tiles(
        lax.all_to_all(outgoing, ("sub", "chip"), split_axis=1, concat_axis=1, tiled=True),
        remote_tiles,
        live,
    )
    result = result.at[:, slot_list].add(-coupled.reshape(columns, peers * capacity, tile))
    return result.reshape(columns, blocks * tile)


def restrict(values, spread):
    return lax.dot_general(values, spread, (((1,), (1,)), ((), ())), precision=HIGH)


def prolong(values, spread):
    return jnp.dot(values, spread, precision=HIGH)


def inner_products(resid, pre):
    return lax.psum(jnp.sum(resid * pre, axis=1), ("grp", "sub", "chip"))


def on_device(
    right_side,
    diag_tiles,
    remote_tiles,
    slot_counts,
    slot_blocks,
    fine_map,
    coarse_map,
    level1_ops,
    coarsest_inverse,
):
    group = lax.axis_index("grp")
    member = lax.axis_index(("sub", "chip"))
    slot_list = slot_blocks[0].reshape(-1)
    live = (jnp.arange(CAP, dtype=jnp.int32)[None, :] < slot_counts[0][:, None]).astype(jnp.float32)
    fine_diag = jnp.diagonal(diag_tiles, axis1=1, axis2=2).reshape(-1)
    spread_fine = (jnp.arange(AGG_DEV, dtype=jnp.int32)[:, None] == fine_map[None, :]).astype(
        jnp.float32
    )
    operator = level1_ops[0]
    spread_coarse = (jnp.arange(AGG2, dtype=jnp.int32)[:, None] == coarse_map[None, :]).astype(
        jnp.float32
    )
    inverse_cols = lax.dynamic_slice_in_dim(coarsest_inverse, group * AGG2, AGG2, 1)

    def apply_fine(vector):
        return fine_apply(vector, diag_tiles, remote_tiles, live, slot_list)

    whole_diag = jnp.diagonal(operator)

    def level_one(coarse_resid):
        gathered = lax.all_gather(coarse_resid, ("sub", "chip"), axis=1, tiled=True)
        guess = OMEGA * gathered / whole_diag
        left = gathered - jnp.dot(guess, operator, precision=HIGH)
        lowest = lax.all_gather(restrict(left, spread_coarse), "grp", axis=1, tiled=True)
        correction = jnp.dot(lowest, inverse_cols, precision=HIGH)
        guess = guess + prolong(correction, spread_coarse)
        guess = guess + OMEGA * (gathered - jnp.dot(guess, operator, precision=HIGH)) / whole_diag
        return (lax.dynamic_slice_in_dim(guess, member * AGG_DEV, AGG_DEV, 1), guess)

    def precondition(resid):
        guess = OMEGA * resid / fine_diag
        applied = apply_fine(guess)
        own_part, group_part = level_one(restrict(resid - applied, spread_fine))
        lifted = prolong(own_part, spread_fine)
        image = apply_fine(guess + lifted)
        guess = guess + lifted
        return guess + OMEGA * (resid - image) / fine_diag

    solution = jnp.zeros_like(right_side)
    residual = right_side
    search = precondition(residual)
    rho = inner_products(residual, search)
    for step in range(ITERS):
        image = apply_fine(search)
        alpha = rho / lax.psum(jnp.sum(search * image, axis=1), ("grp", "sub", "chip"))
        solution = solution + alpha[:, None] * search
        residual = residual - alpha[:, None] * image
        if step + 1 < ITERS:
            pre = precondition(residual)
            rho_next = inner_products(residual, pre)
            search = pre + (rho_next / rho)[:, None] * search
            rho = rho_next
    return (solution, residual)


def solution(mesh):
    placed = (
        P(None, ("grp", "sub", "chip")),
        P(("grp", "sub", "chip"), None, None),
        P(("grp", "sub", "chip"), None, None, None),
        P(("grp", "sub", "chip"), None),
        P(("grp", "sub", "chip"), None, None),
        P(("grp", "sub", "chip")),
        P("grp"),
        P("grp", None, None),
        P(),
    )
    return jax.shard_map(
        on_device,
        mesh=mesh,
        in_specs=placed,
        out_specs=(P(None, ("grp", "sub", "chip")), P(None, ("grp", "sub", "chip"))),
        check_vma=False,
    )
```

profile of v0, /device:TPU:1, one launch (start us, length us, event | category | flops | bytes accessed | tf_op | source)
XLA Modules:
  0.0 597.1 jit_solution(2620536431267968904)
XLA Ops:
  1.7 7.0 %copy.52 = f32[64,128,128]{0,2,1:T(8,128)} copy(f32[64,128,128]{2,1,0:T(8,128)} %param.12) | data formatting | bytes 8388608 | tf_op args[1]
  17.1 8.4 %all-to-all-start = ((f32[64,16,2,128]{3,0,2,1:T(8,128)}), f32[64,16,2,128]{3,0,2,1:T(8,128)S(1)}, u32[]{:S(2)}, u32[]{:S(2)}) async-start(f32[64,16,2,128]{3,0,2,1:T(8,128)} %bitcast.217), calls=%async_computation | async-start | bytes 2097152 | tf_op jit(solution)/shard_map/all_to_all | solution.py:29
  25.6 17.3 %gather_fusion.1 = f32[1024]{0:T(1024)S(1)} fusion(f32[1024,1024]{1,0:T(8,128)} %bitcast.214, s32[1024]{0:T(1024)S(1)} %bitcast.215), kind=kCustom, calls=%fused_computation.7 | custom fusion | bytes 16384 | tf_op jit(solution)/shard_map/jit(diagonal)/cond/branch_0_fun/gather | solution.py:77
  43.1 6.9 %convolution_bitcast_fusion.5 = f32[64,64,128]{2,0,1:T(8,128)} fusion(f32[64,128,128]{2,1,0:T(8,128)} %param.12, f32[8192]{0:T(1024)S(1)} %bitcast.230, f32[64,8192]{1,0:T(8,128)} %param.11), kind=kOutput, calls=%fused_computation.56 | convolution fusion | flops 806354944 | bytes 8421376 | tf_op jit(solution)/shard_map/kbt,bts->kbs/dot_general | solution.py:26
  62.1 34.9 %all_gather.12 = f32[64,1024]{0,1:T(8,128)S(1)} all-gather(f32[64,64]{0,1:T(8,128)S(1)} %fusion.12), channel_id=1, replica_groups=mesh['grp'=8,'sub'=8,'chip'=2] {'sub','chip'}, dimensions={1}, use_global_device_ids=true | all-gather | bytes 278528 | tf_op jit(solution)/shard_map/all_gather | solution.py:80
  102.5 22.0 %all_gather.13 = f32[64,512]{0,1:T(8,128)S(1)} all-gather(f32[64,64]{0,1:T(8,128)S(1)} %fusion.27), channel_id=1, replica_groups=mesh['grp'=8,'sub'=8,'chip'=2] {'grp'}, dimensions={1}, use_global_device_ids=true | all-gather | bytes 147456 | tf_op jit(solution)/shard_map/all_gather | solution.py:83
  140.4 7.9 %convolution_bitcast_fusion.4 = f32[64,64,128]{2,0,1:T(8,128)} fusion(f32[64,128,128]{2,1,0:T(8,128)} %param.12, f32[64,8192]{1,0:T(8,128)} %copy-done.7), kind=kOutput, calls=%fused_computation.55 | convolution fusion | flops 805306368 | bytes 8388608 | tf_op jit(solution)/shard_map/kbt,bts->kbs/dot_general | solution.py:26
  148.3 10.1 %all-to-all-done.1 = f32[64,16,2,128]{3,0,2,1:T(8,128)S(1)} async-done(((f32[64,16,2,128]{3,0,2,1:T(8,128)}), f32[64,16,2,128]{3,0,2,1:T(8,128)S(1)}, u32[]{:S(2)}, u32[]{:S(2)}) %all-to-all-start.1) | async-done | bytes 1048608 | tf_op jit(solution)/shard_map/all_to_all | solution.py:29
  180.6 7.9 %convolution_bitcast_fusion.3 = f32[64,64,128]{2,0,1:T(8,128)} fusion(f32[64,128,128]{2,1,0:T(8,128)} %param.12, f32[64,8192]{1,0:T(8,128)} %copy-done.1), kind=kOutput, calls=%fused_computation.54 | convolution fusion | flops 805306368 | bytes 8388608 | tf_op jit(solution)/shard_map/kbt,bts->kbs/dot_general | solution.py:26
  188.5 7.6 %all-to-all-done.2 = f32[64,16,2,128]{3,0,2,1:T(8,128)S(1)} async-done(((f32[64,16,2,128]{3,0,2,1:T(8,128)}), f32[64,16,2,128]{3,0,2,1:T(8,128)S(1)}, u32[]{:S(2)}, u32[]{:S(2)}) %all-to-all-start.2) | async-done | bytes 1048608 | tf_op jit(solution)/shard_map/all_to_all | solution.py:29
  207.8 65.3 %all-reduce = (f32[64]{0:T(128)S(1)}, f32[64]{0:T(128)S(1)}) all-reduce(f32[64]{0:T(128)S(1)} %get-tuple-element.4, f32[64]{0:T(128)S(1)} %get-tuple-element.3), channel_id=1, replica_groups=mesh['grp'=8,'sub'=8,'chip'=2] {'grp','sub','chip'}, use_global_device_ids=true, to_apply=%region_3.5 | all-reduce | flops 128 | bytes 1024 | tf_op jit(solution)/shard_map/psum | solution.py:46
  287.3 7.9 %convolution_bitcast_fusion.2 = f32[64,64,128]{2,0,1:T(8,128)} fusion(f32[64,128,128]{2,1,0:T(8,128)} %param.12, f32[8,64,8,128]{3,2,1,0:T(8,128)} %copy-done.8), kind=kOutput, calls=%fused_computation.53 | convolution fusion | flops 805306368 | bytes 8388608 | tf_op jit(solution)/shard_map/kbt,bts->kbs/dot_general | solution.py:26
  295.2 8.1 %all-to-all-done.3 = f32[64,16,2,128]{3,0,2,1:T(8,128)S(1)} async-done(((f32[64,16,2,128]{3,0,2,1:T(8,128)}), f32[64,16,2,128]{3,0,2,1:T(8,128)S(1)}, u32[]{:S(2)}, u32[]{:S(2)}) %all-to-all-start.3) | async-done | bytes 1048608 | tf_op jit(solution)/shard_map/all_to_all | solution.py:29
  315.4 33.3 %all_gather.14 = f32[64,1024]{0,1:T(8,128)S(1)} all-gather(f32[64,64]{0,1:T(8,128)S(1)} %fusion.5), channel_id=1, replica_groups=mesh['grp'=8,'sub'=8,'chip'=2] {'sub','chip'}, dimensions={1}, use_global_device_ids=true | all-gather | bytes 278528 | tf_op jit(solution)/shard_map/all_gather | solution.py:80
  354.1 22.4 %all_gather.15 = f32[64,512]{0,1:T(8,128)S(1)} all-gather(f32[64,64]{0,1:T(8,128)S(1)} %fusion.26), channel_id=1, replica_groups=mesh['grp'=8,'sub'=8,'chip'=2] {'grp'}, dimensions={1}, use_global_device_ids=true | all-gather | bytes 147456 | tf_op jit(solution)/shard_map/all_gather | solution.py:83
  392.3 7.9 %convolution_bitcast_fusion.1 = f32[64,64,128]{2,0,1:T(8,128)} fusion(f32[64,128,128]{2,1,0:T(8,128)} %param.12, f32[64,8192]{1,0:T(8,128)} %copy-done.6), kind=kOutput, calls=%fused_computation.52 | convolution fusion | flops 805306368 | bytes 8388608 | tf_op jit(solution)/shard_map/kbt,bts->kbs/dot_general | solution.py:26
  400.2 10.1 %all-to-all-done.4 = f32[64,16,2,128]{3,0,2,1:T(8,128)S(1)} async-done(((f32[64,16,2,128]{3,0,2,1:T(8,128)}), f32[64,16,2,128]{3,0,2,1:T(8,128)S(1)}, u32[]{:S(2)}, u32[]{:S(2)}) %all-to-all-start.4) | async-done | bytes 1048608 | tf_op jit(solution)/shard_map/all_to_all | solution.py:29
  413.3 5.4 scatter_fusion.4
  423.5 63.4 %psum.30 = f32[64]{0:T(128)S(1)} all-reduce(f32[64]{0:T(128)S(1)} %get-tuple-element.7), channel_id=1, replica_groups=mesh['grp'=8,'sub'=8,'chip'=2] {'grp','sub','chip'}, use_global_device_ids=true, to_apply=%region_10.12 | all-reduce | flops 64 | bytes 512 | tf_op jit(solution)/shard_map/psum | solution.py:46
  498.1 8.7 %convolution_bitcast_fusion = f32[64,64,128]{2,0,1:T(8,128)} fusion(f32[64,128,128]{2,1,0:T(8,128)} %param.12, f32[64,8192]{1,0:T(8,128)} %get-tuple-element.8, f32[64,8192]{1,0:T(8,128)} %copy-done.1, f32[64]{0:T(128)S(1)} %div.75), kind=kOutput, calls=%fused_computation.51 | convolution fusion | flops 806354944 | bytes 10486016 | tf_op jit(solution)/shard_map/kbt,bts->kbs/dot_general | solution.py:26
  506.8 7.3 %all-to-all-done.5 = f32[64,16,2,128]{3,0,2,1:T(8,128)S(1)} async-done(((f32[64,16,2,128]{3,0,2,1:T(8,128)}), f32[64,16,2,128]{3,0,2,1:T(8,128)S(1)}, u32[]{:S(2)}, u32[]{:S(2)}) %all-to-all-start.5) | async-done | bytes 1048608 | tf_op jit(solution)/shard_map/all_to_all | solution.py:29
  517.1 5.4 scatter_fusion.5
  525.8 64.7 %psum.31 = f32[64]{0:T(128)S(1)} all-reduce(f32[64]{0:T(128)S(1)} %fusion), channel_id=1, replica_groups=mesh['grp'=8,'sub'=8,'chip'=2] {'grp','sub','chip'}, use_global_device_ids=true, to_apply=%region_13.15 | all-reduce | flops 64 | bytes 512 | tf_op jit(solution)/shard_map/psum | solution.py:104
  590.5 6.2 %fusion.1 = (f32[64,8192]{1,0:T(8,128)}, f32[64,8192]{1,0:T(8,128)}) fusion(f32[64,8192]{1,0:T(8,128)} %get-tuple-element.10, f32[64]{0:T(128)S(1)} %div.76, f32[64,8192]{1,0:T(8,128)} %get-tuple-element.8, f32[64,8192]{1,0:T(8,128)} %copy-done.1, f32[64]{0:T(128)S(1)} %div.75, f32[64]{0:T(128)S(1)} %div.70, f32[64,64,128]{2,0,1:T(8,128)} %scatter_fusion.5), kind=kLoop, calls=%fused_computation.19 | loop fusion | flops 3670016 | bytes 12583680 | tf_op jit(solution)/shard_map/sub | solution.py:106
  (95 shorter events, 149.5 us)
Async XLA Ops:
  0.6 49.4 %copy-start = (f32[16,2,128,128]{3,2,1,0:T(8,128)S(1)}, f32[16,2,128,128]{3,2,1,0:T(8,128)}, u32[]{:S(2)}) copy-start(f32[16,2,128,128]{3,2,1,0:T(8,128)} %param.13) | copy-start | bytes 6291460
  17.1 32.9 %all-to-all-start = ((f32[64,16,2,128]{3,0,2,1:T(8,128)}), f32[64,16,2,128]{3,0,2,1:T(8,128)S(1)}, u32[]{:S(2)}, u32[]{:S(2)}) async-start(f32[64,16,2,128]{3,0,2,1:T(8,128)} %bitcast.217), calls=%async_computation | async-start | bytes 2097152 | tf_op jit(solution)/shard_map/all_to_all | solution.py:29
  25.6 17.4 %copy-start.11 = (s32[1,16]{1,0:T(1,128)S(1)}, s32[1,16]{1,0:T(1,128)}, u32[]{:S(2)}) copy-start(s32[1,16]{1,0:T(1,128)} %param.14) | copy-start | bytes 196
  53.0 5.4 copy-start.9
  97.2 5.0 copy-start.10
  97.2 29.2 %copy-start.2 = (f32[1,1024,1024]{2,1,0:T(8,128)S(1)}, f32[1,1024,1024]{2,1,0:T(8,128)}, u32[]{:S(2)}) copy-start(f32[1,1024,1024]{2,1,0:T(8,128)} %param.18) | copy-start | bytes 12582916
  126.4 2.7 copy-start.4
  130.5 1.3 copy-start.7
  136.7 21.7 %all-to-all-start.1 = ((f32[64,16,2,128]{3,0,2,1:T(8,128)}), f32[64,16,2,128]{3,0,2,1:T(8,128)S(1)}, u32[]{:S(2)}, u32[]{:S(2)}) async-start(f32[64,16,2,128]{3,0,2,1:T(8,128)} %bitcast.220), calls=%async_computation.1 | async-start | bytes 2097152 | tf_op jit(solution)/shard_map/all_to_all | solution.py:29
  170.1 1.3 copy-start.1
  176.4 19.8 %all-to-all-start.2 = ((f32[64,16,2,128]{3,0,2,1:T(8,128)}), f32[64,16,2,128]{3,0,2,1:T(8,128)S(1)}, u32[]{:S(2)}, u32[]{:S(2)}) async-start(f32[64,16,2,128]{3,0,2,1:T(8,128)} %bitcast.221), calls=%async_computation.2 | async-start | bytes 2097152 | tf_op jit(solution)/shard_map/all_to_all | solution.py:29
  277.1 2.0 copy-start.8
  282.5 20.8 %all-to-all-start.3 = ((f32[64,16,2,128]{3,0,2,1:T(8,128)}), f32[64,16,2,128]{3,0,2,1:T(8,128)S(1)}, u32[]{:S(2)}, u32[]{:S(2)}) async-start(f32[64,16,2,128]{3,0,2,1:T(8,128)} %bitcast.218), calls=%async_computation.3 | async-start | bytes 2097152 | tf_op jit(solution)/shard_map/all_to_all | solution.py:29
  348.8 29.6 %copy-start.3 = (f32[1,1024,1024]{2,1,0:T(8,128)S(1)}, f32[1,1024,1024]{2,1,0:T(8,128)}, u32[]{:S(2)}) copy-start(f32[1,1024,1024]{2,1,0:T(8,128)} %param.18) | copy-start | bytes 12582916
  378.4 2.7 copy-start.5
  382.4 1.3 copy-start.6
  388.6 21.7 %all-to-all-start.4 = ((f32[64,16,2,128]{3,0,2,1:T(8,128)}), f32[64,16,2,128]{3,0,2,1:T(8,128)S(1)}, u32[]{:S(2)}, u32[]{:S(2)}) async-start(f32[64,16,2,128]{3,0,2,1:T(8,128)} %bitcast.222), calls=%async_computation.4 | async-start | bytes 2097152 | tf_op jit(solution)/shard_map/all_to_all | solution.py:29
  494.1 20.0 %all-to-all-start.5 = ((f32[64,16,2,128]{3,0,2,1:T(8,128)}), f32[64,16,2,128]{3,0,2,1:T(8,128)S(1)}, u32[]{:S(2)}, u32[]{:S(2)}) async-start(f32[64,16,2,128]{3,0,2,1:T(8,128)} %bitcast.219), calls=%async_computation.5 | async-start | bytes 2097152 | tf_op jit(solution)/shard_map/all_to_all | solution.py:29
where the time goes:
time: 607 us; the launch traced here: 597 us
  blocking collectives  306 us (50%)
  matrix products  94.9 us (16%)
  other arithmetic  71.4 us (12%)
  local copies, waits for them, and re-layouts  51.6 us (9%)
  waiting for transfers between devices  43.2 us (7%)
  starting transfers between devices  28.8 us (5%)
    psum x2, blocking collectives, inner_products(): return lax.psum(jnp.sum(resid * pre, axis=1), ('grp', 'sub', 'chip'))  129 us
    all_gather x2, blocking collectives, level_one(): gathered = lax.all_gather(coarse_resid, ('sub', 'chip'), axis=1, tiled=True)  68.1 us
    psum x1, blocking collectives, on_device(): lax.psum(jnp.sum(search * image, axis=1), ('grp', 'sub', 'chip'))  64.7 us
    dot_general x6, matrix products, fine_apply(): result = jnp.einsum('kbt,bts->kbs', shaped, diag_tiles, precision=HIGH)  47.4 us
    all_gather x2, blocking collectives, level_one(): lax.all_gather(restrict(left, spread_coarse), 'grp', axis=1, tiled=True)  44.4 us
    all_to_all x6, waiting for transfers between devices, fine_apply(): lax.all_to_all(outgoing, ('sub', 'chip'), split_axis=1, concat_axis=1, ti...  43.2 us
    scatter-add x6, other arithmetic, fine_apply(): result.at[:, slot_list]  32.6 us
    all_to_all x6, starting transfers between devices, fine_apply(): lax.all_to_all(outgoing, ('sub', 'chip'), split_axis=1, concat_axis=1, ti...  28.8 us
  transfers between devices with their start and end apart: 6, of which 5 were waited for; matrix products, arithmetic and copies ran while one was open for 11% of the time, Pallas kernels for 0%

commit v1 on v0

v1 whole, which is shorter than its diff:
```python
import functools

import jax
import jax.numpy as jnp
from jax import lax
from jax.experimental import pallas as pl
from jax.experimental.pallas import tpu as pltpu
from jax.sharding import PartitionSpec as P

OMEGA = 0.6
F32 = jnp.float32
BF16 = jnp.bfloat16
COLS = 64
TILE = 128
BLK = 64
SLOTS = 32
PEERS = 16
GROUPS = 8
AGG = 64
NC1 = 1024
STEP = 4
NSTEP = SLOTS // STEP
SIDE = 72
ROWS = 40
VMEM_LIMIT = 56 * 1024 * 1024

GROUP_AXES = ("sub", "chip")
ALL_AXES = ("grp", "sub", "chip")


def params():
    return pltpu.CompilerParams(vmem_limit_bytes=VMEM_LIMIT)


def cost(flops, moved):
    return pl.CostEstimate(flops=flops, bytes_accessed=moved, transcendentals=0)


def split2(x):
    hi = x.astype(BF16)
    lo = (x - hi.astype(F32)).astype(BF16)
    return hi, lo


def split3(x):
    hi = x.astype(BF16)
    rest = x - hi.astype(F32)
    mid = rest.astype(BF16)
    lo = (rest - mid.astype(F32)).astype(BF16)
    return hi, mid, lo


def dot(a, b):
    return jnp.dot(a, b, preferred_element_type=F32)


def dot_nt(a, b):
    return lax.dot_general(a, b, (((1,), (1,)), ((), ())), preferred_element_type=F32)


def mm(x, whi, wlo, nt=False):
    op = dot_nt if nt else dot
    rows = x.shape[0]
    hi, lo = split2(x)
    both = op(jnp.concatenate([hi, lo], axis=0), whi)
    return both[:rows] + both[rows:] + op(hi, wlo)


def mm_exact(x, w, nt=False):
    op = dot_nt if nt else dot
    rows = x.shape[0]
    hi, mid, lo = split3(x)
    three = op(jnp.concatenate([hi, mid, lo], axis=0), w)
    return three[:rows] + three[rows : 2 * rows] + three[2 * rows :]


def exact_mm(w, x):
    hi, mid, lo = split3(x)
    return dot(w, hi) + dot(w, mid) + dot(w, lo)


def eye_mask():
    r = lax.broadcasted_iota(jnp.int32, (TILE, TILE), 0)
    c = lax.broadcasted_iota(jnp.int32, (TILE, TILE), 1)
    return r, c


def tile_diag(tile):
    r, c = eye_mask()
    return jnp.sum(jnp.where(r == c, tile, 0.0), axis=0, keepdims=True)


def off_diag(tile):
    r, c = eye_mask()
    return jnp.where(r == c, 0.0, tile)


def one_hot(row):
    r = lax.broadcasted_iota(jnp.int32, (AGG, row.shape[1]), 0)
    return jnp.where(r == row, 1.0, 0.0).astype(BF16)


def pack_rows(x):
    wide = jnp.concatenate([x[:32], x[32:]], axis=1)
    return wide


def column(row):
    return jnp.broadcast_to(row, (TILE, TILE)).T


def boundary_kernel(slots, *refs):
    tiles, cols, maps, first, second = refs[:STEP], refs[STEP : 2 * STEP], refs[2 * STEP], refs[-2], refs[-1]
    step = pl.program_id(0)
    for i in range(STEP):
        tile = tiles[i][0]
        diag = tile_diag(tile)
        first[i] = OMEGA * cols[i][...] / diag
        r = lax.broadcasted_iota(jnp.int32, (64, TILE), 0)
        c = lax.broadcasted_iota(jnp.int32, (64, TILE), 1)
        below = pltpu.roll(tile[64:], 64, 1)
        second[i, 0:64] = jnp.where((c < 64) & (r > c), below, tile[:64])
        row = maps[slots[step * STEP + i]].astype(F32)
        r8 = lax.broadcasted_iota(jnp.int32, (8, TILE), 0)
        second[i, 64:72] = jnp.where(r8 == 0, diag, jnp.where(r8 == 1, row, 0.0))


def boundary_pack(slot_list, diag_tiles, right_side, maps):
    def tile_spec(i):
        return pl.BlockSpec((1, TILE, TILE), lambda s, p: (p[s * STEP + i], 0, 0))

    def col_spec(i):
        return pl.BlockSpec((COLS, TILE), lambda s, p: (0, p[s * STEP + i]))

    grid = pltpu.PrefetchScalarGridSpec(
        num_scalar_prefetch=1,
        grid=(NSTEP,),
        in_specs=[tile_spec(i) for i in range(STEP)]
        + [col_spec(i) for i in range(STEP)]
        + [pl.BlockSpec((BLK, 1, TILE), lambda s, p: (0, 0, 0))],
        out_specs=[
            pl.BlockSpec((STEP, COLS, TILE), lambda s, p: (s, 0, 0)),
            pl.BlockSpec((STEP, SIDE, TILE), lambda s, p: (s, 0, 0)),
        ],
    )
    return pl.pallas_call(
        boundary_kernel,
        grid_spec=grid,
        out_shape=[
            jax.ShapeDtypeStruct((SLOTS, COLS, TILE), F32),
            jax.ShapeDtypeStruct((SLOTS, SIDE, TILE), F32),
        ],
        compiler_params=params(),
        name="boundary_pack",
    )(slot_list, *([diag_tiles] * STEP), *([right_side] * STEP), maps)


def local_kernel(perm, counts, *refs):
    n = 2 * STEP
    tiles, cols = refs[:n], refs[n : 2 * n]
    remote, maps = refs[2 * n : 2 * n + 2]
    b_slot, b_rest, d_slot, d_rest, hi_rest, lo_rest, rs, rr = refs[2 * n + 2 :]
    step = pl.program_id(0)

    @pl.when(step == 0)
    def _():
        rr[...] = jnp.zeros_like(rr)

    total = rr[...]
    for i in range(n):
        tile = tiles[i][0]
        diag = tile_diag(tile)
        off_hi, off_lo = split2(off_diag(tile))
        b = cols[i][...]
        x = OMEGA * b / diag
        y = b - OMEGA * b - mm(x, off_hi, off_lo)
        slot = i < STEP
        k = i % STEP
        index = perm[(0 if slot else SLOTS) + step * STEP + k]
        spread = one_hot(maps[index])
        total = total + mm_exact(y, spread, nt=True)
        if slot:
            b_slot[k] = b
            d_slot[k] = diag
            j = step * STEP + k
            live = (j % 2) < counts[j // 2]
            rem = remote[k] * jnp.where(live, 1.0, 0.0)
            hi, lo = split2(rem)
            rs[k] = dot_nt(spread, hi) + dot_nt(spread, lo)
        else:
            b_rest[k] = b
            d_rest[k] = diag
            hi_rest[k] = off_hi
            lo_rest[k] = off_lo
    rr[...] = total


def local_part(perm, counts, diag_tiles, right_side, remote, maps):
    def where(i):
        return (0 if i < STEP else SLOTS) + i % STEP

    def tile_spec(i):
        return pl.BlockSpec((1, TILE, TILE), lambda s, p, c: (p[s * STEP + where(i)], 0, 0))

    def col_spec(i):
        return pl.BlockSpec((COLS, TILE), lambda s, p, c: (0, p[s * STEP + where(i)]))

    def out(*shape):
        return pl.BlockSpec((STEP,) + shape, lambda s, p, c: (s, 0, 0))

    n = 2 * STEP
    grid = pltpu.PrefetchScalarGridSpec(
        num_scalar_prefetch=2,
        grid=(NSTEP,),
        in_specs=[tile_spec(i) for i in range(n)]
        + [col_spec(i) for i in range(n)]
        + [
            pl.BlockSpec((STEP, TILE, TILE), lambda s, p, c: (s, 0, 0)),
            pl.BlockSpec((BLK, 1, TILE), lambda s, p, c: (0, 0, 0)),
        ],
        out_specs=[
            out(COLS, TILE),
            out(COLS, TILE),
            out(1, TILE),
            out(1, TILE),
            out(TILE, TILE),
            out(TILE, TILE),
            out(AGG, TILE),
            pl.BlockSpec((COLS, AGG), lambda s, p, c: (0, 0)),
        ],
    )

    def sds(shape, dtype=F32):
        return jax.ShapeDtypeStruct((SLOTS,) + shape, dtype)

    return pl.pallas_call(
        local_kernel,
        grid_spec=grid,
        out_shape=[
            sds((COLS, TILE)),
            sds((COLS, TILE)),
            sds((1, TILE)),
            sds((1, TILE)),
            sds((TILE, TILE), BF16),
            sds((TILE, TILE), BF16),
            sds((AGG, TILE)),
            jax.ShapeDtypeStruct((COLS, AGG), F32),
        ],
        compiler_params=params(),
        cost_estimate=cost(2 * 64 * 3 * 64 * 128 * 128, 16 << 20),
        name="local_part",
    )(perm, counts, *([diag_tiles] * n), *([right_side] * n), remote, maps)


def coarse_kernel(op, cmap, g_out, d_out):
    spread = one_hot(cmap[...])
    product = exact_spread(spread, op)
    pieces = []
    for i in range(NC1 // TILE):
        pieces.append(tile_diag(op[i * TILE : (i + 1) * TILE, i * TILE : (i + 1) * TILE]))
    diag = jnp.concatenate(pieces, axis=1)
    inverse = 1.0 / diag
    d_out[...] = inverse
    g_out[...] = spread.astype(F32) - OMEGA * product * inverse


def exact_spread(spread, op):
    total = None
    for i in range(NC1 // 256):
        rows = slice(i * 256, (i + 1) * 256)
        hi, lo = split2(op[rows, :])
        part = dot(spread[:, rows], hi) + dot(spread[:, rows], lo)
        total = part if total is None else total + part
    return total


def coarse_setup(op, cmap):
    return pl.pallas_call(
        coarse_kernel,
        out_shape=[jax.ShapeDtypeStruct((AGG, NC1), F32), jax.ShapeDtypeStruct((1, NC1), F32)],
        compiler_params=params(),
        cost_estimate=cost(2 * 2 * 64 * 1024 * 1024, 5 << 20),
        name="coarse_setup",
    )(op, cmap)


def first_restrict_kernel(arrived, rs, rr, out):
    total = rr[...]
    for j in range(SLOTS):
        hi, lo = split2(rs[j])
        total = total + mm(arrived[j], hi, lo, nt=True)
    packed = pack_rows(total)
    for q in range(PEERS):
        out[q, 0:32] = packed
        out[q, 32:40] = jnp.zeros((8, TILE), F32)


def first_restrict(arrived, rs, rr):
    return pl.pallas_call(
        first_restrict_kernel,
        out_shape=jax.ShapeDtypeStruct((PEERS, ROWS, TILE), F32),
        compiler_params=params(),
        name="first_restrict",
    )(arrived, rs, rr)


def pair_kernel(perm, counts, *refs):
    tiles, side, remote, hi_out, lo_out, diag_out, map_out = (refs[:STEP],) + tuple(refs[STEP:])
    step = pl.program_id(0)
    r = lax.broadcasted_iota(jnp.int32, (64, TILE), 0)
    c = lax.broadcasted_iota(jnp.int32, (64, TILE), 1)
    for k in range(STEP):
        own = off_diag(tiles[k][0])
        packed = side[k, 0:64]
        top = jnp.where((c >= 64) | (r < c), packed, 0.0)
        bottom = pltpu.roll(jnp.where((c < 64) & (r > c), packed, 0.0), 64, 1)
        half = jnp.concatenate([top, bottom], axis=0)
        other = half + half.T
        j = step * STEP + k
        live = (j % 2) < counts[j // 2]
        rem = remote[k] * jnp.where(live, -1.0, 0.0)
        block = jnp.concatenate(
            [jnp.concatenate([own, rem.T], axis=1), jnp.concatenate([rem, other], axis=1)], axis=0
        )
        hi, lo = split2(block)
        hi_out[k] = hi
        lo_out[k] = lo
        diag_out[k] = side[k, 64:65]
        map_out[k] = side[k, 65:66].astype(jnp.int32)


def pair_setup(perm, counts, diag_tiles, side, remote):
    def tile_spec(i):
        return pl.BlockSpec((1, TILE, TILE), lambda s, p, c: (p[s * STEP + i], 0, 0))

    def spec(*shape):
        return pl.BlockSpec((STEP,) + shape, lambda s, p, c: (s, 0, 0))

    grid = pltpu.PrefetchScalarGridSpec(
        num_scalar_prefetch=2,
        grid=(NSTEP,),
        in_specs=[tile_spec(i) for i in range(STEP)] + [spec(SIDE, TILE), spec(TILE, TILE)],
        out_specs=[spec(2 * TILE, 2 * TILE), spec(2 * TILE, 2 * TILE), spec(1, TILE), spec(1, TILE)],
    )
    return pl.pallas_call(
        pair_kernel,
        grid_spec=grid,
        out_shape=[
            jax.ShapeDtypeStruct((SLOTS, 2 * TILE, 2 * TILE), BF16),
            jax.ShapeDtypeStruct((SLOTS, 2 * TILE, 2 * TILE), BF16),
            jax.ShapeDtypeStruct((SLOTS, 1, TILE), F32),
            jax.ShapeDtypeStruct((SLOTS, 1, TILE), jnp.int32),
        ],
        compiler_params=params(),
        cost_estimate=cost(2 * 64 * 3 * 64 * 128 * 128, 16 << 20),
        name="pair_setup",
    )(perm, counts, *([diag_tiles] * STEP), side, remote)


def gathered_rows(ref, count):
    lane = lax.broadcasted_iota(jnp.int32, (32, TILE), 1) < 64
    tops, bottoms = [], []
    for q in range(0, count, 2):
        a, b = ref[q, 0:32], ref[q + 1, 0:32]
        tops.append(jnp.where(lane, a, pltpu.roll(b, 64, 1)))
        bottoms.append(jnp.where(lane, pltpu.roll(a, 64, 1), b))
    return jnp.concatenate([jnp.concatenate(tops, axis=1), jnp.concatenate(bottoms, axis=1)], axis=0)


def lowest_kernel(arrived, g, x_out, out):
    x = gathered_rows(arrived, PEERS)
    x_out[...] = x
    hi, lo = split2(g[...])
    packed = pack_rows(mm(x, hi, lo, nt=True))
    extra = arrived[0, 32:40]
    for q in range(1, PEERS):
        extra = extra + arrived[q, 32:40]
    for q in range(GROUPS):
        out[q, 0:32] = packed
        out[q, 32:40] = extra


def lowest_part(arrived, g):
    return pl.pallas_call(
        lowest_kernel,
        out_shape=[
            jax.ShapeDtypeStruct((COLS, NC1), F32),
            jax.ShapeDtypeStruct((GROUPS, ROWS, TILE), F32),
        ],
        compiler_params=params(),
        name="lowest_part",
    )(arrived, g)


def smooth_kernel(x_ref, inverse_ref, op, out):
    inverse = inverse_ref[...]
    scaled = x_ref[...] * inverse
    total = None
    for i in range(NC1 // 256):
        rows = slice(i * 256, (i + 1) * 256)
        hi, lo = split2(op[rows, :])
        part = mm(scaled[:, rows], hi, lo)
        total = part if total is None else total + part
    out[...] = 2.0 * OMEGA * scaled - OMEGA * OMEGA * total * inverse


def smooth_part(x, inverse, op):
    return pl.pallas_call(
        smooth_kernel,
        out_shape=jax.ShapeDtypeStruct((COLS, NC1), F32),
        compiler_params=params(),
        cost_estimate=cost(2 * 3 * 64 * 1024 * 1024, 5 << 20),
        name="smooth_part",
    )(x, inverse, op)


def correct_kernel(arrived, inverse_cols, g, h, e_out, dots):
    low = gathered_rows(arrived, GROUPS)
    hi, lo = split2(inverse_cols[...])
    corr = mm(low, hi, lo)
    ghi, glo = split2(g[...])
    e = h[...] + mm(corr, ghi, glo)
    for q in range(PEERS):
        e_out[q] = e[:, q * AGG : (q + 1) * AGG]
    extra = arrived[0, 32:40]
    for q in range(1, GROUPS):
        extra = extra + arrived[q, 32:40]
    dots[...] = extra


def correct_part(arrived, inverse_cols, g, h):
    return pl.pallas_call(
        correct_kernel,
        out_shape=[jax.ShapeDtypeStruct((PEERS, COLS, AGG), F32), jax.ShapeDtypeStruct((8, TILE), F32)],
        compiler_params=params(),
        name="correct_part",
    )(arrived, inverse_cols, g, h)


def apply_block(x, diag, hi, lo):
    xh, xl = split2(x)
    rows = x.shape[0]
    both = dot(jnp.concatenate([xh, xl], axis=0), hi)
    kept = xh.astype(F32) + xl.astype(F32)
    return both[:rows] + both[rows:] + dot(xh, lo) + kept[:, : diag.shape[1]] * diag


def lift(parts, row):
    rows = parts.shape[0] // 3
    three = dot(parts, one_hot(row))
    return three[:rows] + three[rows : 2 * rows] + three[2 * rows :]


def three_parts(e):
    return jnp.concatenate(split3(e), axis=0)


def forward_kernel(
    perm, member, e_own, e_peer, b_slot, b_rest, d_slot, d_rest, x_peer, d_peer, m_peer, hi_pair, lo_pair,
    hi_rest, lo_rest, maps, z_out, w_out, ws_out, out, acc_rr, acc_bz, acc_zw
):
    step = pl.program_id(0)

    @pl.when(step == 0)
    def _():
        acc_rr[...] = jnp.zeros_like(acc_rr)
        acc_bz[...] = jnp.zeros_like(acc_bz)
        acc_zw[...] = jnp.zeros_like(acc_zw)

    e_mine = three_parts(e_own[0])
    e_theirs = [three_parts(e_peer[q]) for q in range(STEP // 2)]
    rr, bz, zw = acc_rr[...], acc_bz[...], acc_zw[...]
    for k in range(STEP):
        index = perm[step * STEP + k]
        row = maps[index]
        diag = jnp.concatenate([d_slot[k], d_peer[k]], axis=1)
        rdiag = OMEGA / diag
        b_own = b_slot[k]
        xp = x_peer[k]
        b_full = jnp.concatenate([b_own, xp * (d_peer[k] * (1.0 / OMEGA))], axis=1)
        up = jnp.concatenate([lift(e_mine, row), lift(e_theirs[k // 2], m_peer[k])], axis=1)
        x = jnp.concatenate([b_own * rdiag[:, :TILE], xp], axis=1) + up
        hi, lo = hi_pair[k], lo_pair[k]
        z = x + (b_full - apply_block(x, diag, hi, lo)) * rdiag
        w = apply_block(z, diag, hi, lo)
        x1 = w * rdiag
        y = w[:, :TILE] - apply_block(x1, diag[:, :TILE], hi[:, :TILE], lo[:, :TILE])
        rr = rr + mm_exact(y, one_hot(row), nt=True)
        bz = bz + b_own * z[:, :TILE]
        zw = zw + z[:, :TILE] * w[:, :TILE]
        z_out[0, k] = z[:, :TILE]
        w_out[0, k] = w[:, :TILE]
        ws_out[k] = w[:, TILE:]
    for k in range(STEP):
        index = perm[SLOTS + step * STEP + k]
        row = maps[index]
        diag = d_rest[k]
        rdiag = OMEGA / diag
        b_own = b_rest[k]
        x = b_own * rdiag + lift(e_mine, row)
        hi, lo = hi_rest[k], lo_rest[k]
        z = x + (b_own - apply_block(x, diag, hi, lo)) * rdiag
        w = apply_block(z, diag, hi, lo)
        x1 = w * rdiag
        y = w - apply_block(x1, diag, hi, lo)
        rr = rr + mm_exact(y, one_hot(row), nt=True)
        bz = bz + b_own * z
        zw = zw + z * w
        z_out[1, k] = z
        w_out[1, k] = w
    acc_rr[...] = rr
    acc_bz[...] = bz
    acc_zw[...] = zw

    @pl.when(step == NSTEP - 1)
    def _():
        packed = pack_rows(rr)
        sums = jnp.sum(jnp.concatenate([bz, zw], axis=0).T, axis=0, keepdims=True)
        r8 = lax.broadcasted_iota(jnp.int32, (8, TILE), 0)
        extra = jnp.where(r8 == 0, sums, 0.0)
        for q in range(PEERS):
            out[q, 0:32] = packed
            out[q, 32:40] = extra


def step_spec(*shape):
    return pl.BlockSpec((STEP,) + shape, lambda s, p, m: (s, 0, 0))


def pair_spec():
    return pl.BlockSpec((2, STEP, COLS, TILE), lambda s, p, m: (0, s, 0, 0))


def e_specs():
    return [
        pl.BlockSpec((1, COLS, AGG), lambda s, p, m: (m[0], 0, 0)),
        pl.BlockSpec((STEP // 2, COLS, AGG), lambda s, p, m: (s, 0, 0)),
    ]


def forward_part(perm, member, e, b_slot, b_rest, d_slot, d_rest, x_peer, d_peer, m_peer, hi_pair, lo_pair, hi_rest, lo_rest, maps):
    grid = pltpu.PrefetchScalarGridSpec(
        num_scalar_prefetch=2,
        grid=(NSTEP,),
        in_specs=e_specs()
        + [
            step_spec(COLS, TILE),
            step_spec(COLS, TILE),
            step_spec(1, TILE),
            step_spec(1, TILE),
            step_spec(COLS, TILE),
            step_spec(1, TILE),
            step_spec(1, TILE),
            step_spec(2 * TILE, 2 * TILE),
            step_spec(2 * TILE, 2 * TILE),
            step_spec(TILE, TILE),
            step_spec(TILE, TILE),
            pl.BlockSpec((BLK, 1, TILE), lambda s, p, m: (0, 0, 0)),
        ],
        out_specs=[
            pair_spec(),
            pair_spec(),
            step_spec(COLS, TILE),
            pl.BlockSpec((PEERS, ROWS, TILE), lambda s, p, m: (0, 0, 0)),
        ],
        scratch_shapes=[pltpu.VMEM((COLS, AGG), F32), pltpu.VMEM((COLS, TILE), F32), pltpu.VMEM((COLS, TILE), F32)],
    )
    return pl.pallas_call(
        forward_kernel,
        grid_spec=grid,
        out_shape=[
            jax.ShapeDtypeStruct((2, SLOTS, COLS, TILE), F32),
            jax.ShapeDtypeStruct((2, SLOTS, COLS, TILE), F32),
            jax.ShapeDtypeStruct((SLOTS, COLS, TILE), F32),
            jax.ShapeDtypeStruct((PEERS, ROWS, TILE), F32),
        ],
        compiler_params=params(),
        name="forward_part",
    )(perm, member, e, e, b_slot, b_rest, d_slot, d_rest, x_peer, d_peer, m_peer, hi_pair, lo_pair, hi_rest, lo_rest, maps)


def second_kernel(
    perm, member, e_own, e_peer, dots, b_slot, b_rest, d_slot, d_rest, d_peer, m_peer, hi_pair, lo_pair,
    hi_rest, lo_rest, maps, z_in, w_in, w_peer, v_out, u_out, out, acc_a, acc_b, acc_c
):
    step = pl.program_id(0)

    @pl.when(step == 0)
    def _():
        acc_a[...] = jnp.zeros_like(acc_a)
        acc_b[...] = jnp.zeros_like(acc_b)
        acc_c[...] = jnp.zeros_like(acc_c)

    col = column(dots[0:1])
    alpha = col[:COLS] / col[COLS:]
    e_mine = three_parts(e_own[0])
    e_theirs = [three_parts(e_peer[q]) for q in range(STEP // 2)]
    sums = [acc_a[...], acc_b[...], acc_c[...]]

    def gather(b, z, w, v, u):
        r1 = b - alpha * w
        z1 = z - alpha * v
        az1 = w - alpha * u
        sums[0] = sums[0] + r1 * z1
        sums[1] = sums[1] + z1 * az1
        sums[2] = sums[2] + (z1 * w + z * az1)

    for k in range(STEP):
        row = maps[perm[step * STEP + k]]
        diag = jnp.concatenate([d_slot[k], d_peer[k]], axis=1)
        rdiag = OMEGA / diag
        w_own = w_in[0, k]
        w = jnp.concatenate([w_own, w_peer[k]], axis=1)
        up = jnp.concatenate([lift(e_mine, row), lift(e_theirs[k // 2], m_peer[k])], axis=1)
        x = w * rdiag + up
        hi, lo = hi_pair[k], lo_pair[k]
        v = x + (w - apply_block(x, diag, hi, lo)) * rdiag
        u = apply_block(v, diag[:, :TILE], hi[:, :TILE], lo[:, :TILE])
        v_own = v[:, :TILE]
        v_out[0, k] = v_own
        u_out[0, k] = u
        gather(b_slot[k], z_in[0, k], w_own, v_own, u)
    for k in range(STEP):
        row = maps[perm[SLOTS + step * STEP + k]]
        diag = d_rest[k]
        rdiag = OMEGA / diag
        w = w_in[1, k]
        x = w * rdiag + lift(e_mine, row)
        hi, lo = hi_rest[k], lo_rest[k]
        v = x + (w - apply_block(x, diag, hi, lo)) * rdiag
        u = apply_block(v, diag, hi, lo)
        v_out[1, k] = v
        u_out[1, k] = u
        gather(b_rest[k], z_in[1, k], w, v, u)
    acc_a[...] = sums[0]
    acc_b[...] = sums[1]
    acc_c[...] = sums[2]

    @pl.when(step == NSTEP - 1)
    def _():
        first = jnp.sum(jnp.concatenate([sums[0], sums[1]], axis=0).T, axis=0, keepdims=True)
        last = jnp.sum(jnp.concatenate([sums[2], sums[2]], axis=0).T, axis=0, keepdims=True)
        r8 = lax.broadcasted_iota(jnp.int32, (8, TILE), 0)
        extra = jnp.where(r8 == 0, first, jnp.where(r8 == 1, last, 0.0))
        for q in range(GROUPS * PEERS):
            out[q] = extra


def second_part(perm, member, e, dots, b_slot, b_rest, d_slot, d_rest, d_peer, m_peer, hi_pair, lo_pair, hi_rest, lo_rest, maps, z, w, w_peer):
    grid = pltpu.PrefetchScalarGridSpec(
        num_scalar_prefetch=2,
        grid=(NSTEP,),
        in_specs=e_specs()
        + [
            pl.BlockSpec((8, TILE), lambda s, p, m: (0, 0)),
            step_spec(COLS, TILE),
            step_spec(COLS, TILE),
            step_spec(1, TILE),
            step_spec(1, TILE),
            step_spec(1, TILE),
            step_spec(1, TILE),
            step_spec(2 * TILE, 2 * TILE),
            step_spec(2 * TILE, 2 * TILE),
            step_spec(TILE, TILE),
            step_spec(TILE, TILE),
            pl.BlockSpec((BLK, 1, TILE), lambda s, p, m: (0, 0, 0)),
            pair_spec(),
            pair_spec(),
            step_spec(COLS, TILE),
        ],
        out_specs=[
            pair_spec(),
            pair_spec(),
            pl.BlockSpec((GROUPS * PEERS, 8, TILE), lambda s, p, m: (0, 0, 0)),
        ],
        scratch_shapes=[pltpu.VMEM((COLS, TILE), F32)] * 3,
    )
    return pl.pallas_call(
        second_kernel,
        grid_spec=grid,
        out_shape=[
            jax.ShapeDtypeStruct((2, SLOTS, COLS, TILE), F32),
            jax.ShapeDtypeStruct((2, SLOTS, COLS, TILE), F32),
            jax.ShapeDtypeStruct((GROUPS * PEERS, 8, TILE), F32),
        ],
        compiler_params=params(),
        name="second_part",
    )(perm, member, e, e, dots, b_slot, b_rest, d_slot, d_rest, d_peer, m_peer, hi_pair, lo_pair, hi_rest, lo_rest, maps, z, w, w_peer)


def combine_kernel(perm, dots, arrived, b_slot, b_rest, z, w, v, u, solution, residual, coef):
    step = pl.program_id(0)

    @pl.when(step == 0)
    def _():
        total = arrived[0]
        for q in range(1, GROUPS * PEERS):
            total = total + arrived[q]
        old = column(dots[0:1])
        one = column(total[0:1])
        two = column(total[1:2])
        rho, zw = old[:COLS], old[COLS:]
        rho_next, zz = one[:COLS], one[COLS:]
        cross = two[:COLS]
        alpha = rho / zw
        beta = rho_next / rho
        alpha_next = rho_next / (zz + beta * cross + beta * beta * zw)
        coef[0] = alpha
        coef[1] = beta
        coef[2] = alpha_next

    alpha, beta, alpha_next = coef[0], coef[1], coef[2]
    for half, b_ref in ((0, b_slot), (1, b_rest)):
        for k in range(STEP):
            index = perm[half * SLOTS + step * STEP + k]
            at = pl.ds(pl.multiple_of(index * TILE, TILE), TILE)
            z0, w0 = z[half, k], w[half, k]
            z1 = z0 - alpha * v[half, k]
            az1 = w0 - alpha * u[half, k]
            solution[:, at] = alpha * z0 + alpha_next * (z1 + beta * z0)
            residual[:, at] = b_ref[k] - alpha * w0 - alpha_next * (az1 + beta * w0)


def combine(perm, dots, arrived, b_slot, b_rest, z, w, v, u):
    def pair():
        return pl.BlockSpec((2, STEP, COLS, TILE), lambda s, p: (0, s, 0, 0))

    def single():
        return pl.BlockSpec((STEP, COLS, TILE), lambda s, p: (s, 0, 0))

    def whole():
        return pl.BlockSpec((COLS, BLK * TILE), lambda s, p: (0, 0))

    grid = pltpu.PrefetchScalarGridSpec(
        num_scalar_prefetch=1,
        grid=(NSTEP,),
        in_specs=[
            pl.BlockSpec((8, TILE), lambda s, p: (0, 0)),
            pl.BlockSpec((GROUPS * PEERS, 8, TILE), lambda s, p: (0, 0, 0)),
            single(),
            single(),
            pair(),
            pair(),
            pair(),
            pair(),
        ],
        out_specs=[whole(), whole()],
        scratch_shapes=[pltpu.VMEM((3, COLS, TILE), F32)],
    )
    return pl.pallas_call(
        combine_kernel,
        grid_spec=grid,
        out_shape=[jax.ShapeDtypeStruct((COLS, BLK * TILE), F32)] * 2,
        compiler_params=params(),
        name="combine",
    )(perm, dots, arrived, b_slot, b_rest, z, w, v, u)


def exchange(x, axes):
    return lax.all_to_all(x, axes, 0, 0, tiled=True)


def on_device(
    right_side,
    diag_tiles,
    remote_tiles,
    slot_counts,
    slot_blocks,
    fine_map,
    coarse_map,
    level1_ops,
    coarsest_inverse,
):
    group = lax.axis_index("grp")
    member = lax.axis_index(GROUP_AXES).astype(jnp.int32).reshape(1)
    slot_list = slot_blocks.reshape(SLOTS)
    counts = slot_counts.reshape(PEERS)
    maps = fine_map.reshape(BLK, 1, TILE)
    remote = remote_tiles.reshape(SLOTS, TILE, TILE)
    operator = level1_ops[0]

    first, second = boundary_pack(slot_list, diag_tiles, right_side, maps)
    x_peer = exchange(first.reshape(PEERS, 2 * COLS, TILE), GROUP_AXES).reshape(SLOTS, COLS, TILE)
    side = exchange(second.reshape(PEERS, 2 * SIDE, TILE), GROUP_AXES).reshape(SLOTS, SIDE, TILE)

    tile_ids = jnp.arange(BLK, dtype=jnp.int32)
    free = jnp.logical_not(jnp.any(slot_list[:, None] == tile_ids[None, :], axis=0)).astype(jnp.int32)
    rank = jnp.sum(jnp.where(tile_ids[None, :] < tile_ids[:, None], free[None, :], 0), axis=1)
    chosen = (rank[None, :] == jnp.arange(SLOTS, dtype=jnp.int32)[:, None]) & (free[None, :] == 1)
    rest_list = jnp.sum(jnp.where(chosen, tile_ids[None, :], 0), axis=1)
    perm = jnp.concatenate([slot_list, rest_list])

    b_slot, b_rest, d_slot, d_rest, hi_rest, lo_rest, rs, rr_local = local_part(
        perm, counts, diag_tiles, right_side, remote, maps
    )
    g, inverse = coarse_setup(operator, coarse_map.reshape(1, NC1))
    inverse_cols = lax.dynamic_slice_in_dim(coarsest_inverse, group * AGG, AGG, 1)

    def level_one(arrived):
        x, outgoing = lowest_part(arrived, g)
        lows = exchange(outgoing, "grp")
        h = smooth_part(x, inverse, operator)
        return correct_part(lows, inverse_cols, g, h)

    gathered = exchange(first_restrict(x_peer, rs, rr_local), GROUP_AXES)
    hi_pair, lo_pair, d_peer, m_peer = pair_setup(perm, counts, diag_tiles, side, remote)
    e, _ = level_one(gathered)
    z, w, w_peer, outgoing = forward_part(
        perm, member, e, b_slot, b_rest, d_slot, d_rest, x_peer, d_peer, m_peer, hi_pair, lo_pair, hi_rest, lo_rest, maps
    )
    e, dots = level_one(exchange(outgoing, GROUP_AXES))
    v, u, outgoing = second_part(
        perm, member, e, dots, b_slot, b_rest, d_slot, d_rest, d_peer, m_peer, hi_pair, lo_pair, hi_rest, lo_rest, maps, z, w, w_peer
    )
    sums = exchange(outgoing, ALL_AXES)
    return tuple(combine(perm, dots, sums, b_slot, b_rest, z, w, v, u))


def solution(mesh):
    placed = (
        P(None, ("grp", "sub", "chip")),
        P(("grp", "sub", "chip"), None, None),
        P(("grp", "sub", "chip"), None, None, None),
        P(("grp", "sub", "chip"), None),
        P(("grp", "sub", "chip"), None, None),
        P(("grp", "sub", "chip")),
        P("grp"),
        P("grp", None, None),
        P(),
    )
    return jax.shard_map(
        on_device,
        mesh=mesh,
        in_specs=placed,
        out_specs=(P(None, ("grp", "sub", "chip")), P(None, ("grp", "sub", "chip"))),
        check_vma=False,
    )
```

time: 607 us -> 218 us (0.36); the launches traced: 597 us -> 217 us
  blocking collectives: 306 us -> 47.3 us
  Pallas kernels: 0 us -> 123 us
  matrix products: 94.9 us -> 0 us
  other arithmetic: 71.4 us -> 0.93 us
  local copies, waits for them, and re-layouts: 51.6 us -> 4.64 us
  waiting for transfers between devices: 43.2 us -> 14.4 us
    psum x3 -> x0, blocking collectives: 193 us -> none  [the longest x2 129 us: inner_products(): return lax.psum(jnp.sum(resid * pre, axis=1), ('grp', 'sub', 'chip'))]
    pallas_call x0 -> x14, Pallas kernels: none -> 123 us  [the longest x1 36.6 us: forward_part(): pl.pallas_call(forward_kernel, grid_spec=grid, out_shape=[jax.ShapeDtypeS...]
    all_gather x4 -> x0, blocking collectives: 113 us -> none  [the longest x2 68.1 us: level_one(): gathered = lax.all_gather(coarse_resid, ('sub', 'chip'), axis=1, tiled=True)]
    dot_general x26 -> x0, matrix products: 94.9 us -> none  [the longest x6 47.4 us: fine_apply(): result = jnp.einsum('kbt,bts->kbs', shaped, diag_tiles, precision=HIGH)]
    all_to_all x0 -> x3, blocking collectives: none -> 47.3 us  [exchange(): return lax.all_to_all(x, axes, 0, 0, tiled=True)]
    scatter-add x6 -> x0, other arithmetic: 32.6 us -> none  [fine_apply(): result.at[:, slot_list]]
    gather x9 -> x0, local copies, waits for them, and re-layouts: 32.3 us -> none  [the longest x1 17.3 us: on_device(): whole_diag = jnp.diagonal(operator)]
    all_to_all x6 -> x4, waiting for transfers between devices: 43.2 us -> 14.4 us  [exchange(): return lax.all_to_all(x, axes, 0, 0, tiled=True)]
  transfers between devices with their start and end apart: 6 -> 4, of which waited for: 5 -> 3; matrix products, arithmetic and copies ran while one was open for 11% -> 1% of each run, Pallas kernels for 0% -> 17%
where the time goes in v1:
time: 218 us; the launch traced here: 217 us
  Pallas kernels  123 us (56%)
  blocking collectives  47.3 us (22%)
  starting transfers between devices  25.5 us (12%)
  waiting for transfers between devices  14.4 us (7%)
  local copies, waits for them, and re-layouts  4.64 us (2%)
    all_to_all x3, blocking collectives, exchange(): return lax.all_to_all(x, axes, 0, 0, tiled=True)  47.3 us
    pallas_call x1, Pallas kernels, forward_part(): pl.pallas_call(forward_kernel, grid_spec=grid, out_shape=[jax.ShapeDtypeS...  36.6 us
    all_to_all x4, starting transfers between devices, exchange(): return lax.all_to_all(x, axes, 0, 0, tiled=True)  25.5 us
    pallas_call x1, Pallas kernels, second_part(): pl.pallas_call(second_kernel, grid_spec=grid, out_shape=[jax.ShapeDtypeSt...  23.4 us
    all_to_all x4, waiting for transfers between devices, exchange(): return lax.all_to_all(x, axes, 0, 0, tiled=True)  14.4 us
    pallas_call x1, Pallas kernels, local_part(): pl.pallas_call(local_kernel, grid_spec=grid, out_shape=[sds((COLS, TILE))...  13 us
    pallas_call x1, Pallas kernels, pair_setup(): pl.pallas_call(pair_kernel, grid_spec=grid, out_shape=[jax.ShapeDtypeStru...  9.89 us
    pallas_call x1, Pallas kernels, combine(): pl.pallas_call(combine_kernel, grid_spec=grid, out_shape=[jax.ShapeDtypeS...  9.68 us
  transfers between devices with their start and end apart: 4, of which 3 were waited for; matrix products, arithmetic and copies ran while one was open for 1% of the time, Pallas kernels for 17%

profile of v1, /device:TPU:1, one launch (start us, length us, event | category | flops | bytes accessed | tf_op | source)
XLA Modules:
  0.0 216.7 jit_solution(8017272016507157326)
XLA Ops:
  2.1 6.6 %boundary_pack.1 = (f32[32,64,128]{2,1,0:T(8,128)}, f32[32,72,128]{2,1,0:T(8,128)}) custom-call(s32[32]{0:T(128)} %reshape.44.slots, f32[64,128,128]{2,1,0:T(8,128)} %refs_3_.5, f32[64,128,128]{2,1,0:T(8,128)} %refs_3_.5, f32[64,128,128]{2,1,0:T(8,128)} %refs_3_.5, f32[64,128,128]{2,1,0:T(8,128)} %refs_3_.5, f32[64,8192]{1,0:T(8,128)} %refs_15_.1, ...), custom_call_target="tpu_custom_call" | custom-call | tf_op jit(solution)/shard_map/boundary_pack/pallas_call | solution.py:146
  8.7 8.4 %all-to-all-start = ((f32[16,128,128]{2,1,0:T(8,128)}), f32[16,128,128]{2,1,0:T(8,128)S(1)}, u32[]{:S(2)}, u32[]{:S(2)}) async-start(f32[16,128,128]{2,1,0:T(8,128)} %bitcast.18), calls=%async_computation | async-start | bytes 2097152 | tf_op jit(solution)/shard_map/all_to_all | solution.py:760
  18.1 13.0 %local_part.1 = (f32[32,64,128]{2,1,0:T(8,128)}, f32[32,64,128]{2,1,0:T(8,128)}, f32[32,1,128]{2,1,0:T(1,128)}, f32[32,1,128]{2,1,0:T(1,128)}, bf16[32,128,128]{...) custom-call(s32[64]{0:T(128)} %pad_add_fusion.perm, s32[16]{0:T(128)} %bitcast.24, ...), custom_call_target="tpu_custom_call" | custom-call | flops 402653184 | bytes 16777216 | tf_op jit(solution)/shard_map/local_part/pallas_call | solution.py:236
  31.1 2.1 all-to-all-done
  34.1 3.2 %first_restrict.1 = f32[16,40,128]{2,1,0:T(8,128)} custom-call(f32[32,64,128]{2,1,0:T(8,128)} %bitcast.13, f32[32,64,128]{2,1,0:T(8,128)} %get-tuple-element.33.rs, f32[64,64]{1,0:T(8,128)} %get-tuple-element.34.rr), custom_call_target="tpu_custom_call" | custom-call | tf_op jit(solution)/shard_map/first_restrict/pallas_call | solution.py:299
  37.3 14.6 %all_to_all.35.arrived = f32[16,40,128]{2,1,0:T(8,128)} all-to-all(f32[16,40,128]{2,1,0:T(8,128)} %first_restrict.1), channel_id=1, replica_groups=mesh['grp'=8,'sub'=8,'chip'=2] {'sub','chip'}, dimensions={0} | all-to-all | bytes 655360 | tf_op jit(solution)/shard_map/all_to_all | solution.py:760
  51.8 3.7 %all-to-all-start.3 = ((f32[16,144,128]{2,1,0:T(8,128)}), f32[16,144,128]{2,1,0:T(8,128)S(1)}, u32[]{:S(2)}, u32[]{:S(2)}) async-start(f32[16,144,128]{2,1,0:T(8,128)} %bitcast.8), calls=%async_computation.3 | async-start | bytes 2359296 | tf_op jit(solution)/shard_map/all_to_all | solution.py:760
  55.6 3.8 %coarse_setup.1 = (f32[64,1024]{1,0:T(8,128)}, f32[1,1024]{1,0:T(1,128)}) custom-call(f32[1024,1024]{1,0:T(8,128)} %bitcast.10, s32[1,1024]{1,0:T(1,128)} %bitcast.23), custom_call_target="tpu_custom_call" | custom-call | flops 268435456 | bytes 5242880 | tf_op jit(solution)/shard_map/coarse_setup/pallas_call | solution.py:278
  59.4 2.1 lowest_part.2
  61.5 10.6 %all-to-all-done.3 = f32[16,144,128]{2,1,0:T(8,128)S(1)} async-done(((f32[16,144,128]{2,1,0:T(8,128)}), f32[16,144,128]{2,1,0:T(8,128)S(1)}, u32[]{:S(2)}, u32[]{:S(2)}) %all-to-all-start.3) | async-done | bytes 1179680 | tf_op jit(solution)/shard_map/all_to_all | solution.py:760
  72.1 7.5 %all-to-all-start.2 = ((f32[8,40,128]{2,1,0:T(8,128)}), f32[8,40,128]{2,1,0:T(8,128)S(1)}, u32[]{:S(2)}, u32[]{:S(2)}) async-start(f32[8,40,128]{2,1,0:T(8,128)} %get-tuple-element.36), calls=%async_computation.2 | async-start | bytes 327680 | tf_op jit(solution)/shard_map/all_to_all | solution.py:760
  80.5 9.9 %pair_setup.1 = (bf16[32,256,256]{2,1,0:T(8,128)(2,1)}, bf16[32,256,256]{2,1,0:T(8,128)(2,1)}, f32[32,1,128]{2,1,0:T(1,128)}, s32[32,1,128]{2,1,0:T(1,128)}) custom-call(s32[64]{0:T(128)} %pad_add_fusion.perm, s32[16]{0:T(128)} %bitcast.25, f32[64,128,128]{2,1,0:T(8,128)} %refs_3_.5, f32[64,128,128]{2,1,0:T(8,128)} %refs_3_.5, f32[64,128,128]{2,1,0:T(8,128)} %refs_3_.5, ...), custom_call_target="tpu_custom_call" | custom-call | flops 402653184 | bytes 16777216 | tf_op jit(solution)/shard_map/pair_setup/pallas_call | solution.py:345
  90.4 3.8 %smooth_part.2.h = f32[64,1024]{1,0:T(8,128)} custom-call(f32[64,1024]{1,0:T(8,128)} %get-tuple-element.37.x_ref, f32[1,1024]{1,0:T(1,128)} %get-tuple-element.38.inverse_ref, f32[1024,1024]{1,0:T(8,128)} %bitcast.11), custom_call_target="tpu_custom_call" | custom-call | flops 402653184 | bytes 5242880 | tf_op jit(solution)/shard_map/smooth_part/pallas_call | solution.py:408
  94.9 2.6 %correct_part.2 = (f32[16,64,64]{2,1,0:T(8,128)}, f32[8,128]{1,0:T(8,128)}) custom-call(f32[8,40,128]{2,1,0:T(8,128)} %copy-done.3, f32[512,64]{1,0:T(8,128)} %constant_dynamic-slice_fusion.inverse_cols, f32[64,1024]{1,0:T(8,128)} %get-tuple-element.35.g, f32[64,1024]{1,0:T(8,128)} %smooth_part.2.h), custom_call_target="tpu_custom_call" | custom-call | tf_op jit(solution)/shard_map/correct_part/pallas_call | solution.py:432
  97.5 36.6 %forward_part.1 = (f32[2,32,64,128]{3,2,1,0:T(8,128)}, f32[2,32,64,128]{3,2,1,0:T(8,128)}, f32[32,64,128]{2,1,0:T(8,128)}, f32[16,40,128]{2,1,0:T(8,128)}) custom-call(s32[64]{0:T(128)} %pad_add_fusion.perm, s32[1]{0:T(128)} %bitcast.member, f32[16,64,64]{2,1,0:T(8,128)} %get-tuple-element.39.e_own.e_peer, f32[16,64,64]{2,1,0:T(8,128)} %get-tuple-element.39.e_own.e_peer, ...), custom_call_target="tpu_custom_call" | custom-call | tf_op jit(solution)/shard_map/forward_part/pallas_call | solution.py:568
  134.1 13.4 %all_to_all.36.arrived = f32[16,40,128]{2,1,0:T(8,128)} all-to-all(f32[16,40,128]{2,1,0:T(8,128)} %get-tuple-element.51), channel_id=1, replica_groups=mesh['grp'=8,'sub'=8,'chip'=2] {'sub','chip'}, dimensions={0} | all-to-all | bytes 655360 | tf_op jit(solution)/shard_map/all_to_all | solution.py:760
  147.6 2.1 lowest_part.3
  149.7 5.9 %all-to-all-start.5 = ((f32[8,40,128]{2,1,0:T(8,128)}), f32[8,40,128]{2,1,0:T(8,128)S(1)}, u32[]{:S(2)}, u32[]{:S(2)}) async-start(f32[8,40,128]{2,1,0:T(8,128)} %get-tuple-element.52), calls=%async_computation.5 | async-start | bytes 327680 | tf_op jit(solution)/shard_map/all_to_all | solution.py:760
  155.5 3.9 %smooth_part.3.h = f32[64,1024]{1,0:T(8,128)} custom-call(f32[64,1024]{1,0:T(8,128)} %get-tuple-element.53.x_ref, f32[1,1024]{1,0:T(1,128)} %get-tuple-element.38.inverse_ref, f32[1024,1024]{1,0:T(8,128)} %bitcast.12), custom_call_target="tpu_custom_call" | custom-call | flops 402653184 | bytes 5242880 | tf_op jit(solution)/shard_map/smooth_part/pallas_call | solution.py:408
  159.4 1.7 all-to-all-done.5.arrived
  161.8 2.6 %correct_part.3 = (f32[16,64,64]{2,1,0:T(8,128)}, f32[8,128]{1,0:T(8,128)}) custom-call(f32[8,40,128]{2,1,0:T(8,128)} %copy-done.4, f32[512,64]{1,0:T(8,128)} %constant_dynamic-slice_fusion.inverse_cols, f32[64,1024]{1,0:T(8,128)} %get-tuple-element.35.g, f32[64,1024]{1,0:T(8,128)} %smooth_part.3.h), custom_call_target="tpu_custom_call" | custom-call | tf_op jit(solution)/shard_map/correct_part/pallas_call | solution.py:432
  164.3 23.4 %second_part.1 = (f32[2,32,64,128]{3,2,1,0:T(8,128)}, f32[2,32,64,128]{3,2,1,0:T(8,128)}, f32[128,8,128]{2,1,0:T(8,128)}) custom-call(s32[64]{0:T(128)} %pad_add_fusion.perm, s32[1]{0:T(128)} %bitcast.member, f32[16,64,64]{2,1,0:T(8,128)} %get-tuple-element.55.e_own.e_peer, f32[16,64,64]{2,1,0:T(8,128)} %get-tuple-element.55.e_own.e_peer, ...), custom_call_target="tpu_custom_call" | custom-call | tf_op jit(solution)/shard_map/second_part/pallas_call | solution.py:678
  187.7 19.3 %all_to_all.37.arrived = f32[128,8,128]{2,1,0:T(8,128)} all-to-all(f32[128,8,128]{2,1,0:T(8,128)} %get-tuple-element.59), channel_id=1, replica_groups=mesh['grp'=8,'sub'=8,'chip'=2] {'grp','sub','chip'}, dimensions={0} | all-to-all | bytes 1048576 | tf_op jit(solution)/shard_map/all_to_all | solution.py:760
  207.0 9.7 %combine.1 = (f32[64,8192]{1,0:T(8,128)}, f32[64,8192]{1,0:T(8,128)}) custom-call(s32[64]{0:T(128)} %pad_add_fusion.perm, f32[8,128]{1,0:T(8,128)} %get-tuple-element.54.dots, f32[128,8,128]{2,1,0:T(8,128)} %all_to_all.37.arrived, f32[32,64,128]{2,1,0:T(8,128)} %get-tuple-element.40.b_slot, f32[32,64,128]{2,1,0:T(8,128)} %get-tuple-element.41.b_rest, ...), custom_call_target="tpu_custom_call" | custom-call | tf_op jit(solution)/shard_map/combine/pallas_call | solution.py:750
  (21 shorter events, 5.6 us)
Async XLA Ops:
  0.6 79.0 %copy-start = (f32[512,512]{1,0:T(8,128)S(1)}, f32[512,512]{1,0:T(8,128)}, u32[]{:S(2)}) copy-start(f32[512,512]{1,0:T(8,128)} %param.17) | copy-start | bytes 3145732
  8.7 8.5 %copy-start.5 = (s32[32]{0:T(128)S(1)}, s32[32]{0:T(128)}, u32[]{:S(2)}) copy-start(s32[32]{0:T(128)} %reshape.44.slots) | copy-start | bytes 388
  8.7 24.4 %all-to-all-start = ((f32[16,128,128]{2,1,0:T(8,128)}), f32[16,128,128]{2,1,0:T(8,128)S(1)}, u32[]{:S(2)}, u32[]{:S(2)}) async-start(f32[16,128,128]{2,1,0:T(8,128)} %bitcast.18), calls=%async_computation | async-start | bytes 2097152 | tf_op jit(solution)/shard_map/all_to_all | solution.py:760
  33.2 1.0 copy-start.1
  51.8 20.3 %all-to-all-start.3 = ((f32[16,144,128]{2,1,0:T(8,128)}), f32[16,144,128]{2,1,0:T(8,128)S(1)}, u32[]{:S(2)}, u32[]{:S(2)}) async-start(f32[16,144,128]{2,1,0:T(8,128)} %bitcast.8), calls=%async_computation.3 | async-start | bytes 2359296 | tf_op jit(solution)/shard_map/all_to_all | solution.py:760
  72.1 8.4 %copy-start.2 = (f32[16,144,128]{2,1,0:T(8,128)}, f32[16,144,128]{2,1,0:T(8,128)S(1)}, u32[]{:S(2)}) copy-start(f32[16,144,128]{2,1,0:T(8,128)S(1)} %all-to-all-done.3) | copy-start | bytes 3538948
  72.1 22.1 %all-to-all-start.2 = ((f32[8,40,128]{2,1,0:T(8,128)}), f32[8,40,128]{2,1,0:T(8,128)S(1)}, u32[]{:S(2)}, u32[]{:S(2)}) async-start(f32[8,40,128]{2,1,0:T(8,128)} %get-tuple-element.36), calls=%async_computation.2 | async-start | bytes 327680 | tf_op jit(solution)/shard_map/all_to_all | solution.py:760
  94.2 0.7 copy-start.3
  149.7 11.4 %all-to-all-start.5 = ((f32[8,40,128]{2,1,0:T(8,128)}), f32[8,40,128]{2,1,0:T(8,128)S(1)}, u32[]{:S(2)}, u32[]{:S(2)}) async-start(f32[8,40,128]{2,1,0:T(8,128)} %get-tuple-element.52), calls=%async_computation.5 | async-start | bytes 327680 | tf_op jit(solution)/shard_map/all_to_all | solution.py:760
  161.1 0.7 copy-start.4

commit v2 on v1

--- a/solution.py
+++ b/solution.py
@@ -18,11 +18,11 @@
 GROUPS = 8
 AGG = 64
 NC1 = 1024
-STEP = 4
+STEP = 8
 NSTEP = SLOTS // STEP
-SIDE = 72
+SIDE = 136
 ROWS = 40
-VMEM_LIMIT = 56 * 1024 * 1024
+VMEM_LIMIT = 24 * 1024 * 1024
 
 GROUP_AXES = ("sub", "chip")
 ALL_AXES = ("grp", "sub", "chip")
@@ -110,19 +110,19 @@
 
 
 def boundary_kernel(slots, *refs):
-    tiles, cols, maps, first, second = refs[:STEP], refs[STEP : 2 * STEP], refs[2 * STEP], refs[-2], refs[-1]
+    tiles, cols, maps, out = refs[:STEP], refs[STEP : 2 * STEP], refs[2 * STEP], refs[-1]
     step = pl.program_id(0)
     for i in range(STEP):
         tile = tiles[i][0]
         diag = tile_diag(tile)
-        first[i] = OMEGA * cols[i][...] / diag
+        out[i, 0:64] = OMEGA * cols[i][...] / diag
         r = lax.broadcasted_iota(jnp.int32, (64, TILE), 0)
         c = lax.broadcasted_iota(jnp.int32, (64, TILE), 1)
         below = pltpu.roll(tile[64:], 64, 1)
-        second[i, 0:64] = jnp.where((c < 64) & (r > c), below, tile[:64])
+        out[i, 64:128] = jnp.where((c < 64) & (r > c), below, tile[:64])
         row = maps[slots[step * STEP + i]].astype(F32)
         r8 = lax.broadcasted_iota(jnp.int32, (8, TILE), 0)
-        second[i, 64:72] = jnp.where(r8 == 0, diag, jnp.where(r8 == 1, row, 0.0))
+        out[i, 128:136] = jnp.where(r8 == 0, diag, jnp.where(r8 == 1, row, 0.0))
 
 
 def boundary_pack(slot_list, diag_tiles, right_side, maps):
@@ -138,18 +138,12 @@
         in_specs=[tile_spec(i) for i in range(STEP)]
         + [col_spec(i) for i in range(STEP)]
         + [pl.BlockSpec((BLK, 1, TILE), lambda s, p: (0, 0, 0))],
-        out_specs=[
-            pl.BlockSpec((STEP, COLS, TILE), lambda s, p: (s, 0, 0)),
-            pl.BlockSpec((STEP, SIDE, TILE), lambda s, p: (s, 0, 0)),
-        ],
+        out_specs=pl.BlockSpec((STEP, SIDE, TILE), lambda s, p: (s, 0, 0)),
     )
     return pl.pallas_call(
         boundary_kernel,
         grid_spec=grid,
-        out_shape=[
-            jax.ShapeDtypeStruct((SLOTS, COLS, TILE), F32),
-            jax.ShapeDtypeStruct((SLOTS, SIDE, TILE), F32),
-        ],
+        out_shape=jax.ShapeDtypeStruct((SLOTS, SIDE, TILE), F32),
         compiler_params=params(),
         name="boundary_pack",
     )(slot_list, *([diag_tiles] * STEP), *([right_side] * STEP), maps)
@@ -166,32 +160,30 @@
     def _():
         rr[...] = jnp.zeros_like(rr)
 
+    index = [perm[(0 if i < STEP else SLOTS) + step * STEP + i % STEP] for i in range(n)]
+    tile = [tiles[i][0] for i in range(n)]
+    diag = [tile_diag(t) for t in tile]
+    off = [split2(off_diag(t)) for t in tile]
+    b = [cols[i][...] for i in range(n)]
+    x = [OMEGA * bb / d for bb, d in zip(b, diag)]
+    y = [bb - OMEGA * bb - mm(xx, *o) for bb, xx, o in zip(b, x, off)]
+    spread = [one_hot(maps[i]) for i in index]
     total = rr[...]
-    for i in range(n):
-        tile = tiles[i][0]
-        diag = tile_diag(tile)
-        off_hi, off_lo = split2(off_diag(tile))
-        b = cols[i][...]
-        x = OMEGA * b / diag
-        y = b - OMEGA * b - mm(x, off_hi, off_lo)
-        slot = i < STEP
-        k = i % STEP
-        index = perm[(0 if slot else SLOTS) + step * STEP + k]
-        spread = one_hot(maps[index])
-        total = total + mm_exact(y, spread, nt=True)
-        if slot:
-            b_slot[k] = b
-            d_slot[k] = diag
-            j = step * STEP + k
-            live = (j % 2) < counts[j // 2]
-            rem = remote[k] * jnp.where(live, 1.0, 0.0)
-            hi, lo = split2(rem)
-            rs[k] = dot_nt(spread, hi) + dot_nt(spread, lo)
-        else:
-            b_rest[k] = b
-            d_rest[k] = diag
-            hi_rest[k] = off_hi
-            lo_rest[k] = off_lo
+    for yy, sp in zip(y, spread):
+        total = total + mm_exact(yy, sp, nt=True)
+    for k in range(STEP):
+        b_slot[k] = b[k]
+        d_slot[k] = diag[k]
+        b_rest[k] = b[STEP + k]
+        d_rest[k] = diag[STEP + k]
+        hi_rest[k], lo_rest[k] = off[STEP + k]
+    scaled = []
+    for k in range(STEP):
+        j = step * STEP + k
+        live = (j % 2) < counts[j // 2]
+        scaled.append(split2(remote[k] * jnp.where(live, 1.0, 0.0)))
+    for k in range(STEP):
+        rs[k] = dot_nt(spread[k], scaled[k][0]) + dot_nt(spread[k], scaled[k][1])
     rr[...] = total
 
 
@@ -288,7 +280,7 @@
     total = rr[...]
     for j in range(SLOTS):
         hi, lo = split2(rs[j])
-        total = total + mm(arrived[j], hi, lo, nt=True)
+        total = total + mm(arrived[j, 0:64], hi, lo, nt=True)
     packed = pack_rows(total)
     for q in range(PEERS):
         out[q, 0:32] = packed
@@ -311,7 +303,7 @@
     c = lax.broadcasted_iota(jnp.int32, (64, TILE), 1)
     for k in range(STEP):
         own = off_diag(tiles[k][0])
-        packed = side[k, 0:64]
+        packed = side[k, 64:128]
         top = jnp.where((c >= 64) | (r < c), packed, 0.0)
         bottom = pltpu.roll(jnp.where((c < 64) & (r > c), packed, 0.0), 64, 1)
         half = jnp.concatenate([top, bottom], axis=0)
@@ -325,8 +317,8 @@
         hi, lo = split2(block)
         hi_out[k] = hi
         lo_out[k] = lo
-        diag_out[k] = side[k, 64:65]
-        map_out[k] = side[k, 65:66].astype(jnp.int32)
+        diag_out[k] = side[k, 128:129]
+        map_out[k] = side[k, 129:130].astype(jnp.int32)
 
 
 def pair_setup(perm, counts, diag_tiles, side, remote):
@@ -470,44 +462,37 @@
     e_mine = three_parts(e_own[0])
     e_theirs = [three_parts(e_peer[q]) for q in range(STEP // 2)]
     rr, bz, zw = acc_rr[...], acc_bz[...], acc_zw[...]
-    for k in range(STEP):
-        index = perm[step * STEP + k]
-        row = maps[index]
-        diag = jnp.concatenate([d_slot[k], d_peer[k]], axis=1)
-        rdiag = OMEGA / diag
-        b_own = b_slot[k]
-        xp = x_peer[k]
-        b_full = jnp.concatenate([b_own, xp * (d_peer[k] * (1.0 / OMEGA))], axis=1)
-        up = jnp.concatenate([lift(e_mine, row), lift(e_theirs[k // 2], m_peer[k])], axis=1)
-        x = jnp.concatenate([b_own * rdiag[:, :TILE], xp], axis=1) + up
-        hi, lo = hi_pair[k], lo_pair[k]
-        z = x + (b_full - apply_block(x, diag, hi, lo)) * rdiag
-        w = apply_block(z, diag, hi, lo)
-        x1 = w * rdiag
-        y = w[:, :TILE] - apply_block(x1, diag[:, :TILE], hi[:, :TILE], lo[:, :TILE])
-        rr = rr + mm_exact(y, one_hot(row), nt=True)
-        bz = bz + b_own * z[:, :TILE]
-        zw = zw + z[:, :TILE] * w[:, :TILE]
-        z_out[0, k] = z[:, :TILE]
-        w_out[0, k] = w[:, :TILE]
-        ws_out[k] = w[:, TILE:]
-    for k in range(STEP):
-        index = perm[SLOTS + step * STEP + k]
-        row = maps[index]
-        diag = d_rest[k]
-        rdiag = OMEGA / diag
-        b_own = b_rest[k]
-        x = b_own * rdiag + lift(e_mine, row)
-        hi, lo = hi_rest[k], lo_rest[k]
-        z = x + (b_own - apply_block(x, diag, hi, lo)) * rdiag
-        w = apply_block(z, diag, hi, lo)
-        x1 = w * rdiag
-        y = w - apply_block(x1, diag, hi, lo)
-        rr = rr + mm_exact(y, one_hot(row), nt=True)
-        bz = bz + b_own * z
-        zw = zw + z * w
-        z_out[1, k] = z
-        w_out[1, k] = w
+    pairs, rest = range(STEP), range(STEP)
+    rows = [maps[perm[step * STEP + k]] for k in pairs] + [maps[perm[SLOTS + step * STEP + k]] for k in rest]
+    b_own = [b_slot[k] for k in pairs] + [b_rest[k] for k in rest]
+    diag = [jnp.concatenate([d_slot[k], d_peer[k]], axis=1) for k in pairs] + [d_rest[k] for k in rest]
+    rdiag = [OMEGA / d for d in diag]
+    mats = [(hi_pair[k], lo_pair[k]) for k in pairs] + [(hi_rest[k], lo_rest[k]) for k in rest]
+    full = [
+        jnp.concatenate([b_own[k], x_peer[k] * (d_peer[k] * (1.0 / OMEGA))], axis=1) for k in pairs
+    ] + b_own[STEP:]
+    ups = [lift(e_mine, row) for row in rows]
+    ups_peer = [lift(e_theirs[k // 2], m_peer[k]) for k in pairs]
+    ups = [jnp.concatenate([ups[k], ups_peer[k]], axis=1) for k in pairs] + ups[STEP:]
+    x = [f * rd + up for f, rd, up in zip(full, rdiag, ups)]
+    image = [apply_block(xx, d, *m) for xx, d, m in zip(x, diag, mats)]
+    z = [xx + (f - im) * rd for xx, f, im, rd in zip(x, full, image, rdiag)]
+    w = [apply_block(zz, d, *m) for zz, d, m in zip(z, diag, mats)]
+    x1 = [ww * rd for ww, rd in zip(w, rdiag)]
+    left = [(m[0][:, :TILE], m[1][:, :TILE]) for m in mats]
+    y = [
+        ww[:, :TILE] - apply_block(xx, d[:, :TILE], *m) for ww, xx, d, m in zip(w, x1, diag, left)
+    ]
+    for row, yy in zip(rows, y):
+        rr = rr + mm_exact(yy, one_hot(row), nt=True)
+    for i in range(2 * STEP):
+        zz, ww = z[i][:, :TILE], w[i][:, :TILE]
+        bz = bz + b_own[i] * zz
+        zw = zw + zz * ww
+        z_out[i // STEP, i % STEP] = zz
+        w_out[i // STEP, i % STEP] = ww
+    for k in pairs:
+        ws_out[k] = w[k][:, TILE:]
     acc_rr[...] = rr
     acc_bz[...] = bz
     acc_zw[...] = zw
@@ -605,33 +590,25 @@
         sums[1] = sums[1] + z1 * az1
         sums[2] = sums[2] + (z1 * w + z * az1)
 
-    for k in range(STEP):
-        row = maps[perm[step * STEP + k]]
-        diag = jnp.concatenate([d_slot[k], d_peer[k]], axis=1)
-        rdiag = OMEGA / diag
-        w_own = w_in[0, k]
-        w = jnp.concatenate([w_own, w_peer[k]], axis=1)
-        up = jnp.concatenate([lift(e_mine, row), lift(e_theirs[k // 2], m_peer[k])], axis=1)
-        x = w * rdiag + up
-        hi, lo = hi_pair[k], lo_pair[k]
-        v = x + (w - apply_block(x, diag, hi, lo)) * rdiag
-        u = apply_block(v, diag[:, :TILE], hi[:, :TILE], lo[:, :TILE])
-        v_own = v[:, :TILE]
-        v_out[0, k] = v_own
-        u_out[0, k] = u
-        gather(b_slot[k], z_in[0, k], w_own, v_own, u)
-    for k in range(STEP):
-        row = maps[perm[SLOTS + step * STEP + k]]
-        diag = d_rest[k]
-        rdiag = OMEGA / diag
-        w = w_in[1, k]
-        x = w * rdiag + lift(e_mine, row)
-        hi, lo = hi_rest[k], lo_rest[k]
-        v = x + (w - apply_block(x, diag, hi, lo)) * rdiag
-        u = apply_block(v, diag, hi, lo)
-        v_out[1, k] = v
-        u_out[1, k] = u
-        gather(b_rest[k], z_in[1, k], w, v, u)
+    pairs, rest = range(STEP), range(STEP)
+    rows = [maps[perm[step * STEP + k]] for k in pairs] + [maps[perm[SLOTS + step * STEP + k]] for k in rest]
+    diag = [jnp.concatenate([d_slot[k], d_peer[k]], axis=1) for k in pairs] + [d_rest[k] for k in rest]
+    rdiag = [OMEGA / d for d in diag]
+    mats = [(hi_pair[k], lo_pair[k]) for k in pairs] + [(hi_rest[k], lo_rest[k]) for k in rest]
+    w = [jnp.concatenate([w_in[0, k], w_peer[k]], axis=1) for k in pairs] + [w_in[1, k] for k in rest]
+    ups = [lift(e_mine, row) for row in rows]
+    ups_peer = [lift(e_theirs[k // 2], m_peer[k]) for k in pairs]
+    ups = [jnp.concatenate([ups[k], ups_peer[k]], axis=1) for k in pairs] + ups[STEP:]
+    x = [ww * rd + up for ww, rd, up in zip(w, rdiag, ups)]
+    image = [apply_block(xx, d, *m) for xx, d, m in zip(x, diag, mats)]
+    v = [xx + (ww - im) * rd for xx, ww, im, rd in zip(x, w, image, rdiag)]
+    left = [(m[0][:, :TILE], m[1][:, :TILE]) for m in mats]
+    u = [apply_block(vv, d[:, :TILE], *m) for vv, d, m in zip(v, diag, left)]
+    for i in range(2 * STEP):
+        vv, b_ref = v[i][:, :TILE], (b_slot if i < STEP else b_rest)
+        v_out[i // STEP, i % STEP] = vv
+        u_out[i // STEP, i % STEP] = u[i]
+        gather(b_ref[i % STEP], z_in[i // STEP, i % STEP], w[i][:, :TILE], vv, u[i])
     acc_a[...] = sums[0]
     acc_b[...] = sums[1]
     acc_c[...] = sums[2]
@@ -779,9 +756,8 @@
     remote = remote_tiles.reshape(SLOTS, TILE, TILE)
     operator = level1_ops[0]
 
-    first, second = boundary_pack(slot_list, diag_tiles, right_side, maps)
-    x_peer = exchange(first.reshape(PEERS, 2 * COLS, TILE), GROUP_AXES).reshape(SLOTS, COLS, TILE)
-    side = exchange(second.reshape(PEERS, 2 * SIDE, TILE), GROUP_AXES).reshape(SLOTS, SIDE, TILE)
+    outgoing = boundary_pack(slot_list, diag_tiles, right_side, maps)
+    side = exchange(outgoing.reshape(PEERS, 2 * SIDE, TILE), GROUP_AXES).reshape(SLOTS, SIDE, TILE)
 
     tile_ids = jnp.arange(BLK, dtype=jnp.int32)
     free = jnp.logical_not(jnp.any(slot_list[:, None] == tile_ids[None, :], axis=0)).astype(jnp.int32)
@@ -802,11 +778,11 @@
         h = smooth_part(x, inverse, operator)
         return correct_part(lows, inverse_cols, g, h)
 
-    gathered = exchange(first_restrict(x_peer, rs, rr_local), GROUP_AXES)
+    gathered = exchange(first_restrict(side, rs, rr_local), GROUP_AXES)
     hi_pair, lo_pair, d_peer, m_peer = pair_setup(perm, counts, diag_tiles, side, remote)
     e, _ = level_one(gathered)
     z, w, w_peer, outgoing = forward_part(
-        perm, member, e, b_slot, b_rest, d_slot, d_rest, x_peer, d_peer, m_peer, hi_pair, lo_pair, hi_rest, lo_rest, maps
+        perm, member, e, b_slot, b_rest, d_slot, d_rest, side, d_peer, m_peer, hi_pair, lo_pair, hi_rest, lo_rest, maps
     )
     e, dots = level_one(exchange(outgoing, GROUP_AXES))
     v, u, outgoing = second_part(

time: 218 us -> 187 us (0.86)
  Pallas kernels: 123 us -> 47.2 us
  local copies, waits for them, and re-layouts: 4.64 us -> 57.8 us
  blocking collectives: 47.3 us -> 29.8 us
  waiting for transfers between devices: 14.4 us -> 21.6 us
  starting transfers between devices: 25.5 us -> 28 us
    unnamed x13 -> x107, local copies, waits for them, and re-layouts: 3.17 us -> 56.9 us
    pallas_call x1, Pallas kernels: 36.6 us -> 11.3 us  [forward_part(): pl.pallas_call(forward_kernel, grid_spec=grid, out_shape=[jax.ShapeDtypeS...]
    all_to_all x3 -> x2, blocking collectives: 47.3 us -> 29.8 us  [exchange(): return lax.all_to_all(x, axes, 0, 0, tiled=True)]
    pallas_call x1, Pallas kernels: 23.4 us -> 7.51 us  [second_part(): pl.pallas_call(second_kernel, grid_spec=grid, out_shape=[jax.ShapeDtypeSt...]
    all_to_all x4, waiting for transfers between devices: 14.4 us -> 21.6 us  [exchange(): return lax.all_to_all(x, axes, 0, 0, tiled=True)]
    pallas_call x1, Pallas kernels: 13 us -> 6.64 us  [local_part(): pl.pallas_call(local_kernel, grid_spec=grid, out_shape=[sds((COLS, TILE))...]
    pallas_call x2, Pallas kernels: 7.71 us -> 1.76 us  [smooth_part(): pl.pallas_call(smooth_kernel, out_shape=jax.ShapeDtypeStruct((COLS, NC1),...]
    pallas_call x1, Pallas kernels: 9.89 us -> 4.39 us  [pair_setup(): pl.pallas_call(pair_kernel, grid_spec=grid, out_shape=[jax.ShapeDtypeStru...]
  transfers between devices with their start and end apart: 4 -> 4, of which waited for: 3 -> 3; matrix products, arithmetic and copies ran while one was open for 1% -> 1% of each run, Pallas kernels for 17% -> 7%
where the time goes in v2:
time: 187 us; the launch traced here: 186 us
  local copies, waits for them, and re-layouts  57.8 us (31%)
  Pallas kernels  47.2 us (25%)
  blocking collectives  29.8 us (16%)
  starting transfers between devices  28 us (15%)
  waiting for transfers between devices  21.6 us (12%)
    unnamed x107, local copies, waits for them, and re-layouts  56.9 us
    all_to_all x2, blocking collectives, exchange(): return lax.all_to_all(x, axes, 0, 0, tiled=True)  29.8 us
    all_to_all x4, starting transfers between devices, exchange(): return lax.all_to_all(x, axes, 0, 0, tiled=True)  28 us
    all_to_all x4, waiting for transfers between devices, exchange(): return lax.all_to_all(x, axes, 0, 0, tiled=True)  21.6 us
    pallas_call x1, Pallas kernels, forward_part(): pl.pallas_call(forward_kernel, grid_spec=grid, out_shape=[jax.ShapeDtypeS...  11.3 us
    pallas_call x1, Pallas kernels, second_part(): pl.pallas_call(second_kernel, grid_spec=grid, out_shape=[jax.ShapeDtypeSt...  7.51 us
    pallas_call x1, Pallas kernels, local_part(): pl.pallas_call(local_kernel, grid_spec=grid, out_shape=[sds((COLS, TILE))...  6.64 us
    pallas_call x1, Pallas kernels, combine(): pl.pallas_call(combine_kernel, grid_spec=grid, out_shape=[jax.ShapeDtypeS...  4.47 us
  transfers between devices with their start and end apart: 4, of which 3 were waited for; matrix products, arithmetic and copies ran while one was open for 1% of the time, Pallas kernels for 7%

profile of v2, /device:TPU:1, one launch (start us, length us, event | category | flops | bytes accessed | tf_op | source)
XLA Modules:
  0.0 185.7 jit_solution(337088036170930577)
XLA Ops:
  1.6 2.2 %copy-done.1 = f32[64,128,128]{2,1,0:T(8,128)S(1)} copy-done((f32[64,128,128]{2,1,0:T(8,128)S(1)}, f32[64,128,128]{2,1,0:T(8,128)}, u32[]{:S(2)}) %copy-start.1) | copy-done | bytes 4194328
  9.2 8.6 %all-to-all-start = ((f32[16,272,128]{2,1,0:T(8,128)}), f32[16,272,128]{2,1,0:T(8,128)}, u32[]{:S(2)}, u32[]{:S(2)}) async-start(f32[16,272,128]{2,1,0:T(8,128)} %bitcast.11), calls=%async_computation | async-start | bytes 4456448 | tf_op jit(solution)/shard_map/all_to_all | solution.py:737
  18.2 2.2 %copy-done.2 = f32[64,128,128]{2,1,0:T(8,128)S(1)} copy-done((f32[64,128,128]{2,1,0:T(8,128)S(1)}, f32[64,128,128]{2,1,0:T(8,128)}, u32[]{:S(2)}) %copy-start.2) | copy-done | bytes 4194328
  22.0 6.6 %local_part.1 = (f32[32,64,128]{2,1,0:T(8,128)S(1)}, f32[32,64,128]{2,1,0:T(8,128)S(1)}, f32[32,1,128]{2,1,0:T(1,128)S(1)}, f32[32,1,128]{2,1,0:T(1,128)S(1)}, b...) custom-call(s32[64]{0:T(128)S(1)} %pad_add_fusion.perm, ...), custom_call_target="tpu_custom_call" | custom-call | flops 402653184 | bytes 16777216 | tf_op jit(solution)/shard_map/local_part/pallas_call | solution.py:228
  33.6 15.8 %all-to-all-done = f32[16,272,128]{2,1,0:T(8,128)} async-done(((f32[16,272,128]{2,1,0:T(8,128)}), f32[16,272,128]{2,1,0:T(8,128)}, u32[]{:S(2)}, u32[]{:S(2)}) %all-to-all-start) | async-done | bytes 2228256 | tf_op jit(solution)/shard_map/all_to_all | solution.py:737
  50.7 3.2 %first_restrict.1 = f32[16,40,128]{2,1,0:T(8,128)} custom-call(f32[32,136,128]{2,1,0:T(8,128)} %bitcast.3.arrived.refs_8_.x_peer, f32[32,64,128]{2,1,0:T(8,128)S(1)} %copy-done.36, f32[64,64]{1,0:T(8,128)S(1)} %get-tuple-element.31.rr), custom_call_target="tpu_custom_call" | custom-call | tf_op jit(solution)/shard_map/first_restrict/pallas_call | solution.py:291
  53.9 6.0 %all-to-all-start.1 = ((f32[16,40,128]{2,1,0:T(8,128)}), f32[16,40,128]{2,1,0:T(8,128)}, u32[]{:S(2)}, u32[]{:S(2)}) async-start(f32[16,40,128]{2,1,0:T(8,128)} %first_restrict.1), calls=%async_computation.1 | async-start | bytes 655360 | tf_op jit(solution)/shard_map/all_to_all | solution.py:737
  59.9 2.2 %copy-done.6 = f32[1,1024,1024]{2,1,0:T(8,128)S(1)} copy-done((f32[1,1024,1024]{2,1,0:T(8,128)S(1)}, f32[1,1024,1024]{2,1,0:T(8,128)}, u32[]{:S(2)}) %copy-start.6) | copy-done | bytes 4194328
  63.1 4.8 %all-to-all-done.1.arrived = f32[16,40,128]{2,1,0:T(8,128)} async-done(((f32[16,40,128]{2,1,0:T(8,128)}), f32[16,40,128]{2,1,0:T(8,128)}, u32[]{:S(2)}, u32[]{:S(2)}) %all-to-all-start.1) | async-done | bytes 327712 | tf_op jit(solution)/shard_map/all_to_all | solution.py:737
  70.6 7.6 %all-to-all-start.2 = ((f32[8,40,128]{2,1,0:T(8,128)}), f32[8,40,128]{2,1,0:T(8,128)}, u32[]{:S(2)}, u32[]{:S(2)}) async-start(f32[8,40,128]{2,1,0:T(8,128)} %copy-done.49), calls=%async_computation.2 | async-start | bytes 327680 | tf_op jit(solution)/shard_map/all_to_all | solution.py:737
  79.1 2.2 %copy-done.3 = f32[64,128,128]{2,1,0:T(8,128)S(1)} copy-done((f32[64,128,128]{2,1,0:T(8,128)S(1)}, f32[64,128,128]{2,1,0:T(8,128)}, u32[]{:S(2)}) %copy-start.3) | copy-done | bytes 4194328
  81.3 4.4 %pair_setup.1 = (bf16[32,256,256]{2,1,0:T(8,128)(2,1)S(1)}, bf16[32,256,256]{2,1,0:T(8,128)(2,1)S(1)}, f32[32,1,128]{2,1,0:T(1,128)S(1)}, s32[32,1,128]{2,1,0:T(1,128)S(1)}) custom-call(s32[64]{0:T(128)S(1)} %pad_add_fusion.perm, s32[16]{0:T(128)S(1)} %bitcast.20, f32[64,128,128]{2,1,0:T(8,128)S(1)} %copy-done.3, f32[64,128,128]{2,1,0:T(8,128)S(1)} %copy-done.3, ...), custom_call_target="tpu_custom_call" | custom-call | flops 402653184 | bytes 16777216 | tf_op jit(solution)/shard_map/pair_setup/pallas_call | solution.py:337
  93.2 2.0 %correct_part.2 = (f32[16,64,64]{2,1,0:T(8,128)S(1)}, f32[8,128]{1,0:T(8,128)}) custom-call(f32[8,40,128]{2,1,0:T(8,128)} %all-to-all-done.2.arrived, f32[512,64]{1,0:T(8,128)S(1)} %copy-done.33, f32[64,1024]{1,0:T(8,128)S(1)} %get-tuple-element.32.g, f32[64,1024]{1,0:T(8,128)S(1)} %copy-done.40), custom_call_target="tpu_custom_call" | custom-call | tf_op jit(solution)/shard_map/correct_part/pallas_call | solution.py:424
  95.3 2.2 %copy-done.10 = bf16[32,256,256]{2,1,0:T(8,128)(2,1)S(1)} copy-done((bf16[32,256,256]{2,1,0:T(8,128)(2,1)S(1)}, bf16[32,256,256]{2,1,0:T(8,128)(2,1)}, u32[]{:S(2)}) %copy-start.10) | copy-done | bytes 4194328
  97.5 2.2 %copy-done.13 = bf16[32,256,256]{2,1,0:T(8,128)(2,1)S(1)} copy-done((bf16[32,256,256]{2,1,0:T(8,128)(2,1)S(1)}, bf16[32,256,256]{2,1,0:T(8,128)(2,1)}, u32[]{:S(2)}) %copy-start.13) | copy-done | bytes 4194328
  102.1 11.3 %forward_part.1 = (f32[2,32,64,128]{3,2,1,0:T(8,128)S(1)}, f32[2,32,64,128]{3,2,1,0:T(8,128)S(1)}, f32[32,64,128]{2,1,0:T(8,128)S(1)}, f32[16,40,128]{2,1,0:T(8,128)S(1)}) custom-call(s32[64]{0:T(128)S(1)} %pad_add_fusion.perm, s32[1]{0:T(128)} %bitcast.member, f32[16,64,64]{2,1,0:T(8,128)S(1)} %get-tuple-element.36.e_own.e_peer, ...), custom_call_target="tpu_custom_call" | custom-call | tf_op jit(solution)/shard_map/forward_part/pallas_call | solution.py:553
  116.0 11.5 %all_to_all.30.arrived = f32[16,40,128]{2,1,0:T(8,128)S(1)} all-to-all(f32[16,40,128]{2,1,0:T(8,128)S(1)} %get-tuple-element.47), channel_id=1, replica_groups=mesh['grp'=8,'sub'=8,'chip'=2] {'sub','chip'}, dimensions={0} | all-to-all | bytes 655360 | tf_op jit(solution)/shard_map/all_to_all | solution.py:737
  129.3 5.8 %all-to-all-start.4 = ((f32[8,40,128]{2,1,0:T(8,128)}), f32[8,40,128]{2,1,0:T(8,128)}, u32[]{:S(2)}, u32[]{:S(2)}) async-start(f32[8,40,128]{2,1,0:T(8,128)} %copy-done.50), calls=%async_computation.4 | async-start | bytes 327680 | tf_op jit(solution)/shard_map/all_to_all | solution.py:737
  135.2 2.2 %copy-done.8 = f32[1,1024,1024]{2,1,0:T(8,128)S(1)} copy-done((f32[1,1024,1024]{2,1,0:T(8,128)S(1)}, f32[1,1024,1024]{2,1,0:T(8,128)}, u32[]{:S(2)}) %copy-start.8) | copy-done | bytes 4194328
  144.3 2.2 %copy-done.11 = bf16[32,256,256]{2,1,0:T(8,128)(2,1)S(1)} copy-done((bf16[32,256,256]{2,1,0:T(8,128)(2,1)S(1)}, bf16[32,256,256]{2,1,0:T(8,128)(2,1)}, u32[]{:S(2)}) %copy-start.11) | copy-done | bytes 4194328
  146.5 2.2 %copy-done.14 = bf16[32,256,256]{2,1,0:T(8,128)(2,1)S(1)} copy-done((bf16[32,256,256]{2,1,0:T(8,128)(2,1)S(1)}, bf16[32,256,256]{2,1,0:T(8,128)(2,1)}, u32[]{:S(2)}) %copy-start.14) | copy-done | bytes 4194328
  155.5 7.5 %second_part.1 = (f32[2,32,64,128]{3,2,1,0:T(8,128)S(1)}, f32[2,32,64,128]{3,2,1,0:T(8,128)S(1)}, f32[128,8,128]{2,1,0:T(8,128)S(1)}) custom-call(s32[64]{0:T(128)S(1)} %pad_add_fusion.perm, s32[1]{0:T(128)} %bitcast.member, f32[16,64,64]{2,1,0:T(8,128)S(1)} %get-tuple-element.51.e_own.e_peer, f32[16,64,64]{2,1,0:T(8,128)S(1)} %get-tuple-element.51.e_own.e_peer, ...), custom_call_target="tpu_custom_call" | custom-call | tf_op jit(solution)/shard_map/second_part/pallas_call | solution.py:655
  163.0 18.2 %all_to_all.31.arrived = f32[128,8,128]{2,1,0:T(8,128)S(1)} all-to-all(f32[128,8,128]{2,1,0:T(8,128)S(1)} %get-tuple-element.55), channel_id=1, replica_groups=mesh['grp'=8,'sub'=8,'chip'=2] {'grp','sub','chip'}, dimensions={0} | all-to-all | bytes 1048576 | tf_op jit(solution)/shard_map/all_to_all | solution.py:737
  181.3 4.5 %combine.1 = (f32[64,8192]{1,0:T(8,128)}, f32[64,8192]{1,0:T(8,128)}) custom-call(s32[64]{0:T(128)S(1)} %pad_add_fusion.perm, f32[8,128]{1,0:T(8,128)S(1)} %get-tuple-element.50.dots, f32[128,8,128]{2,1,0:T(8,128)S(1)} %all_to_all.31.arrived, f32[32,64,128]{2,1,0:T(8,128)S(1)} %copy-done.16, f32[32,64,128]{2,1,0:T(8,128)S(1)} %copy-done.18, ...), custom_call_target="tpu_custom_call" | custom-call | tf_op jit(solution)/shard_map/combine/pallas_call | solution.py:727
  (114 shorter events, 47.2 us)
Async XLA Ops:
  0.6 77.6 %copy-start = (f32[512,512]{1,0:T(8,128)S(1)}, f32[512,512]{1,0:T(8,128)}, u32[]{:S(2)}) copy-start(f32[512,512]{1,0:T(8,128)} %param.17) | copy-start | bytes 3145732
  1.6 2.2 %copy-start.1 = (f32[64,128,128]{2,1,0:T(8,128)S(1)}, f32[64,128,128]{2,1,0:T(8,128)}, u32[]{:S(2)}) copy-start(f32[64,128,128]{2,1,0:T(8,128)} %refs_7_.5) | copy-start | bytes 12582916
  9.2 9.0 %copy-start.5 = (f32[64,8192]{1,0:T(8,128)S(1)}, f32[64,8192]{1,0:T(8,128)}, u32[]{:S(2)}) copy-start(f32[64,8192]{1,0:T(8,128)} %refs_31_.1) | copy-start | bytes 6291460
  9.2 9.0 %copy-start.44 = (s32[8192]{0:T(1024)S(1)}, s32[8192]{0:T(1024)}, u32[]{:S(2)}) copy-start(s32[8192]{0:T(1024)} %param.14) | copy-start | bytes 98308
  9.2 9.0 %copy-start.52 = (s32[1,16]{1,0:T(1,128)S(1)}, s32[1,16]{1,0:T(1,128)}, u32[]{:S(2)}) copy-start(s32[1,16]{1,0:T(1,128)} %param.12) | copy-start | bytes 196
  9.2 40.2 %all-to-all-start = ((f32[16,272,128]{2,1,0:T(8,128)}), f32[16,272,128]{2,1,0:T(8,128)}, u32[]{:S(2)}, u32[]{:S(2)}) async-start(f32[16,272,128]{2,1,0:T(8,128)} %bitcast.11), calls=%async_computation | async-start | bytes 4456448 | tf_op jit(solution)/shard_map/all_to_all | solution.py:737
  18.2 2.2 %copy-start.2 = (f32[64,128,128]{2,1,0:T(8,128)S(1)}, f32[64,128,128]{2,1,0:T(8,128)}, u32[]{:S(2)}) copy-start(f32[64,128,128]{2,1,0:T(8,128)} %refs_7_.5) | copy-start | bytes 12582916
  50.7 9.2 %copy-start.51 = (s32[1024]{0:T(1024)S(1)}, s32[1024]{0:T(1024)}, u32[]{:S(2)}) copy-start(s32[1024]{0:T(1024)} %param.15) | copy-start | bytes 12292
  53.9 14.0 %all-to-all-start.1 = ((f32[16,40,128]{2,1,0:T(8,128)}), f32[16,40,128]{2,1,0:T(8,128)}, u32[]{:S(2)}, u32[]{:S(2)}) async-start(f32[16,40,128]{2,1,0:T(8,128)} %first_restrict.1), calls=%async_computation.1 | async-start | bytes 655360 | tf_op jit(solution)/shard_map/all_to_all | solution.py:737
  59.9 2.2 %copy-start.6 = (f32[1,1024,1024]{2,1,0:T(8,128)S(1)}, f32[1,1024,1024]{2,1,0:T(8,128)}, u32[]{:S(2)}) copy-start(f32[1,1024,1024]{2,1,0:T(8,128)} %param.16) | copy-start | bytes 12582916
  62.1 17.0 %copy-start.21 = (f32[16,2,128,128]{3,2,1,0:T(8,128)S(1)}, f32[16,2,128,128]{3,2,1,0:T(8,128)}, u32[]{:S(2)}) copy-start(f32[16,2,128,128]{3,2,1,0:T(8,128)} %param.11) | copy-start | bytes 6291460
  70.6 20.7 %all-to-all-start.2 = ((f32[8,40,128]{2,1,0:T(8,128)}), f32[8,40,128]{2,1,0:T(8,128)}, u32[]{:S(2)}, u32[]{:S(2)}) async-start(f32[8,40,128]{2,1,0:T(8,128)} %copy-done.49), calls=%async_computation.2 | async-start | bytes 327680 | tf_op jit(solution)/shard_map/all_to_all | solution.py:737
  79.1 2.2 %copy-start.3 = (f32[64,128,128]{2,1,0:T(8,128)S(1)}, f32[64,128,128]{2,1,0:T(8,128)}, u32[]{:S(2)}) copy-start(f32[64,128,128]{2,1,0:T(8,128)} %refs_7_.5) | copy-start | bytes 12582916
  81.3 8.4 %copy-start.7 = (f32[1,1024,1024]{2,1,0:T(8,128)S(1)}, f32[1,1024,1024]{2,1,0:T(8,128)}, u32[]{:S(2)}) copy-start(f32[1,1024,1024]{2,1,0:T(8,128)} %param.16) | copy-start | bytes 12582916
  81.3 8.4 %copy-start.46 = (f32[64,1024]{1,0:T(8,128)S(1)}, f32[64,1024]{1,0:T(8,128)}, u32[]{:S(2)}) copy-start(f32[64,1024]{1,0:T(8,128)} %copy-done.45) | copy-start | bytes 786436
  89.7 5.5 %copy-start.16 = (f32[32,64,128]{2,1,0:T(8,128)S(1)}, f32[32,64,128]{2,1,0:T(8,128)}, u32[]{:S(2)}) copy-start(f32[32,64,128]{2,1,0:T(8,128)} %copy-done.15) | copy-start | bytes 3145732
  89.7 5.5 %copy-start.18 = (f32[32,64,128]{2,1,0:T(8,128)S(1)}, f32[32,64,128]{2,1,0:T(8,128)}, u32[]{:S(2)}) copy-start(f32[32,64,128]{2,1,0:T(8,128)} %copy-done.17) | copy-start | bytes 3145732
  95.3 2.2 %copy-start.10 = (bf16[32,256,256]{2,1,0:T(8,128)(2,1)S(1)}, bf16[32,256,256]{2,1,0:T(8,128)(2,1)}, u32[]{:S(2)}) copy-start(bf16[32,256,256]{2,1,0:T(8,128)(2,1)} %copy-done.9) | copy-start | bytes 12582916
  97.5 2.2 %copy-start.13 = (bf16[32,256,256]{2,1,0:T(8,128)(2,1)S(1)}, bf16[32,256,256]{2,1,0:T(8,128)(2,1)}, u32[]{:S(2)}) copy-start(bf16[32,256,256]{2,1,0:T(8,128)(2,1)} %copy-done.12) | copy-start | bytes 12582916
  116.0 11.9 %copy-start.41 = (f32[32,64,128]{2,1,0:T(8,128)}, f32[32,64,128]{2,1,0:T(8,128)S(1)}, u32[]{:S(2)}) copy-start(f32[32,64,128]{2,1,0:T(8,128)S(1)} %get-tuple-element.54.w_peer) | copy-start | bytes 3145732
  129.3 11.5 %all-to-all-start.4 = ((f32[8,40,128]{2,1,0:T(8,128)}), f32[8,40,128]{2,1,0:T(8,128)}, u32[]{:S(2)}, u32[]{:S(2)}) async-start(f32[8,40,128]{2,1,0:T(8,128)} %copy-done.50), calls=%async_computation.4 | async-start | bytes 327680 | tf_op jit(solution)/shard_map/all_to_all | solution.py:737
  144.3 2.2 %copy-start.11 = (bf16[32,256,256]{2,1,0:T(8,128)(2,1)S(1)}, bf16[32,256,256]{2,1,0:T(8,128)(2,1)}, u32[]{:S(2)}) copy-start(bf16[32,256,256]{2,1,0:T(8,128)(2,1)} %copy-done.9) | copy-start | bytes 12582916
  146.5 2.2 %copy-start.14 = (bf16[32,256,256]{2,1,0:T(8,128)(2,1)S(1)}, bf16[32,256,256]{2,1,0:T(8,128)(2,1)}, u32[]{:S(2)}) copy-start(bf16[32,256,256]{2,1,0:T(8,128)(2,1)} %copy-done.12) | copy-start | bytes 12582916
  155.5 25.7 %copy-start.24 = (f32[2,32,64,128]{3,2,1,0:T(8,128)S(1)}, f32[2,32,64,128]{3,2,1,0:T(8,128)}, u32[]{:S(2)}) copy-start(f32[2,32,64,128]{3,2,1,0:T(8,128)} %copy-done.22) | copy-start | bytes 6291460
  (33 other events, 38.6 us)

commit v3 on v2

--- a/solution.py
+++ b/solution.py
@@ -32,6 +32,14 @@
     return pltpu.CompilerParams(vmem_limit_bytes=VMEM_LIMIT)
 
 
+def hbm(x):
+    return pltpu.with_memory_space_constraint(x, pltpu.HBM)
+
+
+def far(shape, dtype=F32):
+    return pltpu.HBM(shape, dtype)
+
+
 def cost(flops, moved):
     return pl.CostEstimate(flops=flops, bytes_accessed=moved, transcendentals=0)
 
@@ -40,14 +48,6 @@
     hi = x.astype(BF16)
     lo = (x - hi.astype(F32)).astype(BF16)
     return hi, lo
-
-
-def split3(x):
-    hi = x.astype(BF16)
-    rest = x - hi.astype(F32)
-    mid = rest.astype(BF16)
-    lo = (rest - mid.astype(F32)).astype(BF16)
-    return hi, mid, lo
 
 
 def dot(a, b):
@@ -69,14 +69,12 @@
 def mm_exact(x, w, nt=False):
     op = dot_nt if nt else dot
     rows = x.shape[0]
-    hi, mid, lo = split3(x)
-    three = op(jnp.concatenate([hi, mid, lo], axis=0), w)
-    return three[:rows] + three[rows : 2 * rows] + three[2 * rows :]
-
-
-def exact_mm(w, x):
-    hi, mid, lo = split3(x)
-    return dot(w, hi) + dot(w, mid) + dot(w, lo)
+    two = op(jnp.concatenate(split2(x), axis=0), w)
+    return two[:rows] + two[rows:]
+
+
+def beside(a, b):
+    return jnp.concatenate([a, b], axis=1)
 
 
 def eye_mask():
@@ -109,44 +107,60 @@
     return jnp.broadcast_to(row, (TILE, TILE)).T
 
 
-def boundary_kernel(slots, *refs):
-    tiles, cols, maps, out = refs[:STEP], refs[STEP : 2 * STEP], refs[2 * STEP], refs[-1]
-    step = pl.program_id(0)
-    for i in range(STEP):
-        tile = tiles[i][0]
+def boundary_kernel(slots, maps, tiles, cols, out, tile_buf, col_buf, out_buf, tile_sem, col_sem, out_sem):
+    def tile_copy(j):
+        return pltpu.make_async_copy(tiles.at[slots[0, j // 2, j % 2]], tile_buf.at[j], tile_sem.at[j])
+
+    def col_copy(j):
+        at = pl.ds(pl.multiple_of(slots[0, j // 2, j % 2] * TILE, TILE), TILE)
+        return pltpu.make_async_copy(cols.at[:, at], col_buf.at[j], col_sem.at[j])
+
+    def out_copy(j):
+        return pltpu.make_async_copy(out_buf.at[j], out.at[j], out_sem.at[j])
+
+    for j in range(SLOTS):
+        tile_copy(j).start()
+        col_copy(j).start()
+    r = lax.broadcasted_iota(jnp.int32, (64, TILE), 0)
+    c = lax.broadcasted_iota(jnp.int32, (64, TILE), 1)
+    r8 = lax.broadcasted_iota(jnp.int32, (8, TILE), 0)
+    for j in range(SLOTS):
+        tile_copy(j).wait()
+        col_copy(j).wait()
+        tile = tile_buf[j]
         diag = tile_diag(tile)
-        out[i, 0:64] = OMEGA * cols[i][...] / diag
-        r = lax.broadcasted_iota(jnp.int32, (64, TILE), 0)
-        c = lax.broadcasted_iota(jnp.int32, (64, TILE), 1)
+        out_buf[j, 0:64] = col_buf[j] * (OMEGA / diag)
         below = pltpu.roll(tile[64:], 64, 1)
-        out[i, 64:128] = jnp.where((c < 64) & (r > c), below, tile[:64])
-        row = maps[slots[step * STEP + i]].astype(F32)
-        r8 = lax.broadcasted_iota(jnp.int32, (8, TILE), 0)
-        out[i, 128:136] = jnp.where(r8 == 0, diag, jnp.where(r8 == 1, row, 0.0))
-
-
-def boundary_pack(slot_list, diag_tiles, right_side, maps):
-    def tile_spec(i):
-        return pl.BlockSpec((1, TILE, TILE), lambda s, p: (p[s * STEP + i], 0, 0))
-
-    def col_spec(i):
-        return pl.BlockSpec((COLS, TILE), lambda s, p: (0, p[s * STEP + i]))
-
-    grid = pltpu.PrefetchScalarGridSpec(
-        num_scalar_prefetch=1,
-        grid=(NSTEP,),
-        in_specs=[tile_spec(i) for i in range(STEP)]
-        + [col_spec(i) for i in range(STEP)]
-        + [pl.BlockSpec((BLK, 1, TILE), lambda s, p: (0, 0, 0))],
-        out_specs=pl.BlockSpec((STEP, SIDE, TILE), lambda s, p: (s, 0, 0)),
-    )
+        out_buf[j, 64:128] = jnp.where((c < 64) & (r > c), below, tile[:64])
+        row = maps[pl.ds(slots[0, j // 2, j % 2], 1)].astype(F32)
+        out_buf[j, 128:136] = jnp.where(r8 == 0, diag, jnp.where(r8 == 1, row, 0.0))
+        out_copy(j).start()
+    for j in range(SLOTS):
+        out_copy(j).wait()
+
+
+def boundary_pack(slot_blocks, diag_tiles, right_side, maps):
     return pl.pallas_call(
         boundary_kernel,
-        grid_spec=grid,
-        out_shape=jax.ShapeDtypeStruct((SLOTS, SIDE, TILE), F32),
+        in_specs=[
+            pl.BlockSpec(memory_space=pltpu.SMEM),
+            pl.BlockSpec(memory_space=pltpu.VMEM),
+            pl.BlockSpec(memory_space=pl.ANY),
+            pl.BlockSpec(memory_space=pl.ANY),
+        ],
+        out_specs=pl.BlockSpec(memory_space=pl.ANY),
+        out_shape=far((SLOTS, SIDE, TILE)),
+        scratch_shapes=[
+            pltpu.VMEM((SLOTS, TILE, TILE), F32),
+            pltpu.VMEM((SLOTS, COLS, TILE), F32),
+            pltpu.VMEM((SLOTS, SIDE, TILE), F32),
+            pltpu.SemaphoreType.DMA((SLOTS,)),
+            pltpu.SemaphoreType.DMA((SLOTS,)),
+            pltpu.SemaphoreType.DMA((SLOTS,)),
+        ],
         compiler_params=params(),
         name="boundary_pack",
-    )(slot_list, *([diag_tiles] * STEP), *([right_side] * STEP), maps)
+    )(slot_blocks, maps, hbm(diag_tiles), hbm(right_side))
 
 
 def local_kernel(perm, counts, *refs):
@@ -167,10 +181,10 @@
     b = [cols[i][...] for i in range(n)]
     x = [OMEGA * bb / d for bb, d in zip(b, diag)]
     y = [bb - OMEGA * bb - mm(xx, *o) for bb, xx, o in zip(b, x, off)]
-    spread = [one_hot(maps[i]) for i in index]
+    spread = [one_hot(maps[pl.ds(i, 1)]) for i in index]
     total = rr[...]
-    for yy, sp in zip(y, spread):
-        total = total + mm_exact(yy, sp, nt=True)
+    for i in range(0, n, 2):
+        total = total + mm_exact(beside(y[i], y[i + 1]), beside(spread[i], spread[i + 1]), nt=True)
     for k in range(STEP):
         b_slot[k] = b[k]
         d_slot[k] = diag[k]
@@ -208,7 +222,7 @@
         + [col_spec(i) for i in range(n)]
         + [
             pl.BlockSpec((STEP, TILE, TILE), lambda s, p, c: (s, 0, 0)),
-            pl.BlockSpec((BLK, 1, TILE), lambda s, p, c: (0, 0, 0)),
+            pl.BlockSpec((BLK, TILE), lambda s, p, c: (0, 0)),
         ],
         out_specs=[
             out(COLS, TILE),
@@ -223,7 +237,7 @@
     )
 
     def sds(shape, dtype=F32):
-        return jax.ShapeDtypeStruct((SLOTS,) + shape, dtype)
+        return far((SLOTS,) + shape, dtype)
 
     return pl.pallas_call(
         local_kernel,
@@ -241,7 +255,7 @@
         compiler_params=params(),
         cost_estimate=cost(2 * 64 * 3 * 64 * 128 * 128, 16 << 20),
         name="local_part",
-    )(perm, counts, *([diag_tiles] * n), *([right_side] * n), remote, maps)
+    )(perm, counts, *([hbm(diag_tiles)] * n), *([hbm(right_side)] * n), hbm(remote), maps)
 
 
 def coarse_kernel(op, cmap, g_out, d_out):
@@ -276,24 +290,42 @@
     )(op, cmap)
 
 
-def first_restrict_kernel(arrived, rs, rr, out):
-    total = rr[...]
-    for j in range(SLOTS):
-        hi, lo = split2(rs[j])
-        total = total + mm(arrived[j, 0:64], hi, lo, nt=True)
-    packed = pack_rows(total)
-    for q in range(PEERS):
-        out[q, 0:32] = packed
-        out[q, 32:40] = jnp.zeros((8, TILE), F32)
+def first_restrict_kernel(arrived, rs, rr, out, acc):
+    step = pl.program_id(0)
+
+    @pl.when(step == 0)
+    def _():
+        acc[...] = rr[...]
+
+    total = acc[...]
+    for j in range(0, STEP, 2):
+        hi, lo = split2(beside(rs[j], rs[j + 1]))
+        total = total + mm(beside(arrived[j], arrived[j + 1]), hi, lo, nt=True)
+    acc[...] = total
+
+    @pl.when(step == NSTEP - 1)
+    def _():
+        packed = pack_rows(total)
+        for q in range(PEERS):
+            out[q, 0:32] = packed
+            out[q, 32:40] = jnp.zeros((8, TILE), F32)
 
 
 def first_restrict(arrived, rs, rr):
     return pl.pallas_call(
         first_restrict_kernel,
+        grid=(NSTEP,),
+        in_specs=[
+            pl.BlockSpec((STEP, COLS, TILE), lambda s: (s, 0, 0)),
+            pl.BlockSpec((STEP, AGG, TILE), lambda s: (s, 0, 0)),
+            pl.BlockSpec((COLS, AGG), lambda s: (0, 0)),
+        ],
+        out_specs=pl.BlockSpec((PEERS, ROWS, TILE), lambda s: (0, 0, 0)),
         out_shape=jax.ShapeDtypeStruct((PEERS, ROWS, TILE), F32),
+        scratch_shapes=[pltpu.VMEM((COLS, AGG), F32)],
         compiler_params=params(),
         name="first_restrict",
-    )(arrived, rs, rr)
+    )(hbm(arrived), hbm(rs), rr)
 
 
 def pair_kernel(perm, counts, *refs):
@@ -338,15 +370,15 @@
         pair_kernel,
         grid_spec=grid,
         out_shape=[
-            jax.ShapeDtypeStruct((SLOTS, 2 * TILE, 2 * TILE), BF16),
-            jax.ShapeDtypeStruct((SLOTS, 2 * TILE, 2 * TILE), BF16),
-            jax.ShapeDtypeStruct((SLOTS, 1, TILE), F32),
-            jax.ShapeDtypeStruct((SLOTS, 1, TILE), jnp.int32),
+            far((SLOTS, 2 * TILE, 2 * TILE), BF16),
+            far((SLOTS, 2 * TILE, 2 * TILE), BF16),
+            far((SLOTS, 1, TILE)),
+            far((SLOTS, 1, TILE), jnp.int32),
         ],
         compiler_params=params(),
         cost_estimate=cost(2 * 64 * 3 * 64 * 128 * 128, 16 << 20),
         name="pair_setup",
-    )(perm, counts, *([diag_tiles] * STEP), side, remote)
+    )(perm, counts, *([hbm(diag_tiles)] * STEP), hbm(side), hbm(remote))
 
 
 def gathered_rows(ref, count):
@@ -437,14 +469,19 @@
     return both[:rows] + both[rows:] + dot(xh, lo) + kept[:, : diag.shape[1]] * diag
 
 
-def lift(parts, row):
-    rows = parts.shape[0] // 3
-    three = dot(parts, one_hot(row))
-    return three[:rows] + three[rows : 2 * rows] + three[2 * rows :]
-
-
-def three_parts(e):
-    return jnp.concatenate(split3(e), axis=0)
+def lift(parts, spread):
+    rows = parts.shape[0] // 2
+    two = dot(parts, spread)
+    return two[:rows] + two[rows:]
+
+
+def two_parts(e):
+    return jnp.concatenate(split2(e), axis=0)
+
+
+def pair_spread(own, peer):
+    none = jnp.zeros_like(own)
+    return jnp.concatenate([beside(own, none), beside(none, peer)], axis=0)
 
 
 def forward_kernel(
@@ -459,11 +496,11 @@
         acc_bz[...] = jnp.zeros_like(acc_bz)
         acc_zw[...] = jnp.zeros_like(acc_zw)
 
-    e_mine = three_parts(e_own[0])
-    e_theirs = [three_parts(e_peer[q]) for q in range(STEP // 2)]
+    e_mine = two_parts(e_own[0])
+    e_both = [two_parts(beside(e_own[0], e_peer[q])) for q in range(STEP // 2)]
     rr, bz, zw = acc_rr[...], acc_bz[...], acc_zw[...]
     pairs, rest = range(STEP), range(STEP)
-    rows = [maps[perm[step * STEP + k]] for k in pairs] + [maps[perm[SLOTS + step * STEP + k]] for k in rest]
+    rows = [maps[pl.ds(perm[at + step * STEP + k], 1)] for at in (0, SLOTS) for k in pairs]
     b_own = [b_slot[k] for k in pairs] + [b_rest[k] for k in rest]
     diag = [jnp.concatenate([d_slot[k], d_peer[k]], axis=1) for k in pairs] + [d_rest[k] for k in rest]
     rdiag = [OMEGA / d for d in diag]
@@ -471,9 +508,9 @@
     full = [
         jnp.concatenate([b_own[k], x_peer[k] * (d_peer[k] * (1.0 / OMEGA))], axis=1) for k in pairs
     ] + b_own[STEP:]
-    ups = [lift(e_mine, row) for row in rows]
-    ups_peer = [lift(e_theirs[k // 2], m_peer[k]) for k in pairs]
-    ups = [jnp.concatenate([ups[k], ups_peer[k]], axis=1) for k in pairs] + ups[STEP:]
+    spread = [one_hot(row) for row in rows]
+    ups = [lift(e_both[k // 2], pair_spread(spread[k], one_hot(m_peer[k]))) for k in pairs]
+    ups = ups + [lift(e_mine, sp) for sp in spread[STEP:]]
     x = [f * rd + up for f, rd, up in zip(full, rdiag, ups)]
     image = [apply_block(xx, d, *m) for xx, d, m in zip(x, diag, mats)]
     z = [xx + (f - im) * rd for xx, f, im, rd in zip(x, full, image, rdiag)]
@@ -483,8 +520,8 @@
     y = [
         ww[:, :TILE] - apply_block(xx, d[:, :TILE], *m) for ww, xx, d, m in zip(w, x1, diag, left)
     ]
-    for row, yy in zip(rows, y):
-        rr = rr + mm_exact(yy, one_hot(row), nt=True)
+    for i in range(0, 2 * STEP, 2):
+        rr = rr + mm_exact(beside(y[i], y[i + 1]), beside(spread[i], spread[i + 1]), nt=True)
     for i in range(2 * STEP):
         zz, ww = z[i][:, :TILE], w[i][:, :TILE]
         bz = bz + b_own[i] * zz
@@ -540,7 +577,7 @@
             step_spec(2 * TILE, 2 * TILE),
             step_spec(TILE, TILE),
             step_spec(TILE, TILE),
-            pl.BlockSpec((BLK, 1, TILE), lambda s, p, m: (0, 0, 0)),
+            pl.BlockSpec((BLK, TILE), lambda s, p, m: (0, 0)),
         ],
         out_specs=[
             pair_spec(),
@@ -554,14 +591,14 @@
         forward_kernel,
         grid_spec=grid,
         out_shape=[
-            jax.ShapeDtypeStruct((2, SLOTS, COLS, TILE), F32),
-            jax.ShapeDtypeStruct((2, SLOTS, COLS, TILE), F32),
-            jax.ShapeDtypeStruct((SLOTS, COLS, TILE), F32),
+            far((2, SLOTS, COLS, TILE)),
+            far((2, SLOTS, COLS, TILE)),
+            far((SLOTS, COLS, TILE)),
             jax.ShapeDtypeStruct((PEERS, ROWS, TILE), F32),
         ],
         compiler_params=params(),
         name="forward_part",
-    )(perm, member, e, e, b_slot, b_rest, d_slot, d_rest, x_peer, d_peer, m_peer, hi_pair, lo_pair, hi_rest, lo_rest, maps)
+    )(perm, member, e, e, *map(hbm, (b_slot, b_rest, d_slot, d_rest, x_peer, d_peer, m_peer, hi_pair, lo_pair, hi_rest, lo_rest)), maps)
 
 
 def second_kernel(
@@ -578,8 +615,8 @@
 
     col = column(dots[0:1])
     alpha = col[:COLS] / col[COLS:]
-    e_mine = three_parts(e_own[0])
-    e_theirs = [three_parts(e_peer[q]) for q in range(STEP // 2)]
+    e_mine = two_parts(e_own[0])
+    e_both = [two_parts(beside(e_own[0], e_peer[q])) for q in range(STEP // 2)]
     sums = [acc_a[...], acc_b[...], acc_c[...]]
 
     def gather(b, z, w, v, u):
@@ -591,14 +628,14 @@
         sums[2] = sums[2] + (z1 * w + z * az1)
 
     pairs, rest = range(STEP), range(STEP)
-    rows = [maps[perm[step * STEP + k]] for k in pairs] + [maps[perm[SLOTS + step * STEP + k]] for k in rest]
+    rows = [maps[pl.ds(perm[at + step * STEP + k], 1)] for at in (0, SLOTS) for k in pairs]
     diag = [jnp.concatenate([d_slot[k], d_peer[k]], axis=1) for k in pairs] + [d_rest[k] for k in rest]
     rdiag = [OMEGA / d for d in diag]
     mats = [(hi_pair[k], lo_pair[k]) for k in pairs] + [(hi_rest[k], lo_rest[k]) for k in rest]
     w = [jnp.concatenate([w_in[0, k], w_peer[k]], axis=1) for k in pairs] + [w_in[1, k] for k in rest]
-    ups = [lift(e_mine, row) for row in rows]
-    ups_peer = [lift(e_theirs[k // 2], m_peer[k]) for k in pairs]
-    ups = [jnp.concatenate([ups[k], ups_peer[k]], axis=1) for k in pairs] + ups[STEP:]
+    spread = [one_hot(row) for row in rows]
+    ups = [lift(e_both[k // 2], pair_spread(spread[k], one_hot(m_peer[k]))) for k in pairs]
+    ups = ups + [lift(e_mine, sp) for sp in spread[STEP:]]
     x = [ww * rd + up for ww, rd, up in zip(w, rdiag, ups)]
     image = [apply_block(xx, d, *m) for xx, d, m in zip(x, diag, mats)]
     v = [xx + (ww - im) * rd for xx, ww, im, rd in zip(x, w, image, rdiag)]
@@ -640,7 +677,7 @@
             step_spec(2 * TILE, 2 * TILE),
             step_spec(TILE, TILE),
             step_spec(TILE, TILE),
-            pl.BlockSpec((BLK, 1, TILE), lambda s, p, m: (0, 0, 0)),
+            pl.BlockSpec((BLK, TILE), lambda s, p, m: (0, 0)),
             pair_spec(),
             pair_spec(),
             step_spec(COLS, TILE),
@@ -656,13 +693,13 @@
         second_kernel,
         grid_spec=grid,
         out_shape=[
-            jax.ShapeDtypeStruct((2, SLOTS, COLS, TILE), F32),
-            jax.ShapeDtypeStruct((2, SLOTS, COLS, TILE), F32),
+            far((2, SLOTS, COLS, TILE)),
+            far((2, SLOTS, COLS, TILE)),
             jax.ShapeDtypeStruct((GROUPS * PEERS, 8, TILE), F32),
         ],
         compiler_params=params(),
         name="second_part",
-    )(perm, member, e, e, dots, b_slot, b_rest, d_slot, d_rest, d_peer, m_peer, hi_pair, lo_pair, hi_rest, lo_rest, maps, z, w, w_peer)
+    )(perm, member, e, e, dots, *map(hbm, (b_slot, b_rest, d_slot, d_rest, d_peer, m_peer, hi_pair, lo_pair, hi_rest, lo_rest)), maps, *map(hbm, (z, w, w_peer)))
 
 
 def combine_kernel(perm, dots, arrived, b_slot, b_rest, z, w, v, u, solution, residual, coef):
@@ -752,11 +789,11 @@
     member = lax.axis_index(GROUP_AXES).astype(jnp.int32).reshape(1)
     slot_list = slot_blocks.reshape(SLOTS)
     counts = slot_counts.reshape(PEERS)
-    maps = fine_map.reshape(BLK, 1, TILE)
+    maps = fine_map.reshape(BLK, TILE)
     remote = remote_tiles.reshape(SLOTS, TILE, TILE)
     operator = level1_ops[0]
 
-    outgoing = boundary_pack(slot_list, diag_tiles, right_side, maps)
+    outgoing = boundary_pack(slot_blocks, diag_tiles, right_side, maps)
     side = exchange(outgoing.reshape(PEERS, 2 * SIDE, TILE), GROUP_AXES).reshape(SLOTS, SIDE, TILE)
 
     tile_ids = jnp.arange(BLK, dtype=jnp.int32)

time: 187 us -> 160 us (0.86)
  local copies, waits for them, and re-layouts: 57.8 us -> 9.41 us
  Pallas kernels: 47.2 us -> 62.2 us
  waiting for transfers between devices: 21.6 us -> 28.9 us
    unnamed x107 -> x29, local copies, waits for them, and re-layouts: 56.9 us -> 9.2 us
    pallas_call x5, Pallas kernels: 28.1 us -> 41.5 us  [the longest x1 12.2 us: forward_part(): pl.pallas_call(forward_kernel, grid_spec=grid, out_shape=[far((2, SLOTS,...]
    all_to_all x4, waiting for transfers between devices: 21.6 us -> 28.9 us  [exchange(): return lax.all_to_all(x, axes, 0, 0, tiled=True)]
    pallas_call x1, Pallas kernels: 6.64 us -> 9.4 us  [local_part(): pl.pallas_call(local_kernel, grid_spec=grid, out_shape=[sds((COLS, TILE))...]
  transfers between devices with their start and end apart: 4 -> 4, of which waited for: 3 -> 3; matrix products, arithmetic and copies ran while one was open for 1% -> 0% of each run, Pallas kernels for 7% -> 13%
where the time goes in v3:
time: 160 us; the launch traced here: 159 us
  Pallas kernels  62.2 us (39%)
  blocking collectives  29.3 us (18%)
  waiting for transfers between devices  28.9 us (18%)
  starting transfers between devices  27.8 us (17%)
  local copies, waits for them, and re-layouts  9.41 us (6%)
    all_to_all x2, blocking collectives, exchange(): return lax.all_to_all(x, axes, 0, 0, tiled=True)  29.3 us
    all_to_all x4, waiting for transfers between devices, exchange(): return lax.all_to_all(x, axes, 0, 0, tiled=True)  28.9 us
    all_to_all x4, starting transfers between devices, exchange(): return lax.all_to_all(x, axes, 0, 0, tiled=True)  27.8 us
    pallas_call x1, Pallas kernels, forward_part(): pl.pallas_call(forward_kernel, grid_spec=grid, out_shape=[far((2, SLOTS,...  12.2 us
    pallas_call x1, Pallas kernels, second_part(): pl.pallas_call(second_kernel, grid_spec=grid, out_shape=[far((2, SLOTS, C...  11.8 us
    pallas_call x1, Pallas kernels, local_part(): pl.pallas_call(local_kernel, grid_spec=grid, out_shape=[sds((COLS, TILE))...  9.4 us
    unnamed x29, local copies, waits for them, and re-layouts  9.2 us
    pallas_call x1, Pallas kernels, pair_setup(): pl.pallas_call(pair_kernel, grid_spec=grid, out_shape=[far((SLOTS, 2 * TI...  8.27 us
  transfers between devices with their start and end apart: 4, of which 3 were waited for; matrix products, arithmetic and copies ran while one was open for 0% of the time, Pallas kernels for 13%

profile of v3, /device:TPU:1, one launch (start us, length us, event | category | flops | bytes accessed | tf_op | source)
XLA Modules:
  0.0 158.8 jit_solution(4453688207497741806)
XLA Ops:
  2.2 5.5 %boundary_pack.1 = f32[32,136,128]{2,1,0:T(8,128)} custom-call(s32[1,16,2]{2,1,0:T(8,128)S(1)} %copy.15.slots, s32[64,128]{1,0:T(8,128)S(1)} %bitcast.11, f32[64,128,128]{2,1,0:T(8,128)} %refs_7_.3, f32[64,8192]{1,0:T(8,128)} %refs_31_.1), custom_call_target="tpu_custom_call" | custom-call | tf_op jit(solution)/shard_map/boundary_pack/pallas_call | solution.py:143
  7.8 8.5 %all-to-all-start = ((f32[16,272,128]{2,1,0:T(8,128)}), f32[16,272,128]{2,1,0:T(8,128)}, u32[]{:S(2)}, u32[]{:S(2)}) async-start(f32[16,272,128]{2,1,0:T(8,128)} %bitcast.18), calls=%async_computation | async-start | bytes 4456448 | tf_op jit(solution)/shard_map/all_to_all | solution.py:774
  16.8 9.4 %local_part.1 = (f32[32,64,128]{2,1,0:T(8,128)}, f32[32,64,128]{2,1,0:T(8,128)}, f32[32,1,128]{2,1,0:T(1,128)}, f32[32,1,128]{2,1,0:T(1,128)}, bf16[32,128,128]{...) custom-call(s32[64]{0:T(128)S(1)} %pad_add_fusion.perm, ...), custom_call_target="tpu_custom_call" | custom-call | flops 402653184 | bytes 16777216 | tf_op jit(solution)/shard_map/local_part/pallas_call | solution.py:242
  26.2 21.7 %all-to-all-done = f32[16,272,128]{2,1,0:T(8,128)} async-done(((f32[16,272,128]{2,1,0:T(8,128)}), f32[16,272,128]{2,1,0:T(8,128)}, u32[]{:S(2)}, u32[]{:S(2)}) %all-to-all-start) | async-done | bytes 2228256 | tf_op jit(solution)/shard_map/all_to_all | solution.py:774
  47.9 3.7 %first_restrict.1 = f32[16,40,128]{2,1,0:T(8,128)} custom-call(f32[32,136,128]{2,1,0:T(8,128)} %bitcast.3.arrived.refs_8_.x_peer, f32[32,64,128]{2,1,0:T(8,128)} %get-tuple-element.30.rs, f32[64,64]{1,0:T(8,128)S(1)} %get-tuple-element.31.rr), custom_call_target="tpu_custom_call" | custom-call | tf_op jit(solution)/shard_map/first_restrict/pallas_call | solution.py:315
  51.6 5.9 %all-to-all-start.1 = ((f32[16,40,128]{2,1,0:T(8,128)}), f32[16,40,128]{2,1,0:T(8,128)S(1)}, u32[]{:S(2)}, u32[]{:S(2)}) async-start(f32[16,40,128]{2,1,0:T(8,128)} %first_restrict.1), calls=%async_computation.1 | async-start | bytes 655360 | tf_op jit(solution)/shard_map/all_to_all | solution.py:774
  57.6 2.2 %copy-done.1 = f32[1,1024,1024]{2,1,0:T(8,128)S(1)} copy-done((f32[1,1024,1024]{2,1,0:T(8,128)S(1)}, f32[1,1024,1024]{2,1,0:T(8,128)}, u32[]{:S(2)}) %copy-start.1) | copy-done | bytes 4194328
  59.8 1.0 coarse_setup.1
  60.8 4.7 %all-to-all-done.1.arrived = f32[16,40,128]{2,1,0:T(8,128)S(1)} async-done(((f32[16,40,128]{2,1,0:T(8,128)}), f32[16,40,128]{2,1,0:T(8,128)S(1)}, u32[]{:S(2)}, u32[]{:S(2)}) %all-to-all-start.1) | async-done | bytes 327712 | tf_op jit(solution)/shard_map/all_to_all | solution.py:774
  65.5 1.1 lowest_part.2
  66.6 7.6 %all-to-all-start.2 = ((f32[8,40,128]{2,1,0:T(8,128)}), f32[8,40,128]{2,1,0:T(8,128)S(1)}, u32[]{:S(2)}, u32[]{:S(2)}) async-start(f32[8,40,128]{2,1,0:T(8,128)} %get-tuple-element.33), calls=%async_computation.2 | async-start | bytes 327680 | tf_op jit(solution)/shard_map/all_to_all | solution.py:774
  74.3 8.3 %pair_setup.1 = (bf16[32,256,256]{2,1,0:T(8,128)(2,1)}, bf16[32,256,256]{2,1,0:T(8,128)(2,1)}, f32[32,1,128]{2,1,0:T(1,128)}, s32[32,1,128]{2,1,0:T(1,128)}) custom-call(s32[64]{0:T(128)S(1)} %pad_add_fusion.perm, s32[16]{0:T(128)S(1)} %bitcast.17, f32[64,128,128]{2,1,0:T(8,128)} %refs_7_.3, f32[64,128,128]{2,1,0:T(8,128)} %refs_7_.3, ...), custom_call_target="tpu_custom_call" | custom-call | flops 402653184 | bytes 16777216 | tf_op jit(solution)/shard_map/pair_setup/pallas_call | solution.py:369
  83.6 1.1 correct_part.2
  84.7 12.2 %forward_part.1 = (f32[2,32,64,128]{3,2,1,0:T(8,128)}, f32[2,32,64,128]{3,2,1,0:T(8,128)}, f32[32,64,128]{2,1,0:T(8,128)}, f32[16,40,128]{2,1,0:T(8,128)S(1)}) custom-call(s32[64]{0:T(128)S(1)} %pad_add_fusion.perm, s32[1]{0:T(128)} %bitcast.member, f32[16,64,64]{2,1,0:T(8,128)S(1)} %get-tuple-element.36.e_own.e_peer, ...), custom_call_target="tpu_custom_call" | custom-call | tf_op jit(solution)/shard_map/forward_part/pallas_call | solution.py:590
  96.9 11.6 %all_to_all.30.arrived = f32[16,40,128]{2,1,0:T(8,128)S(1)} all-to-all(f32[16,40,128]{2,1,0:T(8,128)S(1)} %get-tuple-element.47), channel_id=1, replica_groups=mesh['grp'=8,'sub'=8,'chip'=2] {'sub','chip'}, dimensions={0} | all-to-all | bytes 655360 | tf_op jit(solution)/shard_map/all_to_all | solution.py:774
  108.5 1.1 lowest_part.3
  109.6 5.8 %all-to-all-start.4 = ((f32[8,40,128]{2,1,0:T(8,128)}), f32[8,40,128]{2,1,0:T(8,128)S(1)}, u32[]{:S(2)}, u32[]{:S(2)}) async-start(f32[8,40,128]{2,1,0:T(8,128)} %get-tuple-element.48), calls=%async_computation.4 | async-start | bytes 327680 | tf_op jit(solution)/shard_map/all_to_all | solution.py:774
  115.4 2.2 %copy-done.3 = f32[1,1024,1024]{2,1,0:T(8,128)S(1)} copy-done((f32[1,1024,1024]{2,1,0:T(8,128)S(1)}, f32[1,1024,1024]{2,1,0:T(8,128)}, u32[]{:S(2)}) %copy-start.3) | copy-done | bytes 4194328
  118.5 2.4 %all-to-all-done.4.arrived = f32[8,40,128]{2,1,0:T(8,128)S(1)} async-done(((f32[8,40,128]{2,1,0:T(8,128)}), f32[8,40,128]{2,1,0:T(8,128)S(1)}, u32[]{:S(2)}, u32[]{:S(2)}) %all-to-all-start.4) | async-done | bytes 163872 | tf_op jit(solution)/shard_map/all_to_all | solution.py:774
  121.6 11.8 %second_part.1 = (f32[2,32,64,128]{3,2,1,0:T(8,128)}, f32[2,32,64,128]{3,2,1,0:T(8,128)}, f32[128,8,128]{2,1,0:T(8,128)S(1)}) custom-call(s32[64]{0:T(128)S(1)} %pad_add_fusion.perm, s32[1]{0:T(128)} %bitcast.member, f32[16,64,64]{2,1,0:T(8,128)S(1)} %get-tuple-element.51.e_own.e_peer, f32[16,64,64]{2,1,0:T(8,128)S(1)} %get-tuple-element.51.e_own.e_peer, ...), custom_call_target="tpu_custom_call" | custom-call | tf_op jit(solution)/shard_map/second_part/pallas_call | solution.py:692
  133.4 17.8 %all_to_all.31.arrived = f32[128,8,128]{2,1,0:T(8,128)S(1)} all-to-all(f32[128,8,128]{2,1,0:T(8,128)S(1)} %get-tuple-element.55), channel_id=1, replica_groups=mesh['grp'=8,'sub'=8,'chip'=2] {'grp','sub','chip'}, dimensions={0} | all-to-all | bytes 1048576 | tf_op jit(solution)/shard_map/all_to_all | solution.py:774
  151.2 1.6 copy-done.8
  152.7 1.6 %copy-done.9 = f32[2,32,64,128]{3,2,1,0:T(8,128)S(1)} copy-done((f32[2,32,64,128]{3,2,1,0:T(8,128)S(1)}, f32[2,32,64,128]{3,2,1,0:T(8,128)}, u32[]{:S(2)}) %copy-start.9) | copy-done | bytes 2097176
  154.3 4.5 %combine.1 = (f32[64,8192]{1,0:T(8,128)}, f32[64,8192]{1,0:T(8,128)}) custom-call(s32[64]{0:T(128)S(1)} %pad_add_fusion.perm, f32[8,128]{1,0:T(8,128)S(1)} %get-tuple-element.50.dots, f32[128,8,128]{2,1,0:T(8,128)S(1)} %all_to_all.31.arrived, f32[32,64,128]{2,1,0:T(8,128)S(1)} %copy-done.4, f32[32,64,128]{2,1,0:T(8,128)S(1)} %copy-done.5, ...), custom_call_target="tpu_custom_call" | custom-call | tf_op jit(solution)/shard_map/combine/pallas_call | solution.py:764
  (36 shorter events, 4.8 us)
Async XLA Ops:
  0.6 73.6 %copy-start = (f32[512,512]{1,0:T(8,128)S(1)}, f32[512,512]{1,0:T(8,128)}, u32[]{:S(2)}) copy-start(f32[512,512]{1,0:T(8,128)} %param.17) | copy-start | bytes 3145732
  1.5 0.8 copy-start.10
  7.7 9.0 %copy-start.11 = (s32[8192]{0:T(1024)S(1)}, s32[8192]{0:T(1024)}, u32[]{:S(2)}) copy-start(s32[8192]{0:T(1024)} %param.14) | copy-start | bytes 98308
  7.8 9.0 %copy-start.13 = (s32[1,16]{1,0:T(1,128)S(1)}, s32[1,16]{1,0:T(1,128)}, u32[]{:S(2)}) copy-start(s32[1,16]{1,0:T(1,128)} %param.12) | copy-start | bytes 196
  7.8 40.1 %all-to-all-start = ((f32[16,272,128]{2,1,0:T(8,128)}), f32[16,272,128]{2,1,0:T(8,128)}, u32[]{:S(2)}, u32[]{:S(2)}) async-start(f32[16,272,128]{2,1,0:T(8,128)} %bitcast.18), calls=%async_computation | async-start | bytes 4456448 | tf_op jit(solution)/shard_map/all_to_all | solution.py:774
  47.9 9.7 %copy-start.12 = (s32[1024]{0:T(1024)S(1)}, s32[1024]{0:T(1024)}, u32[]{:S(2)}) copy-start(s32[1024]{0:T(1024)} %param.15) | copy-start | bytes 12292
  51.6 13.9 %all-to-all-start.1 = ((f32[16,40,128]{2,1,0:T(8,128)}), f32[16,40,128]{2,1,0:T(8,128)S(1)}, u32[]{:S(2)}, u32[]{:S(2)}) async-start(f32[16,40,128]{2,1,0:T(8,128)} %first_restrict.1), calls=%async_computation.1 | async-start | bytes 655360 | tf_op jit(solution)/shard_map/all_to_all | solution.py:774
  57.6 2.2 %copy-start.1 = (f32[1,1024,1024]{2,1,0:T(8,128)S(1)}, f32[1,1024,1024]{2,1,0:T(8,128)}, u32[]{:S(2)}) copy-start(f32[1,1024,1024]{2,1,0:T(8,128)} %param.16) | copy-start | bytes 12582916
  66.6 17.0 %all-to-all-start.2 = ((f32[8,40,128]{2,1,0:T(8,128)}), f32[8,40,128]{2,1,0:T(8,128)S(1)}, u32[]{:S(2)}, u32[]{:S(2)}) async-start(f32[8,40,128]{2,1,0:T(8,128)} %get-tuple-element.33), calls=%async_computation.2 | async-start | bytes 327680 | tf_op jit(solution)/shard_map/all_to_all | solution.py:774
  74.3 8.3 %copy-start.2 = (f32[1,1024,1024]{2,1,0:T(8,128)S(1)}, f32[1,1024,1024]{2,1,0:T(8,128)}, u32[]{:S(2)}) copy-start(f32[1,1024,1024]{2,1,0:T(8,128)} %param.16) | copy-start | bytes 12582916
  109.6 11.4 %all-to-all-start.4 = ((f32[8,40,128]{2,1,0:T(8,128)}), f32[8,40,128]{2,1,0:T(8,128)S(1)}, u32[]{:S(2)}, u32[]{:S(2)}) async-start(f32[8,40,128]{2,1,0:T(8,128)} %get-tuple-element.48), calls=%async_computation.4 | async-start | bytes 327680 | tf_op jit(solution)/shard_map/all_to_all | solution.py:774
  115.4 2.2 %copy-start.3 = (f32[1,1024,1024]{2,1,0:T(8,128)S(1)}, f32[1,1024,1024]{2,1,0:T(8,128)}, u32[]{:S(2)}) copy-start(f32[1,1024,1024]{2,1,0:T(8,128)} %param.16) | copy-start | bytes 12582916
  121.6 29.6 %copy-start.4 = (f32[32,64,128]{2,1,0:T(8,128)S(1)}, f32[32,64,128]{2,1,0:T(8,128)}, u32[]{:S(2)}) copy-start(f32[32,64,128]{2,1,0:T(8,128)} %get-tuple-element.37.b_slot) | copy-start | bytes 3145732
  121.6 29.6 %copy-start.5 = (f32[32,64,128]{2,1,0:T(8,128)S(1)}, f32[32,64,128]{2,1,0:T(8,128)}, u32[]{:S(2)}) copy-start(f32[32,64,128]{2,1,0:T(8,128)} %get-tuple-element.38.b_rest) | copy-start | bytes 3145732
  121.6 29.6 %copy-start.6 = (f32[2,32,64,128]{3,2,1,0:T(8,128)S(1)}, f32[2,32,64,128]{3,2,1,0:T(8,128)}, u32[]{:S(2)}) copy-start(f32[2,32,64,128]{3,2,1,0:T(8,128)} %get-tuple-element.52.z_in.z) | copy-start | bytes 6291460
  121.6 29.6 %copy-start.7 = (f32[2,32,64,128]{3,2,1,0:T(8,128)S(1)}, f32[2,32,64,128]{3,2,1,0:T(8,128)}, u32[]{:S(2)}) copy-start(f32[2,32,64,128]{3,2,1,0:T(8,128)} %get-tuple-element.53.w_in.w) | copy-start | bytes 6291460
  151.2 1.6 %copy-start.8 = (f32[2,32,64,128]{3,2,1,0:T(8,128)S(1)}, f32[2,32,64,128]{3,2,1,0:T(8,128)}, u32[]{:S(2)}) copy-start(f32[2,32,64,128]{3,2,1,0:T(8,128)} %get-tuple-element.56.v) | copy-start | bytes 6291460
  152.7 1.6 %copy-start.9 = (f32[2,32,64,128]{3,2,1,0:T(8,128)S(1)}, f32[2,32,64,128]{3,2,1,0:T(8,128)}, u32[]{:S(2)}) copy-start(f32[2,32,64,128]{3,2,1,0:T(8,128)} %get-tuple-element.57.u) | copy-start | bytes 6291460

commit v4 on v3

--- a/solution.py
+++ b/solution.py
@@ -329,7 +329,7 @@
 
 
 def pair_kernel(perm, counts, *refs):
-    tiles, side, remote, hi_out, lo_out, diag_out, map_out = (refs[:STEP],) + tuple(refs[STEP:])
+    tiles, side, remote, hi_out, lo_out, diag_out, map_out, x_out = (refs[:STEP],) + tuple(refs[STEP:])
     step = pl.program_id(0)
     r = lax.broadcasted_iota(jnp.int32, (64, TILE), 0)
     c = lax.broadcasted_iota(jnp.int32, (64, TILE), 1)
@@ -349,6 +349,7 @@
         hi, lo = split2(block)
         hi_out[k] = hi
         lo_out[k] = lo
+        x_out[k] = side[k, 0:64]
         diag_out[k] = side[k, 128:129]
         map_out[k] = side[k, 129:130].astype(jnp.int32)
 
@@ -364,7 +365,7 @@
         num_scalar_prefetch=2,
         grid=(NSTEP,),
         in_specs=[tile_spec(i) for i in range(STEP)] + [spec(SIDE, TILE), spec(TILE, TILE)],
-        out_specs=[spec(2 * TILE, 2 * TILE), spec(2 * TILE, 2 * TILE), spec(1, TILE), spec(1, TILE)],
+        out_specs=[spec(2 * TILE, 2 * TILE), spec(2 * TILE, 2 * TILE), spec(1, TILE), spec(1, TILE), spec(COLS, TILE)],
     )
     return pl.pallas_call(
         pair_kernel,
@@ -374,6 +375,7 @@
             far((SLOTS, 2 * TILE, 2 * TILE), BF16),
             far((SLOTS, 1, TILE)),
             far((SLOTS, 1, TILE), jnp.int32),
+            far((SLOTS, COLS, TILE)),
         ],
         compiler_params=params(),
         cost_estimate=cost(2 * 64 * 3 * 64 * 128 * 128, 16 << 20),
@@ -416,34 +418,20 @@
     )(arrived, g)
 
 
-def smooth_kernel(x_ref, inverse_ref, op, out):
+def correct_kernel(arrived, inverse_cols, g, x_ref, inverse_ref, op, e_out, dots):
     inverse = inverse_ref[...]
     scaled = x_ref[...] * inverse
     total = None
     for i in range(NC1 // 256):
         rows = slice(i * 256, (i + 1) * 256)
         hi, lo = split2(op[rows, :])
-        part = mm(scaled[:, rows], hi, lo)
-        total = part if total is None else total + part
-    out[...] = 2.0 * OMEGA * scaled - OMEGA * OMEGA * total * inverse
-
-
-def smooth_part(x, inverse, op):
-    return pl.pallas_call(
-        smooth_kernel,
-        out_shape=jax.ShapeDtypeStruct((COLS, NC1), F32),
-        compiler_params=params(),
-        cost_estimate=cost(2 * 3 * 64 * 1024 * 1024, 5 << 20),
-        name="smooth_part",
-    )(x, inverse, op)
-
-
-def correct_kernel(arrived, inverse_cols, g, h, e_out, dots):
+        term = mm(scaled[:, rows], hi, lo)
+        total = term if total is None else total + term
     low = gathered_rows(arrived, GROUPS)
     hi, lo = split2(inverse_cols[...])
     corr = mm(low, hi, lo)
     ghi, glo = split2(g[...])
-    e = h[...] + mm(corr, ghi, glo)
+    e = 2.0 * OMEGA * scaled - OMEGA * OMEGA * total * inverse + mm(corr, ghi, glo)
     for q in range(PEERS):
         e_out[q] = e[:, q * AGG : (q + 1) * AGG]
     extra = arrived[0, 32:40]
@@ -452,13 +440,13 @@
     dots[...] = extra
 
 
-def correct_part(arrived, inverse_cols, g, h):
+def correct_part(arrived, inverse_cols, g, x, inverse, op):
     return pl.pallas_call(
         correct_kernel,
         out_shape=[jax.ShapeDtypeStruct((PEERS, COLS, AGG), F32), jax.ShapeDtypeStruct((8, TILE), F32)],
         compiler_params=params(),
         name="correct_part",
-    )(arrived, inverse_cols, g, h)
+    )(arrived, inverse_cols, g, x, inverse, op)
 
 
 def apply_block(x, diag, hi, lo):
@@ -485,17 +473,39 @@
 
 
 def forward_kernel(
-    perm, member, e_own, e_peer, b_slot, b_rest, d_slot, d_rest, x_peer, d_peer, m_peer, hi_pair, lo_pair,
+    perm, member, e, b_slot, b_rest, d_slot, d_rest, x_peer, d_peer, m_peer, hi_pair, lo_pair,
     hi_rest, lo_rest, maps, z_out, w_out, ws_out, out, acc_rr, acc_bz, acc_zw
 ):
-    step = pl.program_id(0)
-
-    @pl.when(step == 0)
-    def _():
-        acc_rr[...] = jnp.zeros_like(acc_rr)
-        acc_bz[...] = jnp.zeros_like(acc_bz)
-        acc_zw[...] = jnp.zeros_like(acc_zw)
-
+    acc_rr[...] = jnp.zeros_like(acc_rr)
+    acc_bz[...] = jnp.zeros_like(acc_bz)
+    acc_zw[...] = jnp.zeros_like(acc_zw)
+    e_own = e.at[pl.ds(member[0], 1)]
+    views = (e, b_slot, b_rest, d_slot, d_rest, x_peer, d_peer, m_peer, hi_pair, lo_pair, hi_rest, lo_rest, ws_out)
+
+    @pl.loop(0, NSTEP)
+    def _(step):
+        e_peer, *parts = [v.at[part(step, v.shape[0])] for v in views]
+        both = [v.at[:, part(step, SLOTS)] for v in (z_out, w_out)]
+        forward_step(step, perm, e_own, e_peer, *parts[:-1], maps, *both, parts[-1], acc_rr, acc_bz, acc_zw)
+
+    packed = pack_rows(acc_rr[...])
+    sums = jnp.sum(jnp.concatenate([acc_bz[...], acc_zw[...]], axis=0).T, axis=0, keepdims=True)
+    r8 = lax.broadcasted_iota(jnp.int32, (8, TILE), 0)
+    extra = jnp.where(r8 == 0, sums, 0.0)
+    for q in range(PEERS):
+        out[q, 0:32] = packed
+        out[q, 32:40] = extra
+
+
+def part(step, count):
+    size = count // NSTEP
+    return pl.ds(step * size, size)
+
+
+def forward_step(
+    step, perm, e_own, e_peer, b_slot, b_rest, d_slot, d_rest, x_peer, d_peer, m_peer, hi_pair, lo_pair,
+    hi_rest, lo_rest, maps, z_out, w_out, ws_out, acc_rr, acc_bz, acc_zw
+):
     e_mine = two_parts(e_own[0])
     e_both = [two_parts(beside(e_own[0], e_peer[q])) for q in range(STEP // 2)]
     rr, bz, zw = acc_rr[...], acc_bz[...], acc_zw[...]
@@ -534,87 +544,62 @@
     acc_bz[...] = bz
     acc_zw[...] = zw
 
-    @pl.when(step == NSTEP - 1)
-    def _():
-        packed = pack_rows(rr)
-        sums = jnp.sum(jnp.concatenate([bz, zw], axis=0).T, axis=0, keepdims=True)
-        r8 = lax.broadcasted_iota(jnp.int32, (8, TILE), 0)
-        extra = jnp.where(r8 == 0, sums, 0.0)
-        for q in range(PEERS):
-            out[q, 0:32] = packed
-            out[q, 32:40] = extra
-
-
-def step_spec(*shape):
-    return pl.BlockSpec((STEP,) + shape, lambda s, p, m: (s, 0, 0))
-
-
-def pair_spec():
-    return pl.BlockSpec((2, STEP, COLS, TILE), lambda s, p, m: (0, s, 0, 0))
-
-
-def e_specs():
-    return [
-        pl.BlockSpec((1, COLS, AGG), lambda s, p, m: (m[0], 0, 0)),
-        pl.BlockSpec((STEP // 2, COLS, AGG), lambda s, p, m: (s, 0, 0)),
-    ]
-
-
-def forward_part(perm, member, e, b_slot, b_rest, d_slot, d_rest, x_peer, d_peer, m_peer, hi_pair, lo_pair, hi_rest, lo_rest, maps):
-    grid = pltpu.PrefetchScalarGridSpec(
-        num_scalar_prefetch=2,
-        grid=(NSTEP,),
-        in_specs=e_specs()
-        + [
-            step_spec(COLS, TILE),
-            step_spec(COLS, TILE),
-            step_spec(1, TILE),
-            step_spec(1, TILE),
-            step_spec(COLS, TILE),
-            step_spec(1, TILE),
-            step_spec(1, TILE),
-            step_spec(2 * TILE, 2 * TILE),
-            step_spec(2 * TILE, 2 * TILE),
-            step_spec(TILE, TILE),
-            step_spec(TILE, TILE),
-            pl.BlockSpec((BLK, TILE), lambda s, p, m: (0, 0)),
-        ],
-        out_specs=[
-            pair_spec(),
-            pair_spec(),
-            step_spec(COLS, TILE),
-            pl.BlockSpec((PEERS, ROWS, TILE), lambda s, p, m: (0, 0, 0)),
+
+def in_vmem(count):
+    return [pl.BlockSpec(memory_space=pltpu.SMEM)] * 2 + [pl.BlockSpec(memory_space=pltpu.VMEM)] * count
+
+
+def forward_part(perm, member, *arrays):
+    return pl.pallas_call(
+        forward_kernel,
+        in_specs=in_vmem(len(arrays)),
+        out_specs=[pl.BlockSpec(memory_space=pltpu.VMEM)] * 4,
+        out_shape=[
+            jax.ShapeDtypeStruct((2, SLOTS, COLS, TILE), F32),
+            jax.ShapeDtypeStruct((2, SLOTS, COLS, TILE), F32),
+            jax.ShapeDtypeStruct((SLOTS, COLS, TILE), F32),
+            jax.ShapeDtypeStruct((PEERS, ROWS, TILE), F32),
         ],
         scratch_shapes=[pltpu.VMEM((COLS, AGG), F32), pltpu.VMEM((COLS, TILE), F32), pltpu.VMEM((COLS, TILE), F32)],
-    )
-    return pl.pallas_call(
-        forward_kernel,
-        grid_spec=grid,
-        out_shape=[
-            far((2, SLOTS, COLS, TILE)),
-            far((2, SLOTS, COLS, TILE)),
-            far((SLOTS, COLS, TILE)),
-            jax.ShapeDtypeStruct((PEERS, ROWS, TILE), F32),
-        ],
         compiler_params=params(),
         name="forward_part",
-    )(perm, member, e, e, *map(hbm, (b_slot, b_rest, d_slot, d_rest, x_peer, d_peer, m_peer, hi_pair, lo_pair, hi_rest, lo_rest)), maps)
+    )(perm, member, *arrays)
 
 
 def second_kernel(
-    perm, member, e_own, e_peer, dots, b_slot, b_rest, d_slot, d_rest, d_peer, m_peer, hi_pair, lo_pair,
-    hi_rest, lo_rest, maps, z_in, w_in, w_peer, v_out, u_out, out, acc_a, acc_b, acc_c
+    perm, member, e, dots, b_slot, b_rest, d_slot, d_rest, d_peer, m_peer, hi_pair, lo_pair,
+    hi_rest, lo_rest, maps, z_in, w_in, w_peer, v_out, u_out, out, acc_a, acc_b, acc_c, acc_alpha
 ):
-    step = pl.program_id(0)
-
-    @pl.when(step == 0)
-    def _():
-        acc_a[...] = jnp.zeros_like(acc_a)
-        acc_b[...] = jnp.zeros_like(acc_b)
-        acc_c[...] = jnp.zeros_like(acc_c)
-
+    acc_a[...] = jnp.zeros_like(acc_a)
+    acc_b[...] = jnp.zeros_like(acc_b)
+    acc_c[...] = jnp.zeros_like(acc_c)
     col = column(dots[0:1])
-    alpha = col[:COLS] / col[COLS:]
+    acc_alpha[...] = col[:COLS] / col[COLS:]
+    e_own = e.at[pl.ds(member[0], 1)]
+    views = (e, b_slot, b_rest, d_slot, d_rest, d_peer, m_peer, hi_pair, lo_pair, hi_rest, lo_rest, w_peer)
+
+    @pl.loop(0, NSTEP)
+    def _(step):
+        e_peer, *parts = [v.at[part(step, v.shape[0])] for v in views]
+        z_part, w_part, v_part, u_part = [v.at[:, part(step, SLOTS)] for v in (z_in, w_in, v_out, u_out)]
+        second_step(
+            step, perm, e_own, e_peer, *parts[:-1], maps, z_part, w_part, parts[-1], v_part, u_part,
+            acc_a, acc_b, acc_c, acc_alpha
+        )
+
+    first = jnp.sum(jnp.concatenate([acc_a[...], acc_b[...]], axis=0).T, axis=0, keepdims=True)
+    last = jnp.sum(jnp.concatenate([acc_c[...], acc_c[...]], axis=0).T, axis=0, keepdims=True)
+    r8 = lax.broadcasted_iota(jnp.int32, (8, TILE), 0)
+    extra = jnp.where(r8 == 0, first, jnp.where(r8 == 1, last, 0.0))
+    for q in range(GROUPS * PEERS):
+        out[q] = extra
+
+
+def second_step(
+    step, perm, e_own, e_peer, b_slot, b_rest, d_slot, d_rest, d_peer, m_peer, hi_pair, lo_pair,
+    hi_rest, lo_rest, maps, z_in, w_in, w_peer, v_out, u_out, acc_a, acc_b, acc_c, acc_alpha
+):
+    alpha = acc_alpha[...]
     e_mine = two_parts(e_own[0])
     e_both = [two_parts(beside(e_own[0], e_peer[q])) for q in range(STEP // 2)]
     sums = [acc_a[...], acc_b[...], acc_c[...]]
@@ -650,56 +635,21 @@
     acc_b[...] = sums[1]
     acc_c[...] = sums[2]
 
-    @pl.when(step == NSTEP - 1)
-    def _():
-        first = jnp.sum(jnp.concatenate([sums[0], sums[1]], axis=0).T, axis=0, keepdims=True)
-        last = jnp.sum(jnp.concatenate([sums[2], sums[2]], axis=0).T, axis=0, keepdims=True)
-        r8 = lax.broadcasted_iota(jnp.int32, (8, TILE), 0)
-        extra = jnp.where(r8 == 0, first, jnp.where(r8 == 1, last, 0.0))
-        for q in range(GROUPS * PEERS):
-            out[q] = extra
-
-
-def second_part(perm, member, e, dots, b_slot, b_rest, d_slot, d_rest, d_peer, m_peer, hi_pair, lo_pair, hi_rest, lo_rest, maps, z, w, w_peer):
-    grid = pltpu.PrefetchScalarGridSpec(
-        num_scalar_prefetch=2,
-        grid=(NSTEP,),
-        in_specs=e_specs()
-        + [
-            pl.BlockSpec((8, TILE), lambda s, p, m: (0, 0)),
-            step_spec(COLS, TILE),
-            step_spec(COLS, TILE),
-            step_spec(1, TILE),
-            step_spec(1, TILE),
-            step_spec(1, TILE),
-            step_spec(1, TILE),
-            step_spec(2 * TILE, 2 * TILE),
-            step_spec(2 * TILE, 2 * TILE),
-            step_spec(TILE, TILE),
-            step_spec(TILE, TILE),
-            pl.BlockSpec((BLK, TILE), lambda s, p, m: (0, 0)),
-            pair_spec(),
-            pair_spec(),
-            step_spec(COLS, TILE),
-        ],
-        out_specs=[
-            pair_spec(),
-            pair_spec(),
-            pl.BlockSpec((GROUPS * PEERS, 8, TILE), lambda s, p, m: (0, 0, 0)),
-        ],
-        scratch_shapes=[pltpu.VMEM((COLS, TILE), F32)] * 3,
-    )
+
+def second_part(perm, member, *arrays):
     return pl.pallas_call(
         second_kernel,
-        grid_spec=grid,
+        in_specs=in_vmem(len(arrays)),
+        out_specs=[pl.BlockSpec(memory_space=pltpu.VMEM)] * 3,
         out_shape=[
-            far((2, SLOTS, COLS, TILE)),
-            far((2, SLOTS, COLS, TILE)),
+            jax.ShapeDtypeStruct((2, SLOTS, COLS, TILE), F32),
+            jax.ShapeDtypeStruct((2, SLOTS, COLS, TILE), F32),
             jax.ShapeDtypeStruct((GROUPS * PEERS, 8, TILE), F32),
         ],
+        scratch_shapes=[pltpu.VMEM((COLS, TILE), F32)] * 4,
         compiler_params=params(),
         name="second_part",
-    )(perm, member, e, e, dots, *map(hbm, (b_slot, b_rest, d_slot, d_rest, d_peer, m_peer, hi_pair, lo_pair, hi_rest, lo_rest)), maps, *map(hbm, (z, w, w_peer)))
+    )(perm, member, *arrays)
 
 
 def combine_kernel(perm, dots, arrived, b_slot, b_rest, z, w, v, u, solution, residual, coef):
@@ -812,14 +762,15 @@
     def level_one(arrived):
         x, outgoing = lowest_part(arrived, g)
         lows = exchange(outgoing, "grp")
-        h = smooth_part(x, inverse, operator)
-        return correct_part(lows, inverse_cols, g, h)
-
+        return correct_part(lows, inverse_cols, g, x, inverse, operator)
+
+    rr_local, g = lax.optimization_barrier((rr_local, g))
     gathered = exchange(first_restrict(side, rs, rr_local), GROUP_AXES)
-    hi_pair, lo_pair, d_peer, m_peer = pair_setup(perm, counts, diag_tiles, side, remote)
+    hi_pair, lo_pair, d_peer, m_peer, x_peer = pair_setup(perm, counts, diag_tiles, side, remote)
+    gathered, hi_pair = lax.optimization_barrier((gathered, hi_pair))
     e, _ = level_one(gathered)
     z, w, w_peer, outgoing = forward_part(
-        perm, member, e, b_slot, b_rest, d_slot, d_rest, side, d_peer, m_peer, hi_pair, lo_pair, hi_rest, lo_rest, maps
+        perm, member, e, b_slot, b_rest, d_slot, d_rest, x_peer, d_peer, m_peer, hi_pair, lo_pair, hi_rest, lo_rest, maps
     )
     e, dots = level_one(exchange(outgoing, GROUP_AXES))
     v, u, outgoing = second_part(

time: 160 us -> 163 us (1.019)
  blocking collectives: 29.3 us -> 41.9 us
  local copies, waits for them, and re-layouts: 9.41 us -> 18.6 us
  Pallas kernels: 62.2 us -> 54.6 us
  starting transfers between devices: 27.8 us -> 21.8 us
  waiting for transfers between devices: 28.9 us -> 23.3 us
    all_to_all x2 -> x3, blocking collectives: 29.3 us -> 41.9 us  [exchange(): return lax.all_to_all(x, axes, 0, 0, tiled=True)]
    pallas_call x4 -> x2, Pallas kernels: 26 us -> 17.2 us  [the longest x1 9.47 us: forward_part(): pl.pallas_call(forward_kernel, in_specs=in_vmem(len(arrays)), out_specs=[...]
    unnamed x29 -> x55, local copies, waits for them, and re-layouts: 9.2 us -> 17.7 us
    all_to_all x4 -> x3, starting transfers between devices: 27.8 us -> 21.8 us  [exchange(): return lax.all_to_all(x, axes, 0, 0, tiled=True)]
    all_to_all x4 -> x3, waiting for transfers between devices: 28.9 us -> 23.3 us  [exchange(): return lax.all_to_all(x, axes, 0, 0, tiled=True)]
    pallas_call x2, Pallas kernels: 1.69 us -> 4.37 us  [correct_part(): pl.pallas_call(correct_kernel, out_shape=[jax.ShapeDtypeStruct((PEERS, CO...]
  transfers between devices with their start and end apart: 4 -> 3, of which waited for: 3 -> 2; matrix products, arithmetic and copies ran while one was open for 0% -> 1% of each run, Pallas kernels for 13% -> 12%
where the time goes in v4:
time: 163 us; the launch traced here: 162 us
  Pallas kernels  54.6 us (33%)
  blocking collectives  41.9 us (26%)
  waiting for transfers between devices  23.3 us (14%)
  starting transfers between devices  21.8 us (13%)
  local copies, waits for them, and re-layouts  18.6 us (11%)
    all_to_all x3, blocking collectives, exchange(): return lax.all_to_all(x, axes, 0, 0, tiled=True)  41.9 us
    all_to_all x3, waiting for transfers between devices, exchange(): return lax.all_to_all(x, axes, 0, 0, tiled=True)  23.3 us
    all_to_all x3, starting transfers between devices, exchange(): return lax.all_to_all(x, axes, 0, 0, tiled=True)  21.8 us
    unnamed x55, local copies, waits for them, and re-layouts  17.7 us
    pallas_call x1, Pallas kernels, forward_part(): pl.pallas_call(forward_kernel, in_specs=in_vmem(len(arrays)), out_specs=[...  9.47 us
    pallas_call x1, Pallas kernels, local_part(): pl.pallas_call(local_kernel, grid_spec=grid, out_shape=[sds((COLS, TILE))...  9.42 us
    pallas_call x1, Pallas kernels, pair_setup(): pl.pallas_call(pair_kernel, grid_spec=grid, out_shape=[far((SLOTS, 2 * TI...  8.12 us
    pallas_call x1, Pallas kernels, second_part(): pl.pallas_call(second_kernel, in_specs=in_vmem(len(arrays)), out_specs=[p...  7.7 us
  transfers between devices with their start and end apart: 3, of which 2 were waited for; matrix products, arithmetic and copies ran while one was open for 1% of the time, Pallas kernels for 12%

profile of v4, /device:TPU:1, one launch (start us, length us, event | category | flops | bytes accessed | tf_op | source)
XLA Modules:
  0.0 161.5 jit_solution(1239894815191621068)
XLA Ops:
  2.2 5.5 %boundary_pack.1 = f32[32,136,128]{2,1,0:T(8,128)} custom-call(s32[1,16,2]{2,1,0:T(8,128)S(1)} %copy.15.slots, s32[64,128]{1,0:T(8,128)S(1)} %bitcast.11, f32[64,128,128]{2,1,0:T(8,128)} %refs_7_.3, f32[64,8192]{1,0:T(8,128)} %refs_31_.1), custom_call_target="tpu_custom_call" | custom-call | tf_op jit(solution)/shard_map/boundary_pack/pallas_call | solution.py:143
  7.8 8.5 %all-to-all-start = ((f32[16,272,128]{2,1,0:T(8,128)}), f32[16,272,128]{2,1,0:T(8,128)}, u32[]{:S(2)}, u32[]{:S(2)}) async-start(f32[16,272,128]{2,1,0:T(8,128)} %bitcast.18), calls=%async_computation | async-start | bytes 4456448 | tf_op jit(solution)/shard_map/all_to_all | solution.py:724
  16.4 2.2 %copy-done.1 = f32[1,1024,1024]{2,1,0:T(8,128)S(1)} copy-done((f32[1,1024,1024]{2,1,0:T(8,128)S(1)}, f32[1,1024,1024]{2,1,0:T(8,128)}, u32[]{:S(2)}) %copy-start.1) | copy-done | bytes 4194328
  18.6 1.1 coarse_setup.1
  20.0 9.4 %local_part.1 = (f32[32,64,128]{2,1,0:T(8,128)}, f32[32,64,128]{2,1,0:T(8,128)}, f32[32,1,128]{2,1,0:T(1,128)}, f32[32,1,128]{2,1,0:T(1,128)}, bf16[32,128,128]{...) custom-call(s32[64]{0:T(128)S(1)} %pad_add_fusion.perm, ...), custom_call_target="tpu_custom_call" | custom-call | flops 402653184 | bytes 16777216 | tf_op jit(solution)/shard_map/local_part/pallas_call | solution.py:242
  29.4 18.4 %all-to-all-done = f32[16,272,128]{2,1,0:T(8,128)} async-done(((f32[16,272,128]{2,1,0:T(8,128)}), f32[16,272,128]{2,1,0:T(8,128)}, u32[]{:S(2)}, u32[]{:S(2)}) %all-to-all-start) | async-done | bytes 2228256 | tf_op jit(solution)/shard_map/all_to_all | solution.py:724
  47.9 3.7 %first_restrict.1 = f32[16,40,128]{2,1,0:T(8,128)} custom-call(f32[32,136,128]{2,1,0:T(8,128)} %bitcast.3.arrived.refs_8_, f32[32,64,128]{2,1,0:T(8,128)} %get-tuple-element.35.rs, f32[64,64]{1,0:T(8,128)S(1)} %get-tuple-element.38.rr), custom_call_target="tpu_custom_call" | custom-call | tf_op jit(solution)/shard_map/first_restrict/pallas_call | solution.py:315
  51.6 5.9 %all-to-all-start.1 = ((f32[16,40,128]{2,1,0:T(8,128)}), f32[16,40,128]{2,1,0:T(8,128)S(1)}, u32[]{:S(2)}, u32[]{:S(2)}) async-start(f32[16,40,128]{2,1,0:T(8,128)} %first_restrict.1), calls=%async_computation.1 | async-start | bytes 655360 | tf_op jit(solution)/shard_map/all_to_all | solution.py:724
  57.5 8.1 %pair_setup.1 = (bf16[32,256,256]{2,1,0:T(8,128)(2,1)}, bf16[32,256,256]{2,1,0:T(8,128)(2,1)}, f32[32,1,128]{2,1,0:T(1,128)}, s32[32,1,128]{2,1,0:T(1,128)}, f32[32,64,128]{2,1,0:T(8,128)}) custom-call(s32[64]{0:T(128)S(1)} %pad_add_fusion.perm, s32[16]{0:T(128)S(1)} %bitcast.17, f32[64,128,128]{2,1,0:T(8,128)} %refs_7_.3, f32[64,128,128]{2,1,0:T(8,128)} %refs_7_.3, ...), custom_call_target="tpu_custom_call" | custom-call | flops 402653184 | bytes 16777216 | tf_op jit(solution)/shard_map/pair_setup/pallas_call | solution.py:370
  69.2 7.4 %all-to-all-start.2 = ((f32[8,40,128]{2,1,0:T(8,128)}), f32[8,40,128]{2,1,0:T(8,128)}, u32[]{:S(2)}, u32[]{:S(2)}) async-start(f32[8,40,128]{2,1,0:T(8,128)} %copy-done.20), calls=%async_computation.2 | async-start | bytes 327680 | tf_op jit(solution)/shard_map/all_to_all | solution.py:724
  77.5 4.8 %all-to-all-done.2.arrived = f32[8,40,128]{2,1,0:T(8,128)} async-done(((f32[8,40,128]{2,1,0:T(8,128)}), f32[8,40,128]{2,1,0:T(8,128)}, u32[]{:S(2)}, u32[]{:S(2)}) %all-to-all-start.2) | async-done | bytes 163872 | tf_op jit(solution)/shard_map/all_to_all | solution.py:724
  82.3 2.2 %copy-done.2 = f32[1,1024,1024]{2,1,0:T(8,128)S(1)} copy-done((f32[1,1024,1024]{2,1,0:T(8,128)S(1)}, f32[1,1024,1024]{2,1,0:T(8,128)}, u32[]{:S(2)}) %copy-start.2) | copy-done | bytes 4194328
  86.4 3.0 %correct_part.2 = (f32[16,64,64]{2,1,0:T(8,128)S(1)}, f32[8,128]{1,0:T(8,128)}) custom-call(f32[8,40,128]{2,1,0:T(8,128)} %all-to-all-done.2.arrived, f32[512,64]{1,0:T(8,128)S(1)} %copy-done.11, f32[64,1024]{1,0:T(8,128)S(1)} %get-tuple-element.41.g, f32[64,1024]{1,0:T(8,128)S(1)} %copy-done.19, f32[1,1024]{1,0:T(1,128)S(1)} %get-tuple-element.44.inverse_ref, ...), custom_call_target="tpu_custom_call" | custom-call | tf_op jit(solution)/shard_map/correct_part/pallas_call | solution.py:444
  89.5 2.2 %copy-done.5 = bf16[32,256,256]{2,1,0:T(8,128)(2,1)S(1)} copy-done((bf16[32,256,256]{2,1,0:T(8,128)(2,1)S(1)}, bf16[32,256,256]{2,1,0:T(8,128)(2,1)}, u32[]{:S(2)}) %copy-start.5) | copy-done | bytes 4194328
  91.6 1.2 copy-done.9
  92.9 1.2 copy-done.10
  94.1 1.2 copy-done.15
  95.3 9.5 %forward_part.1 = (f32[2,32,64,128]{3,2,1,0:T(8,128)S(1)}, f32[2,32,64,128]{3,2,1,0:T(8,128)S(1)}, f32[32,64,128]{2,1,0:T(8,128)S(1)}, f32[16,40,128]{2,1,0:T(8,128)S(1)}) custom-call(s32[64]{0:T(128)S(1)} %pad_add_fusion.perm, s32[1]{0:T(128)} %bitcast.member, f32[16,64,64]{2,1,0:T(8,128)S(1)} %get-tuple-element.45.e, f32[32,64,128]{2,1,0:T(8,128)S(1)} %copy-done.7, ...), custom_call_target="tpu_custom_call" | custom-call | tf_op jit(solution)/shard_map/forward_part/pallas_call | solution.py:553
  104.8 14.1 %all_to_all.30.arrived = f32[16,40,128]{2,1,0:T(8,128)S(1)} all-to-all(f32[16,40,128]{2,1,0:T(8,128)S(1)} %get-tuple-element.57), channel_id=1, replica_groups=mesh['grp'=8,'sub'=8,'chip'=2] {'sub','chip'}, dimensions={0} | all-to-all | bytes 655360 | tf_op jit(solution)/shard_map/all_to_all | solution.py:724
  119.3 10.1 %all_to_all.31.arrived = f32[8,40,128]{2,1,0:T(8,128)S(1)} all-to-all(f32[8,40,128]{2,1,0:T(8,128)S(1)} %get-tuple-element.58), channel_id=1, replica_groups=mesh['grp'=8,'sub'=8,'chip'=2] {'grp'}, dimensions={0} | all-to-all | bytes 327680 | tf_op jit(solution)/shard_map/all_to_all | solution.py:724
  129.4 1.4 correct_part.3
  131.5 7.7 %second_part.1 = (f32[2,32,64,128]{3,2,1,0:T(8,128)S(1)}, f32[2,32,64,128]{3,2,1,0:T(8,128)S(1)}, f32[128,8,128]{2,1,0:T(8,128)S(1)}) custom-call(s32[64]{0:T(128)S(1)} %pad_add_fusion.perm, s32[1]{0:T(128)} %bitcast.member, f32[16,64,64]{2,1,0:T(8,128)S(1)} %get-tuple-element.61.e, f32[8,128]{1,0:T(8,128)S(1)} %get-tuple-element.60.dots, ...), custom_call_target="tpu_custom_call" | custom-call | tf_op jit(solution)/shard_map/second_part/pallas_call | solution.py:640
  139.2 17.8 %all_to_all.32.arrived = f32[128,8,128]{2,1,0:T(8,128)S(1)} all-to-all(f32[128,8,128]{2,1,0:T(8,128)S(1)} %get-tuple-element.65), channel_id=1, replica_groups=mesh['grp'=8,'sub'=8,'chip'=2] {'grp','sub','chip'}, dimensions={0} | all-to-all | bytes 1048576 | tf_op jit(solution)/shard_map/all_to_all | solution.py:724
  157.0 4.5 %combine.1 = (f32[64,8192]{1,0:T(8,128)}, f32[64,8192]{1,0:T(8,128)}) custom-call(s32[64]{0:T(128)S(1)} %pad_add_fusion.perm, f32[8,128]{1,0:T(8,128)S(1)} %get-tuple-element.60.dots, f32[128,8,128]{2,1,0:T(8,128)S(1)} %all_to_all.32.arrived, f32[32,64,128]{2,1,0:T(8,128)S(1)} %copy-done.7, f32[32,64,128]{2,1,0:T(8,128)S(1)} %copy-done.8, ...), custom_call_target="tpu_custom_call" | custom-call | tf_op jit(solution)/shard_map/combine/pallas_call | solution.py:714
  (59 shorter events, 9.6 us)
Async XLA Ops:
  0.6 76.0 %copy-start = (f32[512,512]{1,0:T(8,128)S(1)}, f32[512,512]{1,0:T(8,128)}, u32[]{:S(2)}) copy-start(f32[512,512]{1,0:T(8,128)} %param.17) | copy-start | bytes 3145732
  7.8 8.6 %copy-start.25 = (s32[1024]{0:T(1024)S(1)}, s32[1024]{0:T(1024)}, u32[]{:S(2)}) copy-start(s32[1024]{0:T(1024)} %param.15) | copy-start | bytes 12292
  7.8 40.1 %all-to-all-start = ((f32[16,272,128]{2,1,0:T(8,128)}), f32[16,272,128]{2,1,0:T(8,128)}, u32[]{:S(2)}, u32[]{:S(2)}) async-start(f32[16,272,128]{2,1,0:T(8,128)} %bitcast.18), calls=%async_computation | async-start | bytes 4456448 | tf_op jit(solution)/shard_map/all_to_all | solution.py:724
  16.4 2.2 %copy-start.1 = (f32[1,1024,1024]{2,1,0:T(8,128)S(1)}, f32[1,1024,1024]{2,1,0:T(8,128)}, u32[]{:S(2)}) copy-start(f32[1,1024,1024]{2,1,0:T(8,128)} %param.16) | copy-start | bytes 12582916
  18.5 1.5 copy-start.17
  18.6 1.5 copy-start.26
  51.6 14.1 %all-to-all-start.1 = ((f32[16,40,128]{2,1,0:T(8,128)}), f32[16,40,128]{2,1,0:T(8,128)S(1)}, u32[]{:S(2)}, u32[]{:S(2)}) async-start(f32[16,40,128]{2,1,0:T(8,128)} %first_restrict.1), calls=%async_computation.1 | async-start | bytes 655360 | tf_op jit(solution)/shard_map/all_to_all | solution.py:724
  57.5 31.9 %copy-start.8 = (f32[32,64,128]{2,1,0:T(8,128)S(1)}, f32[32,64,128]{2,1,0:T(8,128)}, u32[]{:S(2)}) copy-start(f32[32,64,128]{2,1,0:T(8,128)} %get-tuple-element.47.b_rest) | copy-start | bytes 3145732
  66.4 1.0 copy-start.14
  67.4 22.0 %copy-start.7 = (f32[32,64,128]{2,1,0:T(8,128)S(1)}, f32[32,64,128]{2,1,0:T(8,128)}, u32[]{:S(2)}) copy-start(f32[32,64,128]{2,1,0:T(8,128)} %get-tuple-element.46.b_slot) | copy-start | bytes 3145732
  69.2 13.1 %all-to-all-start.2 = ((f32[8,40,128]{2,1,0:T(8,128)}), f32[8,40,128]{2,1,0:T(8,128)}, u32[]{:S(2)}, u32[]{:S(2)}) async-start(f32[8,40,128]{2,1,0:T(8,128)} %copy-done.20), calls=%async_computation.2 | async-start | bytes 327680 | tf_op jit(solution)/shard_map/all_to_all | solution.py:724
  82.3 2.2 %copy-start.2 = (f32[1,1024,1024]{2,1,0:T(8,128)S(1)}, f32[1,1024,1024]{2,1,0:T(8,128)}, u32[]{:S(2)}) copy-start(f32[1,1024,1024]{2,1,0:T(8,128)} %param.16) | copy-start | bytes 12582916
  86.4 3.0 %copy-start.4 = (bf16[32,256,256]{2,1,0:T(8,128)(2,1)S(1)}, bf16[32,256,256]{2,1,0:T(8,128)(2,1)}, u32[]{:S(2)}) copy-start(bf16[32,256,256]{2,1,0:T(8,128)(2,1)} %get-tuple-element.53.hi_pair) | copy-start | bytes 12582916
  86.4 3.0 %copy-start.21 = (f32[32,1,128]{2,1,0:T(1,128)S(1)}, f32[32,1,128]{2,1,0:T(1,128)}, u32[]{:S(2)}) copy-start(f32[32,1,128]{2,1,0:T(1,128)} %get-tuple-element.48.d_slot) | copy-start | bytes 49156
  86.4 3.0 %copy-start.22 = (f32[32,1,128]{2,1,0:T(1,128)S(1)}, f32[32,1,128]{2,1,0:T(1,128)}, u32[]{:S(2)}) copy-start(f32[32,1,128]{2,1,0:T(1,128)} %get-tuple-element.49.d_rest) | copy-start | bytes 49156
  86.4 3.0 %copy-start.23 = (f32[32,1,128]{2,1,0:T(1,128)S(1)}, f32[32,1,128]{2,1,0:T(1,128)}, u32[]{:S(2)}) copy-start(f32[32,1,128]{2,1,0:T(1,128)} %get-tuple-element.51.d_peer) | copy-start | bytes 49156
  86.4 3.0 %copy-start.24 = (s32[32,1,128]{2,1,0:T(1,128)S(1)}, s32[32,1,128]{2,1,0:T(1,128)}, u32[]{:S(2)}) copy-start(s32[32,1,128]{2,1,0:T(1,128)} %get-tuple-element.52.m_peer) | copy-start | bytes 49156
  89.4 2.2 %copy-start.5 = (bf16[32,256,256]{2,1,0:T(8,128)(2,1)S(1)}, bf16[32,256,256]{2,1,0:T(8,128)(2,1)}, u32[]{:S(2)}) copy-start(bf16[32,256,256]{2,1,0:T(8,128)(2,1)} %get-tuple-element.54.lo_pair) | copy-start | bytes 12582916
  91.6 1.2 copy-start.9
  92.9 1.2 copy-start.10
  94.1 1.2 copy-start.15
  95.3 34.0 %copy-start.3 = (f32[1,1024,1024]{2,1,0:T(8,128)S(1)}, f32[1,1024,1024]{2,1,0:T(8,128)}, u32[]{:S(2)}) copy-start(f32[1,1024,1024]{2,1,0:T(8,128)} %param.16) | copy-start | bytes 12582916
  95.3 34.0 %copy-start.12 = (f32[512,64]{1,0:T(8,128)S(1)}, f32[512,64]{1,0:T(8,128)}, u32[]{:S(2)}) copy-start(f32[512,64]{1,0:T(8,128)} %constant_dynamic-slice_fusion.inverse_cols) | copy-start | bytes 393220
  129.3 2.2 %copy-start.6 = (bf16[32,256,256]{2,1,0:T(8,128)(2,1)S(1)}, bf16[32,256,256]{2,1,0:T(8,128)(2,1)}, u32[]{:S(2)}) copy-start(bf16[32,256,256]{2,1,0:T(8,128)(2,1)} %get-tuple-element.54.lo_pair) | copy-start | bytes 12582916
  (6 other events, 4.8 us)

commit v5 on v4

--- a/solution.py
+++ b/solution.py
@@ -107,60 +107,64 @@
     return jnp.broadcast_to(row, (TILE, TILE)).T
 
 
-def boundary_kernel(slots, maps, tiles, cols, out, tile_buf, col_buf, out_buf, tile_sem, col_sem, out_sem):
+def boundary_kernel(slots, maps, tiles, cols, out, map_buf, tile_buf, col_buf, out_buf, map_sem, col_sem, tile_sem, out_sem):
     def tile_copy(j):
-        return pltpu.make_async_copy(tiles.at[slots[0, j // 2, j % 2]], tile_buf.at[j], tile_sem.at[j])
+        return pltpu.make_async_copy(tiles.at[slots[0, j % 2, j // 2]], tile_buf.at[j], tile_sem.at[j])
 
     def col_copy(j):
-        at = pl.ds(pl.multiple_of(slots[0, j // 2, j % 2] * TILE, TILE), TILE)
+        at = pl.ds(pl.multiple_of(slots[0, j % 2, j // 2] * TILE, TILE), TILE)
         return pltpu.make_async_copy(cols.at[:, at], col_buf.at[j], col_sem.at[j])
 
     def out_copy(j):
-        return pltpu.make_async_copy(out_buf.at[j], out.at[j], out_sem.at[j])
-
+        at = pl.ds(j, STEP)
+        return pltpu.make_async_copy(out_buf.at[at], out.at[at], out_sem.at[j // STEP])
+
+    map_copy = pltpu.make_async_copy(maps, map_buf, map_sem)
+    map_copy.start()
     for j in range(SLOTS):
         tile_copy(j).start()
         col_copy(j).start()
     r = lax.broadcasted_iota(jnp.int32, (64, TILE), 0)
     c = lax.broadcasted_iota(jnp.int32, (64, TILE), 1)
     r8 = lax.broadcasted_iota(jnp.int32, (8, TILE), 0)
-    for j in range(SLOTS):
-        tile_copy(j).wait()
-        col_copy(j).wait()
-        tile = tile_buf[j]
-        diag = tile_diag(tile)
-        out_buf[j, 0:64] = col_buf[j] * (OMEGA / diag)
-        below = pltpu.roll(tile[64:], 64, 1)
-        out_buf[j, 64:128] = jnp.where((c < 64) & (r > c), below, tile[:64])
-        row = maps[pl.ds(slots[0, j // 2, j % 2], 1)].astype(F32)
-        out_buf[j, 128:136] = jnp.where(r8 == 0, diag, jnp.where(r8 == 1, row, 0.0))
+    map_copy.wait()
+    for j in range(0, SLOTS, STEP):
+        for k in range(j, j + STEP):
+            tile_copy(k).wait()
+            col_copy(k).wait()
+        tile = [tile_buf[k] for k in range(j, j + STEP)]
+        diag = [tile_diag(t) for t in tile]
+        for k in range(j, j + STEP):
+            t, d = tile[k - j], diag[k - j]
+            out_buf[k, 0:64] = col_buf[k] * (OMEGA / d)
+            below = pltpu.roll(t[64:], 64, 1)
+            out_buf[k, 64:128] = jnp.where((c < 64) & (r > c), below, t[:64])
+            row = map_buf[pl.ds(slots[0, k % 2, k // 2], 1)].astype(F32)
+            out_buf[k, 128:136] = jnp.where(r8 == 0, d, jnp.where(r8 == 1, row, 0.0))
         out_copy(j).start()
-    for j in range(SLOTS):
+    for j in range(0, SLOTS, STEP):
         out_copy(j).wait()
 
 
 def boundary_pack(slot_blocks, diag_tiles, right_side, maps):
     return pl.pallas_call(
         boundary_kernel,
-        in_specs=[
-            pl.BlockSpec(memory_space=pltpu.SMEM),
-            pl.BlockSpec(memory_space=pltpu.VMEM),
-            pl.BlockSpec(memory_space=pl.ANY),
-            pl.BlockSpec(memory_space=pl.ANY),
-        ],
+        in_specs=[pl.BlockSpec(memory_space=pltpu.SMEM)] + [pl.BlockSpec(memory_space=pl.ANY)] * 3,
         out_specs=pl.BlockSpec(memory_space=pl.ANY),
         out_shape=far((SLOTS, SIDE, TILE)),
         scratch_shapes=[
+            pltpu.VMEM((BLK, TILE), jnp.int32),
             pltpu.VMEM((SLOTS, TILE, TILE), F32),
             pltpu.VMEM((SLOTS, COLS, TILE), F32),
             pltpu.VMEM((SLOTS, SIDE, TILE), F32),
+            pltpu.SemaphoreType.DMA,
             pltpu.SemaphoreType.DMA((SLOTS,)),
             pltpu.SemaphoreType.DMA((SLOTS,)),
-            pltpu.SemaphoreType.DMA((SLOTS,)),
+            pltpu.SemaphoreType.DMA((NSTEP,)),
         ],
         compiler_params=params(),
         name="boundary_pack",
-    )(slot_blocks, maps, hbm(diag_tiles), hbm(right_side))
+    )(slot_blocks.transpose(0, 2, 1), hbm(maps), hbm(diag_tiles), hbm(right_side))
 
 
 def local_kernel(perm, counts, *refs):
@@ -290,39 +294,42 @@
     )(op, cmap)
 
 
-def first_restrict_kernel(arrived, rs, rr, out, acc):
-    step = pl.program_id(0)
-
-    @pl.when(step == 0)
-    def _():
-        acc[...] = rr[...]
-
-    total = acc[...]
-    for j in range(0, STEP, 2):
-        hi, lo = split2(beside(rs[j], rs[j + 1]))
-        total = total + mm(beside(arrived[j], arrived[j + 1]), hi, lo, nt=True)
-    acc[...] = total
-
-    @pl.when(step == NSTEP - 1)
-    def _():
-        packed = pack_rows(total)
-        for q in range(PEERS):
-            out[q, 0:32] = packed
-            out[q, 32:40] = jnp.zeros((8, TILE), F32)
+def first_restrict_kernel(arrived, rs, rr, out, x_buf, rs_buf, x_sem, rs_sem):
+    def copies(j):
+        at = pl.ds(j * STEP, STEP)
+        return (
+            pltpu.make_async_copy(arrived.at[at, pl.ds(0, COLS)], x_buf.at[at], x_sem.at[j]),
+            pltpu.make_async_copy(rs.at[at], rs_buf.at[at], rs_sem.at[j]),
+        )
+
+    for j in range(NSTEP):
+        for copy in copies(j):
+            copy.start()
+    total = rr[...]
+    for j in range(NSTEP):
+        for copy in copies(j):
+            copy.wait()
+        for k in range(j * STEP, (j + 1) * STEP, 2):
+            hi, lo = split2(beside(rs_buf[k], rs_buf[k + 1]))
+            total = total + mm(beside(x_buf[k], x_buf[k + 1]), hi, lo, nt=True)
+    packed = pack_rows(total)
+    for q in range(PEERS):
+        out[q, 0:32] = packed
+        out[q, 32:40] = jnp.zeros((8, TILE), F32)
 
 
 def first_restrict(arrived, rs, rr):
     return pl.pallas_call(
         first_restrict_kernel,
-        grid=(NSTEP,),
-        in_specs=[
-            pl.BlockSpec((STEP, COLS, TILE), lambda s: (s, 0, 0)),
-            pl.BlockSpec((STEP, AGG, TILE), lambda s: (s, 0, 0)),
-            pl.BlockSpec((COLS, AGG), lambda s: (0, 0)),
-        ],
-        out_specs=pl.BlockSpec((PEERS, ROWS, TILE), lambda s: (0, 0, 0)),
+        in_specs=[pl.BlockSpec(memory_space=pl.ANY)] * 2 + [pl.BlockSpec(memory_space=pltpu.VMEM)],
+        out_specs=pl.BlockSpec(memory_space=pltpu.VMEM),
         out_shape=jax.ShapeDtypeStruct((PEERS, ROWS, TILE), F32),
-        scratch_shapes=[pltpu.VMEM((COLS, AGG), F32)],
+        scratch_shapes=[
+            pltpu.VMEM((SLOTS, COLS, TILE), F32),
+            pltpu.VMEM((SLOTS, AGG, TILE), F32),
+            pltpu.SemaphoreType.DMA((NSTEP,)),
+            pltpu.SemaphoreType.DMA((NSTEP,)),
+        ],
         compiler_params=params(),
         name="first_restrict",
     )(hbm(arrived), hbm(rs), rr)
@@ -418,7 +425,7 @@
     )(arrived, g)
 
 
-def correct_kernel(arrived, inverse_cols, g, x_ref, inverse_ref, op, e_out, dots):
+def correct_kernel(arrived, inverse_rows, g, x_ref, inverse_ref, op, e_out, dots):
     inverse = inverse_ref[...]
     scaled = x_ref[...] * inverse
     total = None
@@ -428,8 +435,8 @@
         term = mm(scaled[:, rows], hi, lo)
         total = term if total is None else total + term
     low = gathered_rows(arrived, GROUPS)
-    hi, lo = split2(inverse_cols[...])
-    corr = mm(low, hi, lo)
+    hi, lo = split2(inverse_rows[...])
+    corr = mm(low, hi, lo, nt=True)
     ghi, glo = split2(g[...])
     e = 2.0 * OMEGA * scaled - OMEGA * OMEGA * total * inverse + mm(corr, ghi, glo)
     for q in range(PEERS):
@@ -440,13 +447,20 @@
     dots[...] = extra
 
 
-def correct_part(arrived, inverse_cols, g, x, inverse, op):
+def correct_part(arrived, inverse_rows, g, x, inverse, op):
     return pl.pallas_call(
         correct_kernel,
         out_shape=[jax.ShapeDtypeStruct((PEERS, COLS, AGG), F32), jax.ShapeDtypeStruct((8, TILE), F32)],
         compiler_params=params(),
         name="correct_part",
-    )(arrived, inverse_cols, g, x, inverse, op)
+    )(arrived, inverse_rows, g, x, inverse, op)
+
+
+def apply_off(x, hi, lo):
+    xh, xl = split2(x)
+    rows = x.shape[0]
+    both = dot(jnp.concatenate([xh, xl], axis=0), hi)
+    return both[:rows] + both[rows:] + dot(xh, lo)
 
 
 def apply_block(x, diag, hi, lo):
@@ -515,21 +529,18 @@
     diag = [jnp.concatenate([d_slot[k], d_peer[k]], axis=1) for k in pairs] + [d_rest[k] for k in rest]
     rdiag = [OMEGA / d for d in diag]
     mats = [(hi_pair[k], lo_pair[k]) for k in pairs] + [(hi_rest[k], lo_rest[k]) for k in rest]
-    full = [
-        jnp.concatenate([b_own[k], x_peer[k] * (d_peer[k] * (1.0 / OMEGA))], axis=1) for k in pairs
-    ] + b_own[STEP:]
+    x1 = [beside(b_own[k] * rdiag[k][:, :TILE], x_peer[k]) for k in pairs]
+    x1 = x1 + [b * rd for b, rd in zip(b_own[STEP:], rdiag[STEP:])]
     spread = [one_hot(row) for row in rows]
     ups = [lift(e_both[k // 2], pair_spread(spread[k], one_hot(m_peer[k]))) for k in pairs]
     ups = ups + [lift(e_mine, sp) for sp in spread[STEP:]]
-    x = [f * rd + up for f, rd, up in zip(full, rdiag, ups)]
-    image = [apply_block(xx, d, *m) for xx, d, m in zip(x, diag, mats)]
-    z = [xx + (f - im) * rd for xx, f, im, rd in zip(x, full, image, rdiag)]
+    x = [start + up for start, up in zip(x1, ups)]
+    image = [apply_off(xx, *m) for xx, m in zip(x, mats)]
+    z = [(1.0 - OMEGA) * xx + start - im * rd for xx, start, im, rd in zip(x, x1, image, rdiag)]
     w = [apply_block(zz, d, *m) for zz, d, m in zip(z, diag, mats)]
     x1 = [ww * rd for ww, rd in zip(w, rdiag)]
     left = [(m[0][:, :TILE], m[1][:, :TILE]) for m in mats]
-    y = [
-        ww[:, :TILE] - apply_block(xx, d[:, :TILE], *m) for ww, xx, d, m in zip(w, x1, diag, left)
-    ]
+    y = [(1.0 - OMEGA) * ww[:, :TILE] - apply_off(xx, *m) for ww, xx, m in zip(w, x1, left)]
     for i in range(0, 2 * STEP, 2):
         rr = rr + mm_exact(beside(y[i], y[i + 1]), beside(spread[i], spread[i + 1]), nt=True)
     for i in range(2 * STEP):
@@ -621,9 +632,10 @@
     spread = [one_hot(row) for row in rows]
     ups = [lift(e_both[k // 2], pair_spread(spread[k], one_hot(m_peer[k]))) for k in pairs]
     ups = ups + [lift(e_mine, sp) for sp in spread[STEP:]]
-    x = [ww * rd + up for ww, rd, up in zip(w, rdiag, ups)]
-    image = [apply_block(xx, d, *m) for xx, d, m in zip(x, diag, mats)]
-    v = [xx + (ww - im) * rd for xx, ww, im, rd in zip(x, w, image, rdiag)]
+    x1 = [ww * rd for ww, rd in zip(w, rdiag)]
+    x = [start + up for start, up in zip(x1, ups)]
+    image = [apply_off(xx, *m) for xx, m in zip(x, mats)]
+    v = [(1.0 - OMEGA) * xx + start - im * rd for xx, start, im, rd in zip(x, x1, image, rdiag)]
     left = [(m[0][:, :TILE], m[1][:, :TILE]) for m in mats]
     u = [apply_block(vv, d[:, :TILE], *m) for vv, d, m in zip(v, diag, left)]
     for i in range(2 * STEP):
@@ -757,14 +769,14 @@
         perm, counts, diag_tiles, right_side, remote, maps
     )
     g, inverse = coarse_setup(operator, coarse_map.reshape(1, NC1))
-    inverse_cols = lax.dynamic_slice_in_dim(coarsest_inverse, group * AGG, AGG, 1)
+    inverse_rows = lax.dynamic_slice_in_dim(coarsest_inverse, group * AGG, AGG, 0)
 
     def level_one(arrived):
         x, outgoing = lowest_part(arrived, g)
         lows = exchange(outgoing, "grp")
-        return correct_part(lows, inverse_cols, g, x, inverse, operator)
-
-    rr_local, g = lax.optimization_barrier((rr_local, g))
+        return correct_part(lows, inverse_rows, g, x, inverse, operator)
+
+    rr_local, g, inverse_rows = lax.optimization_barrier((rr_local, g, inverse_rows))
     gathered = exchange(first_restrict(side, rs, rr_local), GROUP_AXES)
     hi_pair, lo_pair, d_peer, m_peer, x_peer = pair_setup(perm, counts, diag_tiles, side, remote)
     gathered, hi_pair = lax.optimization_barrier((gathered, hi_pair))

time: 163 us -> 158 us (0.969)
  local copies, waits for them, and re-layouts: 18.6 us -> 14.3 us
    unnamed x55 -> x49, local copies, waits for them, and re-layouts: 17.7 us -> 14.2 us
  transfers between devices with their start and end apart: 3 -> 3, of which waited for: 2 -> 2; matrix products, arithmetic and copies ran while one was open for 1% -> 0% of each run, Pallas kernels for 12% -> 12%
where the time goes in v5:
time: 158 us; the launch traced here: 157 us
  Pallas kernels  53.7 us (34%)
  blocking collectives  41.8 us (26%)
  waiting for transfers between devices  24 us (15%)
  starting transfers between devices  21.9 us (14%)
  local copies, waits for them, and re-layouts  14.3 us (9%)
    all_to_all x3, blocking collectives, exchange(): return lax.all_to_all(x, axes, 0, 0, tiled=True)  41.8 us
    all_to_all x3, waiting for transfers between devices, exchange(): return lax.all_to_all(x, axes, 0, 0, tiled=True)  24 us
    all_to_all x3, starting transfers between devices, exchange(): return lax.all_to_all(x, axes, 0, 0, tiled=True)  21.9 us
    unnamed x49, local copies, waits for them, and re-layouts  14.2 us
    pallas_call x1, Pallas kernels, local_part(): pl.pallas_call(local_kernel, grid_spec=grid, out_shape=[sds((COLS, TILE))...  9.4 us
    pallas_call x1, Pallas kernels, forward_part(): pl.pallas_call(forward_kernel, in_specs=in_vmem(len(arrays)), out_specs=[...  9.27 us
    pallas_call x1, Pallas kernels, pair_setup(): pl.pallas_call(pair_kernel, grid_spec=grid, out_shape=[far((SLOTS, 2 * TI...  8.13 us
    pallas_call x1, Pallas kernels, second_part(): pl.pallas_call(second_kernel, in_specs=in_vmem(len(arrays)), out_specs=[p...  7.48 us
  transfers between devices with their start and end apart: 3, of which 2 were waited for; matrix products, arithmetic and copies ran while one was open for 0% of the time, Pallas kernels for 12%

profile of v5, /device:TPU:1, one launch (start us, length us, event | category | flops | bytes accessed | tf_op | source)
XLA Modules:
  0.0 157.1 jit_solution(12184510576692186098)
XLA Ops:
  1.4 4.5 %boundary_pack.1 = f32[32,136,128]{2,1,0:T(8,128)} custom-call(s32[1,2,16]{2,1,0:T(2,128)S(1)} %bitcast.17, s32[64,128]{1,0:T(8,128)} %bitcast.12, f32[64,128,128]{2,1,0:T(8,128)} %refs_7_.3, f32[64,8192]{1,0:T(8,128)} %refs_31_.1), custom_call_target="tpu_custom_call" | custom-call | tf_op jit(solution)/shard_map/boundary_pack/pallas_call | solution.py:150
  5.9 8.5 %all-to-all-start = ((f32[16,272,128]{2,1,0:T(8,128)}), f32[16,272,128]{2,1,0:T(8,128)}, u32[]{:S(2)}, u32[]{:S(2)}) async-start(f32[16,272,128]{2,1,0:T(8,128)} %bitcast.20), calls=%async_computation | async-start | bytes 4456448 | tf_op jit(solution)/shard_map/all_to_all | solution.py:736
  14.6 2.2 %copy-done.1 = f32[1,1024,1024]{2,1,0:T(8,128)S(1)} copy-done((f32[1,1024,1024]{2,1,0:T(8,128)S(1)}, f32[1,1024,1024]{2,1,0:T(8,128)}, u32[]{:S(2)}) %copy-start.1) | copy-done | bytes 4194328
  18.3 9.4 %local_part.1 = (f32[32,64,128]{2,1,0:T(8,128)}, f32[32,64,128]{2,1,0:T(8,128)}, f32[32,1,128]{2,1,0:T(1,128)}, f32[32,1,128]{2,1,0:T(1,128)}, bf16[32,128,128]{...) custom-call(s32[64]{0:T(128)S(1)} %pad_add_fusion.perm, ...), custom_call_target="tpu_custom_call" | custom-call | flops 402653184 | bytes 16777216 | tf_op jit(solution)/shard_map/local_part/pallas_call | solution.py:246
  27.7 18.3 %all-to-all-done = f32[16,272,128]{2,1,0:T(8,128)} async-done(((f32[16,272,128]{2,1,0:T(8,128)}), f32[16,272,128]{2,1,0:T(8,128)}, u32[]{:S(2)}, u32[]{:S(2)}) %all-to-all-start) | async-done | bytes 2228256 | tf_op jit(solution)/shard_map/all_to_all | solution.py:736
  46.1 3.1 %first_restrict.1 = f32[16,40,128]{2,1,0:T(8,128)} custom-call(f32[32,136,128]{2,1,0:T(8,128)} %bitcast.4.arrived.refs_8_, f32[32,64,128]{2,1,0:T(8,128)} %get-tuple-element.36.rs, f32[64,64]{1,0:T(8,128)S(1)} %get-tuple-element.39.rr), custom_call_target="tpu_custom_call" | custom-call | tf_op jit(solution)/shard_map/first_restrict/pallas_call | solution.py:322
  49.2 6.0 %all-to-all-start.1 = ((f32[16,40,128]{2,1,0:T(8,128)}), f32[16,40,128]{2,1,0:T(8,128)}, u32[]{:S(2)}, u32[]{:S(2)}) async-start(f32[16,40,128]{2,1,0:T(8,128)} %first_restrict.1), calls=%async_computation.1 | async-start | bytes 655360 | tf_op jit(solution)/shard_map/all_to_all | solution.py:736
  55.2 8.1 %pair_setup.1 = (bf16[32,256,256]{2,1,0:T(8,128)(2,1)}, bf16[32,256,256]{2,1,0:T(8,128)(2,1)}, f32[32,1,128]{2,1,0:T(1,128)}, s32[32,1,128]{2,1,0:T(1,128)}, f32[32,64,128]{2,1,0:T(8,128)}) custom-call(s32[64]{0:T(128)S(1)} %pad_add_fusion.perm, s32[16]{0:T(128)S(1)} %bitcast.19, f32[64,128,128]{2,1,0:T(8,128)} %refs_7_.3, f32[64,128,128]{2,1,0:T(8,128)} %refs_7_.3, ...), custom_call_target="tpu_custom_call" | custom-call | flops 402653184 | bytes 16777216 | tf_op jit(solution)/shard_map/pair_setup/pallas_call | solution.py:377
  63.3 1.4 lowest_part.2
  66.1 7.5 %all-to-all-start.2 = ((f32[8,40,128]{2,1,0:T(8,128)}), f32[8,40,128]{2,1,0:T(8,128)}, u32[]{:S(2)}, u32[]{:S(2)}) async-start(f32[8,40,128]{2,1,0:T(8,128)} %copy-done.16), calls=%async_computation.2 | async-start | bytes 327680 | tf_op jit(solution)/shard_map/all_to_all | solution.py:736
  73.6 5.7 %all-to-all-done.2.arrived = f32[8,40,128]{2,1,0:T(8,128)} async-done(((f32[8,40,128]{2,1,0:T(8,128)}), f32[8,40,128]{2,1,0:T(8,128)}, u32[]{:S(2)}, u32[]{:S(2)}) %all-to-all-start.2) | async-done | bytes 163872 | tf_op jit(solution)/shard_map/all_to_all | solution.py:736
  79.2 2.2 %copy-done.2 = f32[1,1024,1024]{2,1,0:T(8,128)S(1)} copy-done((f32[1,1024,1024]{2,1,0:T(8,128)S(1)}, f32[1,1024,1024]{2,1,0:T(8,128)}, u32[]{:S(2)}) %copy-start.2) | copy-done | bytes 4194328
  82.4 3.0 %correct_part.2 = (f32[16,64,64]{2,1,0:T(8,128)S(1)}, f32[8,128]{1,0:T(8,128)}) custom-call(f32[8,40,128]{2,1,0:T(8,128)} %all-to-all-done.2.arrived, f32[64,512]{1,0:T(8,128)S(1)} %constant_dynamic-slice_fusion.inverse_rows, f32[64,1024]{1,0:T(8,128)S(1)} %get-tuple-element.42.g, f32[64,1024]{1,0:T(8,128)S(1)} %copy-done.15, ...), custom_call_target="tpu_custom_call" | custom-call | tf_op jit(solution)/shard_map/correct_part/pallas_call | solution.py:451
  85.5 2.2 %copy-done.5 = bf16[32,256,256]{2,1,0:T(8,128)(2,1)S(1)} copy-done((bf16[32,256,256]{2,1,0:T(8,128)(2,1)S(1)}, bf16[32,256,256]{2,1,0:T(8,128)(2,1)}, u32[]{:S(2)}) %copy-start.5) | copy-done | bytes 4194328
  87.7 1.2 copy-done.9
  88.9 1.2 copy-done.10
  90.2 1.2 copy-done.11
  91.4 9.3 %forward_part.1 = (f32[2,32,64,128]{3,2,1,0:T(8,128)S(1)}, f32[2,32,64,128]{3,2,1,0:T(8,128)S(1)}, f32[32,64,128]{2,1,0:T(8,128)S(1)}, f32[16,40,128]{2,1,0:T(8,128)S(1)}) custom-call(s32[64]{0:T(128)S(1)} %pad_add_fusion.perm, s32[1]{0:T(128)} %bitcast.member, f32[16,64,64]{2,1,0:T(8,128)S(1)} %get-tuple-element.47.e, f32[32,64,128]{2,1,0:T(8,128)S(1)} %copy-done.7, ...), custom_call_target="tpu_custom_call" | custom-call | tf_op jit(solution)/shard_map/forward_part/pallas_call | solution.py:564
  100.7 14.0 %all_to_all.30.arrived = f32[16,40,128]{2,1,0:T(8,128)S(1)} all-to-all(f32[16,40,128]{2,1,0:T(8,128)S(1)} %get-tuple-element.59), channel_id=1, replica_groups=mesh['grp'=8,'sub'=8,'chip'=2] {'sub','chip'}, dimensions={0} | all-to-all | bytes 655360 | tf_op jit(solution)/shard_map/all_to_all | solution.py:736
  115.0 10.1 %all_to_all.31.arrived = f32[8,40,128]{2,1,0:T(8,128)S(1)} all-to-all(f32[8,40,128]{2,1,0:T(8,128)S(1)} %get-tuple-element.60), channel_id=1, replica_groups=mesh['grp'=8,'sub'=8,'chip'=2] {'grp'}, dimensions={0} | all-to-all | bytes 327680 | tf_op jit(solution)/shard_map/all_to_all | solution.py:736
  125.1 1.4 correct_part.3
  127.3 7.5 %second_part.1 = (f32[2,32,64,128]{3,2,1,0:T(8,128)S(1)}, f32[2,32,64,128]{3,2,1,0:T(8,128)S(1)}, f32[128,8,128]{2,1,0:T(8,128)S(1)}) custom-call(s32[64]{0:T(128)S(1)} %pad_add_fusion.perm, s32[1]{0:T(128)} %bitcast.member, f32[16,64,64]{2,1,0:T(8,128)S(1)} %get-tuple-element.63.e, f32[8,128]{1,0:T(8,128)S(1)} %get-tuple-element.62.dots, ...), custom_call_target="tpu_custom_call" | custom-call | tf_op jit(solution)/shard_map/second_part/pallas_call | solution.py:652
  134.8 17.8 %all_to_all.32.arrived = f32[128,8,128]{2,1,0:T(8,128)S(1)} all-to-all(f32[128,8,128]{2,1,0:T(8,128)S(1)} %get-tuple-element.67), channel_id=1, replica_groups=mesh['grp'=8,'sub'=8,'chip'=2] {'grp','sub','chip'}, dimensions={0} | all-to-all | bytes 1048576 | tf_op jit(solution)/shard_map/all_to_all | solution.py:736
  152.6 4.5 %combine.1 = (f32[64,8192]{1,0:T(8,128)}, f32[64,8192]{1,0:T(8,128)}) custom-call(s32[64]{0:T(128)S(1)} %pad_add_fusion.perm, f32[8,128]{1,0:T(8,128)S(1)} %get-tuple-element.62.dots, f32[128,8,128]{2,1,0:T(8,128)S(1)} %all_to_all.32.arrived, f32[32,64,128]{2,1,0:T(8,128)S(1)} %copy-done.7, f32[32,64,128]{2,1,0:T(8,128)S(1)} %copy-done.8, ...), custom_call_target="tpu_custom_call" | custom-call | tf_op jit(solution)/shard_map/combine/pallas_call | solution.py:726
  (53 shorter events, 5.9 us)
Async XLA Ops:
  0.6 27.1 %copy-start = (f32[512,512]{1,0:T(8,128)S(1)}, f32[512,512]{1,0:T(8,128)}, u32[]{:S(2)}) copy-start(f32[512,512]{1,0:T(8,128)} %param.17) | copy-start | bytes 3145732
  5.9 8.7 %copy-start.21 = (s32[1024]{0:T(1024)S(1)}, s32[1024]{0:T(1024)}, u32[]{:S(2)}) copy-start(s32[1024]{0:T(1024)} %param.15) | copy-start | bytes 12292
  5.9 40.1 %all-to-all-start = ((f32[16,272,128]{2,1,0:T(8,128)}), f32[16,272,128]{2,1,0:T(8,128)}, u32[]{:S(2)}, u32[]{:S(2)}) async-start(f32[16,272,128]{2,1,0:T(8,128)} %bitcast.20), calls=%async_computation | async-start | bytes 4456448 | tf_op jit(solution)/shard_map/all_to_all | solution.py:736
  14.6 2.2 %copy-start.1 = (f32[1,1024,1024]{2,1,0:T(8,128)S(1)}, f32[1,1024,1024]{2,1,0:T(8,128)}, u32[]{:S(2)}) copy-start(f32[1,1024,1024]{2,1,0:T(8,128)} %param.16) | copy-start | bytes 12582916
  16.8 1.5 copy-start.12
  16.8 1.5 copy-start.23
  49.2 14.2 %all-to-all-start.1 = ((f32[16,40,128]{2,1,0:T(8,128)}), f32[16,40,128]{2,1,0:T(8,128)}, u32[]{:S(2)}, u32[]{:S(2)}) async-start(f32[16,40,128]{2,1,0:T(8,128)} %first_restrict.1), calls=%async_computation.1 | async-start | bytes 655360 | tf_op jit(solution)/shard_map/all_to_all | solution.py:736
  55.2 30.3 %copy-start.7 = (f32[32,64,128]{2,1,0:T(8,128)S(1)}, f32[32,64,128]{2,1,0:T(8,128)}, u32[]{:S(2)}) copy-start(f32[32,64,128]{2,1,0:T(8,128)} %get-tuple-element.48.b_slot) | copy-start | bytes 3145732
  55.2 30.3 %copy-start.8 = (f32[32,64,128]{2,1,0:T(8,128)S(1)}, f32[32,64,128]{2,1,0:T(8,128)}, u32[]{:S(2)}) copy-start(f32[32,64,128]{2,1,0:T(8,128)} %get-tuple-element.49.b_rest) | copy-start | bytes 3145732
  66.1 13.1 %all-to-all-start.2 = ((f32[8,40,128]{2,1,0:T(8,128)}), f32[8,40,128]{2,1,0:T(8,128)}, u32[]{:S(2)}, u32[]{:S(2)}) async-start(f32[8,40,128]{2,1,0:T(8,128)} %copy-done.16), calls=%async_computation.2 | async-start | bytes 327680 | tf_op jit(solution)/shard_map/all_to_all | solution.py:736
  79.2 2.2 %copy-start.2 = (f32[1,1024,1024]{2,1,0:T(8,128)S(1)}, f32[1,1024,1024]{2,1,0:T(8,128)}, u32[]{:S(2)}) copy-start(f32[1,1024,1024]{2,1,0:T(8,128)} %param.16) | copy-start | bytes 12582916
  81.4 0.9 copy-start.15
  82.4 3.1 %copy-start.4 = (bf16[32,256,256]{2,1,0:T(8,128)(2,1)S(1)}, bf16[32,256,256]{2,1,0:T(8,128)(2,1)}, u32[]{:S(2)}) copy-start(bf16[32,256,256]{2,1,0:T(8,128)(2,1)} %get-tuple-element.55.hi_pair) | copy-start | bytes 12582916
  82.4 3.1 %copy-start.13 = (s32[8192]{0:T(1024)S(1)}, s32[8192]{0:T(1024)}, u32[]{:S(2)}) copy-start(s32[8192]{0:T(1024)} %param.14) | copy-start | bytes 98308
  82.4 3.1 %copy-start.17 = (f32[32,1,128]{2,1,0:T(1,128)S(1)}, f32[32,1,128]{2,1,0:T(1,128)}, u32[]{:S(2)}) copy-start(f32[32,1,128]{2,1,0:T(1,128)} %get-tuple-element.50.d_slot) | copy-start | bytes 49156
  82.4 3.1 %copy-start.18 = (f32[32,1,128]{2,1,0:T(1,128)S(1)}, f32[32,1,128]{2,1,0:T(1,128)}, u32[]{:S(2)}) copy-start(f32[32,1,128]{2,1,0:T(1,128)} %get-tuple-element.51.d_rest) | copy-start | bytes 49156
  82.4 3.1 %copy-start.19 = (f32[32,1,128]{2,1,0:T(1,128)S(1)}, f32[32,1,128]{2,1,0:T(1,128)}, u32[]{:S(2)}) copy-start(f32[32,1,128]{2,1,0:T(1,128)} %get-tuple-element.53.d_peer) | copy-start | bytes 49156
  82.4 3.1 %copy-start.20 = (s32[32,1,128]{2,1,0:T(1,128)S(1)}, s32[32,1,128]{2,1,0:T(1,128)}, u32[]{:S(2)}) copy-start(s32[32,1,128]{2,1,0:T(1,128)} %get-tuple-element.54.m_peer) | copy-start | bytes 49156
  85.5 2.2 %copy-start.5 = (bf16[32,256,256]{2,1,0:T(8,128)(2,1)S(1)}, bf16[32,256,256]{2,1,0:T(8,128)(2,1)}, u32[]{:S(2)}) copy-start(bf16[32,256,256]{2,1,0:T(8,128)(2,1)} %get-tuple-element.56.lo_pair) | copy-start | bytes 12582916
  87.7 1.2 copy-start.9
  88.9 1.2 copy-start.10
  90.1 1.2 copy-start.11
  91.4 33.7 %copy-start.3 = (f32[1,1024,1024]{2,1,0:T(8,128)S(1)}, f32[1,1024,1024]{2,1,0:T(8,128)}, u32[]{:S(2)}) copy-start(f32[1,1024,1024]{2,1,0:T(8,128)} %param.16) | copy-start | bytes 12582916
  125.1 2.2 %copy-start.6 = (bf16[32,256,256]{2,1,0:T(8,128)(2,1)S(1)}, bf16[32,256,256]{2,1,0:T(8,128)(2,1)}, u32[]{:S(2)}) copy-start(bf16[32,256,256]{2,1,0:T(8,128)(2,1)} %get-tuple-element.56.lo_pair) | copy-start | bytes 12582916
  (3 other events, 2.2 us)

commit v6 on v5

--- a/solution.py
+++ b/solution.py
@@ -20,6 +20,8 @@
 NC1 = 1024
 STEP = 8
 NSTEP = SLOTS // STEP
+CHUNK = 16
+CHUNKS = SLOTS // CHUNK
 SIDE = 136
 ROWS = 40
 VMEM_LIMIT = 24 * 1024 * 1024
@@ -459,16 +461,16 @@
 def apply_off(x, hi, lo):
     xh, xl = split2(x)
     rows = x.shape[0]
+    if x.shape[1] == TILE:
+        return dot(beside(xh, xl), jnp.concatenate([hi, hi], axis=0)) + dot(xh, lo)
     both = dot(jnp.concatenate([xh, xl], axis=0), hi)
     return both[:rows] + both[rows:] + dot(xh, lo)
 
 
 def apply_block(x, diag, hi, lo):
     xh, xl = split2(x)
-    rows = x.shape[0]
-    both = dot(jnp.concatenate([xh, xl], axis=0), hi)
     kept = xh.astype(F32) + xl.astype(F32)
-    return both[:rows] + both[rows:] + dot(xh, lo) + kept[:, : diag.shape[1]] * diag
+    return apply_off(x, hi, lo) + kept[:, : diag.shape[1]] * diag
 
 
 def lift(parts, spread):
@@ -496,7 +498,7 @@
     e_own = e.at[pl.ds(member[0], 1)]
     views = (e, b_slot, b_rest, d_slot, d_rest, x_peer, d_peer, m_peer, hi_pair, lo_pair, hi_rest, lo_rest, ws_out)
 
-    @pl.loop(0, NSTEP)
+    @pl.loop(0, CHUNKS)
     def _(step):
         e_peer, *parts = [v.at[part(step, v.shape[0])] for v in views]
         both = [v.at[:, part(step, SLOTS)] for v in (z_out, w_out)]
@@ -512,7 +514,7 @@
 
 
 def part(step, count):
-    size = count // NSTEP
+    size = count // CHUNKS
     return pl.ds(step * size, size)
 
 
@@ -521,19 +523,19 @@
     hi_rest, lo_rest, maps, z_out, w_out, ws_out, acc_rr, acc_bz, acc_zw
 ):
     e_mine = two_parts(e_own[0])
-    e_both = [two_parts(beside(e_own[0], e_peer[q])) for q in range(STEP // 2)]
+    e_both = [two_parts(beside(e_own[0], e_peer[q])) for q in range(CHUNK // 2)]
     rr, bz, zw = acc_rr[...], acc_bz[...], acc_zw[...]
-    pairs, rest = range(STEP), range(STEP)
-    rows = [maps[pl.ds(perm[at + step * STEP + k], 1)] for at in (0, SLOTS) for k in pairs]
+    pairs, rest = range(CHUNK), range(CHUNK)
+    rows = [maps[pl.ds(perm[at + step * CHUNK + k], 1)] for at in (0, SLOTS) for k in pairs]
     b_own = [b_slot[k] for k in pairs] + [b_rest[k] for k in rest]
     diag = [jnp.concatenate([d_slot[k], d_peer[k]], axis=1) for k in pairs] + [d_rest[k] for k in rest]
     rdiag = [OMEGA / d for d in diag]
     mats = [(hi_pair[k], lo_pair[k]) for k in pairs] + [(hi_rest[k], lo_rest[k]) for k in rest]
     x1 = [beside(b_own[k] * rdiag[k][:, :TILE], x_peer[k]) for k in pairs]
-    x1 = x1 + [b * rd for b, rd in zip(b_own[STEP:], rdiag[STEP:])]
+    x1 = x1 + [b * rd for b, rd in zip(b_own[CHUNK:], rdiag[CHUNK:])]
     spread = [one_hot(row) for row in rows]
     ups = [lift(e_both[k // 2], pair_spread(spread[k], one_hot(m_peer[k]))) for k in pairs]
-    ups = ups + [lift(e_mine, sp) for sp in spread[STEP:]]
+    ups = ups + [lift(e_mine, sp) for sp in spread[CHUNK:]]
     x = [start + up for start, up in zip(x1, ups)]
     image = [apply_off(xx, *m) for xx, m in zip(x, mats)]
     z = [(1.0 - OMEGA) * xx + start - im * rd for xx, start, im, rd in zip(x, x1, image, rdiag)]
@@ -541,14 +543,14 @@
     x1 = [ww * rd for ww, rd in zip(w, rdiag)]
     left = [(m[0][:, :TILE], m[1][:, :TILE]) for m in mats]
     y = [(1.0 - OMEGA) * ww[:, :TILE] - apply_off(xx, *m) for ww, xx, m in zip(w, x1, left)]
-    for i in range(0, 2 * STEP, 2):
+    for i in range(0, 2 * CHUNK, 2):
         rr = rr + mm_exact(beside(y[i], y[i + 1]), beside(spread[i], spread[i + 1]), nt=True)
-    for i in range(2 * STEP):
+    for i in range(2 * CHUNK):
         zz, ww = z[i][:, :TILE], w[i][:, :TILE]
         bz = bz + b_own[i] * zz
         zw = zw + zz * ww
-        z_out[i // STEP, i % STEP] = zz
-        w_out[i // STEP, i % STEP] = ww
+        z_out[i // CHUNK, i % CHUNK] = zz
+        w_out[i // CHUNK, i % CHUNK] = ww
     for k in pairs:
         ws_out[k] = w[k][:, TILE:]
     acc_rr[...] = rr
@@ -589,7 +591,7 @@
     e_own = e.at[pl.ds(member[0], 1)]
     views = (e, b_slot, b_rest, d_slot, d_rest, d_peer, m_peer, hi_pair, lo_pair, hi_rest, lo_rest, w_peer)
 
-    @pl.loop(0, NSTEP)
+    @pl.loop(0, CHUNKS)
     def _(step):
         e_peer, *parts = [v.at[part(step, v.shape[0])] for v in views]
         z_part, w_part, v_part, u_part = [v.at[:, part(step, SLOTS)] for v in (z_in, w_in, v_out, u_out)]
@@ -600,10 +602,7 @@
 
     first = jnp.sum(jnp.concatenate([acc_a[...], acc_b[...]], axis=0).T, axis=0, keepdims=True)
     last = jnp.sum(jnp.concatenate([acc_c[...], acc_c[...]], axis=0).T, axis=0, keepdims=True)
-    r8 = lax.broadcasted_iota(jnp.int32, (8, TILE), 0)
-    extra = jnp.where(r8 == 0, first, jnp.where(r8 == 1, last, 0.0))
-    for q in range(GROUPS * PEERS):
-        out[q] = extra
+    out[...] = jnp.broadcast_to(jnp.concatenate([first, last], axis=0), out.shape)
 
 
 def second_step(
@@ -612,7 +611,7 @@
 ):
     alpha = acc_alpha[...]
     e_mine = two_parts(e_own[0])
-    e_both = [two_parts(beside(e_own[0], e_peer[q])) for q in range(STEP // 2)]
+    e_both = [two_parts(beside(e_own[0], e_peer[q])) for q in range(CHUNK // 2)]
     sums = [acc_a[...], acc_b[...], acc_c[...]]
 
     def gather(b, z, w, v, u):
@@ -623,26 +622,26 @@
         sums[1] = sums[1] + z1 * az1
         sums[2] = sums[2] + (z1 * w + z * az1)
 
-    pairs, rest = range(STEP), range(STEP)
-    rows = [maps[pl.ds(perm[at + step * STEP + k], 1)] for at in (0, SLOTS) for k in pairs]
+    pairs, rest = range(CHUNK), range(CHUNK)
+    rows = [maps[pl.ds(perm[at + step * CHUNK + k], 1)] for at in (0, SLOTS) for k in pairs]
     diag = [jnp.concatenate([d_slot[k], d_peer[k]], axis=1) for k in pairs] + [d_rest[k] for k in rest]
     rdiag = [OMEGA / d for d in diag]
     mats = [(hi_pair[k], lo_pair[k]) for k in pairs] + [(hi_rest[k], lo_rest[k]) for k in rest]
     w = [jnp.concatenate([w_in[0, k], w_peer[k]], axis=1) for k in pairs] + [w_in[1, k] for k in rest]
     spread = [one_hot(row) for row in rows]
     ups = [lift(e_both[k // 2], pair_spread(spread[k], one_hot(m_peer[k]))) for k in pairs]
-    ups = ups + [lift(e_mine, sp) for sp in spread[STEP:]]
+    ups = ups + [lift(e_mine, sp) for sp in spread[CHUNK:]]
     x1 = [ww * rd for ww, rd in zip(w, rdiag)]
     x = [start + up for start, up in zip(x1, ups)]
     image = [apply_off(xx, *m) for xx, m in zip(x, mats)]
     v = [(1.0 - OMEGA) * xx + start - im * rd for xx, start, im, rd in zip(x, x1, image, rdiag)]
     left = [(m[0][:, :TILE], m[1][:, :TILE]) for m in mats]
     u = [apply_block(vv, d[:, :TILE], *m) for vv, d, m in zip(v, diag, left)]
-    for i in range(2 * STEP):
-        vv, b_ref = v[i][:, :TILE], (b_slot if i < STEP else b_rest)
-        v_out[i // STEP, i % STEP] = vv
-        u_out[i // STEP, i % STEP] = u[i]
-        gather(b_ref[i % STEP], z_in[i // STEP, i % STEP], w[i][:, :TILE], vv, u[i])
+    for i in range(2 * CHUNK):
+        vv, b_ref = v[i][:, :TILE], (b_slot if i < CHUNK else b_rest)
+        v_out[i // CHUNK, i % CHUNK] = vv
+        u_out[i // CHUNK, i % CHUNK] = u[i]
+        gather(b_ref[i % CHUNK], z_in[i // CHUNK, i % CHUNK], w[i][:, :TILE], vv, u[i])
     acc_a[...] = sums[0]
     acc_b[...] = sums[1]
     acc_c[...] = sums[2]
@@ -656,7 +655,7 @@
         out_shape=[
             jax.ShapeDtypeStruct((2, SLOTS, COLS, TILE), F32),
             jax.ShapeDtypeStruct((2, SLOTS, COLS, TILE), F32),
-            jax.ShapeDtypeStruct((GROUPS * PEERS, 8, TILE), F32),
+            jax.ShapeDtypeStruct((GROUPS * PEERS, 2, TILE), F32),
         ],
         scratch_shapes=[pltpu.VMEM((COLS, TILE), F32)] * 4,
         compiler_params=params(),
@@ -669,9 +668,7 @@
 
     @pl.when(step == 0)
     def _():
-        total = arrived[0]
-        for q in range(1, GROUPS * PEERS):
-            total = total + arrived[q]
+        total = jnp.sum(arrived[...], axis=0)
         old = column(dots[0:1])
         one = column(total[0:1])
         two = column(total[1:2])
@@ -712,7 +709,7 @@
         grid=(NSTEP,),
         in_specs=[
             pl.BlockSpec((8, TILE), lambda s, p: (0, 0)),
-            pl.BlockSpec((GROUPS * PEERS, 8, TILE), lambda s, p: (0, 0, 0)),
+            pl.BlockSpec((GROUPS * PEERS, 2, TILE), lambda s, p: (0, 0, 0)),
             single(),
             single(),
             pair(),
@@ -776,7 +773,7 @@
         lows = exchange(outgoing, "grp")
         return correct_part(lows, inverse_rows, g, x, inverse, operator)
 
-    rr_local, g, inverse_rows = lax.optimization_barrier((rr_local, g, inverse_rows))
+    rr_local, g, inverse_rows, member = lax.optimization_barrier((rr_local, g, inverse_rows, member))
     gathered = exchange(first_restrict(side, rs, rr_local), GROUP_AXES)
     hi_pair, lo_pair, d_peer, m_peer, x_peer = pair_setup(perm, counts, diag_tiles, side, remote)
     gathered, hi_pair = lax.optimization_barrier((gathered, hi_pair))

time: 158 us -> 148 us (0.937)
  blocking collectives: 41.8 us -> 51 us
  starting transfers between devices: 21.9 us -> 14.5 us
  waiting for transfers between devices: 24 us -> 18.4 us
  Pallas kernels: 53.7 us -> 49.9 us
  local copies, waits for them, and re-layouts: 14.3 us -> 12.4 us
    all_to_all x3 -> x4, blocking collectives: 41.8 us -> 51 us  [exchange(): return lax.all_to_all(x, axes, 0, 0, tiled=True)]
    all_to_all x3 -> x2, starting transfers between devices: 21.9 us -> 14.5 us  [exchange(): return lax.all_to_all(x, axes, 0, 0, tiled=True)]
    all_to_all x3 -> x2, waiting for transfers between devices: 24 us -> 18.4 us  [exchange(): return lax.all_to_all(x, axes, 0, 0, tiled=True)]
    unnamed x49 -> x45, local copies, waits for them, and re-layouts: 14.2 us -> 12.3 us
  transfers between devices with their start and end apart: 3 -> 2, of which waited for: 2 -> 1; matrix products, arithmetic and copies ran while one was open for 0% -> 0% of each run, Pallas kernels for 12% -> 13%
where the time goes in v6:
time: 148 us
  blocking collectives  51 us (34%)
  Pallas kernels  49.9 us (34%)
  waiting for transfers between devices  18.4 us (12%)
  starting transfers between devices  14.5 us (10%)
  local copies, waits for them, and re-layouts  12.4 us (8%)
    all_to_all x4, blocking collectives, exchange(): return lax.all_to_all(x, axes, 0, 0, tiled=True)  51 us
    all_to_all x2, waiting for transfers between devices, exchange(): return lax.all_to_all(x, axes, 0, 0, tiled=True)  18.4 us
    all_to_all x2, starting transfers between devices, exchange(): return lax.all_to_all(x, axes, 0, 0, tiled=True)  14.5 us
    unnamed x45, local copies, waits for them, and re-layouts  12.3 us
    pallas_call x1, Pallas kernels, local_part(): pl.pallas_call(local_kernel, grid_spec=grid, out_shape=[sds((COLS, TILE))...  9.35 us
    pallas_call x1, Pallas kernels, pair_setup(): pl.pallas_call(pair_kernel, grid_spec=grid, out_shape=[far((SLOTS, 2 * TI...  8.14 us
    pallas_call x1, Pallas kernels, forward_part(): pl.pallas_call(forward_kernel, in_specs=in_vmem(len(arrays)), out_specs=[...  7.98 us
    pallas_call x1, Pallas kernels, second_part(): pl.pallas_call(second_kernel, in_specs=in_vmem(len(arrays)), out_specs=[p...  6.45 us
  transfers between devices with their start and end apart: 2, of which 1 were waited for; matrix products, arithmetic and copies ran while one was open for 0% of the time, Pallas kernels for 13%

profile of v6, /device:TPU:1, one launch (start us, length us, event | category | flops | bytes accessed | tf_op | source)
XLA Modules:
  0.0 147.6 jit_solution(231993982818643536)
XLA Ops:
  1.4 4.5 %boundary_pack.1 = f32[32,136,128]{2,1,0:T(8,128)} custom-call(s32[1,2,16]{2,1,0:T(2,128)S(1)} %bitcast.17, s32[64,128]{1,0:T(8,128)} %bitcast.12, f32[64,128,128]{2,1,0:T(8,128)} %refs_7_.3, f32[64,8192]{1,0:T(8,128)} %cols.1), custom_call_target="tpu_custom_call" | custom-call | tf_op jit(solution)/shard_map/boundary_pack/pallas_call | solution.py:152
  5.9 8.5 %all-to-all-start = ((f32[16,272,128]{2,1,0:T(8,128)}), f32[16,272,128]{2,1,0:T(8,128)}, u32[]{:S(2)}, u32[]{:S(2)}) async-start(f32[16,272,128]{2,1,0:T(8,128)} %bitcast.20), calls=%async_computation | async-start | bytes 4456448 | tf_op jit(solution)/shard_map/all_to_all | solution.py:733
  14.7 2.2 %copy-done.1 = f32[1,1024,1024]{2,1,0:T(8,128)S(1)} copy-done((f32[1,1024,1024]{2,1,0:T(8,128)S(1)}, f32[1,1024,1024]{2,1,0:T(8,128)}, u32[]{:S(2)}) %copy-start.1) | copy-done | bytes 4194328
  16.8 1.0 coarse_setup.1
  18.2 9.3 %local_part.1 = (f32[32,64,128]{2,1,0:T(8,128)}, f32[32,64,128]{2,1,0:T(8,128)}, f32[32,1,128]{2,1,0:T(1,128)}, f32[32,1,128]{2,1,0:T(1,128)}, bf16[32,128,128]{...) custom-call(s32[64]{0:T(128)S(1)} %pad_add_fusion.perm, ...), custom_call_target="tpu_custom_call" | custom-call | flops 402653184 | bytes 16777216 | tf_op jit(solution)/shard_map/local_part/pallas_call | solution.py:248
  27.6 18.4 %all-to-all-done = f32[16,272,128]{2,1,0:T(8,128)} async-done(((f32[16,272,128]{2,1,0:T(8,128)}), f32[16,272,128]{2,1,0:T(8,128)}, u32[]{:S(2)}, u32[]{:S(2)}) %all-to-all-start) | async-done | bytes 2228256 | tf_op jit(solution)/shard_map/all_to_all | solution.py:733
  46.1 3.1 %first_restrict.1 = f32[16,40,128]{2,1,0:T(8,128)} custom-call(f32[32,136,128]{2,1,0:T(8,128)} %bitcast.8.arrived.refs_8_, f32[32,64,128]{2,1,0:T(8,128)} %get-tuple-element.40.rs, f32[64,64]{1,0:T(8,128)S(1)} %get-tuple-element.41.rr), custom_call_target="tpu_custom_call" | custom-call | tf_op jit(solution)/shard_map/first_restrict/pallas_call | solution.py:324
  49.2 6.0 %all-to-all-start.1 = ((f32[16,40,128]{2,1,0:T(8,128)}), f32[16,40,128]{2,1,0:T(8,128)}, u32[]{:S(2)}, u32[]{:S(2)}) async-start(f32[16,40,128]{2,1,0:T(8,128)} %first_restrict.1), calls=%async_computation.1 | async-start | bytes 655360 | tf_op jit(solution)/shard_map/all_to_all | solution.py:733
  55.2 8.1 %pair_setup.1 = (bf16[32,256,256]{2,1,0:T(8,128)(2,1)}, bf16[32,256,256]{2,1,0:T(8,128)(2,1)}, f32[32,1,128]{2,1,0:T(1,128)}, s32[32,1,128]{2,1,0:T(1,128)}, f32[32,64,128]{2,1,0:T(8,128)}) custom-call(s32[64]{0:T(128)S(1)} %pad_add_fusion.perm, s32[16]{0:T(128)S(1)} %bitcast.19, f32[64,128,128]{2,1,0:T(8,128)} %refs_7_.3, f32[64,128,128]{2,1,0:T(8,128)} %refs_7_.3, ...), custom_call_target="tpu_custom_call" | custom-call | flops 402653184 | bytes 16777216 | tf_op jit(solution)/shard_map/pair_setup/pallas_call | solution.py:379
  63.3 1.4 lowest_part.2
  64.7 12.8 %all_to_all.30.arrived = f32[8,40,128]{2,1,0:T(8,128)S(1)} all-to-all(f32[8,40,128]{2,1,0:T(8,128)S(1)} %get-tuple-element.45), channel_id=1, replica_groups=mesh['grp'=8,'sub'=8,'chip'=2] {'grp'}, dimensions={0} | all-to-all | bytes 327680 | tf_op jit(solution)/shard_map/all_to_all | solution.py:733
  77.5 2.2 %copy-done.2 = f32[1,1024,1024]{2,1,0:T(8,128)S(1)} copy-done((f32[1,1024,1024]{2,1,0:T(8,128)S(1)}, f32[1,1024,1024]{2,1,0:T(8,128)}, u32[]{:S(2)}) %copy-start.2) | copy-done | bytes 4194328
  79.8 1.8 %correct_part.2 = (f32[16,64,64]{2,1,0:T(8,128)S(1)}, f32[8,128]{1,0:T(8,128)}) custom-call(f32[8,40,128]{2,1,0:T(8,128)S(1)} %all_to_all.30.arrived, f32[64,512]{1,0:T(8,128)S(1)} %constant_dynamic-slice_fusion.inverse_rows, f32[64,1024]{1,0:T(8,128)S(1)} %get-tuple-element.44.g, f32[64,1024]{1,0:T(8,128)S(1)} %get-tuple-element.47.x_ref, ...), custom_call_target="tpu_custom_call" | custom-call | tf_op jit(solution)/shard_map/correct_part/pallas_call | solution.py:453
  82.0 2.2 %copy-done.5 = bf16[32,256,256]{2,1,0:T(8,128)(2,1)S(1)} copy-done((bf16[32,256,256]{2,1,0:T(8,128)(2,1)S(1)}, bf16[32,256,256]{2,1,0:T(8,128)(2,1)}, u32[]{:S(2)}) %copy-start.5) | copy-done | bytes 4194328
  84.1 1.2 copy-done.9
  85.4 1.2 copy-done.10
  86.6 1.2 copy-done.11
  87.8 8.0 %forward_part.1 = (f32[2,32,64,128]{3,2,1,0:T(8,128)S(1)}, f32[2,32,64,128]{3,2,1,0:T(8,128)S(1)}, f32[32,64,128]{2,1,0:T(8,128)S(1)}, f32[16,40,128]{2,1,0:T(8,128)S(1)}) custom-call(s32[64]{0:T(128)S(1)} %pad_add_fusion.perm, s32[1]{0:T(128)} %bitcast.5.member, f32[16,64,64]{2,1,0:T(8,128)S(1)} %get-tuple-element.49.e, f32[32,64,128]{2,1,0:T(8,128)S(1)} %copy-done.7, ...), custom_call_target="tpu_custom_call" | custom-call | tf_op jit(solution)/shard_map/forward_part/pallas_call | solution.py:566
  95.8 14.0 %all_to_all.31.arrived = f32[16,40,128]{2,1,0:T(8,128)S(1)} all-to-all(f32[16,40,128]{2,1,0:T(8,128)S(1)} %get-tuple-element.61), channel_id=1, replica_groups=mesh['grp'=8,'sub'=8,'chip'=2] {'sub','chip'}, dimensions={0} | all-to-all | bytes 655360 | tf_op jit(solution)/shard_map/all_to_all | solution.py:733
  110.2 10.1 %all_to_all.32.arrived = f32[8,40,128]{2,1,0:T(8,128)S(1)} all-to-all(f32[8,40,128]{2,1,0:T(8,128)S(1)} %get-tuple-element.62), channel_id=1, replica_groups=mesh['grp'=8,'sub'=8,'chip'=2] {'grp'}, dimensions={0} | all-to-all | bytes 327680 | tf_op jit(solution)/shard_map/all_to_all | solution.py:733
  120.3 1.4 correct_part.3
  122.5 6.5 %second_part.1 = (f32[2,32,64,128]{3,2,1,0:T(8,128)S(1)}, f32[2,32,64,128]{3,2,1,0:T(8,128)S(1)}, f32[128,2,128]{2,1,0:T(2,128)S(1)}) custom-call(s32[64]{0:T(128)S(1)} %pad_add_fusion.perm, s32[1]{0:T(128)} %bitcast.5.member, f32[16,64,64]{2,1,0:T(8,128)S(1)} %get-tuple-element.65.e, f32[8,128]{1,0:T(8,128)S(1)} %get-tuple-element.64.dots, ...), custom_call_target="tpu_custom_call" | custom-call | tf_op jit(solution)/shard_map/second_part/pallas_call | solution.py:651
  128.9 14.1 %all_to_all.33.arrived = f32[128,2,128]{2,1,0:T(2,128)S(1)} all-to-all(f32[128,2,128]{2,1,0:T(2,128)S(1)} %get-tuple-element.69), channel_id=1, replica_groups=mesh['grp'=8,'sub'=8,'chip'=2] {'grp','sub','chip'}, dimensions={0} | all-to-all | bytes 262144 | tf_op jit(solution)/shard_map/all_to_all | solution.py:733
  143.1 4.5 %combine.1 = (f32[64,8192]{1,0:T(8,128)}, f32[64,8192]{1,0:T(8,128)}) custom-call(s32[64]{0:T(128)S(1)} %pad_add_fusion.perm, f32[8,128]{1,0:T(8,128)S(1)} %get-tuple-element.64.dots, f32[128,2,128]{2,1,0:T(2,128)S(1)} %all_to_all.33.arrived, f32[32,64,128]{2,1,0:T(8,128)S(1)} %copy-done.7, f32[32,64,128]{2,1,0:T(8,128)S(1)} %copy-done.8, ...), custom_call_target="tpu_custom_call" | custom-call | tf_op jit(solution)/shard_map/combine/pallas_call | solution.py:723
  (48 shorter events, 2.9 us)
Async XLA Ops:
  0.6 27.0 %copy-start = (f32[512,512]{1,0:T(8,128)S(1)}, f32[512,512]{1,0:T(8,128)}, u32[]{:S(2)}) copy-start(f32[512,512]{1,0:T(8,128)} %param.17) | copy-start | bytes 3145732
  0.6 0.8 copy-start.19
  5.9 8.5 %copy-start.20 = (s32[1,16,2]{1,2,0:T(2,128)S(1)}, s32[1,16,2]{1,2,0:T(2,128)}, u32[]{:S(2)}) copy-start(s32[1,16,2]{1,2,0:T(2,128)} %param.13) | copy-start | bytes 388
  5.9 8.7 %copy-start.18 = (s32[1024]{0:T(1024)S(1)}, s32[1024]{0:T(1024)}, u32[]{:S(2)}) copy-start(s32[1024]{0:T(1024)} %param.15) | copy-start | bytes 12292
  5.9 40.1 %all-to-all-start = ((f32[16,272,128]{2,1,0:T(8,128)}), f32[16,272,128]{2,1,0:T(8,128)}, u32[]{:S(2)}, u32[]{:S(2)}) async-start(f32[16,272,128]{2,1,0:T(8,128)} %bitcast.20), calls=%async_computation | async-start | bytes 4456448 | tf_op jit(solution)/shard_map/all_to_all | solution.py:733
  14.6 2.2 %copy-start.1 = (f32[1,1024,1024]{2,1,0:T(8,128)S(1)}, f32[1,1024,1024]{2,1,0:T(8,128)}, u32[]{:S(2)}) copy-start(f32[1,1024,1024]{2,1,0:T(8,128)} %param.16) | copy-start | bytes 12582916
  16.8 1.4 copy-start.12
  16.8 1.4 copy-start.21
  49.2 14.2 %all-to-all-start.1 = ((f32[16,40,128]{2,1,0:T(8,128)}), f32[16,40,128]{2,1,0:T(8,128)}, u32[]{:S(2)}, u32[]{:S(2)}) async-start(f32[16,40,128]{2,1,0:T(8,128)} %first_restrict.1), calls=%async_computation.1 | async-start | bytes 655360 | tf_op jit(solution)/shard_map/all_to_all | solution.py:733
  55.1 26.5 %copy-start.7 = (f32[32,64,128]{2,1,0:T(8,128)S(1)}, f32[32,64,128]{2,1,0:T(8,128)}, u32[]{:S(2)}) copy-start(f32[32,64,128]{2,1,0:T(8,128)} %get-tuple-element.50.b_slot) | copy-start | bytes 3145732
  55.2 26.5 %copy-start.8 = (f32[32,64,128]{2,1,0:T(8,128)S(1)}, f32[32,64,128]{2,1,0:T(8,128)}, u32[]{:S(2)}) copy-start(f32[32,64,128]{2,1,0:T(8,128)} %get-tuple-element.51.b_rest) | copy-start | bytes 3145732
  77.5 2.2 %copy-start.2 = (f32[1,1024,1024]{2,1,0:T(8,128)S(1)}, f32[1,1024,1024]{2,1,0:T(8,128)}, u32[]{:S(2)}) copy-start(f32[1,1024,1024]{2,1,0:T(8,128)} %param.16) | copy-start | bytes 12582916
  79.7 2.2 %copy-start.4 = (bf16[32,256,256]{2,1,0:T(8,128)(2,1)S(1)}, bf16[32,256,256]{2,1,0:T(8,128)(2,1)}, u32[]{:S(2)}) copy-start(bf16[32,256,256]{2,1,0:T(8,128)(2,1)} %get-tuple-element.57.hi_pair) | copy-start | bytes 12582916
  79.7 2.2 %copy-start.13 = (s32[8192]{0:T(1024)S(1)}, s32[8192]{0:T(1024)}, u32[]{:S(2)}) copy-start(s32[8192]{0:T(1024)} %param.14) | copy-start | bytes 98308
  79.7 2.2 %copy-start.14 = (f32[32,1,128]{2,1,0:T(1,128)S(1)}, f32[32,1,128]{2,1,0:T(1,128)}, u32[]{:S(2)}) copy-start(f32[32,1,128]{2,1,0:T(1,128)} %get-tuple-element.52.d_slot) | copy-start | bytes 49156
  79.7 2.2 %copy-start.15 = (f32[32,1,128]{2,1,0:T(1,128)S(1)}, f32[32,1,128]{2,1,0:T(1,128)}, u32[]{:S(2)}) copy-start(f32[32,1,128]{2,1,0:T(1,128)} %get-tuple-element.53.d_rest) | copy-start | bytes 49156
  79.7 2.2 %copy-start.16 = (f32[32,1,128]{2,1,0:T(1,128)S(1)}, f32[32,1,128]{2,1,0:T(1,128)}, u32[]{:S(2)}) copy-start(f32[32,1,128]{2,1,0:T(1,128)} %get-tuple-element.55.d_peer) | copy-start | bytes 49156
  79.8 2.2 %copy-start.17 = (s32[32,1,128]{2,1,0:T(1,128)S(1)}, s32[32,1,128]{2,1,0:T(1,128)}, u32[]{:S(2)}) copy-start(s32[32,1,128]{2,1,0:T(1,128)} %get-tuple-element.56.m_peer) | copy-start | bytes 49156
  81.9 2.2 %copy-start.5 = (bf16[32,256,256]{2,1,0:T(8,128)(2,1)S(1)}, bf16[32,256,256]{2,1,0:T(8,128)(2,1)}, u32[]{:S(2)}) copy-start(bf16[32,256,256]{2,1,0:T(8,128)(2,1)} %get-tuple-element.58.lo_pair) | copy-start | bytes 12582916
  84.1 1.2 copy-start.9
  85.4 1.2 copy-start.10
  86.6 1.2 copy-start.11
  87.8 32.5 %copy-start.3 = (f32[1,1024,1024]{2,1,0:T(8,128)S(1)}, f32[1,1024,1024]{2,1,0:T(8,128)}, u32[]{:S(2)}) copy-start(f32[1,1024,1024]{2,1,0:T(8,128)} %param.16) | copy-start | bytes 12582916
  120.3 2.2 %copy-start.6 = (bf16[32,256,256]{2,1,0:T(8,128)(2,1)S(1)}, bf16[32,256,256]{2,1,0:T(8,128)(2,1)}, u32[]{:S(2)}) copy-start(bf16[32,256,256]{2,1,0:T(8,128)(2,1)} %get-tuple-element.58.lo_pair) | copy-start | bytes 12582916

commit v7 on v6

--- a/solution.py
+++ b/solution.py
@@ -36,6 +36,10 @@
 
 def hbm(x):
     return pltpu.with_memory_space_constraint(x, pltpu.HBM)
+
+
+def near(shape, dtype=F32):
+    return pltpu.VMEM(shape, dtype)
 
 
 def far(shape, dtype=F32):
@@ -423,11 +427,17 @@
             jax.ShapeDtypeStruct((GROUPS, ROWS, TILE), F32),
         ],
         compiler_params=params(),
+        cost_estimate=cost(20_000_000_000, 32 << 20),
         name="lowest_part",
     )(arrived, g)
 
 
-def correct_kernel(arrived, inverse_rows, g, x_ref, inverse_ref, op, e_out, dots):
+def level_one(arrived, inverse_rows, g, x_ref, inverse_ref, op, e_out):
+    low = gathered_rows(arrived, GROUPS)
+    hi, lo = split2(inverse_rows[...])
+    corr = mm(low, hi, lo, nt=True)
+    ghi, glo = split2(g[...])
+    lifted = mm(corr, ghi, glo)
     inverse = inverse_ref[...]
     scaled = x_ref[...] * inverse
     total = None
@@ -436,26 +446,9 @@
         hi, lo = split2(op[rows, :])
         term = mm(scaled[:, rows], hi, lo)
         total = term if total is None else total + term
-    low = gathered_rows(arrived, GROUPS)
-    hi, lo = split2(inverse_rows[...])
-    corr = mm(low, hi, lo, nt=True)
-    ghi, glo = split2(g[...])
-    e = 2.0 * OMEGA * scaled - OMEGA * OMEGA * total * inverse + mm(corr, ghi, glo)
+    e = 2.0 * OMEGA * scaled - OMEGA * OMEGA * total * inverse + lifted
     for q in range(PEERS):
         e_out[q] = e[:, q * AGG : (q + 1) * AGG]
-    extra = arrived[0, 32:40]
-    for q in range(1, GROUPS):
-        extra = extra + arrived[q, 32:40]
-    dots[...] = extra
-
-
-def correct_part(arrived, inverse_rows, g, x, inverse, op):
-    return pl.pallas_call(
-        correct_kernel,
-        out_shape=[jax.ShapeDtypeStruct((PEERS, COLS, AGG), F32), jax.ShapeDtypeStruct((8, TILE), F32)],
-        compiler_params=params(),
-        name="correct_part",
-    )(arrived, inverse_rows, g, x, inverse, op)
 
 
 def apply_off(x, hi, lo):
@@ -489,9 +482,10 @@
 
 
 def forward_kernel(
-    perm, member, e, b_slot, b_rest, d_slot, d_rest, x_peer, d_peer, m_peer, hi_pair, lo_pair,
-    hi_rest, lo_rest, maps, z_out, w_out, ws_out, out, acc_rr, acc_bz, acc_zw
+    perm, member, arrived, inverse_rows, g, x, inverse, op, b_slot, b_rest, d_slot, d_rest, x_peer, d_peer, m_peer,
+    hi_pair, lo_pair, hi_rest, lo_rest, maps, z_out, w_out, ws_out, out, e, acc_rr, acc_bz, acc_zw
 ):
+    level_one(arrived, inverse_rows, g, x, inverse, op, e)
     acc_rr[...] = jnp.zeros_like(acc_rr)
     acc_bz[...] = jnp.zeros_like(acc_bz)
     acc_zw[...] = jnp.zeros_like(acc_zw)
@@ -558,31 +552,41 @@
     acc_zw[...] = zw
 
 
-def in_vmem(count):
-    return [pl.BlockSpec(memory_space=pltpu.SMEM)] * 2 + [pl.BlockSpec(memory_space=pltpu.VMEM)] * count
-
-
-def forward_part(perm, member, *arrays):
+def specs(smem, vmem):
+    return [pl.BlockSpec(memory_space=pltpu.SMEM)] * smem + [pl.BlockSpec(memory_space=pltpu.VMEM)] * vmem
+
+
+def forward_part(scalars, arrays):
     return pl.pallas_call(
         forward_kernel,
-        in_specs=in_vmem(len(arrays)),
-        out_specs=[pl.BlockSpec(memory_space=pltpu.VMEM)] * 4,
+        in_specs=specs(len(scalars), len(arrays)),
+        out_specs=specs(0, 4),
         out_shape=[
-            jax.ShapeDtypeStruct((2, SLOTS, COLS, TILE), F32),
-            jax.ShapeDtypeStruct((2, SLOTS, COLS, TILE), F32),
-            jax.ShapeDtypeStruct((SLOTS, COLS, TILE), F32),
+            near((2, SLOTS, COLS, TILE)),
+            near((2, SLOTS, COLS, TILE)),
+            near((SLOTS, COLS, TILE)),
             jax.ShapeDtypeStruct((PEERS, ROWS, TILE), F32),
         ],
-        scratch_shapes=[pltpu.VMEM((COLS, AGG), F32), pltpu.VMEM((COLS, TILE), F32), pltpu.VMEM((COLS, TILE), F32)],
+        scratch_shapes=[
+            pltpu.VMEM((PEERS, COLS, AGG), F32),
+            pltpu.VMEM((COLS, AGG), F32),
+            pltpu.VMEM((COLS, TILE), F32),
+            pltpu.VMEM((COLS, TILE), F32),
+        ],
         compiler_params=params(),
         name="forward_part",
-    )(perm, member, *arrays)
+    )(*scalars, *arrays)
 
 
 def second_kernel(
-    perm, member, e, dots, b_slot, b_rest, d_slot, d_rest, d_peer, m_peer, hi_pair, lo_pair,
-    hi_rest, lo_rest, maps, z_in, w_in, w_peer, v_out, u_out, out, acc_a, acc_b, acc_c, acc_alpha
+    perm, member, arrived, inverse_rows, g, x, inverse, op, b_slot, b_rest, d_slot, d_rest, d_peer, m_peer, hi_pair, lo_pair,
+    hi_rest, lo_rest, maps, z_in, w_in, w_peer, v_out, u_out, out, dots, e, acc_a, acc_b, acc_c, acc_alpha
 ):
+    extra = arrived[0, 32:40]
+    for q in range(1, GROUPS):
+        extra = extra + arrived[q, 32:40]
+    dots[...] = extra
+    level_one(arrived, inverse_rows, g, x, inverse, op, e)
     acc_a[...] = jnp.zeros_like(acc_a)
     acc_b[...] = jnp.zeros_like(acc_b)
     acc_c[...] = jnp.zeros_like(acc_c)
@@ -647,20 +651,21 @@
     acc_c[...] = sums[2]
 
 
-def second_part(perm, member, *arrays):
+def second_part(scalars, arrays):
     return pl.pallas_call(
         second_kernel,
-        in_specs=in_vmem(len(arrays)),
-        out_specs=[pl.BlockSpec(memory_space=pltpu.VMEM)] * 3,
+        in_specs=specs(len(scalars), len(arrays)),
+        out_specs=specs(0, 4),
         out_shape=[
-            jax.ShapeDtypeStruct((2, SLOTS, COLS, TILE), F32),
-            jax.ShapeDtypeStruct((2, SLOTS, COLS, TILE), F32),
+            near((2, SLOTS, COLS, TILE)),
+            near((2, SLOTS, COLS, TILE)),
             jax.ShapeDtypeStruct((GROUPS * PEERS, 2, TILE), F32),
-        ],
-        scratch_shapes=[pltpu.VMEM((COLS, TILE), F32)] * 4,
+            jax.ShapeDtypeStruct((8, TILE), F32),
+        ],
+        scratch_shapes=[pltpu.VMEM((PEERS, COLS, AGG), F32)] + [pltpu.VMEM((COLS, TILE), F32)] * 4,
         compiler_params=params(),
         name="second_part",
-    )(perm, member, *arrays)
+    )(*scalars, *arrays)
 
 
 def combine_kernel(perm, dots, arrived, b_slot, b_rest, z, w, v, u, solution, residual, coef):
@@ -768,23 +773,21 @@
     g, inverse = coarse_setup(operator, coarse_map.reshape(1, NC1))
     inverse_rows = lax.dynamic_slice_in_dim(coarsest_inverse, group * AGG, AGG, 0)
 
-    def level_one(arrived):
-        x, outgoing = lowest_part(arrived, g)
-        lows = exchange(outgoing, "grp")
-        return correct_part(lows, inverse_rows, g, x, inverse, operator)
-
     rr_local, g, inverse_rows, member = lax.optimization_barrier((rr_local, g, inverse_rows, member))
     gathered = exchange(first_restrict(side, rs, rr_local), GROUP_AXES)
     hi_pair, lo_pair, d_peer, m_peer, x_peer = pair_setup(perm, counts, diag_tiles, side, remote)
     gathered, hi_pair = lax.optimization_barrier((gathered, hi_pair))
-    e, _ = level_one(gathered)
+
+    scalars = (perm, member)
+    x, outgoing = lowest_part(gathered, g)
+    coarse = (exchange(outgoing, "grp"), inverse_rows, g, x, inverse)
+    fixed = (d_slot, d_rest, d_peer, m_peer, hi_pair, lo_pair, hi_rest, lo_rest, maps)
     z, w, w_peer, outgoing = forward_part(
-        perm, member, e, b_slot, b_rest, d_slot, d_rest, x_peer, d_peer, m_peer, hi_pair, lo_pair, hi_rest, lo_rest, maps
+        scalars, coarse + (operator, b_slot, b_rest, d_slot, d_rest, x_peer) + fixed[2:]
     )
-    e, dots = level_one(exchange(outgoing, GROUP_AXES))
-    v, u, outgoing = second_part(
-        perm, member, e, dots, b_slot, b_rest, d_slot, d_rest, d_peer, m_peer, hi_pair, lo_pair, hi_rest, lo_rest, maps, z, w, w_peer
-    )
+    x, outgoing = lowest_part(exchange(outgoing, GROUP_AXES), g)
+    coarse = (exchange(outgoing, "grp"), inverse_rows, g, x, inverse)
+    v, u, outgoing, dots = second_part(scalars, coarse + (operator, b_slot, b_rest) + fixed + (z, w, w_peer))
     sums = exchange(outgoing, ALL_AXES)
     return tuple(combine(perm, dots, sums, b_slot, b_rest, z, w, v, u))
 

time: 148 us -> 139 us (0.939)
  local copies, waits for them, and re-layouts: 12.4 us -> 3.22 us
    unnamed x45 -> x39, local copies, waits for them, and re-layouts: 12.3 us -> 3.11 us
    pallas_call x4 -> x2, Pallas kernels: 17.6 us -> 17.7 us  [the longest x1 9.54 us: forward_part(): pl.pallas_call(forward_kernel, in_specs=specs(len(scalars), len(arrays)),...]
  transfers between devices with their start and end apart: 2 -> 2, of which waited for: 1 -> 1; matrix products, arithmetic and copies ran while one was open for 0% -> 0% of each run, Pallas kernels for 13% -> 14%
where the time goes in v7:
time: 139 us; the launch traced here: 138 us
  blocking collectives  51.3 us (37%)
  Pallas kernels  49.2 us (35%)
  waiting for transfers between devices  18.3 us (13%)
  starting transfers between devices  14.5 us (10%)
  local copies, waits for them, and re-layouts  3.22 us (2%)
    all_to_all x4, blocking collectives, exchange(): return lax.all_to_all(x, axes, 0, 0, tiled=True)  51.3 us
    all_to_all x2, waiting for transfers between devices, exchange(): return lax.all_to_all(x, axes, 0, 0, tiled=True)  18.3 us
    all_to_all x2, starting transfers between devices, exchange(): return lax.all_to_all(x, axes, 0, 0, tiled=True)  14.5 us
    pallas_call x1, Pallas kernels, forward_part(): pl.pallas_call(forward_kernel, in_specs=specs(len(scalars), len(arrays)),...  9.54 us
    pallas_call x1, Pallas kernels, local_part(): pl.pallas_call(local_kernel, grid_spec=grid, out_shape=[sds((COLS, TILE))...  9.39 us
    pallas_call x1, Pallas kernels, pair_setup(): pl.pallas_call(pair_kernel, grid_spec=grid, out_shape=[far((SLOTS, 2 * TI...  8.19 us
    pallas_call x1, Pallas kernels, second_part(): pl.pallas_call(second_kernel, in_specs=specs(len(scalars), len(arrays)),...  8.16 us
    pallas_call x1, Pallas kernels, combine(): pl.pallas_call(combine_kernel, grid_spec=grid, out_shape=[jax.ShapeDtypeS...  4.51 us
  transfers between devices with their start and end apart: 2, of which 1 were waited for; matrix products, arithmetic and copies ran while one was open for 0% of the time, Pallas kernels for 14%

profile of v7, /device:TPU:1, one launch (start us, length us, event | category | flops | bytes accessed | tf_op | source)
XLA Modules:
  0.0 137.9 jit_solution(16515876107034996223)
XLA Ops:
  0.7 0.8 copy-done.16
  1.4 4.5 %boundary_pack.1 = f32[32,136,128]{2,1,0:T(8,128)} custom-call(s32[1,2,16]{2,1,0:T(2,128)S(1)} %bitcast.17, s32[64,128]{1,0:T(8,128)} %bitcast.12, f32[64,128,128]{2,1,0:T(8,128)} %refs_7_.3, f32[64,8192]{1,0:T(8,128)} %cols.1), custom_call_target="tpu_custom_call" | custom-call | tf_op jit(solution)/shard_map/boundary_pack/pallas_call | solution.py:156
  6.0 8.5 %all-to-all-start = ((f32[16,272,128]{2,1,0:T(8,128)}), f32[16,272,128]{2,1,0:T(8,128)}, u32[]{:S(2)}, u32[]{:S(2)}) async-start(f32[16,272,128]{2,1,0:T(8,128)} %bitcast.20), calls=%async_computation | async-start | bytes 4456448 | tf_op jit(solution)/shard_map/all_to_all | solution.py:738
  14.5 0.1 copy.13
  14.5 0.1 reshape.38
  14.7 2.2 %copy-done.1 = f32[1,1024,1024]{2,1,0:T(8,128)S(1)} copy-done((f32[1,1024,1024]{2,1,0:T(8,128)S(1)}, f32[1,1024,1024]{2,1,0:T(8,128)}, u32[]{:S(2)}) %copy-start.1) | copy-done | bytes 4194328
  16.8 1.0 coarse_setup.1
  17.9 0.1 fusion
  18.0 0.1 select_reduce_fusion
  18.1 0.1 select_reduce_fusion.1
  18.3 9.4 %local_part.1 = (f32[32,64,128]{2,1,0:T(8,128)}, f32[32,64,128]{2,1,0:T(8,128)}, f32[32,1,128]{2,1,0:T(1,128)}, f32[32,1,128]{2,1,0:T(1,128)}, bf16[32,128,128]{...) custom-call(s32[64]{0:T(128)S(1)} %pad_add_fusion.perm, ...), custom_call_target="tpu_custom_call" | custom-call | flops 402653184 | bytes 16777216 | tf_op jit(solution)/shard_map/local_part/pallas_call | solution.py:252
  27.7 18.3 %all-to-all-done = f32[16,272,128]{2,1,0:T(8,128)} async-done(((f32[16,272,128]{2,1,0:T(8,128)}), f32[16,272,128]{2,1,0:T(8,128)}, u32[]{:S(2)}, u32[]{:S(2)}) %all-to-all-start) | async-done | bytes 2228256 | tf_op jit(solution)/shard_map/all_to_all | solution.py:738
  46.0 3.1 %first_restrict.1 = f32[16,40,128]{2,1,0:T(8,128)} custom-call(f32[32,136,128]{2,1,0:T(8,128)} %bitcast.8.arrived.refs_8_, f32[32,64,128]{2,1,0:T(8,128)} %get-tuple-element.38.rs, f32[64,64]{1,0:T(8,128)S(1)} %get-tuple-element.39.rr), custom_call_target="tpu_custom_call" | custom-call | tf_op jit(solution)/shard_map/first_restrict/pallas_call | solution.py:328
  49.1 6.0 %all-to-all-start.1 = ((f32[16,40,128]{2,1,0:T(8,128)}), f32[16,40,128]{2,1,0:T(8,128)S(1)}, u32[]{:S(2)}, u32[]{:S(2)}) async-start(f32[16,40,128]{2,1,0:T(8,128)} %first_restrict.1), calls=%async_computation.1 | async-start | bytes 655360 | tf_op jit(solution)/shard_map/all_to_all | solution.py:738
  55.1 8.2 %pair_setup.1 = (bf16[32,256,256]{2,1,0:T(8,128)(2,1)}, bf16[32,256,256]{2,1,0:T(8,128)(2,1)}, f32[32,1,128]{2,1,0:T(1,128)}, s32[32,1,128]{2,1,0:T(1,128)}, f32[32,64,128]{2,1,0:T(8,128)}) custom-call(s32[64]{0:T(128)S(1)} %pad_add_fusion.perm, s32[16]{0:T(128)S(1)} %bitcast.19, f32[64,128,128]{2,1,0:T(8,128)} %refs_7_.3, f32[64,128,128]{2,1,0:T(8,128)} %refs_7_.3, ...), custom_call_target="tpu_custom_call" | custom-call | flops 402653184 | bytes 16777216 | tf_op jit(solution)/shard_map/pair_setup/pallas_call | solution.py:383
  63.5 0.4 lowest_part.2
  63.9 13.0 %all_to_all.30.arrived = f32[8,40,128]{2,1,0:T(8,128)S(1)} all-to-all(f32[8,40,128]{2,1,0:T(8,128)S(1)} %get-tuple-element.43), channel_id=1, replica_groups=mesh['grp'=8,'sub'=8,'chip'=2] {'grp'}, dimensions={0} | all-to-all | bytes 327680 | tf_op jit(solution)/shard_map/all_to_all | solution.py:738
  76.9 9.5 %forward_part.1 = (f32[2,32,64,128]{3,2,1,0:T(8,128)S(1)}, f32[2,32,64,128]{3,2,1,0:T(8,128)S(1)}, f32[32,64,128]{2,1,0:T(8,128)S(1)}, f32[16,40,128]{2,1,0:T(8,128)S(1)}) custom-call(s32[64]{0:T(128)S(1)} %pad_add_fusion.perm, s32[1]{0:T(128)} %bitcast.5.member, f32[8,40,128]{2,1,0:T(8,128)S(1)} %all_to_all.30.arrived, ...), custom_call_target="tpu_custom_call" | custom-call | tf_op jit(solution)/shard_map/forward_part/pallas_call | solution.py:560
  86.5 14.1 %all_to_all.31.arrived = f32[16,40,128]{2,1,0:T(8,128)S(1)} all-to-all(f32[16,40,128]{2,1,0:T(8,128)S(1)} %get-tuple-element.58), channel_id=1, replica_groups=mesh['grp'=8,'sub'=8,'chip'=2] {'sub','chip'}, dimensions={0} | all-to-all | bytes 655360 | tf_op jit(solution)/shard_map/all_to_all | solution.py:738
  100.6 0.4 lowest_part.3
  101.0 10.1 %all_to_all.32.arrived = f32[8,40,128]{2,1,0:T(8,128)S(1)} all-to-all(f32[8,40,128]{2,1,0:T(8,128)S(1)} %get-tuple-element.59), channel_id=1, replica_groups=mesh['grp'=8,'sub'=8,'chip'=2] {'grp'}, dimensions={0} | all-to-all | bytes 327680 | tf_op jit(solution)/shard_map/all_to_all | solution.py:738
  111.1 8.2 %second_part.1 = (f32[2,32,64,128]{3,2,1,0:T(8,128)S(1)}, f32[2,32,64,128]{3,2,1,0:T(8,128)S(1)}, f32[128,2,128]{2,1,0:T(2,128)S(1)}, f32[8,128]{1,0:T(8,128)S(1)}) custom-call(s32[64]{0:T(128)S(1)} %pad_add_fusion.perm, s32[1]{0:T(128)} %bitcast.5.member, f32[8,40,128]{2,1,0:T(8,128)S(1)} %all_to_all.32.arrived, ...), custom_call_target="tpu_custom_call" | custom-call | tf_op jit(solution)/shard_map/second_part/pallas_call | solution.py:655
  119.3 14.1 %all_to_all.33.arrived = f32[128,2,128]{2,1,0:T(2,128)S(1)} all-to-all(f32[128,2,128]{2,1,0:T(2,128)S(1)} %get-tuple-element.65), channel_id=1, replica_groups=mesh['grp'=8,'sub'=8,'chip'=2] {'grp','sub','chip'}, dimensions={0} | all-to-all | bytes 262144 | tf_op jit(solution)/shard_map/all_to_all | solution.py:738
  133.4 4.5 %combine.1 = (f32[64,8192]{1,0:T(8,128)}, f32[64,8192]{1,0:T(8,128)}) custom-call(s32[64]{0:T(128)S(1)} %pad_add_fusion.perm, f32[8,128]{1,0:T(8,128)S(1)} %get-tuple-element.64.dots, f32[128,2,128]{2,1,0:T(2,128)S(1)} %all_to_all.33.arrived, f32[32,64,128]{2,1,0:T(8,128)S(1)} %copy-done.5, f32[32,64,128]{2,1,0:T(8,128)S(1)} %copy-done.6, ...), custom_call_target="tpu_custom_call" | custom-call | tf_op jit(solution)/shard_map/combine/pallas_call | solution.py:728
  (40 shorter events, 0.2 us)
Async XLA Ops:
  0.6 27.1 %copy-start = (f32[512,512]{1,0:T(8,128)S(1)}, f32[512,512]{1,0:T(8,128)}, u32[]{:S(2)}) copy-start(f32[512,512]{1,0:T(8,128)} %param.17) | copy-start | bytes 3145732
  0.6 0.8 copy-start.16
  5.9 8.5 %copy-start.17 = (s32[1,16,2]{1,2,0:T(2,128)S(1)}, s32[1,16,2]{1,2,0:T(2,128)}, u32[]{:S(2)}) copy-start(s32[1,16,2]{1,2,0:T(2,128)} %param.13) | copy-start | bytes 388
  5.9 8.7 %copy-start.15 = (s32[1024]{0:T(1024)S(1)}, s32[1024]{0:T(1024)}, u32[]{:S(2)}) copy-start(s32[1024]{0:T(1024)} %param.15) | copy-start | bytes 12292
  6.0 40.1 %all-to-all-start = ((f32[16,272,128]{2,1,0:T(8,128)}), f32[16,272,128]{2,1,0:T(8,128)}, u32[]{:S(2)}, u32[]{:S(2)}) async-start(f32[16,272,128]{2,1,0:T(8,128)} %bitcast.20), calls=%async_computation | async-start | bytes 4456448 | tf_op jit(solution)/shard_map/all_to_all | solution.py:738
  14.6 2.2 %copy-start.1 = (f32[1,1024,1024]{2,1,0:T(8,128)S(1)}, f32[1,1024,1024]{2,1,0:T(8,128)}, u32[]{:S(2)}) copy-start(f32[1,1024,1024]{2,1,0:T(8,128)} %param.16) | copy-start | bytes 12582916
  16.8 1.5 %copy-start.10 = (s32[8192]{0:T(1024)S(1)}, s32[8192]{0:T(1024)}, u32[]{:S(2)}) copy-start(s32[8192]{0:T(1024)} %param.14) | copy-start | bytes 98308
  16.8 1.5 %copy-start.18 = (s32[1,16]{1,0:T(1,128)S(1)}, s32[1,16]{1,0:T(1,128)}, u32[]{:S(2)}) copy-start(s32[1,16]{1,0:T(1,128)} %param.12) | copy-start | bytes 196
  49.1 14.2 %all-to-all-start.1 = ((f32[16,40,128]{2,1,0:T(8,128)}), f32[16,40,128]{2,1,0:T(8,128)S(1)}, u32[]{:S(2)}, u32[]{:S(2)}) async-start(f32[16,40,128]{2,1,0:T(8,128)} %first_restrict.1), calls=%async_computation.1 | async-start | bytes 655360 | tf_op jit(solution)/shard_map/all_to_all | solution.py:738
  63.3 13.5 %copy-start.2 = (f32[1,1024,1024]{2,1,0:T(8,128)S(1)}, f32[1,1024,1024]{2,1,0:T(8,128)}, u32[]{:S(2)}) copy-start(f32[1,1024,1024]{2,1,0:T(8,128)} %param.16) | copy-start | bytes 12582916
  63.3 13.5 %copy-start.3 = (bf16[32,256,256]{2,1,0:T(8,128)(2,1)S(1)}, bf16[32,256,256]{2,1,0:T(8,128)(2,1)}, u32[]{:S(2)}) copy-start(bf16[32,256,256]{2,1,0:T(8,128)(2,1)} %get-tuple-element.54.hi_pair) | copy-start | bytes 12582916
  63.4 13.5 %copy-start.4 = (bf16[32,256,256]{2,1,0:T(8,128)(2,1)S(1)}, bf16[32,256,256]{2,1,0:T(8,128)(2,1)}, u32[]{:S(2)}) copy-start(bf16[32,256,256]{2,1,0:T(8,128)(2,1)} %get-tuple-element.55.lo_pair) | copy-start | bytes 12582916
  63.4 13.5 %copy-start.5 = (f32[32,64,128]{2,1,0:T(8,128)S(1)}, f32[32,64,128]{2,1,0:T(8,128)}, u32[]{:S(2)}) copy-start(f32[32,64,128]{2,1,0:T(8,128)} %get-tuple-element.47.b_slot) | copy-start | bytes 3145732
  63.4 13.5 %copy-start.6 = (f32[32,64,128]{2,1,0:T(8,128)S(1)}, f32[32,64,128]{2,1,0:T(8,128)}, u32[]{:S(2)}) copy-start(f32[32,64,128]{2,1,0:T(8,128)} %get-tuple-element.48.b_rest) | copy-start | bytes 3145732
  63.4 13.5 %copy-start.7 = (bf16[32,128,128]{2,1,0:T(8,128)(2,1)S(1)}, bf16[32,128,128]{2,1,0:T(8,128)(2,1)}, u32[]{:S(2)}) copy-start(bf16[32,128,128]{2,1,0:T(8,128)(2,1)} %get-tuple-element.56.hi_rest) | copy-start | bytes 3145732
  63.4 13.5 %copy-start.8 = (bf16[32,128,128]{2,1,0:T(8,128)(2,1)S(1)}, bf16[32,128,128]{2,1,0:T(8,128)(2,1)}, u32[]{:S(2)}) copy-start(bf16[32,128,128]{2,1,0:T(8,128)(2,1)} %get-tuple-element.57.lo_rest) | copy-start | bytes 3145732
  63.4 13.5 %copy-start.9 = (f32[32,64,128]{2,1,0:T(8,128)S(1)}, f32[32,64,128]{2,1,0:T(8,128)}, u32[]{:S(2)}) copy-start(f32[32,64,128]{2,1,0:T(8,128)} %get-tuple-element.51.x_peer) | copy-start | bytes 3145732
  63.4 13.5 %copy-start.11 = (f32[32,1,128]{2,1,0:T(1,128)S(1)}, f32[32,1,128]{2,1,0:T(1,128)}, u32[]{:S(2)}) copy-start(f32[32,1,128]{2,1,0:T(1,128)} %get-tuple-element.49.d_slot) | copy-start | bytes 49156
  63.4 13.5 %copy-start.12 = (f32[32,1,128]{2,1,0:T(1,128)S(1)}, f32[32,1,128]{2,1,0:T(1,128)}, u32[]{:S(2)}) copy-start(f32[32,1,128]{2,1,0:T(1,128)} %get-tuple-element.50.d_rest) | copy-start | bytes 49156
  63.4 13.5 %copy-start.13 = (f32[32,1,128]{2,1,0:T(1,128)S(1)}, f32[32,1,128]{2,1,0:T(1,128)}, u32[]{:S(2)}) copy-start(f32[32,1,128]{2,1,0:T(1,128)} %get-tuple-element.52.d_peer) | copy-start | bytes 49156
  63.4 13.5 %copy-start.14 = (s32[32,1,128]{2,1,0:T(1,128)S(1)}, s32[32,1,128]{2,1,0:T(1,128)}, u32[]{:S(2)}) copy-start(s32[32,1,128]{2,1,0:T(1,128)} %get-tuple-element.53.m_peer) | copy-start | bytes 49156

commit v8 on v7

--- a/solution.py
+++ b/solution.py
@@ -22,16 +22,16 @@
 NSTEP = SLOTS // STEP
 CHUNK = 16
 CHUNKS = SLOTS // CHUNK
-SIDE = 136
+SIDE = 264
+PEER_STEP = 4
 ROWS = 40
-VMEM_LIMIT = 24 * 1024 * 1024
 
 GROUP_AXES = ("sub", "chip")
 ALL_AXES = ("grp", "sub", "chip")
 
 
-def params():
-    return pltpu.CompilerParams(vmem_limit_bytes=VMEM_LIMIT)
+def params(mib=20):
+    return pltpu.CompilerParams(vmem_limit_bytes=mib * 1024 * 1024)
 
 
 def hbm(x):
@@ -122,7 +122,7 @@
         return pltpu.make_async_copy(cols.at[:, at], col_buf.at[j], col_sem.at[j])
 
     def out_copy(j):
-        at = pl.ds(j, STEP)
+        at = pl.ds(j // 2, PEER_STEP)
         return pltpu.make_async_copy(out_buf.at[at], out.at[at], out_sem.at[j // STEP])
 
     map_copy = pltpu.make_async_copy(maps, map_buf, map_sem)
@@ -142,11 +142,16 @@
         diag = [tile_diag(t) for t in tile]
         for k in range(j, j + STEP):
             t, d = tile[k - j], diag[k - j]
-            out_buf[k, 0:64] = col_buf[k] * (OMEGA / d)
+            q, base = k // 2, (k % 2) * 128
+            out_buf[q, base : base + 64] = col_buf[k] * (OMEGA / d)
             below = pltpu.roll(t[64:], 64, 1)
-            out_buf[k, 64:128] = jnp.where((c < 64) & (r > c), below, t[:64])
-            row = map_buf[pl.ds(slots[0, k % 2, k // 2], 1)].astype(F32)
-            out_buf[k, 128:136] = jnp.where(r8 == 0, d, jnp.where(r8 == 1, row, 0.0))
+            out_buf[q, base + 64 : base + 128] = jnp.where((c < 64) & (r > c), below, t[:64])
+        for k in range(j, j + STEP, 2):
+            own = [map_buf[pl.ds(slots[0, i, k // 2], 1)].astype(F32) for i in range(2)]
+            d0, d1 = diag[k - j], diag[k - j + 1]
+            out_buf[k // 2, 256:264] = jnp.where(
+                r8 == 0, d0, jnp.where(r8 == 1, own[0], jnp.where(r8 == 2, d1, jnp.where(r8 == 3, own[1], 0.0)))
+            )
         out_copy(j).start()
     for j in range(0, SLOTS, STEP):
         out_copy(j).wait()
@@ -157,12 +162,12 @@
         boundary_kernel,
         in_specs=[pl.BlockSpec(memory_space=pltpu.SMEM)] + [pl.BlockSpec(memory_space=pl.ANY)] * 3,
         out_specs=pl.BlockSpec(memory_space=pl.ANY),
-        out_shape=far((SLOTS, SIDE, TILE)),
+        out_shape=far((PEERS, SIDE, TILE)),
         scratch_shapes=[
             pltpu.VMEM((BLK, TILE), jnp.int32),
             pltpu.VMEM((SLOTS, TILE, TILE), F32),
             pltpu.VMEM((SLOTS, COLS, TILE), F32),
-            pltpu.VMEM((SLOTS, SIDE, TILE), F32),
+            pltpu.VMEM((PEERS, SIDE, TILE), F32),
             pltpu.SemaphoreType.DMA,
             pltpu.SemaphoreType.DMA((SLOTS,)),
             pltpu.SemaphoreType.DMA((SLOTS,)),
@@ -177,7 +182,7 @@
     n = 2 * STEP
     tiles, cols = refs[:n], refs[n : 2 * n]
     remote, maps = refs[2 * n : 2 * n + 2]
-    b_slot, b_rest, d_slot, d_rest, hi_rest, lo_rest, rs, rr = refs[2 * n + 2 :]
+    b_slot, b_rest, d_slot, d_rest, hi_rest, lo_rest, hi_top, lo_top, hi_side, lo_side, rs, rr = refs[2 * n + 2 :]
     step = pl.program_id(0)
 
     @pl.when(step == 0)
@@ -201,13 +206,18 @@
         b_rest[k] = b[STEP + k]
         d_rest[k] = diag[STEP + k]
         hi_rest[k], lo_rest[k] = off[STEP + k]
-    scaled = []
+    coupling, turned = [], []
     for k in range(STEP):
         j = step * STEP + k
         live = (j % 2) < counts[j // 2]
-        scaled.append(split2(remote[k] * jnp.where(live, 1.0, 0.0)))
+        scaled = remote[k] * jnp.where(live, -1.0, 0.0)
+        coupling.append(split2(scaled))
+        turned.append(split2(scaled.T))
     for k in range(STEP):
-        rs[k] = dot_nt(spread[k], scaled[k][0]) + dot_nt(spread[k], scaled[k][1])
+        rs[k] = -(dot_nt(spread[k], coupling[k][0]) + dot_nt(spread[k], coupling[k][1]))
+        hi_top[k] = beside(off[k][0], turned[k][0])
+        lo_top[k] = beside(off[k][1], turned[k][1])
+        hi_side[k], lo_side[k] = coupling[k]
     rr[...] = total
 
 
@@ -239,6 +249,10 @@
             out(COLS, TILE),
             out(1, TILE),
             out(1, TILE),
+            out(TILE, TILE),
+            out(TILE, TILE),
+            out(TILE, 2 * TILE),
+            out(TILE, 2 * TILE),
             out(TILE, TILE),
             out(TILE, TILE),
             out(AGG, TILE),
@@ -259,6 +273,10 @@
             sds((1, TILE)),
             sds((TILE, TILE), BF16),
             sds((TILE, TILE), BF16),
+            sds((TILE, 2 * TILE), BF16),
+            sds((TILE, 2 * TILE), BF16),
+            sds((TILE, TILE), BF16),
+            sds((TILE, TILE), BF16),
             sds((AGG, TILE)),
             jax.ShapeDtypeStruct((COLS, AGG), F32),
         ],
@@ -268,9 +286,16 @@
     )(perm, counts, *([hbm(diag_tiles)] * n), *([hbm(right_side)] * n), hbm(remote), maps)
 
 
-def coarse_kernel(op, cmap, g_out, d_out):
+def coarse_kernel(op, cmap, g_out, d_out, hi_out, lo_out):
     spread = one_hot(cmap[...])
-    product = exact_spread(spread, op)
+    product = None
+    for i in range(NC1 // 256):
+        rows = slice(i * 256, (i + 1) * 256)
+        hi, lo = split2(op[rows, :])
+        hi_out[rows, :] = hi
+        lo_out[rows, :] = lo
+        term = dot(spread[:, rows], hi) + dot(spread[:, rows], lo)
+        product = term if product is None else product + term
     pieces = []
     for i in range(NC1 // TILE):
         pieces.append(tile_diag(op[i * TILE : (i + 1) * TILE, i * TILE : (i + 1) * TILE]))
@@ -280,20 +305,15 @@
     g_out[...] = spread.astype(F32) - OMEGA * product * inverse
 
 
-def exact_spread(spread, op):
-    total = None
-    for i in range(NC1 // 256):
-        rows = slice(i * 256, (i + 1) * 256)
-        hi, lo = split2(op[rows, :])
-        part = dot(spread[:, rows], hi) + dot(spread[:, rows], lo)
-        total = part if total is None else total + part
-    return total
-
-
 def coarse_setup(op, cmap):
     return pl.pallas_call(
         coarse_kernel,
-        out_shape=[jax.ShapeDtypeStruct((AGG, NC1), F32), jax.ShapeDtypeStruct((1, NC1), F32)],
+        out_shape=[
+            jax.ShapeDtypeStruct((AGG, NC1), F32),
+            jax.ShapeDtypeStruct((1, NC1), F32),
+            far((NC1, NC1), BF16),
+            far((NC1, NC1), BF16),
+        ],
         compiler_params=params(),
         cost_estimate=cost(2 * 2 * 64 * 1024 * 1024, 5 << 20),
         name="coarse_setup",
@@ -302,11 +322,11 @@
 
 def first_restrict_kernel(arrived, rs, rr, out, x_buf, rs_buf, x_sem, rs_sem):
     def copies(j):
-        at = pl.ds(j * STEP, STEP)
-        return (
-            pltpu.make_async_copy(arrived.at[at, pl.ds(0, COLS)], x_buf.at[at], x_sem.at[j]),
-            pltpu.make_async_copy(rs.at[at], rs_buf.at[at], rs_sem.at[j]),
-        )
+        peers, slots = pl.ds(j * PEER_STEP, PEER_STEP), pl.ds(j * STEP, STEP)
+        return [
+            pltpu.make_async_copy(arrived.at[peers, pl.ds(c * 128, COLS)], x_buf.at[c, peers], x_sem.at[c, j])
+            for c in range(2)
+        ] + [pltpu.make_async_copy(rs.at[slots], rs_buf.at[slots], rs_sem.at[j])]
 
     for j in range(NSTEP):
         for copy in copies(j):
@@ -315,13 +335,10 @@
     for j in range(NSTEP):
         for copy in copies(j):
             copy.wait()
-        for k in range(j * STEP, (j + 1) * STEP, 2):
-            hi, lo = split2(beside(rs_buf[k], rs_buf[k + 1]))
-            total = total + mm(beside(x_buf[k], x_buf[k + 1]), hi, lo, nt=True)
-    packed = pack_rows(total)
-    for q in range(PEERS):
-        out[q, 0:32] = packed
-        out[q, 32:40] = jnp.zeros((8, TILE), F32)
+        for q in range(j * PEER_STEP, (j + 1) * PEER_STEP):
+            hi, lo = split2(beside(rs_buf[2 * q], rs_buf[2 * q + 1]))
+            total = total + mm(beside(x_buf[0, q], x_buf[1, q]), hi, lo, nt=True)
+    out[...] = jnp.broadcast_to(pack_rows(total), out.shape)
 
 
 def first_restrict(arrived, rs, rr):
@@ -329,71 +346,55 @@
         first_restrict_kernel,
         in_specs=[pl.BlockSpec(memory_space=pl.ANY)] * 2 + [pl.BlockSpec(memory_space=pltpu.VMEM)],
         out_specs=pl.BlockSpec(memory_space=pltpu.VMEM),
-        out_shape=jax.ShapeDtypeStruct((PEERS, ROWS, TILE), F32),
+        out_shape=jax.ShapeDtypeStruct((PEERS, 32, TILE), F32),
         scratch_shapes=[
-            pltpu.VMEM((SLOTS, COLS, TILE), F32),
+            pltpu.VMEM((2, PEERS, COLS, TILE), F32),
             pltpu.VMEM((SLOTS, AGG, TILE), F32),
+            pltpu.SemaphoreType.DMA((2, NSTEP)),
             pltpu.SemaphoreType.DMA((NSTEP,)),
-            pltpu.SemaphoreType.DMA((NSTEP,)),
-        ],
-        compiler_params=params(),
+        ],
+        compiler_params=params(8),
         name="first_restrict",
     )(hbm(arrived), hbm(rs), rr)
 
 
-def pair_kernel(perm, counts, *refs):
-    tiles, side, remote, hi_out, lo_out, diag_out, map_out, x_out = (refs[:STEP],) + tuple(refs[STEP:])
-    step = pl.program_id(0)
+def pair_kernel(side0, side1, extra, hi_out, lo_out, diag_out, map_out):
     r = lax.broadcasted_iota(jnp.int32, (64, TILE), 0)
     c = lax.broadcasted_iota(jnp.int32, (64, TILE), 1)
     for k in range(STEP):
-        own = off_diag(tiles[k][0])
-        packed = side[k, 64:128]
+        packed = (side0, side1)[k % 2][k // 2]
         top = jnp.where((c >= 64) | (r < c), packed, 0.0)
         bottom = pltpu.roll(jnp.where((c < 64) & (r > c), packed, 0.0), 64, 1)
         half = jnp.concatenate([top, bottom], axis=0)
-        other = half + half.T
-        j = step * STEP + k
-        live = (j % 2) < counts[j // 2]
-        rem = remote[k] * jnp.where(live, -1.0, 0.0)
-        block = jnp.concatenate(
-            [jnp.concatenate([own, rem.T], axis=1), jnp.concatenate([rem, other], axis=1)], axis=0
-        )
-        hi, lo = split2(block)
-        hi_out[k] = hi
-        lo_out[k] = lo
-        x_out[k] = side[k, 0:64]
-        diag_out[k] = side[k, 128:129]
-        map_out[k] = side[k, 129:130].astype(jnp.int32)
-
-
-def pair_setup(perm, counts, diag_tiles, side, remote):
-    def tile_spec(i):
-        return pl.BlockSpec((1, TILE, TILE), lambda s, p, c: (p[s * STEP + i], 0, 0))
-
+        hi_out[k], lo_out[k] = split2(half + half.T)
+        at = 2 * (k % 2)
+        diag_out[k] = extra[k // 2, at : at + 1]
+        map_out[k] = extra[k // 2, at + 1 : at + 2].astype(jnp.int32)
+
+
+def pair_setup(side):
     def spec(*shape):
-        return pl.BlockSpec((STEP,) + shape, lambda s, p, c: (s, 0, 0))
-
-    grid = pltpu.PrefetchScalarGridSpec(
-        num_scalar_prefetch=2,
-        grid=(NSTEP,),
-        in_specs=[tile_spec(i) for i in range(STEP)] + [spec(SIDE, TILE), spec(TILE, TILE)],
-        out_specs=[spec(2 * TILE, 2 * TILE), spec(2 * TILE, 2 * TILE), spec(1, TILE), spec(1, TILE), spec(COLS, TILE)],
-    )
+        return pl.BlockSpec((STEP,) + shape, lambda s: (s, 0, 0))
+
     return pl.pallas_call(
         pair_kernel,
-        grid_spec=grid,
+        grid=(NSTEP,),
+        in_specs=[
+            pl.BlockSpec((PEER_STEP, 64, TILE), lambda s: (s, 1, 0)),
+            pl.BlockSpec((PEER_STEP, 64, TILE), lambda s: (s, 3, 0)),
+            pl.BlockSpec((PEER_STEP, 8, TILE), lambda s: (s, 32, 0)),
+        ],
+        out_specs=[spec(TILE, TILE), spec(TILE, TILE), spec(1, TILE), spec(1, TILE)],
         out_shape=[
-            far((SLOTS, 2 * TILE, 2 * TILE), BF16),
-            far((SLOTS, 2 * TILE, 2 * TILE), BF16),
+            far((SLOTS, TILE, TILE), BF16),
+            far((SLOTS, TILE, TILE), BF16),
             far((SLOTS, 1, TILE)),
             far((SLOTS, 1, TILE), jnp.int32),
-            far((SLOTS, COLS, TILE)),
         ],
         compiler_params=params(),
         cost_estimate=cost(2 * 64 * 3 * 64 * 128 * 128, 16 << 20),
         name="pair_setup",
-    )(perm, counts, *([hbm(diag_tiles)] * STEP), hbm(side), hbm(remote))
+    )(*([hbm(side)] * 3))
 
 
 def gathered_rows(ref, count):
@@ -411,12 +412,12 @@
     x_out[...] = x
     hi, lo = split2(g[...])
     packed = pack_rows(mm(x, hi, lo, nt=True))
-    extra = arrived[0, 32:40]
-    for q in range(1, PEERS):
-        extra = extra + arrived[q, 32:40]
-    for q in range(GROUPS):
-        out[q, 0:32] = packed
-        out[q, 32:40] = extra
+    if arrived.shape[1] == ROWS:
+        extra = arrived[0, 32:40]
+        for q in range(1, PEERS):
+            extra = extra + arrived[q, 32:40]
+        packed = jnp.concatenate([packed, extra], axis=0)
+    out[...] = jnp.broadcast_to(packed, out.shape)
 
 
 def lowest_part(arrived, g):
@@ -424,15 +425,15 @@
         lowest_kernel,
         out_shape=[
             jax.ShapeDtypeStruct((COLS, NC1), F32),
-            jax.ShapeDtypeStruct((GROUPS, ROWS, TILE), F32),
-        ],
-        compiler_params=params(),
+            jax.ShapeDtypeStruct((GROUPS, arrived.shape[1], TILE), F32),
+        ],
+        compiler_params=params(6),
         cost_estimate=cost(20_000_000_000, 32 << 20),
         name="lowest_part",
     )(arrived, g)
 
 
-def level_one(arrived, inverse_rows, g, x_ref, inverse_ref, op, e_out):
+def level_one(arrived, inverse_rows, g, x_ref, inverse_ref, op_hi, op_lo, e_out):
     low = gathered_rows(arrived, GROUPS)
     hi, lo = split2(inverse_rows[...])
     corr = mm(low, hi, lo, nt=True)
@@ -443,8 +444,7 @@
     total = None
     for i in range(NC1 // 256):
         rows = slice(i * 256, (i + 1) * 256)
-        hi, lo = split2(op[rows, :])
-        term = mm(scaled[:, rows], hi, lo)
+        term = mm(scaled[:, rows], op_hi[rows, :], op_lo[rows, :])
         total = term if total is None else total + term
     e = 2.0 * OMEGA * scaled - OMEGA * OMEGA * total * inverse + lifted
     for q in range(PEERS):
@@ -476,21 +476,25 @@
     return jnp.concatenate(split2(e), axis=0)
 
 
+def block(top, side, peer, k):
+    return jnp.concatenate([top[k], beside(side[k], peer[k])], axis=0)
+
+
 def pair_spread(own, peer):
     none = jnp.zeros_like(own)
     return jnp.concatenate([beside(own, none), beside(none, peer)], axis=0)
 
 
 def forward_kernel(
-    perm, member, arrived, inverse_rows, g, x, inverse, op, b_slot, b_rest, d_slot, d_rest, x_peer, d_peer, m_peer,
-    hi_pair, lo_pair, hi_rest, lo_rest, maps, z_out, w_out, ws_out, out, e, acc_rr, acc_bz, acc_zw
+    perm, member, arrived, inverse_rows, g, x, inverse, op_hi, op_lo, b_slot, b_rest, d_slot, d_rest, x_peer, d_peer, m_peer,
+    hi_top, lo_top, hi_side, lo_side, hi_peer, lo_peer, hi_rest, lo_rest, maps, z_out, w_out, ws_out, out, e, acc_rr, acc_bz, acc_zw
 ):
-    level_one(arrived, inverse_rows, g, x, inverse, op, e)
+    level_one(arrived, inverse_rows, g, x, inverse, op_hi, op_lo, e)
     acc_rr[...] = jnp.zeros_like(acc_rr)
     acc_bz[...] = jnp.zeros_like(acc_bz)
     acc_zw[...] = jnp.zeros_like(acc_zw)
     e_own = e.at[pl.ds(member[0], 1)]
-    views = (e, b_slot, b_rest, d_slot, d_rest, x_peer, d_peer, m_peer, hi_pair, lo_pair, hi_rest, lo_rest, ws_out)
+    views = (e, b_slot, b_rest, d_slot, d_rest, x_peer, d_peer, m_peer, hi_top, lo_top, hi_side, lo_side, hi_peer, lo_peer, hi_rest, lo_rest, ws_out)
 
     @pl.loop(0, CHUNKS)
     def _(step):
@@ -513,8 +517,8 @@
 
 
 def forward_step(
-    step, perm, e_own, e_peer, b_slot, b_rest, d_slot, d_rest, x_peer, d_peer, m_peer, hi_pair, lo_pair,
-    hi_rest, lo_rest, maps, z_out, w_out, ws_out, acc_rr, acc_bz, acc_zw
+    step, perm, e_own, e_peer, b_slot, b_rest, d_slot, d_rest, x_peer, d_peer, m_peer,
+    hi_top, lo_top, hi_side, lo_side, hi_peer, lo_peer, hi_rest, lo_rest, maps, z_out, w_out, ws_out, acc_rr, acc_bz, acc_zw
 ):
     e_mine = two_parts(e_own[0])
     e_both = [two_parts(beside(e_own[0], e_peer[q])) for q in range(CHUNK // 2)]
@@ -524,8 +528,10 @@
     b_own = [b_slot[k] for k in pairs] + [b_rest[k] for k in rest]
     diag = [jnp.concatenate([d_slot[k], d_peer[k]], axis=1) for k in pairs] + [d_rest[k] for k in rest]
     rdiag = [OMEGA / d for d in diag]
-    mats = [(hi_pair[k], lo_pair[k]) for k in pairs] + [(hi_rest[k], lo_rest[k]) for k in rest]
-    x1 = [beside(b_own[k] * rdiag[k][:, :TILE], x_peer[k]) for k in pairs]
+    mats = [(block(hi_top, hi_side, hi_peer, k), block(lo_top, lo_side, lo_peer, k)) for k in pairs]
+    mats = mats + [(hi_rest[k], lo_rest[k]) for k in rest]
+    peers = [x_peer[k // 2, (k % 2) * 128 : (k % 2) * 128 + COLS] for k in pairs]
+    x1 = [beside(b_own[k] * rdiag[k][:, :TILE], peers[k]) for k in pairs]
     x1 = x1 + [b * rd for b, rd in zip(b_own[CHUNK:], rdiag[CHUNK:])]
     spread = [one_hot(row) for row in rows]
     ups = [lift(e_both[k // 2], pair_spread(spread[k], one_hot(m_peer[k]))) for k in pairs]
@@ -573,27 +579,27 @@
             pltpu.VMEM((COLS, TILE), F32),
             pltpu.VMEM((COLS, TILE), F32),
         ],
-        compiler_params=params(),
+        compiler_params=params(10),
         name="forward_part",
     )(*scalars, *arrays)
 
 
 def second_kernel(
-    perm, member, arrived, inverse_rows, g, x, inverse, op, b_slot, b_rest, d_slot, d_rest, d_peer, m_peer, hi_pair, lo_pair,
-    hi_rest, lo_rest, maps, z_in, w_in, w_peer, v_out, u_out, out, dots, e, acc_a, acc_b, acc_c, acc_alpha
+    perm, member, arrived, inverse_rows, g, x, inverse, op_hi, op_lo, b_slot, b_rest, d_slot, d_rest, d_peer, m_peer,
+    hi_top, lo_top, hi_side, lo_side, hi_peer, lo_peer, hi_rest, lo_rest, maps, z_in, w_in, w_peer, v_out, u_out, out, dots, e, acc_a, acc_b, acc_c, acc_alpha
 ):
     extra = arrived[0, 32:40]
     for q in range(1, GROUPS):
         extra = extra + arrived[q, 32:40]
     dots[...] = extra
-    level_one(arrived, inverse_rows, g, x, inverse, op, e)
+    level_one(arrived, inverse_rows, g, x, inverse, op_hi, op_lo, e)
     acc_a[...] = jnp.zeros_like(acc_a)
     acc_b[...] = jnp.zeros_like(acc_b)
     acc_c[...] = jnp.zeros_like(acc_c)
     col = column(dots[0:1])
     acc_alpha[...] = col[:COLS] / col[COLS:]
     e_own = e.at[pl.ds(member[0], 1)]
-    views = (e, b_slot, b_rest, d_slot, d_rest, d_peer, m_peer, hi_pair, lo_pair, hi_rest, lo_rest, w_peer)
+    views = (e, b_slot, b_rest, d_slot, d_rest, d_peer, m_peer, hi_top, lo_top, hi_side, lo_side, hi_peer, lo_peer, hi_rest, lo_rest, w_peer)
 
     @pl.loop(0, CHUNKS)
     def _(step):
@@ -610,8 +616,8 @@
 
 
 def second_step(
-    step, perm, e_own, e_peer, b_slot, b_rest, d_slot, d_rest, d_peer, m_peer, hi_pair, lo_pair,
-    hi_rest, lo_rest, maps, z_in, w_in, w_peer, v_out, u_out, acc_a, acc_b, acc_c, acc_alpha
+    step, perm, e_own, e_peer, b_slot, b_rest, d_slot, d_rest, d_peer, m_peer,
+    hi_top, lo_top, hi_side, lo_side, hi_peer, lo_peer, hi_rest, lo_rest, maps, z_in, w_in, w_peer, v_out, u_out, acc_a, acc_b, acc_c, acc_alpha
 ):
     alpha = acc_alpha[...]
     e_mine = two_parts(e_own[0])
@@ -630,7 +636,8 @@
     rows = [maps[pl.ds(perm[at + step * CHUNK + k], 1)] for at in (0, SLOTS) for k in pairs]
     diag = [jnp.concatenate([d_slot[k], d_peer[k]], axis=1) for k in pairs] + [d_rest[k] for k in rest]
     rdiag = [OMEGA / d for d in diag]
-    mats = [(hi_pair[k], lo_pair[k]) for k in pairs] + [(hi_rest[k], lo_rest[k]) for k in rest]
+    mats = [(block(hi_top, hi_side, hi_peer, k), block(lo_top, lo_side, lo_peer, k)) for k in pairs]
+    mats = mats + [(hi_rest[k], lo_rest[k]) for k in rest]
     w = [jnp.concatenate([w_in[0, k], w_peer[k]], axis=1) for k in pairs] + [w_in[1, k] for k in rest]
     spread = [one_hot(row) for row in rows]
     ups = [lift(e_both[k // 2], pair_spread(spread[k], one_hot(m_peer[k]))) for k in pairs]
@@ -663,75 +670,58 @@
             jax.ShapeDtypeStruct((8, TILE), F32),
         ],
         scratch_shapes=[pltpu.VMEM((PEERS, COLS, AGG), F32)] + [pltpu.VMEM((COLS, TILE), F32)] * 4,
-        compiler_params=params(),
+        compiler_params=params(10),
         name="second_part",
     )(*scalars, *arrays)
 
 
-def combine_kernel(perm, dots, arrived, b_slot, b_rest, z, w, v, u, solution, residual, coef):
-    step = pl.program_id(0)
-
-    @pl.when(step == 0)
-    def _():
-        total = jnp.sum(arrived[...], axis=0)
-        old = column(dots[0:1])
-        one = column(total[0:1])
-        two = column(total[1:2])
-        rho, zw = old[:COLS], old[COLS:]
-        rho_next, zz = one[:COLS], one[COLS:]
-        cross = two[:COLS]
-        alpha = rho / zw
-        beta = rho_next / rho
-        alpha_next = rho_next / (zz + beta * cross + beta * beta * zw)
-        coef[0] = alpha
-        coef[1] = beta
-        coef[2] = alpha_next
-
-    alpha, beta, alpha_next = coef[0], coef[1], coef[2]
-    for half, b_ref in ((0, b_slot), (1, b_rest)):
-        for k in range(STEP):
-            index = perm[half * SLOTS + step * STEP + k]
-            at = pl.ds(pl.multiple_of(index * TILE, TILE), TILE)
-            z0, w0 = z[half, k], w[half, k]
-            z1 = z0 - alpha * v[half, k]
-            az1 = w0 - alpha * u[half, k]
-            solution[:, at] = alpha * z0 + alpha_next * (z1 + beta * z0)
-            residual[:, at] = b_ref[k] - alpha * w0 - alpha_next * (az1 + beta * w0)
-
-
-def combine(perm, dots, arrived, b_slot, b_rest, z, w, v, u):
-    def pair():
-        return pl.BlockSpec((2, STEP, COLS, TILE), lambda s, p: (0, s, 0, 0))
-
-    def single():
-        return pl.BlockSpec((STEP, COLS, TILE), lambda s, p: (s, 0, 0))
-
-    def whole():
-        return pl.BlockSpec((COLS, BLK * TILE), lambda s, p: (0, 0))
-
-    grid = pltpu.PrefetchScalarGridSpec(
-        num_scalar_prefetch=1,
-        grid=(NSTEP,),
-        in_specs=[
-            pl.BlockSpec((8, TILE), lambda s, p: (0, 0)),
-            pl.BlockSpec((GROUPS * PEERS, 2, TILE), lambda s, p: (0, 0, 0)),
-            single(),
-            single(),
-            pair(),
-            pair(),
-            pair(),
-            pair(),
-        ],
-        out_specs=[whole(), whole()],
-        scratch_shapes=[pltpu.VMEM((3, COLS, TILE), F32)],
-    )
+def combine_kernel(where, dots, arrived, b, z, w, v, u, solution, residual, sol_buf, res_buf, sem):
+    total = jnp.sum(arrived[...], axis=0)
+    old = column(dots[0:1])
+    one = column(total[0:1])
+    two = column(total[1:2])
+    rho, zw = old[:COLS], old[COLS:]
+    rho_next, zz = one[:COLS], one[COLS:]
+    alpha = rho / zw
+    beta = rho_next / rho
+    alpha_next = rho_next / (zz + beta * two[:COLS] + beta * beta * zw)
+    first = alpha + alpha_next * (1.0 + beta)
+    second = alpha_next * alpha
+
+    def copies(i):
+        at = pl.ds(i * (STEP * TILE), STEP * TILE)
+        return (
+            pltpu.make_async_copy(sol_buf.at[:, at], solution.at[:, at], sem.at[0, i]),
+            pltpu.make_async_copy(res_buf.at[:, at], residual.at[:, at], sem.at[1, i]),
+        )
+
+    for i in range(BLK // STEP):
+        for t in range(i * STEP, (i + 1) * STEP):
+            half, k = where[t] // SLOTS, lax.rem(where[t], SLOTS)
+            at = slice(t * TILE, (t + 1) * TILE)
+            sol_buf[:, at] = first * z[half, k] - second * v[half, k]
+            res_buf[:, at] = b[:, at] - first * w[half, k] + second * u[half, k]
+        for copy in copies(i):
+            copy.start()
+    for i in range(BLK // STEP):
+        for copy in copies(i):
+            copy.wait()
+
+
+def combine(where, dots, arrived, b, z, w, v, u):
     return pl.pallas_call(
         combine_kernel,
-        grid_spec=grid,
-        out_shape=[jax.ShapeDtypeStruct((COLS, BLK * TILE), F32)] * 2,
-        compiler_params=params(),
+        in_specs=specs(1, 7),
+        out_specs=[pl.BlockSpec(memory_space=pl.ANY)] * 2,
+        out_shape=[far((COLS, BLK * TILE))] * 2,
+        scratch_shapes=[
+            pltpu.VMEM((COLS, BLK * TILE), F32),
+            pltpu.VMEM((COLS, BLK * TILE), F32),
+            pltpu.SemaphoreType.DMA((2, BLK // STEP)),
+        ],
+        compiler_params=params(8),
         name="combine",
-    )(perm, dots, arrived, b_slot, b_rest, z, w, v, u)
+    )(where, dots, arrived, b, z, w, v, u)
 
 
 def exchange(x, axes):
@@ -758,7 +748,7 @@
     operator = level1_ops[0]
 
     outgoing = boundary_pack(slot_blocks, diag_tiles, right_side, maps)
-    side = exchange(outgoing.reshape(PEERS, 2 * SIDE, TILE), GROUP_AXES).reshape(SLOTS, SIDE, TILE)
+    side = exchange(outgoing, GROUP_AXES)
 
     tile_ids = jnp.arange(BLK, dtype=jnp.int32)
     free = jnp.logical_not(jnp.any(slot_list[:, None] == tile_ids[None, :], axis=0)).astype(jnp.int32)
@@ -766,30 +756,33 @@
     chosen = (rank[None, :] == jnp.arange(SLOTS, dtype=jnp.int32)[:, None]) & (free[None, :] == 1)
     rest_list = jnp.sum(jnp.where(chosen, tile_ids[None, :], 0), axis=1)
     perm = jnp.concatenate([slot_list, rest_list])
-
-    b_slot, b_rest, d_slot, d_rest, hi_rest, lo_rest, rs, rr_local = local_part(
+    where = jnp.sum(jnp.where(perm[None, :] == tile_ids[:, None], tile_ids[None, :], 0), axis=1)
+
+    b_slot, b_rest, d_slot, d_rest, hi_rest, lo_rest, hi_top, lo_top, hi_side, lo_side, rs, rr_local = local_part(
         perm, counts, diag_tiles, right_side, remote, maps
     )
-    g, inverse = coarse_setup(operator, coarse_map.reshape(1, NC1))
+    g, inverse, op_hi, op_lo = coarse_setup(operator, coarse_map.reshape(1, NC1))
     inverse_rows = lax.dynamic_slice_in_dim(coarsest_inverse, group * AGG, AGG, 0)
 
-    rr_local, g, inverse_rows, member = lax.optimization_barrier((rr_local, g, inverse_rows, member))
+    rr_local, g, inverse_rows, member, where = lax.optimization_barrier(
+        (rr_local, g, inverse_rows, member, where)
+    )
     gathered = exchange(first_restrict(side, rs, rr_local), GROUP_AXES)
-    hi_pair, lo_pair, d_peer, m_peer, x_peer = pair_setup(perm, counts, diag_tiles, side, remote)
-    gathered, hi_pair = lax.optimization_barrier((gathered, hi_pair))
+    hi_peer, lo_peer, d_peer, m_peer = pair_setup(side)
+    gathered, hi_peer = lax.optimization_barrier((gathered, hi_peer))
 
     scalars = (perm, member)
     x, outgoing = lowest_part(gathered, g)
     coarse = (exchange(outgoing, "grp"), inverse_rows, g, x, inverse)
-    fixed = (d_slot, d_rest, d_peer, m_peer, hi_pair, lo_pair, hi_rest, lo_rest, maps)
+    fixed = (d_slot, d_rest, d_peer, m_peer, hi_top, lo_top, hi_side, lo_side, hi_peer, lo_peer, hi_rest, lo_rest, maps)
     z, w, w_peer, outgoing = forward_part(
-        scalars, coarse + (operator, b_slot, b_rest, d_slot, d_rest, x_peer) + fixed[2:]
+        scalars, coarse + (op_hi, op_lo, b_slot, b_rest, d_slot, d_rest, side) + fixed[2:]
     )
     x, outgoing = lowest_part(exchange(outgoing, GROUP_AXES), g)
     coarse = (exchange(outgoing, "grp"), inverse_rows, g, x, inverse)
-    v, u, outgoing, dots = second_part(scalars, coarse + (operator, b_slot, b_rest) + fixed + (z, w, w_peer))
+    v, u, outgoing, dots = second_part(scalars, coarse + (op_hi, op_lo, b_slot, b_rest) + fixed + (z, w, w_peer))
     sums = exchange(outgoing, ALL_AXES)
-    return tuple(combine(perm, dots, sums, b_slot, b_rest, z, w, v, u))
+    return tuple(combine(where, dots, sums, right_side, z, w, v, u))
 
 
 def solution(mesh):

time: 139 us -> 134 us (0.964)
  blocking collectives: 51.3 us -> 47.9 us
  Pallas kernels: 49.2 us -> 46 us
  local copies, waits for them, and re-layouts: 3.22 us -> 5.32 us
    pallas_call x2, Pallas kernels: 12.7 us -> 7.24 us  [the longest x1 4.25 us: pair_setup(): pl.pallas_call(pair_kernel, grid=(NSTEP,), in_specs=[pl.BlockSpec((PEER_S...]
    all_to_all x4, blocking collectives: 51.3 us -> 47.9 us  [exchange(): return lax.all_to_all(x, axes, 0, 0, tiled=True)]
    unnamed x39 -> x59, local copies, waits for them, and re-layouts: 3.11 us -> 5.21 us
    pallas_call x1, Pallas kernels: 1.04 us -> 2.81 us  [coarse_setup(): pl.pallas_call(coarse_kernel, out_shape=[jax.ShapeDtypeStruct((AGG, NC1),...]
  transfers between devices with their start and end apart: 2 -> 2, of which waited for: 1 -> 2; matrix products, arithmetic and copies ran while one was open for 0% -> 1% of each run, Pallas kernels for 14% -> 13%
where the time goes in v8:
time: 134 us; the launch traced here: 133 us
  blocking collectives  47.9 us (36%)
  Pallas kernels  46 us (34%)
  waiting for transfers between devices  18 us (13%)
  starting transfers between devices  14.3 us (11%)
  local copies, waits for them, and re-layouts  5.32 us (4%)
    all_to_all x4, blocking collectives, exchange(): return lax.all_to_all(x, axes, 0, 0, tiled=True)  47.9 us
    all_to_all x2, waiting for transfers between devices, exchange(): return lax.all_to_all(x, axes, 0, 0, tiled=True)  18 us
    all_to_all x2, starting transfers between devices, exchange(): return lax.all_to_all(x, axes, 0, 0, tiled=True)  14.3 us
    pallas_call x1, Pallas kernels, local_part(): pl.pallas_call(local_kernel, grid_spec=grid, out_shape=[sds((COLS, TILE))...  10.3 us
    pallas_call x1, Pallas kernels, forward_part(): pl.pallas_call(forward_kernel, in_specs=specs(len(scalars), len(arrays)),...  9.56 us
    pallas_call x1, Pallas kernels, second_part(): pl.pallas_call(second_kernel, in_specs=specs(len(scalars), len(arrays)),...  8.21 us
    unnamed x59, local copies, waits for them, and re-layouts  5.21 us
    pallas_call x1, Pallas kernels, boundary_pack(): pl.pallas_call(boundary_kernel, in_specs=[pl.BlockSpec(memory_space=pltpu...  4.49 us
  transfers between devices with their start and end apart: 2, of which 2 were waited for; matrix products, arithmetic and copies ran while one was open for 1% of the time, Pallas kernels for 13%

profile of v8, /device:TPU:1, one launch (start us, length us, event | category | flops | bytes accessed | tf_op | source)
XLA Modules:
  0.0 133.2 jit_solution(12500730451162306509)
XLA Ops:
  0.7 0.8 copy-done.26
  1.4 4.5 %boundary_pack.1 = f32[16,264,128]{2,1,0:T(8,128)} custom-call(s32[1,2,16]{2,1,0:T(2,128)S(1)} %bitcast.13, s32[64,128]{1,0:T(8,128)} %bitcast.8, f32[64,128,128]{2,1,0:T(8,128)} %tiles.1, f32[64,8192]{1,0:T(8,128)} %b.1), custom_call_target="tpu_custom_call" | custom-call | tf_op jit(solution)/shard_map/boundary_pack/pallas_call | solution.py:161
  5.9 8.4 %all-to-all-start = ((f32[16,264,128]{2,1,0:T(8,128)}), f32[16,264,128]{2,1,0:T(8,128)S(1)}, u32[]{:S(2)}, u32[]{:S(2)}) async-start(f32[16,264,128]{2,1,0:T(8,128)} %boundary_pack.1), calls=%async_computation | async-start | bytes 4325376 | tf_op jit(solution)/shard_map/all_to_all | solution.py:728
  14.6 2.2 %copy-done.16 = f32[1,1024,1024]{2,1,0:T(8,128)S(1)} copy-done((f32[1,1024,1024]{2,1,0:T(8,128)S(1)}, f32[1,1024,1024]{2,1,0:T(8,128)}, u32[]{:S(2)}) %copy-start.16) | copy-done | bytes 4194328
  16.8 2.8 %coarse_setup.1 = (f32[64,1024]{1,0:T(8,128)S(1)}, f32[1,1024]{1,0:T(1,128)S(1)}, bf16[1024,1024]{1,0:T(8,128)(2,1)}, bf16[1024,1024]{1,0:T(8,128)(2,1)}) custom-call(f32[1024,1024]{1,0:T(8,128)S(1)} %bitcast.7, s32[1,1024]{1,0:T(1,128)S(1)} %bitcast.12), custom_call_target="tpu_custom_call" | custom-call | flops 268435456 | bytes 5242880 | tf_op jit(solution)/shard_map/coarse_setup/pallas_call | solution.py:309
  19.8 0.1 select_reduce_fusion.2
  20.0 10.3 %local_part.1 = (f32[32,64,128]{2,1,0:T(8,128)}, f32[32,64,128]{2,1,0:T(8,128)}, f32[32,1,128]{2,1,0:T(1,128)}, f32[32,1,128]{2,1,0:T(1,128)}, bf16[32,128,128]{...) custom-call(s32[64]{0:T(128)S(1)} %pad_add_fusion.perm, ...), custom_call_target="tpu_custom_call" | custom-call | flops 402653184 | bytes 16777216 | tf_op jit(solution)/shard_map/local_part/pallas_call | solution.py:266
  30.3 0.1 select_reduce_fusion.where
  30.4 14.7 %all-to-all-done.arrived.side0.side1.extra.x_peer = f32[16,264,128]{2,1,0:T(8,128)S(1)} async-done(((f32[16,264,128]{2,1,0:T(8,128)}), f32[16,264,128]{2,1,0:T(8,128)S(1)}, u32[]{:S(2)}, u32[]{:S(2)}) %all-to-all-start) | async-done | bytes 2162720 | tf_op jit(solution)/shard_map/all_to_all | solution.py:728
  45.2 1.4 %copy-done.2 = f32[16,264,128]{2,1,0:T(8,128)} copy-done((f32[16,264,128]{2,1,0:T(8,128)}, f32[16,264,128]{2,1,0:T(8,128)S(1)}, u32[]{:S(2)}) %copy-start.2) | copy-done | bytes 2162712
  46.5 2.6 %first_restrict.1 = f32[16,32,128]{2,1,0:T(8,128)S(1)} custom-call(f32[16,264,128]{2,1,0:T(8,128)} %copy-done.2, f32[32,64,128]{2,1,0:T(8,128)} %get-tuple-element.45.rs, f32[64,64]{1,0:T(8,128)S(1)} %get-tuple-element.46.rr), custom_call_target="tpu_custom_call" | custom-call | tf_op jit(solution)/shard_map/first_restrict/pallas_call | solution.py:345
  49.2 0.7 copy-done.19
  49.8 5.8 %all-to-all-start.1 = ((f32[16,32,128]{2,1,0:T(8,128)}), f32[16,32,128]{2,1,0:T(8,128)S(1)}, u32[]{:S(2)}, u32[]{:S(2)}) async-start(f32[16,32,128]{2,1,0:T(8,128)} %copy-done.19), calls=%async_computation.1 | async-start | bytes 524288 | tf_op jit(solution)/shard_map/all_to_all | solution.py:728
  55.7 4.3 %pair_setup.1 = (bf16[32,128,128]{2,1,0:T(8,128)(2,1)}, bf16[32,128,128]{2,1,0:T(8,128)(2,1)}, f32[32,1,128]{2,1,0:T(1,128)}, s32[32,1,128]{2,1,0:T(1,128)}) custom-call(f32[16,264,128]{2,1,0:T(8,128)} %copy-done.2, f32[16,264,128]{2,1,0:T(8,128)} %copy-done.2, f32[16,264,128]{2,1,0:T(8,128)} %copy-done.2), custom_call_target="tpu_custom_call" | custom-call | flops 402653184 | bytes 16777216 | tf_op jit(solution)/shard_map/pair_setup/pallas_call | solution.py:379
  60.0 3.3 %all-to-all-done.1.arrived = f32[16,32,128]{2,1,0:T(8,128)S(1)} async-done(((f32[16,32,128]{2,1,0:T(8,128)}), f32[16,32,128]{2,1,0:T(8,128)S(1)}, u32[]{:S(2)}, u32[]{:S(2)}) %all-to-all-start.1) | async-done | bytes 262176 | tf_op jit(solution)/shard_map/all_to_all | solution.py:728
  63.4 0.4 lowest_part.2
  63.8 12.9 %all_to_all.30.arrived = f32[8,32,128]{2,1,0:T(8,128)S(1)} all-to-all(f32[8,32,128]{2,1,0:T(8,128)S(1)} %get-tuple-element.50), channel_id=1, replica_groups=mesh['grp'=8,'sub'=8,'chip'=2] {'grp'}, dimensions={0} | all-to-all | bytes 262144 | tf_op jit(solution)/shard_map/all_to_all | solution.py:728
  76.8 9.6 %forward_part.1 = (f32[2,32,64,128]{3,2,1,0:T(8,128)S(1)}, f32[2,32,64,128]{3,2,1,0:T(8,128)S(1)}, f32[32,64,128]{2,1,0:T(8,128)S(1)}, f32[16,40,128]{2,1,0:T(8,128)S(1)}) custom-call(s32[64]{0:T(128)S(1)} %pad_add_fusion.perm, s32[1]{0:T(128)} %bitcast.5.member, f32[8,32,128]{2,1,0:T(8,128)S(1)} %all_to_all.30.arrived, ...), custom_call_target="tpu_custom_call" | custom-call | tf_op jit(solution)/shard_map/forward_part/pallas_call | solution.py:566
  86.4 10.9 %all_to_all.31.arrived = f32[16,40,128]{2,1,0:T(8,128)S(1)} all-to-all(f32[16,40,128]{2,1,0:T(8,128)S(1)} %get-tuple-element.70), channel_id=1, replica_groups=mesh['grp'=8,'sub'=8,'chip'=2] {'sub','chip'}, dimensions={0} | all-to-all | bytes 655360 | tf_op jit(solution)/shard_map/all_to_all | solution.py:728
  97.3 0.4 lowest_part.3
  97.7 10.0 %all_to_all.32.arrived = f32[8,40,128]{2,1,0:T(8,128)S(1)} all-to-all(f32[8,40,128]{2,1,0:T(8,128)S(1)} %get-tuple-element.71), channel_id=1, replica_groups=mesh['grp'=8,'sub'=8,'chip'=2] {'grp'}, dimensions={0} | all-to-all | bytes 327680 | tf_op jit(solution)/shard_map/all_to_all | solution.py:728
  107.7 8.2 %second_part.1 = (f32[2,32,64,128]{3,2,1,0:T(8,128)S(1)}, f32[2,32,64,128]{3,2,1,0:T(8,128)S(1)}, f32[128,2,128]{2,1,0:T(2,128)S(1)}, f32[8,128]{1,0:T(8,128)S(1)}) custom-call(s32[64]{0:T(128)S(1)} %pad_add_fusion.perm, s32[1]{0:T(128)} %bitcast.5.member, f32[8,40,128]{2,1,0:T(8,128)S(1)} %all_to_all.32.arrived, ...), custom_call_target="tpu_custom_call" | custom-call | tf_op jit(solution)/shard_map/second_part/pallas_call | solution.py:662
  115.9 14.1 %all_to_all.33.arrived = f32[128,2,128]{2,1,0:T(2,128)S(1)} all-to-all(f32[128,2,128]{2,1,0:T(2,128)S(1)} %get-tuple-element.77), channel_id=1, replica_groups=mesh['grp'=8,'sub'=8,'chip'=2] {'grp','sub','chip'}, dimensions={0} | all-to-all | bytes 262144 | tf_op jit(solution)/shard_map/all_to_all | solution.py:728
  130.1 3.0 %combine.1 = (f32[64,8192]{1,0:T(8,128)}, f32[64,8192]{1,0:T(8,128)}) custom-call(s32[64]{0:T(128)S(1)} %select_reduce_fusion.where, f32[8,128]{1,0:T(8,128)S(1)} %get-tuple-element.76.dots, f32[128,2,128]{2,1,0:T(2,128)S(1)} %all_to_all.33.arrived, f32[64,8192]{1,0:T(8,128)S(1)} %copy-done.1, f32[2,32,64,128]{3,2,1,0:T(8,128)S(1)} %get-tuple-element.73.z_in.z, ...), custom_call_target="tpu_custom_call" | custom-call | tf_op jit(solution)/shard_map/combine/pallas_call | solution.py:712
  (61 shorter events, 0.6 us)
Async XLA Ops:
  0.6 29.8 %copy-start = (f32[512,512]{1,0:T(8,128)S(1)}, f32[512,512]{1,0:T(8,128)}, u32[]{:S(2)}) copy-start(f32[512,512]{1,0:T(8,128)} %param.17) | copy-start | bytes 3145732
  5.9 8.5 %copy-start.27 = (s32[1,16,2]{1,2,0:T(2,128)S(1)}, s32[1,16,2]{1,2,0:T(2,128)}, u32[]{:S(2)}) copy-start(s32[1,16,2]{1,2,0:T(2,128)} %param.13) | copy-start | bytes 388
  5.9 8.7 %copy-start.25 = (s32[1024]{0:T(1024)S(1)}, s32[1024]{0:T(1024)}, u32[]{:S(2)}) copy-start(s32[1024]{0:T(1024)} %param.15) | copy-start | bytes 12292
  5.9 39.2 %all-to-all-start = ((f32[16,264,128]{2,1,0:T(8,128)}), f32[16,264,128]{2,1,0:T(8,128)S(1)}, u32[]{:S(2)}, u32[]{:S(2)}) async-start(f32[16,264,128]{2,1,0:T(8,128)} %boundary_pack.1), calls=%async_computation | async-start | bytes 4325376 | tf_op jit(solution)/shard_map/all_to_all | solution.py:728
  19.6 10.7 %copy-start.17 = (f32[64,1024]{1,0:T(8,128)}, f32[64,1024]{1,0:T(8,128)S(1)}, u32[]{:S(2)}) copy-start(f32[64,1024]{1,0:T(8,128)S(1)} %get-tuple-element.49.g) | copy-start | bytes 786436
  49.8 13.4 %all-to-all-start.1 = ((f32[16,32,128]{2,1,0:T(8,128)}), f32[16,32,128]{2,1,0:T(8,128)S(1)}, u32[]{:S(2)}, u32[]{:S(2)}) async-start(f32[16,32,128]{2,1,0:T(8,128)} %copy-done.19), calls=%async_computation.1 | async-start | bytes 524288 | tf_op jit(solution)/shard_map/all_to_all | solution.py:728
  63.2 13.4 %copy-start.3 = (f32[16,264,128]{2,1,0:T(8,128)S(1)}, f32[16,264,128]{2,1,0:T(8,128)}, u32[]{:S(2)}) copy-start(f32[16,264,128]{2,1,0:T(8,128)} %copy-done.2) | copy-start | bytes 6488068
  63.2 13.4 %copy-start.4 = (bf16[1024,1024]{1,0:T(8,128)(2,1)S(1)}, bf16[1024,1024]{1,0:T(8,128)(2,1)}, u32[]{:S(2)}) copy-start(bf16[1024,1024]{1,0:T(8,128)(2,1)} %get-tuple-element.54.op_hi) | copy-start | bytes 6291460
  63.2 13.4 %copy-start.5 = (bf16[1024,1024]{1,0:T(8,128)(2,1)S(1)}, bf16[1024,1024]{1,0:T(8,128)(2,1)}, u32[]{:S(2)}) copy-start(bf16[1024,1024]{1,0:T(8,128)(2,1)} %get-tuple-element.55.op_lo) | copy-start | bytes 6291460
  63.3 13.4 %copy-start.6 = (bf16[32,128,256]{2,1,0:T(8,128)(2,1)S(1)}, bf16[32,128,256]{2,1,0:T(8,128)(2,1)}, u32[]{:S(2)}) copy-start(bf16[32,128,256]{2,1,0:T(8,128)(2,1)} %get-tuple-element.62.hi_top) | copy-start | bytes 6291460
  63.3 13.4 %copy-start.7 = (bf16[32,128,256]{2,1,0:T(8,128)(2,1)S(1)}, bf16[32,128,256]{2,1,0:T(8,128)(2,1)}, u32[]{:S(2)}) copy-start(bf16[32,128,256]{2,1,0:T(8,128)(2,1)} %get-tuple-element.63.lo_top) | copy-start | bytes 6291460
  63.3 13.4 %copy-start.8 = (f32[32,64,128]{2,1,0:T(8,128)S(1)}, f32[32,64,128]{2,1,0:T(8,128)}, u32[]{:S(2)}) copy-start(f32[32,64,128]{2,1,0:T(8,128)} %get-tuple-element.56.b_slot) | copy-start | bytes 3145732
  63.3 13.4 %copy-start.9 = (f32[32,64,128]{2,1,0:T(8,128)S(1)}, f32[32,64,128]{2,1,0:T(8,128)}, u32[]{:S(2)}) copy-start(f32[32,64,128]{2,1,0:T(8,128)} %get-tuple-element.57.b_rest) | copy-start | bytes 3145732
  63.3 13.4 %copy-start.10 = (bf16[32,128,128]{2,1,0:T(8,128)(2,1)S(1)}, bf16[32,128,128]{2,1,0:T(8,128)(2,1)}, u32[]{:S(2)}) copy-start(bf16[32,128,128]{2,1,0:T(8,128)(2,1)} %get-tuple-element.68.hi_rest) | copy-start | bytes 3145732
  63.3 13.4 %copy-start.11 = (bf16[32,128,128]{2,1,0:T(8,128)(2,1)S(1)}, bf16[32,128,128]{2,1,0:T(8,128)(2,1)}, u32[]{:S(2)}) copy-start(bf16[32,128,128]{2,1,0:T(8,128)(2,1)} %get-tuple-element.69.lo_rest) | copy-start | bytes 3145732
  63.3 13.4 %copy-start.12 = (bf16[32,128,128]{2,1,0:T(8,128)(2,1)S(1)}, bf16[32,128,128]{2,1,0:T(8,128)(2,1)}, u32[]{:S(2)}) copy-start(bf16[32,128,128]{2,1,0:T(8,128)(2,1)} %get-tuple-element.64.hi_side) | copy-start | bytes 3145732
  63.3 13.4 %copy-start.13 = (bf16[32,128,128]{2,1,0:T(8,128)(2,1)S(1)}, bf16[32,128,128]{2,1,0:T(8,128)(2,1)}, u32[]{:S(2)}) copy-start(bf16[32,128,128]{2,1,0:T(8,128)(2,1)} %get-tuple-element.65.lo_side) | copy-start | bytes 3145732
  63.3 13.4 %copy-start.14 = (bf16[32,128,128]{2,1,0:T(8,128)(2,1)S(1)}, bf16[32,128,128]{2,1,0:T(8,128)(2,1)}, u32[]{:S(2)}) copy-start(bf16[32,128,128]{2,1,0:T(8,128)(2,1)} %get-tuple-element.66.hi_peer) | copy-start | bytes 3145732
  63.4 13.4 %copy-start.15 = (bf16[32,128,128]{2,1,0:T(8,128)(2,1)S(1)}, bf16[32,128,128]{2,1,0:T(8,128)(2,1)}, u32[]{:S(2)}) copy-start(bf16[32,128,128]{2,1,0:T(8,128)(2,1)} %get-tuple-element.67.lo_peer) | copy-start | bytes 3145732
  63.4 13.4 %copy-start.21 = (f32[32,1,128]{2,1,0:T(1,128)S(1)}, f32[32,1,128]{2,1,0:T(1,128)}, u32[]{:S(2)}) copy-start(f32[32,1,128]{2,1,0:T(1,128)} %get-tuple-element.58.d_slot) | copy-start | bytes 49156
  63.4 13.4 %copy-start.22 = (f32[32,1,128]{2,1,0:T(1,128)S(1)}, f32[32,1,128]{2,1,0:T(1,128)}, u32[]{:S(2)}) copy-start(f32[32,1,128]{2,1,0:T(1,128)} %get-tuple-element.59.d_rest) | copy-start | bytes 49156
  63.4 13.4 %copy-start.23 = (f32[32,1,128]{2,1,0:T(1,128)S(1)}, f32[32,1,128]{2,1,0:T(1,128)}, u32[]{:S(2)}) copy-start(f32[32,1,128]{2,1,0:T(1,128)} %get-tuple-element.60.d_peer) | copy-start | bytes 49156
  63.4 13.4 %copy-start.24 = (s32[32,1,128]{2,1,0:T(1,128)S(1)}, s32[32,1,128]{2,1,0:T(1,128)}, u32[]{:S(2)}) copy-start(s32[32,1,128]{2,1,0:T(1,128)} %get-tuple-element.61.m_peer) | copy-start | bytes 49156
  107.7 22.4 %copy-start.1 = (f32[64,8192]{1,0:T(8,128)S(1)}, f32[64,8192]{1,0:T(8,128)}, u32[]{:S(2)}) copy-start(f32[64,8192]{1,0:T(8,128)} %b.1) | copy-start | bytes 6291460
  (7 other events, 19.1 us)

commit v9 on v8

--- a/solution.py
+++ b/solution.py
@@ -206,7 +206,7 @@
         b_rest[k] = b[STEP + k]
         d_rest[k] = diag[STEP + k]
         hi_rest[k], lo_rest[k] = off[STEP + k]
-    coupling, turned = [], []
+    coupling, turned, restricted = [], [], []
     for k in range(STEP):
         j = step * STEP + k
         live = (j % 2) < counts[j // 2]
@@ -214,10 +214,12 @@
         coupling.append(split2(scaled))
         turned.append(split2(scaled.T))
     for k in range(STEP):
-        rs[k] = -(dot_nt(spread[k], coupling[k][0]) + dot_nt(spread[k], coupling[k][1]))
+        restricted.append(-(dot_nt(coupling[k][0], spread[k]) + dot_nt(coupling[k][1], spread[k])))
         hi_top[k] = beside(off[k][0], turned[k][0])
         lo_top[k] = beside(off[k][1], turned[k][1])
         hi_side[k], lo_side[k] = coupling[k]
+    for q in range(PEER_STEP):
+        rs[q, 0], rs[q, 1] = split2(beside(restricted[2 * q], restricted[2 * q + 1]))
     rr[...] = total
 
 
@@ -255,7 +257,7 @@
             out(TILE, 2 * TILE),
             out(TILE, TILE),
             out(TILE, TILE),
-            out(AGG, TILE),
+            pl.BlockSpec((PEER_STEP, 2, TILE, TILE), lambda s, p, c: (s, 0, 0, 0)),
             pl.BlockSpec((COLS, AGG), lambda s, p, c: (0, 0)),
         ],
     )
@@ -277,7 +279,7 @@
             sds((TILE, 2 * TILE), BF16),
             sds((TILE, TILE), BF16),
             sds((TILE, TILE), BF16),
-            sds((AGG, TILE)),
+            far((PEERS, 2, TILE, TILE), BF16),
             jax.ShapeDtypeStruct((COLS, AGG), F32),
         ],
         compiler_params=params(),
@@ -320,81 +322,62 @@
     )(op, cmap)
 
 
-def first_restrict_kernel(arrived, rs, rr, out, x_buf, rs_buf, x_sem, rs_sem):
-    def copies(j):
-        peers, slots = pl.ds(j * PEER_STEP, PEER_STEP), pl.ds(j * STEP, STEP)
-        return [
-            pltpu.make_async_copy(arrived.at[peers, pl.ds(c * 128, COLS)], x_buf.at[c, peers], x_sem.at[c, j])
-            for c in range(2)
-        ] + [pltpu.make_async_copy(rs.at[slots], rs_buf.at[slots], rs_sem.at[j])]
+def first_restrict_kernel(arrived, rs, rr, out, hi_out, lo_out, diag_out, map_out, rs_buf, rs_sem):
+    def copy(j):
+        at = pl.ds(j * PEER_STEP, PEER_STEP)
+        return pltpu.make_async_copy(rs.at[at], rs_buf.at[at], rs_sem.at[j])
 
     for j in range(NSTEP):
-        for copy in copies(j):
-            copy.start()
-    total = rr[...]
-    for j in range(NSTEP):
-        for copy in copies(j):
-            copy.wait()
-        for q in range(j * PEER_STEP, (j + 1) * PEER_STEP):
-            hi, lo = split2(beside(rs_buf[2 * q], rs_buf[2 * q + 1]))
-            total = total + mm(beside(x_buf[0, q], x_buf[1, q]), hi, lo, nt=True)
-    out[...] = jnp.broadcast_to(pack_rows(total), out.shape)
-
-
-def first_restrict(arrived, rs, rr):
-    return pl.pallas_call(
-        first_restrict_kernel,
-        in_specs=[pl.BlockSpec(memory_space=pl.ANY)] * 2 + [pl.BlockSpec(memory_space=pltpu.VMEM)],
-        out_specs=pl.BlockSpec(memory_space=pltpu.VMEM),
-        out_shape=jax.ShapeDtypeStruct((PEERS, 32, TILE), F32),
-        scratch_shapes=[
-            pltpu.VMEM((2, PEERS, COLS, TILE), F32),
-            pltpu.VMEM((SLOTS, AGG, TILE), F32),
-            pltpu.SemaphoreType.DMA((2, NSTEP)),
-            pltpu.SemaphoreType.DMA((NSTEP,)),
-        ],
-        compiler_params=params(8),
-        name="first_restrict",
-    )(hbm(arrived), hbm(rs), rr)
-
-
-def pair_kernel(side0, side1, extra, hi_out, lo_out, diag_out, map_out):
+        copy(j).start()
     r = lax.broadcasted_iota(jnp.int32, (64, TILE), 0)
     c = lax.broadcasted_iota(jnp.int32, (64, TILE), 1)
-    for k in range(STEP):
-        packed = (side0, side1)[k % 2][k // 2]
+    for k in range(SLOTS):
+        q, base, at = k // 2, 128 * (k % 2) + 64, 256 + 2 * (k % 2)
+        packed = arrived[q, base : base + 64]
         top = jnp.where((c >= 64) | (r < c), packed, 0.0)
         bottom = pltpu.roll(jnp.where((c < 64) & (r > c), packed, 0.0), 64, 1)
         half = jnp.concatenate([top, bottom], axis=0)
         hi_out[k], lo_out[k] = split2(half + half.T)
-        at = 2 * (k % 2)
-        diag_out[k] = extra[k // 2, at : at + 1]
-        map_out[k] = extra[k // 2, at + 1 : at + 2].astype(jnp.int32)
-
-
-def pair_setup(side):
-    def spec(*shape):
-        return pl.BlockSpec((STEP,) + shape, lambda s: (s, 0, 0))
-
+        diag_out[k] = arrived[q, at : at + 1]
+        map_out[k] = arrived[q, at + 1 : at + 2].astype(jnp.int32)
+    main, rest = [], []
+    for j in range(NSTEP):
+        copy(j).wait()
+        for q in range(j * PEER_STEP, (j + 1) * PEER_STEP):
+            hi0, lo0 = split2(arrived[q, 0:COLS])
+            hi1, lo1 = split2(arrived[q, 128 : 128 + COLS])
+            main.append(dot(jnp.concatenate([hi0, lo0, hi1, lo1], axis=0), rs_buf[q, 0]))
+            rest.append(dot(jnp.concatenate([hi0, hi1], axis=0), rs_buf[q, 1]))
+    main, rest = sum(main), sum(rest)
+    first = main[:COLS] + main[COLS : 2 * COLS] + rest[:COLS]
+    second = main[2 * COLS : 3 * COLS] + main[3 * COLS :] + rest[COLS:]
+    total = rr[...] + first[:, :AGG] + second[:, AGG:]
+    out[...] = jnp.broadcast_to(pack_rows(total), out.shape)
+
+
+def first_restrict(arrived, rs, rr):
     return pl.pallas_call(
-        pair_kernel,
-        grid=(NSTEP,),
+        first_restrict_kernel,
         in_specs=[
-            pl.BlockSpec((PEER_STEP, 64, TILE), lambda s: (s, 1, 0)),
-            pl.BlockSpec((PEER_STEP, 64, TILE), lambda s: (s, 3, 0)),
-            pl.BlockSpec((PEER_STEP, 8, TILE), lambda s: (s, 32, 0)),
-        ],
-        out_specs=[spec(TILE, TILE), spec(TILE, TILE), spec(1, TILE), spec(1, TILE)],
+            pl.BlockSpec(memory_space=pltpu.VMEM),
+            pl.BlockSpec(memory_space=pl.ANY),
+            pl.BlockSpec(memory_space=pltpu.VMEM),
+        ],
+        out_specs=[pl.BlockSpec(memory_space=pltpu.VMEM)] * 5,
         out_shape=[
-            far((SLOTS, TILE, TILE), BF16),
-            far((SLOTS, TILE, TILE), BF16),
-            far((SLOTS, 1, TILE)),
-            far((SLOTS, 1, TILE), jnp.int32),
-        ],
-        compiler_params=params(),
-        cost_estimate=cost(2 * 64 * 3 * 64 * 128 * 128, 16 << 20),
-        name="pair_setup",
-    )(*([hbm(side)] * 3))
+            jax.ShapeDtypeStruct((PEERS, 32, TILE), F32),
+            near((SLOTS, TILE, TILE), BF16),
+            near((SLOTS, TILE, TILE), BF16),
+            near((SLOTS, 1, TILE)),
+            near((SLOTS, 1, TILE), jnp.int32),
+        ],
+        scratch_shapes=[
+            pltpu.VMEM((PEERS, 2, TILE, TILE), BF16),
+            pltpu.SemaphoreType.DMA((NSTEP,)),
+        ],
+        compiler_params=params(8),
+        name="first_restrict",
+    )(pltpu.with_memory_space_constraint(arrived, pltpu.VMEM), hbm(rs), rr)
 
 
 def gathered_rows(ref, count):
@@ -767,9 +750,8 @@
     rr_local, g, inverse_rows, member, where = lax.optimization_barrier(
         (rr_local, g, inverse_rows, member, where)
     )
-    gathered = exchange(first_restrict(side, rs, rr_local), GROUP_AXES)
-    hi_peer, lo_peer, d_peer, m_peer = pair_setup(side)
-    gathered, hi_peer = lax.optimization_barrier((gathered, hi_peer))
+    outgoing, hi_peer, lo_peer, d_peer, m_peer = first_restrict(side, rs, rr_local)
+    gathered = exchange(outgoing, GROUP_AXES)
 
     scalars = (perm, member)
     x, outgoing = lowest_part(gathered, g)

time: 134 us -> 130 us (0.970)
  blocking collectives: 47.9 us -> 61.1 us
  Pallas kernels: 46 us -> 39.9 us
  starting transfers between devices: 14.3 us -> 8.44 us
  waiting for transfers between devices: 18 us -> 14.7 us
  local copies, waits for them, and re-layouts: 5.32 us -> 3.23 us
    all_to_all x4 -> x5, blocking collectives: 47.9 us -> 61.1 us  [exchange(): return lax.all_to_all(x, axes, 0, 0, tiled=True)]
    all_to_all x2 -> x1, starting transfers between devices: 14.3 us -> 8.44 us  [exchange(): return lax.all_to_all(x, axes, 0, 0, tiled=True)]
    pallas_call x1 -> x0, Pallas kernels: 4.25 us -> none  [pair_setup(): pl.pallas_call(pair_kernel, grid=(NSTEP,), in_specs=[pl.BlockSpec((PEER_S...]
    all_to_all x2 -> x1, waiting for transfers between devices: 18 us -> 14.7 us  [exchange(): return lax.all_to_all(x, axes, 0, 0, tiled=True)]
    unnamed x59 -> x45, local copies, waits for them, and re-layouts: 5.21 us -> 3.12 us
  transfers between devices with their start and end apart: 2 -> 1, of which waited for: 2 -> 1; matrix products, arithmetic and copies ran while one was open for 1% -> 1% of each run, Pallas kernels for 13% -> 10%
where the time goes in v9:
time: 130 us; the launch traced here: 129 us
  blocking collectives  61.1 us (47%)
  Pallas kernels  39.9 us (31%)
  waiting for transfers between devices  14.7 us (11%)
  starting transfers between devices  8.44 us (6%)
  local copies, waits for them, and re-layouts  3.23 us (2%)
    all_to_all x5, blocking collectives, exchange(): return lax.all_to_all(x, axes, 0, 0, tiled=True)  61.1 us
    all_to_all x1, waiting for transfers between devices, exchange(): return lax.all_to_all(x, axes, 0, 0, tiled=True)  14.7 us
    pallas_call x1, Pallas kernels, local_part(): pl.pallas_call(local_kernel, grid_spec=grid, out_shape=[sds((COLS, TILE))...  10.2 us
    pallas_call x1, Pallas kernels, forward_part(): pl.pallas_call(forward_kernel, in_specs=specs(len(scalars), len(arrays)),...  8.97 us
    all_to_all x1, starting transfers between devices, exchange(): return lax.all_to_all(x, axes, 0, 0, tiled=True)  8.44 us
    pallas_call x1, Pallas kernels, second_part(): pl.pallas_call(second_kernel, in_specs=specs(len(scalars), len(arrays)),...  7.24 us
    pallas_call x1, Pallas kernels, boundary_pack(): pl.pallas_call(boundary_kernel, in_specs=[pl.BlockSpec(memory_space=pltpu...  4.47 us
    unnamed x45, local copies, waits for them, and re-layouts  3.12 us
  transfers between devices with their start and end apart: 1, of which 1 were waited for; matrix products, arithmetic and copies ran while one was open for 1% of the time, Pallas kernels for 10%

profile of v9, /device:TPU:1, one launch (start us, length us, event | category | flops | bytes accessed | tf_op | source)
XLA Modules:
  0.0 129.0 jit_solution(8930701316519793628)
XLA Ops:
  0.7 0.8 copy-done.19
  1.4 4.5 %boundary_pack.1 = f32[16,264,128]{2,1,0:T(8,128)} custom-call(s32[1,2,16]{2,1,0:T(2,128)S(1)} %bitcast.13, s32[64,128]{1,0:T(8,128)} %bitcast.8, f32[64,128,128]{2,1,0:T(8,128)} %tiles.1, f32[64,8192]{1,0:T(8,128)} %b.1), custom_call_target="tpu_custom_call" | custom-call | tf_op jit(solution)/shard_map/boundary_pack/pallas_call | solution.py:161
  5.9 8.4 %all-to-all-start = ((f32[16,264,128]{2,1,0:T(8,128)}), f32[16,264,128]{2,1,0:T(8,128)S(1)}, u32[]{:S(2)}, u32[]{:S(2)}) async-start(f32[16,264,128]{2,1,0:T(8,128)} %boundary_pack.1), calls=%async_computation | async-start | bytes 4325376 | tf_op jit(solution)/shard_map/all_to_all | solution.py:711
  14.4 0.1 copy.13
  14.5 0.1 reshape.33
  14.6 2.2 %copy-done.12 = f32[1,1024,1024]{2,1,0:T(8,128)S(1)} copy-done((f32[1,1024,1024]{2,1,0:T(8,128)S(1)}, f32[1,1024,1024]{2,1,0:T(8,128)}, u32[]{:S(2)}) %copy-start.12) | copy-done | bytes 4194328
  16.8 2.9 %coarse_setup.1 = (f32[64,1024]{1,0:T(8,128)S(1)}, f32[1,1024]{1,0:T(1,128)S(1)}, bf16[1024,1024]{1,0:T(8,128)(2,1)}, bf16[1024,1024]{1,0:T(8,128)(2,1)}) custom-call(f32[1024,1024]{1,0:T(8,128)S(1)} %bitcast.7, s32[1,1024]{1,0:T(1,128)S(1)} %bitcast.12), custom_call_target="tpu_custom_call" | custom-call | flops 268435456 | bytes 5242880 | tf_op jit(solution)/shard_map/coarse_setup/pallas_call | solution.py:311
  19.6 0.1 fusion
  19.7 0.1 select_reduce_fusion.1
  19.8 0.1 select_reduce_fusion.2
  20.0 10.2 %local_part.1 = (f32[32,64,128]{2,1,0:T(8,128)}, f32[32,64,128]{2,1,0:T(8,128)}, f32[32,1,128]{2,1,0:T(1,128)}, f32[32,1,128]{2,1,0:T(1,128)}, bf16[32,128,128]{...) custom-call(s32[64]{0:T(128)S(1)} %pad_add_fusion.perm, ...), custom_call_target="tpu_custom_call" | custom-call | flops 402653184 | bytes 16777216 | tf_op jit(solution)/shard_map/local_part/pallas_call | solution.py:268
  30.3 0.1 select_reduce_fusion.where
  30.4 14.7 %all-to-all-done.arrived.x_peer = f32[16,264,128]{2,1,0:T(8,128)S(1)} async-done(((f32[16,264,128]{2,1,0:T(8,128)}), f32[16,264,128]{2,1,0:T(8,128)S(1)}, u32[]{:S(2)}, u32[]{:S(2)}) %all-to-all-start) | async-done | bytes 2162720 | tf_op jit(solution)/shard_map/all_to_all | solution.py:711
  45.1 2.4 %first_restrict.1 = (f32[16,32,128]{2,1,0:T(8,128)S(1)}, bf16[32,128,128]{2,1,0:T(8,128)(2,1)S(1)}, bf16[32,128,128]{2,1,0:T(8,128)(2,1)S(1)}, f32[32,1,128]{2,1,0:T(1,128)S(1)}, s32[32,1,128]{2,1,0:T(1,128)S(1)}) custom-call(f32[16,264,128]{2,1,0:T(8,128)S(1)} %all-to-all-done.arrived.x_peer, bf16[16,2,128,128]{3,2,1,0:T(8,128)(2,1)} %get-tuple-element.44.rs, ...), custom_call_target="tpu_custom_call" | custom-call | tf_op jit(solution)/shard_map/first_restrict/pallas_call | solution.py:359
  47.5 13.2 %all_to_all.30.arrived = f32[16,32,128]{2,1,0:T(8,128)S(1)} all-to-all(f32[16,32,128]{2,1,0:T(8,128)S(1)} %get-tuple-element.46), channel_id=1, replica_groups=mesh['grp'=8,'sub'=8,'chip'=2] {'sub','chip'}, dimensions={0} | all-to-all | bytes 524288 | tf_op jit(solution)/shard_map/all_to_all | solution.py:711
  60.8 0.4 lowest_part.2
  61.2 12.8 %all_to_all.31.arrived = f32[8,32,128]{2,1,0:T(8,128)S(1)} all-to-all(f32[8,32,128]{2,1,0:T(8,128)S(1)} %get-tuple-element.48), channel_id=1, replica_groups=mesh['grp'=8,'sub'=8,'chip'=2] {'grp'}, dimensions={0} | all-to-all | bytes 262144 | tf_op jit(solution)/shard_map/all_to_all | solution.py:711
  74.1 9.0 %forward_part.1 = (f32[2,32,64,128]{3,2,1,0:T(8,128)S(1)}, f32[2,32,64,128]{3,2,1,0:T(8,128)S(1)}, f32[32,64,128]{2,1,0:T(8,128)S(1)}, f32[16,40,128]{2,1,0:T(8,128)S(1)}) custom-call(s32[64]{0:T(128)S(1)} %pad_add_fusion.perm, s32[1]{0:T(128)} %bitcast.5.member, f32[8,32,128]{2,1,0:T(8,128)S(1)} %all_to_all.31.arrived, ...), custom_call_target="tpu_custom_call" | custom-call | tf_op jit(solution)/shard_map/forward_part/pallas_call | solution.py:549
  83.1 10.9 %all_to_all.32.arrived = f32[16,40,128]{2,1,0:T(8,128)S(1)} all-to-all(f32[16,40,128]{2,1,0:T(8,128)S(1)} %get-tuple-element.68), channel_id=1, replica_groups=mesh['grp'=8,'sub'=8,'chip'=2] {'sub','chip'}, dimensions={0} | all-to-all | bytes 655360 | tf_op jit(solution)/shard_map/all_to_all | solution.py:711
  94.0 0.4 lowest_part.3
  94.4 10.0 %all_to_all.33.arrived = f32[8,40,128]{2,1,0:T(8,128)S(1)} all-to-all(f32[8,40,128]{2,1,0:T(8,128)S(1)} %get-tuple-element.69), channel_id=1, replica_groups=mesh['grp'=8,'sub'=8,'chip'=2] {'grp'}, dimensions={0} | all-to-all | bytes 327680 | tf_op jit(solution)/shard_map/all_to_all | solution.py:711
  104.4 7.2 %second_part.1 = (f32[2,32,64,128]{3,2,1,0:T(8,128)S(1)}, f32[2,32,64,128]{3,2,1,0:T(8,128)S(1)}, f32[128,2,128]{2,1,0:T(2,128)S(1)}, f32[8,128]{1,0:T(8,128)S(1)}) custom-call(s32[64]{0:T(128)S(1)} %pad_add_fusion.perm, s32[1]{0:T(128)} %bitcast.5.member, f32[8,40,128]{2,1,0:T(8,128)S(1)} %all_to_all.33.arrived, ...), custom_call_target="tpu_custom_call" | custom-call | tf_op jit(solution)/shard_map/second_part/pallas_call | solution.py:645
  111.7 14.2 %all_to_all.34.arrived = f32[128,2,128]{2,1,0:T(2,128)S(1)} all-to-all(f32[128,2,128]{2,1,0:T(2,128)S(1)} %get-tuple-element.75), channel_id=1, replica_groups=mesh['grp'=8,'sub'=8,'chip'=2] {'grp','sub','chip'}, dimensions={0} | all-to-all | bytes 262144 | tf_op jit(solution)/shard_map/all_to_all | solution.py:711
  125.8 3.0 %combine.1 = (f32[64,8192]{1,0:T(8,128)}, f32[64,8192]{1,0:T(8,128)}) custom-call(s32[64]{0:T(128)S(1)} %select_reduce_fusion.where, f32[8,128]{1,0:T(8,128)S(1)} %get-tuple-element.74.dots, f32[128,2,128]{2,1,0:T(2,128)S(1)} %all_to_all.34.arrived, f32[64,8192]{1,0:T(8,128)S(1)} %copy-done.1, f32[2,32,64,128]{3,2,1,0:T(8,128)S(1)} %get-tuple-element.71.z_in.z, ...), custom_call_target="tpu_custom_call" | custom-call | tf_op jit(solution)/shard_map/combine/pallas_call | solution.py:695
  (45 shorter events, 0.2 us)
Async XLA Ops:
  0.6 29.8 %copy-start = (f32[512,512]{1,0:T(8,128)S(1)}, f32[512,512]{1,0:T(8,128)}, u32[]{:S(2)}) copy-start(f32[512,512]{1,0:T(8,128)} %param.17) | copy-start | bytes 3145732
  0.6 0.8 copy-start.19
  5.9 8.5 %copy-start.20 = (s32[1,16,2]{1,2,0:T(2,128)S(1)}, s32[1,16,2]{1,2,0:T(2,128)}, u32[]{:S(2)}) copy-start(s32[1,16,2]{1,2,0:T(2,128)} %param.13) | copy-start | bytes 388
  5.9 8.7 %copy-start.18 = (s32[1024]{0:T(1024)S(1)}, s32[1024]{0:T(1024)}, u32[]{:S(2)}) copy-start(s32[1024]{0:T(1024)} %param.15) | copy-start | bytes 12292
  5.9 39.2 %all-to-all-start = ((f32[16,264,128]{2,1,0:T(8,128)}), f32[16,264,128]{2,1,0:T(8,128)S(1)}, u32[]{:S(2)}, u32[]{:S(2)}) async-start(f32[16,264,128]{2,1,0:T(8,128)} %boundary_pack.1), calls=%async_computation | async-start | bytes 4325376 | tf_op jit(solution)/shard_map/all_to_all | solution.py:711
  14.6 2.2 %copy-start.12 = (f32[1,1024,1024]{2,1,0:T(8,128)S(1)}, f32[1,1024,1024]{2,1,0:T(8,128)}, u32[]{:S(2)}) copy-start(f32[1,1024,1024]{2,1,0:T(8,128)} %param.16) | copy-start | bytes 12582916
  16.8 3.3 %copy-start.15 = (s32[8192]{0:T(1024)S(1)}, s32[8192]{0:T(1024)}, u32[]{:S(2)}) copy-start(s32[8192]{0:T(1024)} %param.14) | copy-start | bytes 98308
  16.8 3.3 %copy-start.21 = (s32[1,16]{1,0:T(1,128)S(1)}, s32[1,16]{1,0:T(1,128)}, u32[]{:S(2)}) copy-start(s32[1,16]{1,0:T(1,128)} %param.12) | copy-start | bytes 196
  19.6 10.7 %copy-start.13 = (f32[64,1024]{1,0:T(8,128)}, f32[64,1024]{1,0:T(8,128)S(1)}, u32[]{:S(2)}) copy-start(f32[64,1024]{1,0:T(8,128)S(1)} %get-tuple-element.47.g) | copy-start | bytes 786436
  45.1 15.6 %copy-start.14 = (f32[64,1024]{1,0:T(8,128)S(1)}, f32[64,1024]{1,0:T(8,128)}, u32[]{:S(2)}) copy-start(f32[64,1024]{1,0:T(8,128)} %copy-done.13) | copy-start | bytes 786436
  60.7 13.3 %copy-start.2 = (bf16[1024,1024]{1,0:T(8,128)(2,1)S(1)}, bf16[1024,1024]{1,0:T(8,128)(2,1)}, u32[]{:S(2)}) copy-start(bf16[1024,1024]{1,0:T(8,128)(2,1)} %get-tuple-element.52.op_hi) | copy-start | bytes 6291460
  60.7 13.3 %copy-start.3 = (bf16[1024,1024]{1,0:T(8,128)(2,1)S(1)}, bf16[1024,1024]{1,0:T(8,128)(2,1)}, u32[]{:S(2)}) copy-start(bf16[1024,1024]{1,0:T(8,128)(2,1)} %get-tuple-element.53.op_lo) | copy-start | bytes 6291460
  60.7 13.3 %copy-start.4 = (bf16[32,128,256]{2,1,0:T(8,128)(2,1)S(1)}, bf16[32,128,256]{2,1,0:T(8,128)(2,1)}, u32[]{:S(2)}) copy-start(bf16[32,128,256]{2,1,0:T(8,128)(2,1)} %get-tuple-element.60.hi_top) | copy-start | bytes 6291460
  60.7 13.3 %copy-start.5 = (bf16[32,128,256]{2,1,0:T(8,128)(2,1)S(1)}, bf16[32,128,256]{2,1,0:T(8,128)(2,1)}, u32[]{:S(2)}) copy-start(bf16[32,128,256]{2,1,0:T(8,128)(2,1)} %get-tuple-element.61.lo_top) | copy-start | bytes 6291460
  60.8 13.3 %copy-start.6 = (f32[32,64,128]{2,1,0:T(8,128)S(1)}, f32[32,64,128]{2,1,0:T(8,128)}, u32[]{:S(2)}) copy-start(f32[32,64,128]{2,1,0:T(8,128)} %get-tuple-element.54.b_slot) | copy-start | bytes 3145732
  60.8 13.3 %copy-start.7 = (f32[32,64,128]{2,1,0:T(8,128)S(1)}, f32[32,64,128]{2,1,0:T(8,128)}, u32[]{:S(2)}) copy-start(f32[32,64,128]{2,1,0:T(8,128)} %get-tuple-element.55.b_rest) | copy-start | bytes 3145732
  60.8 13.3 %copy-start.8 = (bf16[32,128,128]{2,1,0:T(8,128)(2,1)S(1)}, bf16[32,128,128]{2,1,0:T(8,128)(2,1)}, u32[]{:S(2)}) copy-start(bf16[32,128,128]{2,1,0:T(8,128)(2,1)} %get-tuple-element.66.hi_rest) | copy-start | bytes 3145732
  60.8 13.3 %copy-start.9 = (bf16[32,128,128]{2,1,0:T(8,128)(2,1)S(1)}, bf16[32,128,128]{2,1,0:T(8,128)(2,1)}, u32[]{:S(2)}) copy-start(bf16[32,128,128]{2,1,0:T(8,128)(2,1)} %get-tuple-element.67.lo_rest) | copy-start | bytes 3145732
  60.8 13.3 %copy-start.10 = (bf16[32,128,128]{2,1,0:T(8,128)(2,1)S(1)}, bf16[32,128,128]{2,1,0:T(8,128)(2,1)}, u32[]{:S(2)}) copy-start(bf16[32,128,128]{2,1,0:T(8,128)(2,1)} %get-tuple-element.62.hi_side) | copy-start | bytes 3145732
  60.8 13.3 %copy-start.11 = (bf16[32,128,128]{2,1,0:T(8,128)(2,1)S(1)}, bf16[32,128,128]{2,1,0:T(8,128)(2,1)}, u32[]{:S(2)}) copy-start(bf16[32,128,128]{2,1,0:T(8,128)(2,1)} %get-tuple-element.63.lo_side) | copy-start | bytes 3145732
  60.8 13.3 %copy-start.16 = (f32[32,1,128]{2,1,0:T(1,128)S(1)}, f32[32,1,128]{2,1,0:T(1,128)}, u32[]{:S(2)}) copy-start(f32[32,1,128]{2,1,0:T(1,128)} %get-tuple-element.56.d_slot) | copy-start | bytes 49156
  60.8 13.3 %copy-start.17 = (f32[32,1,128]{2,1,0:T(1,128)S(1)}, f32[32,1,128]{2,1,0:T(1,128)}, u32[]{:S(2)}) copy-start(f32[32,1,128]{2,1,0:T(1,128)} %get-tuple-element.57.d_rest) | copy-start | bytes 49156
  104.4 21.4 %copy-start.1 = (f32[64,8192]{1,0:T(8,128)S(1)}, f32[64,8192]{1,0:T(8,128)}, u32[]{:S(2)}) copy-start(f32[64,8192]{1,0:T(8,128)} %b.1) | copy-start | bytes 6291460

commit v10 on v9

--- a/solution.py
+++ b/solution.py
@@ -113,7 +113,7 @@
     return jnp.broadcast_to(row, (TILE, TILE)).T
 
 
-def boundary_kernel(slots, maps, tiles, cols, out, map_buf, tile_buf, col_buf, out_buf, map_sem, col_sem, tile_sem, out_sem):
+def boundary_kernel(slots_in, maps, tiles, cols, out, slots, slot_sem, map_buf, tile_buf, col_buf, out_buf, map_sem, col_sem, tile_sem, out_sem):
     def tile_copy(j):
         return pltpu.make_async_copy(tiles.at[slots[0, j % 2, j // 2]], tile_buf.at[j], tile_sem.at[j])
 
@@ -125,8 +125,11 @@
         at = pl.ds(j // 2, PEER_STEP)
         return pltpu.make_async_copy(out_buf.at[at], out.at[at], out_sem.at[j // STEP])
 
+    slot_copy = pltpu.make_async_copy(slots_in, slots, slot_sem)
+    slot_copy.start()
     map_copy = pltpu.make_async_copy(maps, map_buf, map_sem)
     map_copy.start()
+    slot_copy.wait()
     for j in range(SLOTS):
         tile_copy(j).start()
         col_copy(j).start()
@@ -160,10 +163,12 @@
 def boundary_pack(slot_blocks, diag_tiles, right_side, maps):
     return pl.pallas_call(
         boundary_kernel,
-        in_specs=[pl.BlockSpec(memory_space=pltpu.SMEM)] + [pl.BlockSpec(memory_space=pl.ANY)] * 3,
+        in_specs=[pl.BlockSpec(memory_space=pl.ANY)] * 4,
         out_specs=pl.BlockSpec(memory_space=pl.ANY),
         out_shape=far((PEERS, SIDE, TILE)),
         scratch_shapes=[
+            pltpu.SMEM((1, 2, PEERS), jnp.int32),
+            pltpu.SemaphoreType.DMA,
             pltpu.VMEM((BLK, TILE), jnp.int32),
             pltpu.VMEM((SLOTS, TILE, TILE), F32),
             pltpu.VMEM((SLOTS, COLS, TILE), F32),
@@ -175,14 +180,16 @@
         ],
         compiler_params=params(),
         name="boundary_pack",
-    )(slot_blocks.transpose(0, 2, 1), hbm(maps), hbm(diag_tiles), hbm(right_side))
+    )(hbm(slot_blocks.transpose(0, 2, 1)), hbm(maps), hbm(diag_tiles), hbm(right_side))
 
 
 def local_kernel(perm, counts, *refs):
     n = 2 * STEP
     tiles, cols = refs[:n], refs[n : 2 * n]
     remote, maps = refs[2 * n : 2 * n + 2]
-    b_slot, b_rest, d_slot, d_rest, hi_rest, lo_rest, hi_top, lo_top, hi_side, lo_side, rs, rr = refs[2 * n + 2 :]
+    b_slot, b_rest, d_slot, d_rest, hi_rest, lo_rest, hi_top, lo_top, hi_side, lo_side, s_slot, s_rest, rs, rr = (
+        refs[2 * n + 2 :]
+    )
     step = pl.program_id(0)
 
     @pl.when(step == 0)
@@ -206,6 +213,8 @@
         b_rest[k] = b[STEP + k]
         d_rest[k] = diag[STEP + k]
         hi_rest[k], lo_rest[k] = off[STEP + k]
+        s_slot[k] = spread[k]
+        s_rest[k] = spread[STEP + k]
     coupling, turned, restricted = [], [], []
     for k in range(STEP):
         j = step * STEP + k
@@ -257,6 +266,8 @@
             out(TILE, 2 * TILE),
             out(TILE, TILE),
             out(TILE, TILE),
+            out(AGG, TILE),
+            out(AGG, TILE),
             pl.BlockSpec((PEER_STEP, 2, TILE, TILE), lambda s, p, c: (s, 0, 0, 0)),
             pl.BlockSpec((COLS, AGG), lambda s, p, c: (0, 0)),
         ],
@@ -279,6 +290,8 @@
             sds((TILE, 2 * TILE), BF16),
             sds((TILE, TILE), BF16),
             sds((TILE, TILE), BF16),
+            sds((AGG, TILE), BF16),
+            sds((AGG, TILE), BF16),
             far((PEERS, 2, TILE, TILE), BF16),
             jax.ShapeDtypeStruct((COLS, AGG), F32),
         ],
@@ -322,7 +335,7 @@
     )(op, cmap)
 
 
-def first_restrict_kernel(arrived, rs, rr, out, hi_out, lo_out, diag_out, map_out, rs_buf, rs_sem):
+def first_restrict_kernel(arrived, rs, rr, out, hi_out, lo_out, diag_out, spread_out, rs_buf, rs_sem):
     def copy(j):
         at = pl.ds(j * PEER_STEP, PEER_STEP)
         return pltpu.make_async_copy(rs.at[at], rs_buf.at[at], rs_sem.at[j])
@@ -339,7 +352,7 @@
         half = jnp.concatenate([top, bottom], axis=0)
         hi_out[k], lo_out[k] = split2(half + half.T)
         diag_out[k] = arrived[q, at : at + 1]
-        map_out[k] = arrived[q, at + 1 : at + 2].astype(jnp.int32)
+        spread_out[k] = one_hot(arrived[q, at + 1 : at + 2].astype(jnp.int32))
     main, rest = [], []
     for j in range(NSTEP):
         copy(j).wait()
@@ -369,7 +382,7 @@
             near((SLOTS, TILE, TILE), BF16),
             near((SLOTS, TILE, TILE), BF16),
             near((SLOTS, 1, TILE)),
-            near((SLOTS, 1, TILE), jnp.int32),
+            near((SLOTS, AGG, TILE), BF16),
         ],
         scratch_shapes=[
             pltpu.VMEM((PEERS, 2, TILE, TILE), BF16),
@@ -469,21 +482,21 @@
 
 
 def forward_kernel(
-    perm, member, arrived, inverse_rows, g, x, inverse, op_hi, op_lo, b_slot, b_rest, d_slot, d_rest, x_peer, d_peer, m_peer,
-    hi_top, lo_top, hi_side, lo_side, hi_peer, lo_peer, hi_rest, lo_rest, maps, z_out, w_out, ws_out, out, e, acc_rr, acc_bz, acc_zw
+    member, arrived, inverse_rows, g, x, inverse, op_hi, op_lo, b_slot, b_rest, d_slot, d_rest, x_peer, d_peer, s_slot, s_rest, s_peer,
+    hi_top, lo_top, hi_side, lo_side, hi_peer, lo_peer, hi_rest, lo_rest, z_out, w_out, ws_out, out, e, acc_rr, acc_bz, acc_zw
 ):
     level_one(arrived, inverse_rows, g, x, inverse, op_hi, op_lo, e)
     acc_rr[...] = jnp.zeros_like(acc_rr)
     acc_bz[...] = jnp.zeros_like(acc_bz)
     acc_zw[...] = jnp.zeros_like(acc_zw)
     e_own = e.at[pl.ds(member[0], 1)]
-    views = (e, b_slot, b_rest, d_slot, d_rest, x_peer, d_peer, m_peer, hi_top, lo_top, hi_side, lo_side, hi_peer, lo_peer, hi_rest, lo_rest, ws_out)
+    views = (e, b_slot, b_rest, d_slot, d_rest, x_peer, d_peer, s_slot, s_rest, s_peer, hi_top, lo_top, hi_side, lo_side, hi_peer, lo_peer, hi_rest, lo_rest, ws_out)
 
     @pl.loop(0, CHUNKS)
     def _(step):
         e_peer, *parts = [v.at[part(step, v.shape[0])] for v in views]
         both = [v.at[:, part(step, SLOTS)] for v in (z_out, w_out)]
-        forward_step(step, perm, e_own, e_peer, *parts[:-1], maps, *both, parts[-1], acc_rr, acc_bz, acc_zw)
+        forward_step(e_own, e_peer, *parts[:-1], *both, parts[-1], acc_rr, acc_bz, acc_zw)
 
     packed = pack_rows(acc_rr[...])
     sums = jnp.sum(jnp.concatenate([acc_bz[...], acc_zw[...]], axis=0).T, axis=0, keepdims=True)
@@ -500,14 +513,13 @@
 
 
 def forward_step(
-    step, perm, e_own, e_peer, b_slot, b_rest, d_slot, d_rest, x_peer, d_peer, m_peer,
-    hi_top, lo_top, hi_side, lo_side, hi_peer, lo_peer, hi_rest, lo_rest, maps, z_out, w_out, ws_out, acc_rr, acc_bz, acc_zw
+    e_own, e_peer, b_slot, b_rest, d_slot, d_rest, x_peer, d_peer, s_slot, s_rest, s_peer,
+    hi_top, lo_top, hi_side, lo_side, hi_peer, lo_peer, hi_rest, lo_rest, z_out, w_out, ws_out, acc_rr, acc_bz, acc_zw
 ):
     e_mine = two_parts(e_own[0])
     e_both = [two_parts(beside(e_own[0], e_peer[q])) for q in range(CHUNK // 2)]
     rr, bz, zw = acc_rr[...], acc_bz[...], acc_zw[...]
     pairs, rest = range(CHUNK), range(CHUNK)
-    rows = [maps[pl.ds(perm[at + step * CHUNK + k], 1)] for at in (0, SLOTS) for k in pairs]
     b_own = [b_slot[k] for k in pairs] + [b_rest[k] for k in rest]
     diag = [jnp.concatenate([d_slot[k], d_peer[k]], axis=1) for k in pairs] + [d_rest[k] for k in rest]
     rdiag = [OMEGA / d for d in diag]
@@ -516,8 +528,8 @@
     peers = [x_peer[k // 2, (k % 2) * 128 : (k % 2) * 128 + COLS] for k in pairs]
     x1 = [beside(b_own[k] * rdiag[k][:, :TILE], peers[k]) for k in pairs]
     x1 = x1 + [b * rd for b, rd in zip(b_own[CHUNK:], rdiag[CHUNK:])]
-    spread = [one_hot(row) for row in rows]
-    ups = [lift(e_both[k // 2], pair_spread(spread[k], one_hot(m_peer[k]))) for k in pairs]
+    spread = [s_slot[k] for k in pairs] + [s_rest[k] for k in rest]
+    ups = [lift(e_both[k // 2], pair_spread(spread[k], s_peer[k])) for k in pairs]
     ups = ups + [lift(e_mine, sp) for sp in spread[CHUNK:]]
     x = [start + up for start, up in zip(x1, ups)]
     image = [apply_off(xx, *m) for xx, m in zip(x, mats)]
@@ -568,8 +580,8 @@
 
 
 def second_kernel(
-    perm, member, arrived, inverse_rows, g, x, inverse, op_hi, op_lo, b_slot, b_rest, d_slot, d_rest, d_peer, m_peer,
-    hi_top, lo_top, hi_side, lo_side, hi_peer, lo_peer, hi_rest, lo_rest, maps, z_in, w_in, w_peer, v_out, u_out, out, dots, e, acc_a, acc_b, acc_c, acc_alpha
+    member, arrived, inverse_rows, g, x, inverse, op_hi, op_lo, b_slot, b_rest, d_slot, d_rest, d_peer, s_slot, s_rest, s_peer,
+    hi_top, lo_top, hi_side, lo_side, hi_peer, lo_peer, hi_rest, lo_rest, z_in, w_in, w_peer, v_out, u_out, out, dots, e, acc_a, acc_b, acc_c, acc_alpha
 ):
     extra = arrived[0, 32:40]
     for q in range(1, GROUPS):
@@ -582,14 +594,14 @@
     col = column(dots[0:1])
     acc_alpha[...] = col[:COLS] / col[COLS:]
     e_own = e.at[pl.ds(member[0], 1)]
-    views = (e, b_slot, b_rest, d_slot, d_rest, d_peer, m_peer, hi_top, lo_top, hi_side, lo_side, hi_peer, lo_peer, hi_rest, lo_rest, w_peer)
+    views = (e, b_slot, b_rest, d_slot, d_rest, d_peer, s_slot, s_rest, s_peer, hi_top, lo_top, hi_side, lo_side, hi_peer, lo_peer, hi_rest, lo_rest, w_peer)
 
     @pl.loop(0, CHUNKS)
     def _(step):
         e_peer, *parts = [v.at[part(step, v.shape[0])] for v in views]
         z_part, w_part, v_part, u_part = [v.at[:, part(step, SLOTS)] for v in (z_in, w_in, v_out, u_out)]
         second_step(
-            step, perm, e_own, e_peer, *parts[:-1], maps, z_part, w_part, parts[-1], v_part, u_part,
+            e_own, e_peer, *parts[:-1], z_part, w_part, parts[-1], v_part, u_part,
             acc_a, acc_b, acc_c, acc_alpha
         )
 
@@ -599,8 +611,8 @@
 
 
 def second_step(
-    step, perm, e_own, e_peer, b_slot, b_rest, d_slot, d_rest, d_peer, m_peer,
-    hi_top, lo_top, hi_side, lo_side, hi_peer, lo_peer, hi_rest, lo_rest, maps, z_in, w_in, w_peer, v_out, u_out, acc_a, acc_b, acc_c, acc_alpha
+    e_own, e_peer, b_slot, b_rest, d_slot, d_rest, d_peer, s_slot, s_rest, s_peer,
+    hi_top, lo_top, hi_side, lo_side, hi_peer, lo_peer, hi_rest, lo_rest, z_in, w_in, w_peer, v_out, u_out, acc_a, acc_b, acc_c, acc_alpha
 ):
     alpha = acc_alpha[...]
     e_mine = two_parts(e_own[0])
@@ -616,14 +628,13 @@
         sums[2] = sums[2] + (z1 * w + z * az1)
 
     pairs, rest = range(CHUNK), range(CHUNK)
-    rows = [maps[pl.ds(perm[at + step * CHUNK + k], 1)] for at in (0, SLOTS) for k in pairs]
     diag = [jnp.concatenate([d_slot[k], d_peer[k]], axis=1) for k in pairs] + [d_rest[k] for k in rest]
     rdiag = [OMEGA / d for d in diag]
     mats = [(block(hi_top, hi_side, hi_peer, k), block(lo_top, lo_side, lo_peer, k)) for k in pairs]
     mats = mats + [(hi_rest[k], lo_rest[k]) for k in rest]
     w = [jnp.concatenate([w_in[0, k], w_peer[k]], axis=1) for k in pairs] + [w_in[1, k] for k in rest]
-    spread = [one_hot(row) for row in rows]
-    ups = [lift(e_both[k // 2], pair_spread(spread[k], one_hot(m_peer[k]))) for k in pairs]
+    spread = [s_slot[k] for k in pairs] + [s_rest[k] for k in rest]
+    ups = [lift(e_both[k // 2], pair_spread(spread[k], s_peer[k])) for k in pairs]
     ups = ups + [lift(e_mine, sp) for sp in spread[CHUNK:]]
     x1 = [ww * rd for ww, rd in zip(w, rdiag)]
     x = [start + up for start, up in zip(x1, ups)]
@@ -741,8 +752,9 @@
     perm = jnp.concatenate([slot_list, rest_list])
     where = jnp.sum(jnp.where(perm[None, :] == tile_ids[:, None], tile_ids[None, :], 0), axis=1)
 
-    b_slot, b_rest, d_slot, d_rest, hi_rest, lo_rest, hi_top, lo_top, hi_side, lo_side, rs, rr_local = local_part(
-        perm, counts, diag_tiles, right_side, remote, maps
+    b_slot, b_rest, d_slot, d_rest, hi_rest, lo_rest, hi_top, lo_top, hi_side, lo_side, s_slot, s_rest, rs, rr_local = (
+        local_part(
+        perm, counts, diag_tiles, right_side, remote, maps)
     )
     g, inverse, op_hi, op_lo = coarse_setup(operator, coarse_map.reshape(1, NC1))
     inverse_rows = lax.dynamic_slice_in_dim(coarsest_inverse, group * AGG, AGG, 0)
@@ -750,13 +762,13 @@
     rr_local, g, inverse_rows, member, where = lax.optimization_barrier(
         (rr_local, g, inverse_rows, member, where)
     )
-    outgoing, hi_peer, lo_peer, d_peer, m_peer = first_restrict(side, rs, rr_local)
+    outgoing, hi_peer, lo_peer, d_peer, s_peer = first_restrict(side, rs, rr_local)
     gathered = exchange(outgoing, GROUP_AXES)
 
-    scalars = (perm, member)
+    scalars = (member,)
     x, outgoing = lowest_part(gathered, g)
     coarse = (exchange(outgoing, "grp"), inverse_rows, g, x, inverse)
-    fixed = (d_slot, d_rest, d_peer, m_peer, hi_top, lo_top, hi_side, lo_side, hi_peer, lo_peer, hi_rest, lo_rest, maps)
+    fixed = (d_slot, d_rest, d_peer, s_slot, s_rest, s_peer, hi_top, lo_top, hi_side, lo_side, hi_peer, lo_peer, hi_rest, lo_rest)
     z, w, w_peer, outgoing = forward_part(
         scalars, coarse + (op_hi, op_lo, b_slot, b_rest, d_slot, d_rest, side) + fixed[2:]
     )

time: 130 us -> 129 us (level)
    unnamed x45 -> x47, local copies, waits for them, and re-layouts: 3.12 us -> 2.37 us
  transfers between devices with their start and end apart: 1 -> 1, of which waited for: 1 -> 1; matrix products, arithmetic and copies ran while one was open for 1% -> 1% of each run, Pallas kernels for 10% -> 11%
where the time goes in v10:
time: 129 us; the launch traced here: 128 us
  blocking collectives  61.1 us (47%)
  Pallas kernels  40.7 us (32%)
  waiting for transfers between devices  14.1 us (11%)
  starting transfers between devices  8.44 us (7%)
  local copies, waits for them, and re-layouts  2.47 us (2%)
    all_to_all x5, blocking collectives, exchange(): return lax.all_to_all(x, axes, 0, 0, tiled=True)  61.1 us
    all_to_all x1, waiting for transfers between devices, exchange(): return lax.all_to_all(x, axes, 0, 0, tiled=True)  14.1 us
    pallas_call x1, Pallas kernels, local_part(): pl.pallas_call(local_kernel, grid_spec=grid, out_shape=[sds((COLS, TILE))...  10.9 us
    pallas_call x1, Pallas kernels, forward_part(): pl.pallas_call(forward_kernel, in_specs=specs(len(scalars), len(arrays)),...  9.06 us
    all_to_all x1, starting transfers between devices, exchange(): return lax.all_to_all(x, axes, 0, 0, tiled=True)  8.44 us
    pallas_call x1, Pallas kernels, second_part(): pl.pallas_call(second_kernel, in_specs=specs(len(scalars), len(arrays)),...  7.44 us
    pallas_call x1, Pallas kernels, boundary_pack(): pl.pallas_call(boundary_kernel, in_specs=[pl.BlockSpec(memory_space=pl.AN...  4.26 us
    pallas_call x1, Pallas kernels, combine(): pl.pallas_call(combine_kernel, in_specs=specs(1, 7), out_specs=[pl.BlockS...  3.01 us
  transfers between devices with their start and end apart: 1, of which 1 were waited for; matrix products, arithmetic and copies ran while one was open for 1% of the time, Pallas kernels for 11%

profile of v10, /device:TPU:1, one launch (start us, length us, event | category | flops | bytes accessed | tf_op | source)
XLA Modules:
  0.0 128.5 jit_solution(1333709839928886135)
XLA Ops:
  0.6 4.3 %boundary_pack.1 = f32[16,264,128]{2,1,0:T(8,128)} custom-call(s32[1,2,16]{2,1,0:T(2,128)} %bitcast.13, s32[64,128]{1,0:T(8,128)} %bitcast.8, f32[64,128,128]{2,1,0:T(8,128)} %tiles.1, f32[64,8192]{1,0:T(8,128)} %b.1), custom_call_target="tpu_custom_call" | custom-call | tf_op jit(solution)/shard_map/boundary_pack/pallas_call | solution.py:164
  4.9 8.4 %all-to-all-start = ((f32[16,264,128]{2,1,0:T(8,128)}), f32[16,264,128]{2,1,0:T(8,128)S(1)}, u32[]{:S(2)}, u32[]{:S(2)}) async-start(f32[16,264,128]{2,1,0:T(8,128)} %boundary_pack.1), calls=%async_computation | async-start | bytes 4325376 | tf_op jit(solution)/shard_map/all_to_all | solution.py:722
  13.4 0.1 copy.13
  13.5 0.1 reshape.33
  13.6 2.2 %copy-done.12 = f32[1,1024,1024]{2,1,0:T(8,128)S(1)} copy-done((f32[1,1024,1024]{2,1,0:T(8,128)S(1)}, f32[1,1024,1024]{2,1,0:T(8,128)}, u32[]{:S(2)}) %copy-start.12) | copy-done | bytes 4194328
  15.8 2.8 %coarse_setup.1 = (f32[64,1024]{1,0:T(8,128)S(1)}, f32[1,1024]{1,0:T(1,128)S(1)}, bf16[1024,1024]{1,0:T(8,128)(2,1)}, bf16[1024,1024]{1,0:T(8,128)(2,1)}) custom-call(f32[1024,1024]{1,0:T(8,128)S(1)} %bitcast.7, s32[1,1024]{1,0:T(1,128)S(1)} %bitcast.10), custom_call_target="tpu_custom_call" | custom-call | flops 268435456 | bytes 5242880 | tf_op jit(solution)/shard_map/coarse_setup/pallas_call | solution.py:324
  18.6 0.1 fusion
  18.7 0.1 select_reduce_fusion.1
  18.8 0.1 select_reduce_fusion.2
  19.0 0.1 pad_add_fusion.perm
  19.0 10.9 %local_part.1 = (f32[32,64,128]{2,1,0:T(8,128)}, f32[32,64,128]{2,1,0:T(8,128)}, f32[32,1,128]{2,1,0:T(1,128)}, f32[32,1,128]{2,1,0:T(1,128)}, bf16[32,128,128]{...) custom-call(s32[64]{0:T(128)S(1)} %pad_add_fusion.perm, ...), custom_call_target="tpu_custom_call" | custom-call | flops 402653184 | bytes 16777216 | tf_op jit(solution)/shard_map/local_part/pallas_call | solution.py:279
  29.9 0.1 select_reduce_fusion.where
  30.1 14.1 %all-to-all-done.arrived.x_peer = f32[16,264,128]{2,1,0:T(8,128)S(1)} async-done(((f32[16,264,128]{2,1,0:T(8,128)}), f32[16,264,128]{2,1,0:T(8,128)S(1)}, u32[]{:S(2)}, u32[]{:S(2)}) %all-to-all-start) | async-done | bytes 2162720 | tf_op jit(solution)/shard_map/all_to_all | solution.py:722
  44.2 2.5 %first_restrict.1 = (f32[16,32,128]{2,1,0:T(8,128)S(1)}, bf16[32,128,128]{2,1,0:T(8,128)(2,1)S(1)}, bf16[32,128,128]{2,1,0:T(8,128)(2,1)S(1)}, f32[32,1,128]{2,1,0:T(1,128)S(1)}, bf16[32,64,128]{2,1,0:T(8,128)(2,1)S(1)}) custom-call(f32[16,264,128]{2,1,0:T(8,128)S(1)} %all-to-all-done.arrived.x_peer, bf16[16,2,128,128]{3,2,1,0:T(8,128)(2,1)} %get-tuple-element.46.rs, ...), custom_call_target="tpu_custom_call" | custom-call | tf_op jit(solution)/shard_map/first_restrict/pallas_call | solution.py:372
  46.6 13.2 %all_to_all.30.arrived = f32[16,32,128]{2,1,0:T(8,128)S(1)} all-to-all(f32[16,32,128]{2,1,0:T(8,128)S(1)} %get-tuple-element.48), channel_id=1, replica_groups=mesh['grp'=8,'sub'=8,'chip'=2] {'sub','chip'}, dimensions={0} | all-to-all | bytes 524288 | tf_op jit(solution)/shard_map/all_to_all | solution.py:722
  59.9 0.4 lowest_part.2
  60.3 12.9 %all_to_all.31.arrived = f32[8,32,128]{2,1,0:T(8,128)S(1)} all-to-all(f32[8,32,128]{2,1,0:T(8,128)S(1)} %get-tuple-element.50), channel_id=1, replica_groups=mesh['grp'=8,'sub'=8,'chip'=2] {'grp'}, dimensions={0} | all-to-all | bytes 262144 | tf_op jit(solution)/shard_map/all_to_all | solution.py:722
  73.3 9.1 %forward_part.1 = (f32[2,32,64,128]{3,2,1,0:T(8,128)S(1)}, f32[2,32,64,128]{3,2,1,0:T(8,128)S(1)}, f32[32,64,128]{2,1,0:T(8,128)S(1)}, f32[16,40,128]{2,1,0:T(8,128)S(1)}) custom-call(s32[1]{0:T(128)} %bitcast.5.member, f32[8,32,128]{2,1,0:T(8,128)S(1)} %all_to_all.31.arrived, f32[64,512]{1,0:T(8,128)S(1)} %constant_dynamic-slice_fusion.inverse_rows, ...), custom_call_target="tpu_custom_call" | custom-call | tf_op jit(solution)/shard_map/forward_part/pallas_call | solution.py:561
  82.4 10.9 %all_to_all.32.arrived = f32[16,40,128]{2,1,0:T(8,128)S(1)} all-to-all(f32[16,40,128]{2,1,0:T(8,128)S(1)} %get-tuple-element.72), channel_id=1, replica_groups=mesh['grp'=8,'sub'=8,'chip'=2] {'sub','chip'}, dimensions={0} | all-to-all | bytes 655360 | tf_op jit(solution)/shard_map/all_to_all | solution.py:722
  93.3 0.4 lowest_part.3
  93.7 10.0 %all_to_all.33.arrived = f32[8,40,128]{2,1,0:T(8,128)S(1)} all-to-all(f32[8,40,128]{2,1,0:T(8,128)S(1)} %get-tuple-element.73), channel_id=1, replica_groups=mesh['grp'=8,'sub'=8,'chip'=2] {'grp'}, dimensions={0} | all-to-all | bytes 327680 | tf_op jit(solution)/shard_map/all_to_all | solution.py:722
  103.7 7.4 %second_part.1 = (f32[2,32,64,128]{3,2,1,0:T(8,128)S(1)}, f32[2,32,64,128]{3,2,1,0:T(8,128)S(1)}, f32[128,2,128]{2,1,0:T(2,128)S(1)}, f32[8,128]{1,0:T(8,128)S(1)}) custom-call(s32[1]{0:T(128)} %bitcast.5.member, f32[8,40,128]{2,1,0:T(8,128)S(1)} %all_to_all.33.arrived, f32[64,512]{1,0:T(8,128)S(1)} %constant_dynamic-slice_fusion.inverse_rows, ...), custom_call_target="tpu_custom_call" | custom-call | tf_op jit(solution)/shard_map/second_part/pallas_call | solution.py:656
  111.2 14.1 %all_to_all.34.arrived = f32[128,2,128]{2,1,0:T(2,128)S(1)} all-to-all(f32[128,2,128]{2,1,0:T(2,128)S(1)} %get-tuple-element.79), channel_id=1, replica_groups=mesh['grp'=8,'sub'=8,'chip'=2] {'grp','sub','chip'}, dimensions={0} | all-to-all | bytes 262144 | tf_op jit(solution)/shard_map/all_to_all | solution.py:722
  125.3 3.0 %combine.1 = (f32[64,8192]{1,0:T(8,128)}, f32[64,8192]{1,0:T(8,128)}) custom-call(s32[64]{0:T(128)S(1)} %select_reduce_fusion.where, f32[8,128]{1,0:T(8,128)S(1)} %get-tuple-element.78.dots, f32[128,2,128]{2,1,0:T(2,128)S(1)} %all_to_all.34.arrived, f32[64,8192]{1,0:T(8,128)S(1)} %copy-done.1, f32[2,32,64,128]{3,2,1,0:T(8,128)S(1)} %get-tuple-element.75.z_in.z, ...), custom_call_target="tpu_custom_call" | custom-call | tf_op jit(solution)/shard_map/combine/pallas_call | solution.py:706
  (47 shorter events, 0.1 us)
Async XLA Ops:
  0.6 29.4 %copy-start = (f32[512,512]{1,0:T(8,128)S(1)}, f32[512,512]{1,0:T(8,128)}, u32[]{:S(2)}) copy-start(f32[512,512]{1,0:T(8,128)} %param.17) | copy-start | bytes 3145732
  4.9 8.5 %copy-start.22 = (s32[1,16,2]{1,2,0:T(2,128)S(1)}, s32[1,16,2]{1,2,0:T(2,128)}, u32[]{:S(2)}) copy-start(s32[1,16,2]{1,2,0:T(2,128)} %param.13) | copy-start | bytes 388
  4.9 8.7 %copy-start.20 = (s32[1024]{0:T(1024)S(1)}, s32[1024]{0:T(1024)}, u32[]{:S(2)}) copy-start(s32[1024]{0:T(1024)} %param.15) | copy-start | bytes 12292
  4.9 39.2 %all-to-all-start = ((f32[16,264,128]{2,1,0:T(8,128)}), f32[16,264,128]{2,1,0:T(8,128)S(1)}, u32[]{:S(2)}, u32[]{:S(2)}) async-start(f32[16,264,128]{2,1,0:T(8,128)} %boundary_pack.1), calls=%async_computation | async-start | bytes 4325376 | tf_op jit(solution)/shard_map/all_to_all | solution.py:722
  13.6 2.2 %copy-start.12 = (f32[1,1024,1024]{2,1,0:T(8,128)S(1)}, f32[1,1024,1024]{2,1,0:T(8,128)}, u32[]{:S(2)}) copy-start(f32[1,1024,1024]{2,1,0:T(8,128)} %param.16) | copy-start | bytes 12582916
  15.8 3.3 %copy-start.17 = (s32[8192]{0:T(1024)S(1)}, s32[8192]{0:T(1024)}, u32[]{:S(2)}) copy-start(s32[8192]{0:T(1024)} %param.14) | copy-start | bytes 98308
  15.8 3.3 %copy-start.21 = (s32[1,16]{1,0:T(1,128)S(1)}, s32[1,16]{1,0:T(1,128)}, u32[]{:S(2)}) copy-start(s32[1,16]{1,0:T(1,128)} %param.12) | copy-start | bytes 196
  18.6 11.3 %copy-start.15 = (f32[64,1024]{1,0:T(8,128)}, f32[64,1024]{1,0:T(8,128)S(1)}, u32[]{:S(2)}) copy-start(f32[64,1024]{1,0:T(8,128)S(1)} %get-tuple-element.49.g) | copy-start | bytes 786436
  44.2 15.7 %copy-start.16 = (f32[64,1024]{1,0:T(8,128)S(1)}, f32[64,1024]{1,0:T(8,128)}, u32[]{:S(2)}) copy-start(f32[64,1024]{1,0:T(8,128)} %copy-done.15) | copy-start | bytes 786436
  59.8 13.4 %copy-start.2 = (bf16[1024,1024]{1,0:T(8,128)(2,1)S(1)}, bf16[1024,1024]{1,0:T(8,128)(2,1)}, u32[]{:S(2)}) copy-start(bf16[1024,1024]{1,0:T(8,128)(2,1)} %get-tuple-element.54.op_hi) | copy-start | bytes 6291460
  59.8 13.4 %copy-start.3 = (bf16[1024,1024]{1,0:T(8,128)(2,1)S(1)}, bf16[1024,1024]{1,0:T(8,128)(2,1)}, u32[]{:S(2)}) copy-start(bf16[1024,1024]{1,0:T(8,128)(2,1)} %get-tuple-element.55.op_lo) | copy-start | bytes 6291460
  59.8 13.4 %copy-start.4 = (bf16[32,128,256]{2,1,0:T(8,128)(2,1)S(1)}, bf16[32,128,256]{2,1,0:T(8,128)(2,1)}, u32[]{:S(2)}) copy-start(bf16[32,128,256]{2,1,0:T(8,128)(2,1)} %get-tuple-element.64.hi_top) | copy-start | bytes 6291460
  59.8 13.4 %copy-start.5 = (bf16[32,128,256]{2,1,0:T(8,128)(2,1)S(1)}, bf16[32,128,256]{2,1,0:T(8,128)(2,1)}, u32[]{:S(2)}) copy-start(bf16[32,128,256]{2,1,0:T(8,128)(2,1)} %get-tuple-element.65.lo_top) | copy-start | bytes 6291460
  59.8 13.4 %copy-start.6 = (f32[32,64,128]{2,1,0:T(8,128)S(1)}, f32[32,64,128]{2,1,0:T(8,128)}, u32[]{:S(2)}) copy-start(f32[32,64,128]{2,1,0:T(8,128)} %get-tuple-element.56.b_slot) | copy-start | bytes 3145732
  59.8 13.4 %copy-start.7 = (f32[32,64,128]{2,1,0:T(8,128)S(1)}, f32[32,64,128]{2,1,0:T(8,128)}, u32[]{:S(2)}) copy-start(f32[32,64,128]{2,1,0:T(8,128)} %get-tuple-element.57.b_rest) | copy-start | bytes 3145732
  59.9 13.4 %copy-start.8 = (bf16[32,128,128]{2,1,0:T(8,128)(2,1)S(1)}, bf16[32,128,128]{2,1,0:T(8,128)(2,1)}, u32[]{:S(2)}) copy-start(bf16[32,128,128]{2,1,0:T(8,128)(2,1)} %get-tuple-element.70.hi_rest) | copy-start | bytes 3145732
  59.9 13.4 %copy-start.9 = (bf16[32,128,128]{2,1,0:T(8,128)(2,1)S(1)}, bf16[32,128,128]{2,1,0:T(8,128)(2,1)}, u32[]{:S(2)}) copy-start(bf16[32,128,128]{2,1,0:T(8,128)(2,1)} %get-tuple-element.71.lo_rest) | copy-start | bytes 3145732
  59.9 13.4 %copy-start.10 = (bf16[32,128,128]{2,1,0:T(8,128)(2,1)S(1)}, bf16[32,128,128]{2,1,0:T(8,128)(2,1)}, u32[]{:S(2)}) copy-start(bf16[32,128,128]{2,1,0:T(8,128)(2,1)} %get-tuple-element.66.hi_side) | copy-start | bytes 3145732
  59.9 13.4 %copy-start.11 = (bf16[32,128,128]{2,1,0:T(8,128)(2,1)S(1)}, bf16[32,128,128]{2,1,0:T(8,128)(2,1)}, u32[]{:S(2)}) copy-start(bf16[32,128,128]{2,1,0:T(8,128)(2,1)} %get-tuple-element.67.lo_side) | copy-start | bytes 3145732
  59.9 13.4 %copy-start.13 = (bf16[32,64,128]{2,1,0:T(8,128)(2,1)S(1)}, bf16[32,64,128]{2,1,0:T(8,128)(2,1)}, u32[]{:S(2)}) copy-start(bf16[32,64,128]{2,1,0:T(8,128)(2,1)} %get-tuple-element.61.s_slot) | copy-start | bytes 1572868
  59.9 13.4 %copy-start.14 = (bf16[32,64,128]{2,1,0:T(8,128)(2,1)S(1)}, bf16[32,64,128]{2,1,0:T(8,128)(2,1)}, u32[]{:S(2)}) copy-start(bf16[32,64,128]{2,1,0:T(8,128)(2,1)} %get-tuple-element.62.s_rest) | copy-start | bytes 1572868
  59.9 13.4 %copy-start.18 = (f32[32,1,128]{2,1,0:T(1,128)S(1)}, f32[32,1,128]{2,1,0:T(1,128)}, u32[]{:S(2)}) copy-start(f32[32,1,128]{2,1,0:T(1,128)} %get-tuple-element.58.d_slot) | copy-start | bytes 49156
  59.9 13.4 %copy-start.19 = (f32[32,1,128]{2,1,0:T(1,128)S(1)}, f32[32,1,128]{2,1,0:T(1,128)}, u32[]{:S(2)}) copy-start(f32[32,1,128]{2,1,0:T(1,128)} %get-tuple-element.59.d_rest) | copy-start | bytes 49156
  103.7 21.6 %copy-start.1 = (f32[64,8192]{1,0:T(8,128)S(1)}, f32[64,8192]{1,0:T(8,128)}, u32[]{:S(2)}) copy-start(f32[64,8192]{1,0:T(8,128)} %b.1) | copy-start | bytes 6291460

commit v11 on v10

--- a/solution.py
+++ b/solution.py
@@ -187,14 +187,16 @@
     n = 2 * STEP
     tiles, cols = refs[:n], refs[n : 2 * n]
     remote, maps = refs[2 * n : 2 * n + 2]
-    b_slot, b_rest, d_slot, d_rest, hi_rest, lo_rest, hi_top, lo_top, hi_side, lo_side, s_slot, s_rest, rs, rr = (
-        refs[2 * n + 2 :]
-    )
+    b_slot, b_rest, d_slot, d_rest, hi_rest, lo_rest, hi_top, lo_top, hi_side, lo_side, s_slot, s_rest = refs[
+        2 * n + 2 : 2 * n + 14
+    ]
+    z_rest, w_rest, hi_unit, lo_unit, rr_unit, rs, rr = refs[2 * n + 14 :]
     step = pl.program_id(0)
 
     @pl.when(step == 0)
     def _():
         rr[...] = jnp.zeros_like(rr)
+        rr_unit[...] = jnp.zeros_like(rr_unit)
 
     index = [perm[(0 if i < STEP else SLOTS) + step * STEP + i % STEP] for i in range(n)]
     tile = [tiles[i][0] for i in range(n)]
@@ -202,8 +204,26 @@
     off = [split2(off_diag(t)) for t in tile]
     b = [cols[i][...] for i in range(n)]
     x = [OMEGA * bb / d for bb, d in zip(b, diag)]
-    y = [bb - OMEGA * bb - mm(xx, *o) for bb, xx, o in zip(b, x, off)]
     spread = [one_hot(maps[pl.ds(i, 1)]) for i in index]
+    rest = range(STEP, n)
+    rdiag = [OMEGA / diag[i] for i in rest]
+    start = [jnp.concatenate([x[i], jnp.zeros_like(x[i])], axis=0) for i in rest]
+    both = [jnp.concatenate([x[i], spread[i].astype(F32)], axis=0) for i in rest]
+    image = [apply_off(xx, *off[i]) for xx, i in zip(both, rest)]
+    z = [(1.0 - OMEGA) * xx + st - im * rd for xx, st, im, rd in zip(both, start, image, rdiag)]
+    w = [apply_block(zz, diag[i], *off[i]) for zz, i in zip(z, rest)]
+    left = [(1.0 - OMEGA) * ww - apply_off(ww * rd, *off[i]) for ww, rd, i in zip(w, rdiag, rest)]
+    unit_total = rr_unit[...]
+    for k in range(0, STEP, 2):
+        pair = beside(spread[STEP + k], spread[STEP + k + 1])
+        unit_total = unit_total + mm_exact(beside(left[k], left[k + 1]), pair, nt=True)
+    rr_unit[...] = unit_total
+    for k in range(STEP):
+        z_rest[k] = z[k][:COLS]
+        w_rest[k] = w[k][:COLS]
+        hi_unit[k], lo_unit[k] = split2(beside(z[k][COLS:], w[k][COLS:]))
+    y = [b[i] - OMEGA * b[i] - mm(x[i], *off[i]) for i in range(STEP)]
+    y = y + [b[i] - OMEGA * b[i] - im[:COLS] for i, im in zip(rest, image)]
     total = rr[...]
     for i in range(0, n, 2):
         total = total + mm_exact(beside(y[i], y[i + 1]), beside(spread[i], spread[i + 1]), nt=True)
@@ -268,6 +288,11 @@
             out(TILE, TILE),
             out(AGG, TILE),
             out(AGG, TILE),
+            out(COLS, TILE),
+            out(COLS, TILE),
+            out(AGG, 2 * TILE),
+            out(AGG, 2 * TILE),
+            pl.BlockSpec((COLS + AGG, AGG), lambda s, p, c: (0, 0)),
             pl.BlockSpec((PEER_STEP, 2, TILE, TILE), lambda s, p, c: (s, 0, 0, 0)),
             pl.BlockSpec((COLS, AGG), lambda s, p, c: (0, 0)),
         ],
@@ -292,6 +317,11 @@
             sds((TILE, TILE), BF16),
             sds((AGG, TILE), BF16),
             sds((AGG, TILE), BF16),
+            sds((COLS, TILE)),
+            sds((COLS, TILE)),
+            sds((AGG, 2 * TILE), BF16),
+            sds((AGG, 2 * TILE), BF16),
+            jax.ShapeDtypeStruct((COLS + AGG, AGG), F32),
             far((PEERS, 2, TILE, TILE), BF16),
             jax.ShapeDtypeStruct((COLS, AGG), F32),
         ],
@@ -482,15 +512,20 @@
 
 
 def forward_kernel(
-    member, arrived, inverse_rows, g, x, inverse, op_hi, op_lo, b_slot, b_rest, d_slot, d_rest, x_peer, d_peer, s_slot, s_rest, s_peer,
-    hi_top, lo_top, hi_side, lo_side, hi_peer, lo_peer, hi_rest, lo_rest, z_out, w_out, ws_out, out, e, acc_rr, acc_bz, acc_zw
+    member, arrived, inverse_rows, g, x, inverse, op_hi, op_lo, b_slot, b_rest, d_slot, x_peer, d_peer, s_slot, s_peer,
+    hi_top, lo_top, hi_side, lo_side, hi_peer, lo_peer, z_rest, w_rest, hi_unit, lo_unit, rr_unit,
+    z_out, w_out, ws_out, out, e, acc_rr, acc_bz, acc_zw
 ):
     level_one(arrived, inverse_rows, g, x, inverse, op_hi, op_lo, e)
-    acc_rr[...] = jnp.zeros_like(acc_rr)
+    e_own = e.at[pl.ds(member[0], 1)]
+    unit_hi, unit_lo = split2(rr_unit[COLS:])
+    acc_rr[...] = rr_unit[:COLS] + mm(e_own[0], unit_hi, unit_lo)
     acc_bz[...] = jnp.zeros_like(acc_bz)
     acc_zw[...] = jnp.zeros_like(acc_zw)
-    e_own = e.at[pl.ds(member[0], 1)]
-    views = (e, b_slot, b_rest, d_slot, d_rest, x_peer, d_peer, s_slot, s_rest, s_peer, hi_top, lo_top, hi_side, lo_side, hi_peer, lo_peer, hi_rest, lo_rest, ws_out)
+    views = (
+        e, b_slot, b_rest, d_slot, x_peer, d_peer, s_slot, s_peer, hi_top, lo_top, hi_side, lo_side, hi_peer, lo_peer,
+        z_rest, w_rest, hi_unit, lo_unit, ws_out
+    )
 
     @pl.loop(0, CHUNKS)
     def _(step):
@@ -513,24 +548,20 @@
 
 
 def forward_step(
-    e_own, e_peer, b_slot, b_rest, d_slot, d_rest, x_peer, d_peer, s_slot, s_rest, s_peer,
-    hi_top, lo_top, hi_side, lo_side, hi_peer, lo_peer, hi_rest, lo_rest, z_out, w_out, ws_out, acc_rr, acc_bz, acc_zw
+    e_own, e_peer, b_slot, b_rest, d_slot, x_peer, d_peer, s_slot, s_peer, hi_top, lo_top, hi_side, lo_side,
+    hi_peer, lo_peer, z_rest, w_rest, hi_unit, lo_unit, z_out, w_out, ws_out, acc_rr, acc_bz, acc_zw
 ):
     e_mine = two_parts(e_own[0])
     e_both = [two_parts(beside(e_own[0], e_peer[q])) for q in range(CHUNK // 2)]
     rr, bz, zw = acc_rr[...], acc_bz[...], acc_zw[...]
-    pairs, rest = range(CHUNK), range(CHUNK)
-    b_own = [b_slot[k] for k in pairs] + [b_rest[k] for k in rest]
-    diag = [jnp.concatenate([d_slot[k], d_peer[k]], axis=1) for k in pairs] + [d_rest[k] for k in rest]
+    pairs = range(CHUNK)
+    diag = [beside(d_slot[k], d_peer[k]) for k in pairs]
     rdiag = [OMEGA / d for d in diag]
     mats = [(block(hi_top, hi_side, hi_peer, k), block(lo_top, lo_side, lo_peer, k)) for k in pairs]
-    mats = mats + [(hi_rest[k], lo_rest[k]) for k in rest]
     peers = [x_peer[k // 2, (k % 2) * 128 : (k % 2) * 128 + COLS] for k in pairs]
-    x1 = [beside(b_own[k] * rdiag[k][:, :TILE], peers[k]) for k in pairs]
-    x1 = x1 + [b * rd for b, rd in zip(b_own[CHUNK:], rdiag[CHUNK:])]
-    spread = [s_slot[k] for k in pairs] + [s_rest[k] for k in rest]
+    x1 = [beside(b_slot[k] * rdiag[k][:, :TILE], peers[k]) for k in pairs]
+    spread = [s_slot[k] for k in pairs]
     ups = [lift(e_both[k // 2], pair_spread(spread[k], s_peer[k])) for k in pairs]
-    ups = ups + [lift(e_mine, sp) for sp in spread[CHUNK:]]
     x = [start + up for start, up in zip(x1, ups)]
     image = [apply_off(xx, *m) for xx, m in zip(x, mats)]
     z = [(1.0 - OMEGA) * xx + start - im * rd for xx, start, im, rd in zip(x, x1, image, rdiag)]
@@ -538,16 +569,22 @@
     x1 = [ww * rd for ww, rd in zip(w, rdiag)]
     left = [(m[0][:, :TILE], m[1][:, :TILE]) for m in mats]
     y = [(1.0 - OMEGA) * ww[:, :TILE] - apply_off(xx, *m) for ww, xx, m in zip(w, x1, left)]
-    for i in range(0, 2 * CHUNK, 2):
+    for i in range(0, CHUNK, 2):
         rr = rr + mm_exact(beside(y[i], y[i + 1]), beside(spread[i], spread[i + 1]), nt=True)
-    for i in range(2 * CHUNK):
-        zz, ww = z[i][:, :TILE], w[i][:, :TILE]
-        bz = bz + b_own[i] * zz
-        zw = zw + zz * ww
-        z_out[i // CHUNK, i % CHUNK] = zz
-        w_out[i // CHUNK, i % CHUNK] = ww
     for k in pairs:
         ws_out[k] = w[k][:, TILE:]
+    z = [zz[:, :TILE] for zz in z]
+    w = [ww[:, :TILE] for ww in w]
+    for k in range(CHUNK):
+        two = dot(e_mine, hi_unit[k])
+        found = two[:COLS] + two[COLS:] + dot(e_mine[:COLS], lo_unit[k])
+        z.append(z_rest[k] + found[:, :TILE])
+        w.append(w_rest[k] + found[:, TILE:])
+    for i in range(2 * CHUNK):
+        bz = bz + (b_slot if i < CHUNK else b_rest)[i % CHUNK] * z[i]
+        zw = zw + z[i] * w[i]
+        z_out[i // CHUNK, i % CHUNK] = z[i]
+        w_out[i // CHUNK, i % CHUNK] = w[i]
     acc_rr[...] = rr
     acc_bz[...] = bz
     acc_zw[...] = zw
@@ -752,10 +789,11 @@
     perm = jnp.concatenate([slot_list, rest_list])
     where = jnp.sum(jnp.where(perm[None, :] == tile_ids[:, None], tile_ids[None, :], 0), axis=1)
 
-    b_slot, b_rest, d_slot, d_rest, hi_rest, lo_rest, hi_top, lo_top, hi_side, lo_side, s_slot, s_rest, rs, rr_local = (
-        local_part(
-        perm, counts, diag_tiles, right_side, remote, maps)
+    *local, rs, rr_local = local_part(
+        perm, counts, diag_tiles, right_side, remote, maps
     )
+    b_slot, b_rest, d_slot, d_rest, hi_rest, lo_rest, hi_top, lo_top, hi_side, lo_side, s_slot, s_rest = local[:12]
+    affine = tuple(local[12:])
     g, inverse, op_hi, op_lo = coarse_setup(operator, coarse_map.reshape(1, NC1))
     inverse_rows = lax.dynamic_slice_in_dim(coarsest_inverse, group * AGG, AGG, 0)
 
@@ -768,13 +806,19 @@
     scalars = (member,)
     x, outgoing = lowest_part(gathered, g)
     coarse = (exchange(outgoing, "grp"), inverse_rows, g, x, inverse)
-    fixed = (d_slot, d_rest, d_peer, s_slot, s_rest, s_peer, hi_top, lo_top, hi_side, lo_side, hi_peer, lo_peer, hi_rest, lo_rest)
+    pairs = (hi_top, lo_top, hi_side, lo_side, hi_peer, lo_peer)
     z, w, w_peer, outgoing = forward_part(
-        scalars, coarse + (op_hi, op_lo, b_slot, b_rest, d_slot, d_rest, side) + fixed[2:]
+        scalars, coarse + (op_hi, op_lo, b_slot, b_rest, d_slot, side, d_peer, s_slot, s_peer) + pairs + affine
     )
     x, outgoing = lowest_part(exchange(outgoing, GROUP_AXES), g)
     coarse = (exchange(outgoing, "grp"), inverse_rows, g, x, inverse)
-    v, u, outgoing, dots = second_part(scalars, coarse + (op_hi, op_lo, b_slot, b_rest) + fixed + (z, w, w_peer))
+    v, u, outgoing, dots = second_part(
+        scalars,
+        coarse
+        + (op_hi, op_lo, b_slot, b_rest, d_slot, d_rest, d_peer, s_slot, s_rest, s_peer)
+        + pairs
+        + (hi_rest, lo_rest, z, w, w_peer),
+    )
     sums = exchange(outgoing, ALL_AXES)
     return tuple(combine(where, dots, sums, right_side, z, w, v, u))
 

time: 129 us -> 127 us (0.984)
  waiting for transfers between devices: 14.1 us -> 11.5 us
    pallas_call x1, Pallas kernels: 10.9 us -> 13.5 us  [local_part(): pl.pallas_call(local_kernel, grid_spec=grid, out_shape=[sds((COLS, TILE))...]
    all_to_all x1, waiting for transfers between devices: 14.1 us -> 11.5 us  [exchange(): return lax.all_to_all(x, axes, 0, 0, tiled=True)]
    pallas_call x1, Pallas kernels: 9.06 us -> 7.35 us  [forward_part(): pl.pallas_call(forward_kernel, in_specs=specs(len(scalars), len(arrays)),...]
  transfers between devices with their start and end apart: 1 -> 1, of which waited for: 1 -> 1; matrix products, arithmetic and copies ran while one was open for 1% -> 1% of each run, Pallas kernels for 11% -> 13%
where the time goes in v11:
time: 127 us
  blocking collectives  61.3 us (48%)
  Pallas kernels  41.6 us (33%)
  waiting for transfers between devices  11.5 us (9%)
  starting transfers between devices  8.44 us (7%)
  local copies, waits for them, and re-layouts  2.49 us (2%)
    all_to_all x5, blocking collectives, exchange(): return lax.all_to_all(x, axes, 0, 0, tiled=True)  61.3 us
    pallas_call x1, Pallas kernels, local_part(): pl.pallas_call(local_kernel, grid_spec=grid, out_shape=[sds((COLS, TILE))...  13.5 us
    all_to_all x1, waiting for transfers between devices, exchange(): return lax.all_to_all(x, axes, 0, 0, tiled=True)  11.5 us
    all_to_all x1, starting transfers between devices, exchange(): return lax.all_to_all(x, axes, 0, 0, tiled=True)  8.44 us
    pallas_call x1, Pallas kernels, second_part(): pl.pallas_call(second_kernel, in_specs=specs(len(scalars), len(arrays)),...  7.49 us
    pallas_call x1, Pallas kernels, forward_part(): pl.pallas_call(forward_kernel, in_specs=specs(len(scalars), len(arrays)),...  7.35 us
    pallas_call x1, Pallas kernels, boundary_pack(): pl.pallas_call(boundary_kernel, in_specs=[pl.BlockSpec(memory_space=pl.AN...  4.26 us
    pallas_call x1, Pallas kernels, combine(): pl.pallas_call(combine_kernel, in_specs=specs(1, 7), out_specs=[pl.BlockS...  2.99 us
  transfers between devices with their start and end apart: 1, of which 1 were waited for; matrix products, arithmetic and copies ran while one was open for 1% of the time, Pallas kernels for 13%

profile of v11, /device:TPU:1, one launch (start us, length us, event | category | flops | bytes accessed | tf_op | source)
XLA Modules:
  0.0 127.0 jit_solution(5523567427657831669)
XLA Ops:
  0.6 4.3 %boundary_pack.1 = f32[16,264,128]{2,1,0:T(8,128)} custom-call(s32[1,2,16]{2,1,0:T(2,128)} %bitcast.13, s32[64,128]{1,0:T(8,128)} %bitcast.8, f32[64,128,128]{2,1,0:T(8,128)} %tiles.1, f32[64,8192]{1,0:T(8,128)} %b.1), custom_call_target="tpu_custom_call" | custom-call | tf_op jit(solution)/shard_map/boundary_pack/pallas_call | solution.py:164
  4.9 8.4 %all-to-all-start = ((f32[16,264,128]{2,1,0:T(8,128)}), f32[16,264,128]{2,1,0:T(8,128)S(1)}, u32[]{:S(2)}, u32[]{:S(2)}) async-start(f32[16,264,128]{2,1,0:T(8,128)} %boundary_pack.1), calls=%async_computation | async-start | bytes 4325376 | tf_op jit(solution)/shard_map/all_to_all | solution.py:759
  13.4 0.1 copy.13
  13.5 0.1 reshape.33
  13.6 2.2 %copy-done.10 = f32[1,1024,1024]{2,1,0:T(8,128)S(1)} copy-done((f32[1,1024,1024]{2,1,0:T(8,128)S(1)}, f32[1,1024,1024]{2,1,0:T(8,128)}, u32[]{:S(2)}) %copy-start.10) | copy-done | bytes 4194328
  15.8 2.8 %coarse_setup.1 = (f32[64,1024]{1,0:T(8,128)S(1)}, f32[1,1024]{1,0:T(1,128)S(1)}, bf16[1024,1024]{1,0:T(8,128)(2,1)}, bf16[1024,1024]{1,0:T(8,128)(2,1)}) custom-call(f32[1024,1024]{1,0:T(8,128)S(1)} %bitcast.7, s32[1,1024]{1,0:T(1,128)S(1)} %bitcast.10), custom_call_target="tpu_custom_call" | custom-call | flops 268435456 | bytes 5242880 | tf_op jit(solution)/shard_map/coarse_setup/pallas_call | solution.py:354
  18.6 0.1 fusion
  18.7 0.1 select_reduce_fusion.1
  18.8 0.1 select_reduce_fusion.2
  18.9 0.1 pad_add_fusion.perm
  19.0 13.5 %local_part.1 = (f32[32,64,128]{2,1,0:T(8,128)}, f32[32,64,128]{2,1,0:T(8,128)}, f32[32,1,128]{2,1,0:T(1,128)}, f32[32,1,128]{2,1,0:T(1,128)}, bf16[32,128,128]{...) custom-call(s32[64]{0:T(128)S(1)} %pad_add_fusion.perm, ...), custom_call_target="tpu_custom_call" | custom-call | flops 402653184 | bytes 16777216 | tf_op jit(solution)/shard_map/local_part/pallas_call | solution.py:304
  32.5 0.1 select_reduce_fusion.where
  32.7 11.5 %all-to-all-done.arrived.x_peer = f32[16,264,128]{2,1,0:T(8,128)S(1)} async-done(((f32[16,264,128]{2,1,0:T(8,128)}), f32[16,264,128]{2,1,0:T(8,128)S(1)}, u32[]{:S(2)}, u32[]{:S(2)}) %all-to-all-start) | async-done | bytes 2162720 | tf_op jit(solution)/shard_map/all_to_all | solution.py:759
  44.2 2.5 %first_restrict.1 = (f32[16,32,128]{2,1,0:T(8,128)S(1)}, bf16[32,128,128]{2,1,0:T(8,128)(2,1)S(1)}, bf16[32,128,128]{2,1,0:T(8,128)(2,1)S(1)}, f32[32,1,128]{2,1,0:T(1,128)S(1)}, bf16[32,64,128]{2,1,0:T(8,128)(2,1)S(1)}) custom-call(f32[16,264,128]{2,1,0:T(8,128)S(1)} %all-to-all-done.arrived.x_peer, bf16[16,2,128,128]{3,2,1,0:T(8,128)(2,1)} %get-tuple-element.51.rs, ...), custom_call_target="tpu_custom_call" | custom-call | tf_op jit(solution)/shard_map/first_restrict/pallas_call | solution.py:402
  46.6 13.2 %all_to_all.30.arrived = f32[16,32,128]{2,1,0:T(8,128)S(1)} all-to-all(f32[16,32,128]{2,1,0:T(8,128)S(1)} %get-tuple-element.53), channel_id=1, replica_groups=mesh['grp'=8,'sub'=8,'chip'=2] {'sub','chip'}, dimensions={0} | all-to-all | bytes 524288 | tf_op jit(solution)/shard_map/all_to_all | solution.py:759
  59.9 0.4 lowest_part.2
  60.3 12.9 %all_to_all.31.arrived = f32[8,32,128]{2,1,0:T(8,128)S(1)} all-to-all(f32[8,32,128]{2,1,0:T(8,128)S(1)} %get-tuple-element.55), channel_id=1, replica_groups=mesh['grp'=8,'sub'=8,'chip'=2] {'grp'}, dimensions={0} | all-to-all | bytes 262144 | tf_op jit(solution)/shard_map/all_to_all | solution.py:759
  73.3 7.3 %forward_part.1 = (f32[2,32,64,128]{3,2,1,0:T(8,128)S(1)}, f32[2,32,64,128]{3,2,1,0:T(8,128)S(1)}, f32[32,64,128]{2,1,0:T(8,128)S(1)}, f32[16,40,128]{2,1,0:T(8,128)S(1)}) custom-call(s32[1]{0:T(128)} %bitcast.5.member, f32[8,32,128]{2,1,0:T(8,128)S(1)} %all_to_all.31.arrived, f32[64,512]{1,0:T(8,128)S(1)} %constant_dynamic-slice_fusion.inverse_rows, ...), custom_call_target="tpu_custom_call" | custom-call | tf_op jit(solution)/shard_map/forward_part/pallas_call | solution.py:598
  80.7 10.9 %all_to_all.32.arrived = f32[16,40,128]{2,1,0:T(8,128)S(1)} all-to-all(f32[16,40,128]{2,1,0:T(8,128)S(1)} %get-tuple-element.78), channel_id=1, replica_groups=mesh['grp'=8,'sub'=8,'chip'=2] {'sub','chip'}, dimensions={0} | all-to-all | bytes 655360 | tf_op jit(solution)/shard_map/all_to_all | solution.py:759
  91.6 0.4 lowest_part.3
  92.0 10.2 %all_to_all.33.arrived = f32[8,40,128]{2,1,0:T(8,128)S(1)} all-to-all(f32[8,40,128]{2,1,0:T(8,128)S(1)} %get-tuple-element.79), channel_id=1, replica_groups=mesh['grp'=8,'sub'=8,'chip'=2] {'grp'}, dimensions={0} | all-to-all | bytes 327680 | tf_op jit(solution)/shard_map/all_to_all | solution.py:759
  102.2 7.5 %second_part.1 = (f32[2,32,64,128]{3,2,1,0:T(8,128)S(1)}, f32[2,32,64,128]{3,2,1,0:T(8,128)S(1)}, f32[128,2,128]{2,1,0:T(2,128)S(1)}, f32[8,128]{1,0:T(8,128)S(1)}) custom-call(s32[1]{0:T(128)} %bitcast.5.member, f32[8,40,128]{2,1,0:T(8,128)S(1)} %all_to_all.33.arrived, f32[64,512]{1,0:T(8,128)S(1)} %constant_dynamic-slice_fusion.inverse_rows, ...), custom_call_target="tpu_custom_call" | custom-call | tf_op jit(solution)/shard_map/second_part/pallas_call | solution.py:693
  109.7 14.1 %all_to_all.34.arrived = f32[128,2,128]{2,1,0:T(2,128)S(1)} all-to-all(f32[128,2,128]{2,1,0:T(2,128)S(1)} %get-tuple-element.89), channel_id=1, replica_groups=mesh['grp'=8,'sub'=8,'chip'=2] {'grp','sub','chip'}, dimensions={0} | all-to-all | bytes 262144 | tf_op jit(solution)/shard_map/all_to_all | solution.py:759
  123.8 3.0 %combine.1 = (f32[64,8192]{1,0:T(8,128)}, f32[64,8192]{1,0:T(8,128)}) custom-call(s32[64]{0:T(128)S(1)} %select_reduce_fusion.where, f32[8,128]{1,0:T(8,128)S(1)} %get-tuple-element.88.dots, f32[128,2,128]{2,1,0:T(2,128)S(1)} %all_to_all.34.arrived, f32[64,8192]{1,0:T(8,128)S(1)} %copy-done.1, f32[2,32,64,128]{3,2,1,0:T(8,128)S(1)} %get-tuple-element.85.z_in.z, ...), custom_call_target="tpu_custom_call" | custom-call | tf_op jit(solution)/shard_map/combine/pallas_call | solution.py:743
  (55 shorter events, 0.2 us)
Async XLA Ops:
  0.6 32.0 %copy-start = (f32[512,512]{1,0:T(8,128)S(1)}, f32[512,512]{1,0:T(8,128)}, u32[]{:S(2)}) copy-start(f32[512,512]{1,0:T(8,128)} %param.17) | copy-start | bytes 3145732
  4.9 8.7 %copy-start.24 = (s32[1024]{0:T(1024)S(1)}, s32[1024]{0:T(1024)}, u32[]{:S(2)}) copy-start(s32[1024]{0:T(1024)} %param.15) | copy-start | bytes 12292
  4.9 39.2 %all-to-all-start = ((f32[16,264,128]{2,1,0:T(8,128)}), f32[16,264,128]{2,1,0:T(8,128)S(1)}, u32[]{:S(2)}, u32[]{:S(2)}) async-start(f32[16,264,128]{2,1,0:T(8,128)} %boundary_pack.1), calls=%async_computation | async-start | bytes 4325376 | tf_op jit(solution)/shard_map/all_to_all | solution.py:759
  18.6 13.9 %copy-start.12 = (f32[64,1024]{1,0:T(8,128)}, f32[64,1024]{1,0:T(8,128)S(1)}, u32[]{:S(2)}) copy-start(f32[64,1024]{1,0:T(8,128)S(1)} %get-tuple-element.54.g) | copy-start | bytes 786436
  44.2 15.7 %copy-start.13 = (f32[64,1024]{1,0:T(8,128)S(1)}, f32[64,1024]{1,0:T(8,128)}, u32[]{:S(2)}) copy-start(f32[64,1024]{1,0:T(8,128)} %copy-done.12) | copy-start | bytes 786436
  59.8 13.4 %copy-start.2 = (bf16[1024,1024]{1,0:T(8,128)(2,1)S(1)}, bf16[1024,1024]{1,0:T(8,128)(2,1)}, u32[]{:S(2)}) copy-start(bf16[1024,1024]{1,0:T(8,128)(2,1)} %get-tuple-element.59.op_hi) | copy-start | bytes 6291460
  59.8 13.4 %copy-start.3 = (bf16[1024,1024]{1,0:T(8,128)(2,1)S(1)}, bf16[1024,1024]{1,0:T(8,128)(2,1)}, u32[]{:S(2)}) copy-start(bf16[1024,1024]{1,0:T(8,128)(2,1)} %get-tuple-element.60.op_lo) | copy-start | bytes 6291460
  59.8 13.4 %copy-start.4 = (bf16[32,128,256]{2,1,0:T(8,128)(2,1)S(1)}, bf16[32,128,256]{2,1,0:T(8,128)(2,1)}, u32[]{:S(2)}) copy-start(bf16[32,128,256]{2,1,0:T(8,128)(2,1)} %get-tuple-element.67.hi_top) | copy-start | bytes 6291460
  59.8 13.4 %copy-start.5 = (bf16[32,128,256]{2,1,0:T(8,128)(2,1)S(1)}, bf16[32,128,256]{2,1,0:T(8,128)(2,1)}, u32[]{:S(2)}) copy-start(bf16[32,128,256]{2,1,0:T(8,128)(2,1)} %get-tuple-element.68.lo_top) | copy-start | bytes 6291460
  59.8 13.4 %copy-start.6 = (f32[32,64,128]{2,1,0:T(8,128)S(1)}, f32[32,64,128]{2,1,0:T(8,128)}, u32[]{:S(2)}) copy-start(f32[32,64,128]{2,1,0:T(8,128)} %get-tuple-element.61.b_slot) | copy-start | bytes 3145732
  59.9 13.4 %copy-start.7 = (f32[32,64,128]{2,1,0:T(8,128)S(1)}, f32[32,64,128]{2,1,0:T(8,128)}, u32[]{:S(2)}) copy-start(f32[32,64,128]{2,1,0:T(8,128)} %get-tuple-element.62.b_rest) | copy-start | bytes 3145732
  59.9 13.4 %copy-start.8 = (bf16[32,128,128]{2,1,0:T(8,128)(2,1)S(1)}, bf16[32,128,128]{2,1,0:T(8,128)(2,1)}, u32[]{:S(2)}) copy-start(bf16[32,128,128]{2,1,0:T(8,128)(2,1)} %get-tuple-element.69.hi_side) | copy-start | bytes 3145732
  59.9 13.4 %copy-start.9 = (bf16[32,128,128]{2,1,0:T(8,128)(2,1)S(1)}, bf16[32,128,128]{2,1,0:T(8,128)(2,1)}, u32[]{:S(2)}) copy-start(bf16[32,128,128]{2,1,0:T(8,128)(2,1)} %get-tuple-element.70.lo_side) | copy-start | bytes 3145732
  59.9 13.4 %copy-start.11 = (bf16[32,64,128]{2,1,0:T(8,128)(2,1)S(1)}, bf16[32,64,128]{2,1,0:T(8,128)(2,1)}, u32[]{:S(2)}) copy-start(bf16[32,64,128]{2,1,0:T(8,128)(2,1)} %get-tuple-element.65.s_slot) | copy-start | bytes 1572868
  59.9 13.4 %copy-start.16 = (f32[32,64,128]{2,1,0:T(8,128)S(1)}, f32[32,64,128]{2,1,0:T(8,128)}, u32[]{:S(2)}) copy-start(f32[32,64,128]{2,1,0:T(8,128)} %get-tuple-element.73.z_rest) | copy-start | bytes 3145732
  59.9 13.4 %copy-start.17 = (f32[32,64,128]{2,1,0:T(8,128)S(1)}, f32[32,64,128]{2,1,0:T(8,128)}, u32[]{:S(2)}) copy-start(f32[32,64,128]{2,1,0:T(8,128)} %get-tuple-element.74.w_rest) | copy-start | bytes 3145732
  59.9 13.4 %copy-start.18 = (bf16[32,64,256]{2,1,0:T(8,128)(2,1)S(1)}, bf16[32,64,256]{2,1,0:T(8,128)(2,1)}, u32[]{:S(2)}) copy-start(bf16[32,64,256]{2,1,0:T(8,128)(2,1)} %get-tuple-element.75.hi_unit) | copy-start | bytes 3145732
  59.9 13.4 %copy-start.19 = (bf16[32,64,256]{2,1,0:T(8,128)(2,1)S(1)}, bf16[32,64,256]{2,1,0:T(8,128)(2,1)}, u32[]{:S(2)}) copy-start(bf16[32,64,256]{2,1,0:T(8,128)(2,1)} %get-tuple-element.76.lo_unit) | copy-start | bytes 3145732
  59.9 13.4 %copy-start.22 = (f32[32,1,128]{2,1,0:T(1,128)S(1)}, f32[32,1,128]{2,1,0:T(1,128)}, u32[]{:S(2)}) copy-start(f32[32,1,128]{2,1,0:T(1,128)} %get-tuple-element.63.d_slot) | copy-start | bytes 49156
  91.6 10.6 %copy-start.14 = (bf16[32,128,128]{2,1,0:T(8,128)(2,1)S(1)}, bf16[32,128,128]{2,1,0:T(8,128)(2,1)}, u32[]{:S(2)}) copy-start(bf16[32,128,128]{2,1,0:T(8,128)(2,1)} %get-tuple-element.83.hi_rest) | copy-start | bytes 3145732
  91.6 10.6 %copy-start.15 = (bf16[32,128,128]{2,1,0:T(8,128)(2,1)S(1)}, bf16[32,128,128]{2,1,0:T(8,128)(2,1)}, u32[]{:S(2)}) copy-start(bf16[32,128,128]{2,1,0:T(8,128)(2,1)} %get-tuple-element.84.lo_rest) | copy-start | bytes 3145732
  91.6 10.6 %copy-start.20 = (bf16[32,64,128]{2,1,0:T(8,128)(2,1)S(1)}, bf16[32,64,128]{2,1,0:T(8,128)(2,1)}, u32[]{:S(2)}) copy-start(bf16[32,64,128]{2,1,0:T(8,128)(2,1)} %get-tuple-element.82.s_rest) | copy-start | bytes 1572868
  91.6 10.6 %copy-start.23 = (f32[32,1,128]{2,1,0:T(1,128)S(1)}, f32[32,1,128]{2,1,0:T(1,128)}, u32[]{:S(2)}) copy-start(f32[32,1,128]{2,1,0:T(1,128)} %get-tuple-element.81.d_rest) | copy-start | bytes 49156
  102.2 21.7 %copy-start.1 = (f32[64,8192]{1,0:T(8,128)S(1)}, f32[64,8192]{1,0:T(8,128)}, u32[]{:S(2)}) copy-start(f32[64,8192]{1,0:T(8,128)} %b.1) | copy-start | bytes 6291460
  (4 other events, 17.1 us)

commit v12 on v11

--- a/solution.py
+++ b/solution.py
@@ -187,10 +187,8 @@
     n = 2 * STEP
     tiles, cols = refs[:n], refs[n : 2 * n]
     remote, maps = refs[2 * n : 2 * n + 2]
-    b_slot, b_rest, d_slot, d_rest, hi_rest, lo_rest, hi_top, lo_top, hi_side, lo_side, s_slot, s_rest = refs[
-        2 * n + 2 : 2 * n + 14
-    ]
-    z_rest, w_rest, hi_unit, lo_unit, rr_unit, rs, rr = refs[2 * n + 14 :]
+    b_slot, b_rest, d_slot, hi_top, lo_top, hi_side, lo_side, s_slot = refs[2 * n + 2 : 2 * n + 10]
+    z_rest, w_rest, v_rest, u_rest, hi_unit, lo_unit, rr_unit, rs, rr = refs[2 * n + 10 :]
     step = pl.program_id(0)
 
     @pl.when(step == 0)
@@ -212,7 +210,11 @@
     image = [apply_off(xx, *off[i]) for xx, i in zip(both, rest)]
     z = [(1.0 - OMEGA) * xx + st - im * rd for xx, st, im, rd in zip(both, start, image, rdiag)]
     w = [apply_block(zz, diag[i], *off[i]) for zz, i in zip(z, rest)]
-    left = [(1.0 - OMEGA) * ww - apply_off(ww * rd, *off[i]) for ww, rd, i in zip(w, rdiag, rest)]
+    start = [ww * rd for ww, rd in zip(w, rdiag)]
+    again = [apply_off(xx, *off[i]) for xx, i in zip(start, rest)]
+    left = [(1.0 - OMEGA) * ww - im for ww, im in zip(w, again)]
+    v = [(2.0 - OMEGA) * xx - im * rd for xx, im, rd in zip(start, again, rdiag)]
+    u = [apply_block(vv, diag[i], *off[i]) for vv, i in zip(v, rest)]
     unit_total = rr_unit[...]
     for k in range(0, STEP, 2):
         pair = beside(spread[STEP + k], spread[STEP + k + 1])
@@ -221,7 +223,10 @@
     for k in range(STEP):
         z_rest[k] = z[k][:COLS]
         w_rest[k] = w[k][:COLS]
-        hi_unit[k], lo_unit[k] = split2(beside(z[k][COLS:], w[k][COLS:]))
+        v_rest[k] = v[k][:COLS]
+        u_rest[k] = u[k][:COLS]
+        units = [beside(v[k][COLS:], u[k][COLS:]), beside(z[k][COLS:], w[k][COLS:])]
+        hi_unit[k], lo_unit[k] = split2(jnp.concatenate(units, axis=0))
     y = [b[i] - OMEGA * b[i] - mm(x[i], *off[i]) for i in range(STEP)]
     y = y + [b[i] - OMEGA * b[i] - im[:COLS] for i, im in zip(rest, image)]
     total = rr[...]
@@ -231,10 +236,7 @@
         b_slot[k] = b[k]
         d_slot[k] = diag[k]
         b_rest[k] = b[STEP + k]
-        d_rest[k] = diag[STEP + k]
-        hi_rest[k], lo_rest[k] = off[STEP + k]
         s_slot[k] = spread[k]
-        s_rest[k] = spread[STEP + k]
     coupling, turned, restricted = [], [], []
     for k in range(STEP):
         j = step * STEP + k
@@ -279,19 +281,17 @@
             out(COLS, TILE),
             out(COLS, TILE),
             out(1, TILE),
-            out(1, TILE),
-            out(TILE, TILE),
-            out(TILE, TILE),
             out(TILE, 2 * TILE),
             out(TILE, 2 * TILE),
             out(TILE, TILE),
             out(TILE, TILE),
             out(AGG, TILE),
-            out(AGG, TILE),
             out(COLS, TILE),
             out(COLS, TILE),
-            out(AGG, 2 * TILE),
-            out(AGG, 2 * TILE),
+            out(COLS, TILE),
+            out(COLS, TILE),
+            out(2 * AGG, 2 * TILE),
+            out(2 * AGG, 2 * TILE),
             pl.BlockSpec((COLS + AGG, AGG), lambda s, p, c: (0, 0)),
             pl.BlockSpec((PEER_STEP, 2, TILE, TILE), lambda s, p, c: (s, 0, 0, 0)),
             pl.BlockSpec((COLS, AGG), lambda s, p, c: (0, 0)),
@@ -308,19 +308,17 @@
             sds((COLS, TILE)),
             sds((COLS, TILE)),
             sds((1, TILE)),
-            sds((1, TILE)),
-            sds((TILE, TILE), BF16),
-            sds((TILE, TILE), BF16),
             sds((TILE, 2 * TILE), BF16),
             sds((TILE, 2 * TILE), BF16),
             sds((TILE, TILE), BF16),
             sds((TILE, TILE), BF16),
             sds((AGG, TILE), BF16),
-            sds((AGG, TILE), BF16),
             sds((COLS, TILE)),
             sds((COLS, TILE)),
-            sds((AGG, 2 * TILE), BF16),
-            sds((AGG, 2 * TILE), BF16),
+            sds((COLS, TILE)),
+            sds((COLS, TILE)),
+            sds((2 * AGG, 2 * TILE), BF16),
+            sds((2 * AGG, 2 * TILE), BF16),
             jax.ShapeDtypeStruct((COLS + AGG, AGG), F32),
             far((PEERS, 2, TILE, TILE), BF16),
             jax.ShapeDtypeStruct((COLS, AGG), F32),
@@ -514,10 +512,11 @@
 def forward_kernel(
     member, arrived, inverse_rows, g, x, inverse, op_hi, op_lo, b_slot, b_rest, d_slot, x_peer, d_peer, s_slot, s_peer,
     hi_top, lo_top, hi_side, lo_side, hi_peer, lo_peer, z_rest, w_rest, hi_unit, lo_unit, rr_unit,
-    z_out, w_out, ws_out, out, e, acc_rr, acc_bz, acc_zw
+    z_out, w_out, ws_out, out, e_keep, e, acc_rr, acc_bz, acc_zw
 ):
     level_one(arrived, inverse_rows, g, x, inverse, op_hi, op_lo, e)
     e_own = e.at[pl.ds(member[0], 1)]
+    e_keep[...] = e_own[0]
     unit_hi, unit_lo = split2(rr_unit[COLS:])
     acc_rr[...] = rr_unit[:COLS] + mm(e_own[0], unit_hi, unit_lo)
     acc_bz[...] = jnp.zeros_like(acc_bz)
@@ -576,8 +575,8 @@
     z = [zz[:, :TILE] for zz in z]
     w = [ww[:, :TILE] for ww in w]
     for k in range(CHUNK):
-        two = dot(e_mine, hi_unit[k])
-        found = two[:COLS] + two[COLS:] + dot(e_mine[:COLS], lo_unit[k])
+        two = dot(e_mine, hi_unit[k, AGG:])
+        found = two[:COLS] + two[COLS:] + dot(e_mine[:COLS], lo_unit[k, AGG:])
         z.append(z_rest[k] + found[:, :TILE])
         w.append(w_rest[k] + found[:, TILE:])
     for i in range(2 * CHUNK):
@@ -598,12 +597,13 @@
     return pl.pallas_call(
         forward_kernel,
         in_specs=specs(len(scalars), len(arrays)),
-        out_specs=specs(0, 4),
+        out_specs=specs(0, 5),
         out_shape=[
             near((2, SLOTS, COLS, TILE)),
             near((2, SLOTS, COLS, TILE)),
             near((SLOTS, COLS, TILE)),
             jax.ShapeDtypeStruct((PEERS, ROWS, TILE), F32),
+            jax.ShapeDtypeStruct((COLS, AGG), F32),
         ],
         scratch_shapes=[
             pltpu.VMEM((PEERS, COLS, AGG), F32),
@@ -617,8 +617,9 @@
 
 
 def second_kernel(
-    member, arrived, inverse_rows, g, x, inverse, op_hi, op_lo, b_slot, b_rest, d_slot, d_rest, d_peer, s_slot, s_rest, s_peer,
-    hi_top, lo_top, hi_side, lo_side, hi_peer, lo_peer, hi_rest, lo_rest, z_in, w_in, w_peer, v_out, u_out, out, dots, e, acc_a, acc_b, acc_c, acc_alpha
+    member, arrived, inverse_rows, g, x, inverse, op_hi, op_lo, e_first, b_slot, b_rest, d_slot, d_peer, s_slot, s_peer,
+    hi_top, lo_top, hi_side, lo_side, hi_peer, lo_peer, z_in, w_in, w_peer, v_rest, u_rest, hi_unit, lo_unit,
+    v_out, u_out, out, dots, e, acc_a, acc_b, acc_c, acc_alpha
 ):
     extra = arrived[0, 32:40]
     for q in range(1, GROUPS):
@@ -631,16 +632,16 @@
     col = column(dots[0:1])
     acc_alpha[...] = col[:COLS] / col[COLS:]
     e_own = e.at[pl.ds(member[0], 1)]
-    views = (e, b_slot, b_rest, d_slot, d_rest, d_peer, s_slot, s_rest, s_peer, hi_top, lo_top, hi_side, lo_side, hi_peer, lo_peer, hi_rest, lo_rest, w_peer)
+    views = (
+        e, b_slot, b_rest, d_slot, d_peer, s_slot, s_peer, hi_top, lo_top, hi_side, lo_side, hi_peer, lo_peer,
+        v_rest, u_rest, hi_unit, lo_unit, w_peer
+    )
 
     @pl.loop(0, CHUNKS)
     def _(step):
         e_peer, *parts = [v.at[part(step, v.shape[0])] for v in views]
-        z_part, w_part, v_part, u_part = [v.at[:, part(step, SLOTS)] for v in (z_in, w_in, v_out, u_out)]
-        second_step(
-            e_own, e_peer, *parts[:-1], z_part, w_part, parts[-1], v_part, u_part,
-            acc_a, acc_b, acc_c, acc_alpha
-        )
+        both = [v.at[:, part(step, SLOTS)] for v in (z_in, w_in, v_out, u_out)]
+        second_step(e_first, e_own, e_peer, *parts, *both, acc_a, acc_b, acc_c, acc_alpha)
 
     first = jnp.sum(jnp.concatenate([acc_a[...], acc_b[...]], axis=0).T, axis=0, keepdims=True)
     last = jnp.sum(jnp.concatenate([acc_c[...], acc_c[...]], axis=0).T, axis=0, keepdims=True)
@@ -648,11 +649,11 @@
 
 
 def second_step(
-    e_own, e_peer, b_slot, b_rest, d_slot, d_rest, d_peer, s_slot, s_rest, s_peer,
-    hi_top, lo_top, hi_side, lo_side, hi_peer, lo_peer, hi_rest, lo_rest, z_in, w_in, w_peer, v_out, u_out, acc_a, acc_b, acc_c, acc_alpha
+    e_first, e_own, e_peer, b_slot, b_rest, d_slot, d_peer, s_slot, s_peer, hi_top, lo_top, hi_side, lo_side,
+    hi_peer, lo_peer, v_rest, u_rest, hi_unit, lo_unit, w_peer, z_in, w_in, v_out, u_out, acc_a, acc_b, acc_c, acc_alpha
 ):
     alpha = acc_alpha[...]
-    e_mine = two_parts(e_own[0])
+    e_twice = two_parts(beside(e_first[...], e_own[0]))
     e_both = [two_parts(beside(e_own[0], e_peer[q])) for q in range(CHUNK // 2)]
     sums = [acc_a[...], acc_b[...], acc_c[...]]
 
@@ -664,26 +665,29 @@
         sums[1] = sums[1] + z1 * az1
         sums[2] = sums[2] + (z1 * w + z * az1)
 
-    pairs, rest = range(CHUNK), range(CHUNK)
-    diag = [jnp.concatenate([d_slot[k], d_peer[k]], axis=1) for k in pairs] + [d_rest[k] for k in rest]
+    pairs = range(CHUNK)
+    diag = [beside(d_slot[k], d_peer[k]) for k in pairs]
     rdiag = [OMEGA / d for d in diag]
     mats = [(block(hi_top, hi_side, hi_peer, k), block(lo_top, lo_side, lo_peer, k)) for k in pairs]
-    mats = mats + [(hi_rest[k], lo_rest[k]) for k in rest]
-    w = [jnp.concatenate([w_in[0, k], w_peer[k]], axis=1) for k in pairs] + [w_in[1, k] for k in rest]
-    spread = [s_slot[k] for k in pairs] + [s_rest[k] for k in rest]
-    ups = [lift(e_both[k // 2], pair_spread(spread[k], s_peer[k])) for k in pairs]
-    ups = ups + [lift(e_mine, sp) for sp in spread[CHUNK:]]
+    w = [beside(w_in[0, k], w_peer[k]) for k in pairs]
+    ups = [lift(e_both[k // 2], pair_spread(s_slot[k], s_peer[k])) for k in pairs]
     x1 = [ww * rd for ww, rd in zip(w, rdiag)]
     x = [start + up for start, up in zip(x1, ups)]
     image = [apply_off(xx, *m) for xx, m in zip(x, mats)]
     v = [(1.0 - OMEGA) * xx + start - im * rd for xx, start, im, rd in zip(x, x1, image, rdiag)]
     left = [(m[0][:, :TILE], m[1][:, :TILE]) for m in mats]
     u = [apply_block(vv, d[:, :TILE], *m) for vv, d, m in zip(v, diag, left)]
+    v = [vv[:, :TILE] for vv in v]
+    for k in range(CHUNK):
+        two = dot(e_twice, hi_unit[k])
+        found = two[:COLS] + two[COLS:] + dot(e_twice[:COLS], lo_unit[k])
+        v.append(v_rest[k] + found[:, :TILE])
+        u.append(u_rest[k] + found[:, TILE:])
     for i in range(2 * CHUNK):
-        vv, b_ref = v[i][:, :TILE], (b_slot if i < CHUNK else b_rest)
-        v_out[i // CHUNK, i % CHUNK] = vv
-        u_out[i // CHUNK, i % CHUNK] = u[i]
-        gather(b_ref[i % CHUNK], z_in[i // CHUNK, i % CHUNK], w[i][:, :TILE], vv, u[i])
+        half, k = i // CHUNK, i % CHUNK
+        v_out[half, k] = v[i]
+        u_out[half, k] = u[i]
+        gather((b_slot, b_rest)[half][k], z_in[half, k], w_in[half, k], v[i], u[i])
     acc_a[...] = sums[0]
     acc_b[...] = sums[1]
     acc_c[...] = sums[2]
@@ -792,8 +796,8 @@
     *local, rs, rr_local = local_part(
         perm, counts, diag_tiles, right_side, remote, maps
     )
-    b_slot, b_rest, d_slot, d_rest, hi_rest, lo_rest, hi_top, lo_top, hi_side, lo_side, s_slot, s_rest = local[:12]
-    affine = tuple(local[12:])
+    b_slot, b_rest, d_slot, hi_top, lo_top, hi_side, lo_side, s_slot = local[:8]
+    z_rest, w_rest, v_rest, u_rest, hi_unit, lo_unit, rr_unit = local[8:]
     g, inverse, op_hi, op_lo = coarse_setup(operator, coarse_map.reshape(1, NC1))
     inverse_rows = lax.dynamic_slice_in_dim(coarsest_inverse, group * AGG, AGG, 0)
 
@@ -807,17 +811,21 @@
     x, outgoing = lowest_part(gathered, g)
     coarse = (exchange(outgoing, "grp"), inverse_rows, g, x, inverse)
     pairs = (hi_top, lo_top, hi_side, lo_side, hi_peer, lo_peer)
-    z, w, w_peer, outgoing = forward_part(
-        scalars, coarse + (op_hi, op_lo, b_slot, b_rest, d_slot, side, d_peer, s_slot, s_peer) + pairs + affine
+    z, w, w_peer, outgoing, e_first = forward_part(
+        scalars,
+        coarse
+        + (op_hi, op_lo, b_slot, b_rest, d_slot, side, d_peer, s_slot, s_peer)
+        + pairs
+        + (z_rest, w_rest, hi_unit, lo_unit, rr_unit),
     )
     x, outgoing = lowest_part(exchange(outgoing, GROUP_AXES), g)
     coarse = (exchange(outgoing, "grp"), inverse_rows, g, x, inverse)
     v, u, outgoing, dots = second_part(
         scalars,
         coarse
-        + (op_hi, op_lo, b_slot, b_rest, d_slot, d_rest, d_peer, s_slot, s_rest, s_peer)
+        + (op_hi, op_lo, e_first, b_slot, b_rest, d_slot, d_peer, s_slot, s_peer)
         + pairs
-        + (hi_rest, lo_rest, z, w, w_peer),
+        + (z, w, w_peer, v_rest, u_rest, hi_unit, lo_unit),
     )
     sums = exchange(outgoing, ALL_AXES)
     return tuple(combine(where, dots, sums, right_side, z, w, v, u))

time: 127 us -> 126 us (level)
  waiting for transfers between devices: 11.5 us -> 10.1 us
    all_to_all x1, waiting for transfers between devices: 11.5 us -> 10.1 us  [exchange(): return lax.all_to_all(x, axes, 0, 0, tiled=True)]
    pallas_call x1, Pallas kernels: 13.5 us -> 14.8 us  [local_part(): pl.pallas_call(local_kernel, grid_spec=grid, out_shape=[sds((COLS, TILE))...]
  transfers between devices with their start and end apart: 1 -> 1, of which waited for: 1 -> 1; matrix products, arithmetic and copies ran while one was open for 1% -> 1% of each run, Pallas kernels for 13% -> 14%
where the time goes in v12:
time: 126 us
  blocking collectives  61.2 us (49%)
  Pallas kernels  41.9 us (33%)
  waiting for transfers between devices  10.1 us (8%)
  starting transfers between devices  8.44 us (7%)
  local copies, waits for them, and re-layouts  2.48 us (2%)
    all_to_all x5, blocking collectives, exchange(): return lax.all_to_all(x, axes, 0, 0, tiled=True)  61.2 us
    pallas_call x1, Pallas kernels, local_part(): pl.pallas_call(local_kernel, grid_spec=grid, out_shape=[sds((COLS, TILE))...  14.8 us
    all_to_all x1, waiting for transfers between devices, exchange(): return lax.all_to_all(x, axes, 0, 0, tiled=True)  10.1 us
    all_to_all x1, starting transfers between devices, exchange(): return lax.all_to_all(x, axes, 0, 0, tiled=True)  8.44 us
    pallas_call x1, Pallas kernels, forward_part(): pl.pallas_call(forward_kernel, in_specs=specs(len(scalars), len(arrays)),...  7.39 us
    pallas_call x1, Pallas kernels, second_part(): pl.pallas_call(second_kernel, in_specs=specs(len(scalars), len(arrays)),...  6.4 us
    pallas_call x1, Pallas kernels, boundary_pack(): pl.pallas_call(boundary_kernel, in_specs=[pl.BlockSpec(memory_space=pl.AN...  4.25 us
    pallas_call x1, Pallas kernels, combine(): pl.pallas_call(combine_kernel, in_specs=specs(1, 7), out_specs=[pl.BlockS...  2.99 us
  transfers between devices with their start and end apart: 1, of which 1 were waited for; matrix products, arithmetic and copies ran while one was open for 1% of the time, Pallas kernels for 14%

profile of v12, /device:TPU:1, one launch (start us, length us, event | category | flops | bytes accessed | tf_op | source)
XLA Modules:
  0.0 125.9 jit_solution(1277885643886226494)
XLA Ops:
  0.6 4.3 %boundary_pack.1 = f32[16,264,128]{2,1,0:T(8,128)} custom-call(s32[1,2,16]{2,1,0:T(2,128)} %bitcast.13, s32[64,128]{1,0:T(8,128)} %bitcast.8, f32[64,128,128]{2,1,0:T(8,128)} %tiles.1, f32[64,8192]{1,0:T(8,128)} %b.1), custom_call_target="tpu_custom_call" | custom-call | tf_op jit(solution)/shard_map/boundary_pack/pallas_call | solution.py:164
  4.9 8.4 %all-to-all-start = ((f32[16,264,128]{2,1,0:T(8,128)}), f32[16,264,128]{2,1,0:T(8,128)S(1)}, u32[]{:S(2)}, u32[]{:S(2)}) async-start(f32[16,264,128]{2,1,0:T(8,128)} %boundary_pack.1), calls=%async_computation | async-start | bytes 4325376 | tf_op jit(solution)/shard_map/all_to_all | solution.py:763
  13.4 0.1 copy.13
  13.5 0.1 reshape.33
  13.6 2.2 %copy-done.12 = f32[1,1024,1024]{2,1,0:T(8,128)S(1)} copy-done((f32[1,1024,1024]{2,1,0:T(8,128)S(1)}, f32[1,1024,1024]{2,1,0:T(8,128)}, u32[]{:S(2)}) %copy-start.12) | copy-done | bytes 4194328
  15.8 2.8 %coarse_setup.1 = (f32[64,1024]{1,0:T(8,128)S(1)}, f32[1,1024]{1,0:T(1,128)S(1)}, bf16[1024,1024]{1,0:T(8,128)(2,1)}, bf16[1024,1024]{1,0:T(8,128)(2,1)}) custom-call(f32[1024,1024]{1,0:T(8,128)S(1)} %bitcast.7, s32[1,1024]{1,0:T(1,128)S(1)} %bitcast.10), custom_call_target="tpu_custom_call" | custom-call | flops 268435456 | bytes 5242880 | tf_op jit(solution)/shard_map/coarse_setup/pallas_call | solution.py:352
  18.6 0.1 fusion
  18.7 0.1 select_reduce_fusion.1
  18.8 0.1 select_reduce_fusion.2
  18.9 0.1 pad_add_fusion.perm
  19.0 14.8 %local_part.1 = (f32[32,64,128]{2,1,0:T(8,128)}, f32[32,64,128]{2,1,0:T(8,128)}, f32[32,1,128]{2,1,0:T(1,128)}, bf16[32,128,256]{2,1,0:T(8,128)(2,1)}, bf16[32,1...) custom-call(s32[64]{0:T(128)S(1)} %pad_add_fusion.perm, ...), custom_call_target="tpu_custom_call" | custom-call | flops 402653184 | bytes 16777216 | tf_op jit(solution)/shard_map/local_part/pallas_call | solution.py:304
  33.9 0.1 select_reduce_fusion.where
  34.0 10.1 %all-to-all-done.arrived.x_peer = f32[16,264,128]{2,1,0:T(8,128)S(1)} async-done(((f32[16,264,128]{2,1,0:T(8,128)}), f32[16,264,128]{2,1,0:T(8,128)S(1)}, u32[]{:S(2)}, u32[]{:S(2)}) %all-to-all-start) | async-done | bytes 2162720 | tf_op jit(solution)/shard_map/all_to_all | solution.py:763
  44.2 2.5 %first_restrict.1 = (f32[16,32,128]{2,1,0:T(8,128)S(1)}, bf16[32,128,128]{2,1,0:T(8,128)(2,1)S(1)}, bf16[32,128,128]{2,1,0:T(8,128)(2,1)S(1)}, f32[32,1,128]{2,1,0:T(1,128)S(1)}, bf16[32,64,128]{2,1,0:T(8,128)(2,1)S(1)}) custom-call(f32[16,264,128]{2,1,0:T(8,128)S(1)} %all-to-all-done.arrived.x_peer, bf16[16,2,128,128]{3,2,1,0:T(8,128)(2,1)} %get-tuple-element.50.rs, ...), custom_call_target="tpu_custom_call" | custom-call | tf_op jit(solution)/shard_map/first_restrict/pallas_call | solution.py:400
  46.6 13.2 %all_to_all.30.arrived = f32[16,32,128]{2,1,0:T(8,128)S(1)} all-to-all(f32[16,32,128]{2,1,0:T(8,128)S(1)} %get-tuple-element.52), channel_id=1, replica_groups=mesh['grp'=8,'sub'=8,'chip'=2] {'sub','chip'}, dimensions={0} | all-to-all | bytes 524288 | tf_op jit(solution)/shard_map/all_to_all | solution.py:763
  59.9 0.4 lowest_part.2
  60.3 12.9 %all_to_all.31.arrived = f32[8,32,128]{2,1,0:T(8,128)S(1)} all-to-all(f32[8,32,128]{2,1,0:T(8,128)S(1)} %get-tuple-element.54), channel_id=1, replica_groups=mesh['grp'=8,'sub'=8,'chip'=2] {'grp'}, dimensions={0} | all-to-all | bytes 262144 | tf_op jit(solution)/shard_map/all_to_all | solution.py:763
  73.3 7.4 %forward_part.1 = (f32[2,32,64,128]{3,2,1,0:T(8,128)S(1)}, f32[2,32,64,128]{3,2,1,0:T(8,128)S(1)}, f32[32,64,128]{2,1,0:T(8,128)S(1)}, f32[16,40,128]{2,1,0:T(8,128)S(1)}, f32[64,64]{1,0:T(8,128)S(1)}) custom-call(s32[1]{0:T(128)} %bitcast.5.member, f32[8,32,128]{2,1,0:T(8,128)S(1)} %all_to_all.31.arrived, ...), custom_call_target="tpu_custom_call" | custom-call | tf_op jit(solution)/shard_map/forward_part/pallas_call | solution.py:597
  80.7 10.9 %all_to_all.32.arrived = f32[16,40,128]{2,1,0:T(8,128)S(1)} all-to-all(f32[16,40,128]{2,1,0:T(8,128)S(1)} %get-tuple-element.77), channel_id=1, replica_groups=mesh['grp'=8,'sub'=8,'chip'=2] {'sub','chip'}, dimensions={0} | all-to-all | bytes 655360 | tf_op jit(solution)/shard_map/all_to_all | solution.py:763
  91.6 0.4 lowest_part.3
  92.0 10.2 %all_to_all.33.arrived = f32[8,40,128]{2,1,0:T(8,128)S(1)} all-to-all(f32[8,40,128]{2,1,0:T(8,128)S(1)} %get-tuple-element.78), channel_id=1, replica_groups=mesh['grp'=8,'sub'=8,'chip'=2] {'grp'}, dimensions={0} | all-to-all | bytes 327680 | tf_op jit(solution)/shard_map/all_to_all | solution.py:763
  102.2 6.4 %second_part.1 = (f32[2,32,64,128]{3,2,1,0:T(8,128)S(1)}, f32[2,32,64,128]{3,2,1,0:T(8,128)S(1)}, f32[128,2,128]{2,1,0:T(2,128)S(1)}, f32[8,128]{1,0:T(8,128)S(1)}) custom-call(s32[1]{0:T(128)} %bitcast.5.member, f32[8,40,128]{2,1,0:T(8,128)S(1)} %all_to_all.33.arrived, f32[64,512]{1,0:T(8,128)S(1)} %constant_dynamic-slice_fusion.inverse_rows, ...), custom_call_target="tpu_custom_call" | custom-call | tf_op jit(solution)/shard_map/second_part/pallas_call | solution.py:697
  108.6 14.1 %all_to_all.34.arrived = f32[128,2,128]{2,1,0:T(2,128)S(1)} all-to-all(f32[128,2,128]{2,1,0:T(2,128)S(1)} %get-tuple-element.87), channel_id=1, replica_groups=mesh['grp'=8,'sub'=8,'chip'=2] {'grp','sub','chip'}, dimensions={0} | all-to-all | bytes 262144 | tf_op jit(solution)/shard_map/all_to_all | solution.py:763
  122.7 3.0 %combine.1 = (f32[64,8192]{1,0:T(8,128)}, f32[64,8192]{1,0:T(8,128)}) custom-call(s32[64]{0:T(128)S(1)} %select_reduce_fusion.where, f32[8,128]{1,0:T(8,128)S(1)} %get-tuple-element.86.dots, f32[128,2,128]{2,1,0:T(2,128)S(1)} %all_to_all.34.arrived, f32[64,8192]{1,0:T(8,128)S(1)} %copy-done.1, f32[2,32,64,128]{3,2,1,0:T(8,128)S(1)} %get-tuple-element.81.z_in.z, ...), custom_call_target="tpu_custom_call" | custom-call | tf_op jit(solution)/shard_map/combine/pallas_call | solution.py:747
  (51 shorter events, 0.1 us)
Async XLA Ops:
  0.6 33.3 %copy-start = (f32[512,512]{1,0:T(8,128)S(1)}, f32[512,512]{1,0:T(8,128)}, u32[]{:S(2)}) copy-start(f32[512,512]{1,0:T(8,128)} %param.17) | copy-start | bytes 3145732
  4.9 8.5 %copy-start.24 = (s32[1,16,2]{1,2,0:T(2,128)S(1)}, s32[1,16,2]{1,2,0:T(2,128)}, u32[]{:S(2)}) copy-start(s32[1,16,2]{1,2,0:T(2,128)} %param.13) | copy-start | bytes 388
  4.9 8.7 %copy-start.22 = (s32[1024]{0:T(1024)S(1)}, s32[1024]{0:T(1024)}, u32[]{:S(2)}) copy-start(s32[1024]{0:T(1024)} %param.15) | copy-start | bytes 12292
  4.9 39.2 %all-to-all-start = ((f32[16,264,128]{2,1,0:T(8,128)}), f32[16,264,128]{2,1,0:T(8,128)S(1)}, u32[]{:S(2)}, u32[]{:S(2)}) async-start(f32[16,264,128]{2,1,0:T(8,128)} %boundary_pack.1), calls=%async_computation | async-start | bytes 4325376 | tf_op jit(solution)/shard_map/all_to_all | solution.py:763
  15.8 3.2 %copy-start.23 = (s32[1,16]{1,0:T(1,128)S(1)}, s32[1,16]{1,0:T(1,128)}, u32[]{:S(2)}) copy-start(s32[1,16]{1,0:T(1,128)} %param.12) | copy-start | bytes 196
  18.6 15.3 %copy-start.14 = (f32[64,1024]{1,0:T(8,128)}, f32[64,1024]{1,0:T(8,128)S(1)}, u32[]{:S(2)}) copy-start(f32[64,1024]{1,0:T(8,128)S(1)} %get-tuple-element.53.g) | copy-start | bytes 786436
  44.2 15.6 %copy-start.15 = (f32[64,1024]{1,0:T(8,128)S(1)}, f32[64,1024]{1,0:T(8,128)}, u32[]{:S(2)}) copy-start(f32[64,1024]{1,0:T(8,128)} %copy-done.14) | copy-start | bytes 786436
  59.8 13.4 %copy-start.2 = (bf16[1024,1024]{1,0:T(8,128)(2,1)S(1)}, bf16[1024,1024]{1,0:T(8,128)(2,1)}, u32[]{:S(2)}) copy-start(bf16[1024,1024]{1,0:T(8,128)(2,1)} %get-tuple-element.58.op_hi) | copy-start | bytes 6291460
  59.8 13.4 %copy-start.3 = (bf16[1024,1024]{1,0:T(8,128)(2,1)S(1)}, bf16[1024,1024]{1,0:T(8,128)(2,1)}, u32[]{:S(2)}) copy-start(bf16[1024,1024]{1,0:T(8,128)(2,1)} %get-tuple-element.59.op_lo) | copy-start | bytes 6291460
  59.8 13.4 %copy-start.4 = (bf16[32,128,256]{2,1,0:T(8,128)(2,1)S(1)}, bf16[32,128,256]{2,1,0:T(8,128)(2,1)}, u32[]{:S(2)}) copy-start(bf16[32,128,256]{2,1,0:T(8,128)(2,1)} %get-tuple-element.66.hi_top) | copy-start | bytes 6291460
  59.8 13.4 %copy-start.5 = (bf16[32,128,256]{2,1,0:T(8,128)(2,1)S(1)}, bf16[32,128,256]{2,1,0:T(8,128)(2,1)}, u32[]{:S(2)}) copy-start(bf16[32,128,256]{2,1,0:T(8,128)(2,1)} %get-tuple-element.67.lo_top) | copy-start | bytes 6291460
  59.8 13.4 %copy-start.6 = (bf16[32,128,256]{2,1,0:T(8,128)(2,1)S(1)}, bf16[32,128,256]{2,1,0:T(8,128)(2,1)}, u32[]{:S(2)}) copy-start(bf16[32,128,256]{2,1,0:T(8,128)(2,1)} %get-tuple-element.74.hi_unit) | copy-start | bytes 6291460
  59.8 13.4 %copy-start.7 = (bf16[32,128,256]{2,1,0:T(8,128)(2,1)S(1)}, bf16[32,128,256]{2,1,0:T(8,128)(2,1)}, u32[]{:S(2)}) copy-start(bf16[32,128,256]{2,1,0:T(8,128)(2,1)} %get-tuple-element.75.lo_unit) | copy-start | bytes 6291460
  59.8 13.4 %copy-start.8 = (f32[32,64,128]{2,1,0:T(8,128)S(1)}, f32[32,64,128]{2,1,0:T(8,128)}, u32[]{:S(2)}) copy-start(f32[32,64,128]{2,1,0:T(8,128)} %get-tuple-element.60.b_slot) | copy-start | bytes 3145732
  59.9 13.4 %copy-start.9 = (f32[32,64,128]{2,1,0:T(8,128)S(1)}, f32[32,64,128]{2,1,0:T(8,128)}, u32[]{:S(2)}) copy-start(f32[32,64,128]{2,1,0:T(8,128)} %get-tuple-element.61.b_rest) | copy-start | bytes 3145732
  59.9 13.4 %copy-start.10 = (bf16[32,128,128]{2,1,0:T(8,128)(2,1)S(1)}, bf16[32,128,128]{2,1,0:T(8,128)(2,1)}, u32[]{:S(2)}) copy-start(bf16[32,128,128]{2,1,0:T(8,128)(2,1)} %get-tuple-element.68.hi_side) | copy-start | bytes 3145732
  59.9 13.4 %copy-start.11 = (bf16[32,128,128]{2,1,0:T(8,128)(2,1)S(1)}, bf16[32,128,128]{2,1,0:T(8,128)(2,1)}, u32[]{:S(2)}) copy-start(bf16[32,128,128]{2,1,0:T(8,128)(2,1)} %get-tuple-element.69.lo_side) | copy-start | bytes 3145732
  59.9 13.4 %copy-start.13 = (bf16[32,64,128]{2,1,0:T(8,128)(2,1)S(1)}, bf16[32,64,128]{2,1,0:T(8,128)(2,1)}, u32[]{:S(2)}) copy-start(bf16[32,64,128]{2,1,0:T(8,128)(2,1)} %get-tuple-element.64.s_slot) | copy-start | bytes 1572868
  59.9 13.4 %copy-start.18 = (f32[32,64,128]{2,1,0:T(8,128)S(1)}, f32[32,64,128]{2,1,0:T(8,128)}, u32[]{:S(2)}) copy-start(f32[32,64,128]{2,1,0:T(8,128)} %get-tuple-element.72.z_rest) | copy-start | bytes 3145732
  59.9 13.4 %copy-start.19 = (f32[32,64,128]{2,1,0:T(8,128)S(1)}, f32[32,64,128]{2,1,0:T(8,128)}, u32[]{:S(2)}) copy-start(f32[32,64,128]{2,1,0:T(8,128)} %get-tuple-element.73.w_rest) | copy-start | bytes 3145732
  59.9 13.4 %copy-start.21 = (f32[32,1,128]{2,1,0:T(1,128)S(1)}, f32[32,1,128]{2,1,0:T(1,128)}, u32[]{:S(2)}) copy-start(f32[32,1,128]{2,1,0:T(1,128)} %get-tuple-element.62.d_slot) | copy-start | bytes 49156
  91.6 10.6 %copy-start.16 = (f32[32,64,128]{2,1,0:T(8,128)S(1)}, f32[32,64,128]{2,1,0:T(8,128)}, u32[]{:S(2)}) copy-start(f32[32,64,128]{2,1,0:T(8,128)} %get-tuple-element.84.v_rest) | copy-start | bytes 3145732
  91.6 10.6 %copy-start.17 = (f32[32,64,128]{2,1,0:T(8,128)S(1)}, f32[32,64,128]{2,1,0:T(8,128)}, u32[]{:S(2)}) copy-start(f32[32,64,128]{2,1,0:T(8,128)} %get-tuple-element.85.u_rest) | copy-start | bytes 3145732
  102.2 20.5 %copy-start.1 = (f32[64,8192]{1,0:T(8,128)S(1)}, f32[64,8192]{1,0:T(8,128)}, u32[]{:S(2)}) copy-start(f32[64,8192]{1,0:T(8,128)} %b.1) | copy-start | bytes 6291460
  (2 other events, 5.4 us)

commit v13 on v12

--- a/solution.py
+++ b/solution.py
@@ -20,7 +20,7 @@
 NC1 = 1024
 STEP = 8
 NSTEP = SLOTS // STEP
-CHUNK = 16
+CHUNK = 32
 CHUNKS = SLOTS // CHUNK
 SIDE = 264
 PEER_STEP = 4

time: 126 us -> 126 us (level)
  no operation moved by 1% of the time
where the time goes in v13:
time: 126 us
  blocking collectives  61.3 us (49%)
  Pallas kernels  41.7 us (33%)
  waiting for transfers between devices  10.1 us (8%)
  starting transfers between devices  8.44 us (7%)
  local copies, waits for them, and re-layouts  2.48 us (2%)
    all_to_all x5, blocking collectives, exchange(): return lax.all_to_all(x, axes, 0, 0, tiled=True)  61.3 us
    pallas_call x1, Pallas kernels, local_part(): pl.pallas_call(local_kernel, grid_spec=grid, out_shape=[sds((COLS, TILE))...  14.8 us
    all_to_all x1, waiting for transfers between devices, exchange(): return lax.all_to_all(x, axes, 0, 0, tiled=True)  10.1 us
    all_to_all x1, starting transfers between devices, exchange(): return lax.all_to_all(x, axes, 0, 0, tiled=True)  8.44 us
    pallas_call x1, Pallas kernels, forward_part(): pl.pallas_call(forward_kernel, in_specs=specs(len(scalars), len(arrays)),...  7.2 us
    pallas_call x1, Pallas kernels, second_part(): pl.pallas_call(second_kernel, in_specs=specs(len(scalars), len(arrays)),...  6.33 us
    pallas_call x1, Pallas kernels, boundary_pack(): pl.pallas_call(boundary_kernel, in_specs=[pl.BlockSpec(memory_space=pl.AN...  4.25 us
    pallas_call x1, Pallas kernels, combine(): pl.pallas_call(combine_kernel, in_specs=specs(1, 7), out_specs=[pl.BlockS...  2.99 us
  transfers between devices with their start and end apart: 1, of which 1 were waited for; matrix products, arithmetic and copies ran while one was open for 1% of the time, Pallas kernels for 14%

profile of v13, /device:TPU:1, one launch (start us, length us, event | category | flops | bytes accessed | tf_op | source)
XLA Modules:
  0.0 125.6 jit_solution(16116344970846978368)
XLA Ops:
  0.6 4.2 %boundary_pack.1 = f32[16,264,128]{2,1,0:T(8,128)} custom-call(s32[1,2,16]{2,1,0:T(2,128)} %bitcast.13, s32[64,128]{1,0:T(8,128)} %bitcast.8, f32[64,128,128]{2,1,0:T(8,128)} %tiles.1, f32[64,8192]{1,0:T(8,128)} %b.1), custom_call_target="tpu_custom_call" | custom-call | tf_op jit(solution)/shard_map/boundary_pack/pallas_call | solution.py:164
  4.9 8.4 %all-to-all-start = ((f32[16,264,128]{2,1,0:T(8,128)}), f32[16,264,128]{2,1,0:T(8,128)S(1)}, u32[]{:S(2)}, u32[]{:S(2)}) async-start(f32[16,264,128]{2,1,0:T(8,128)} %boundary_pack.1), calls=%async_computation | async-start | bytes 4325376 | tf_op jit(solution)/shard_map/all_to_all | solution.py:763
  13.4 0.1 copy.13
  13.5 0.1 reshape.33
  13.6 2.2 %copy-done.12 = f32[1,1024,1024]{2,1,0:T(8,128)S(1)} copy-done((f32[1,1024,1024]{2,1,0:T(8,128)S(1)}, f32[1,1024,1024]{2,1,0:T(8,128)}, u32[]{:S(2)}) %copy-start.12) | copy-done | bytes 4194328
  15.8 2.8 %coarse_setup.1 = (f32[64,1024]{1,0:T(8,128)S(1)}, f32[1,1024]{1,0:T(1,128)S(1)}, bf16[1024,1024]{1,0:T(8,128)(2,1)}, bf16[1024,1024]{1,0:T(8,128)(2,1)}) custom-call(f32[1024,1024]{1,0:T(8,128)S(1)} %bitcast.7, s32[1,1024]{1,0:T(1,128)S(1)} %bitcast.10), custom_call_target="tpu_custom_call" | custom-call | flops 268435456 | bytes 5242880 | tf_op jit(solution)/shard_map/coarse_setup/pallas_call | solution.py:352
  18.6 0.1 fusion
  18.7 0.1 select_reduce_fusion.1
  18.8 0.1 select_reduce_fusion.2
  18.9 0.1 pad_add_fusion.perm
  19.0 14.8 %local_part.1 = (f32[32,64,128]{2,1,0:T(8,128)}, f32[32,64,128]{2,1,0:T(8,128)}, f32[32,1,128]{2,1,0:T(1,128)}, bf16[32,128,256]{2,1,0:T(8,128)(2,1)}, bf16[32,1...) custom-call(s32[64]{0:T(128)S(1)} %pad_add_fusion.perm, ...), custom_call_target="tpu_custom_call" | custom-call | flops 402653184 | bytes 16777216 | tf_op jit(solution)/shard_map/local_part/pallas_call | solution.py:304
  33.9 0.1 select_reduce_fusion.where
  34.0 10.1 %all-to-all-done.arrived.x_peer = f32[16,264,128]{2,1,0:T(8,128)S(1)} async-done(((f32[16,264,128]{2,1,0:T(8,128)}), f32[16,264,128]{2,1,0:T(8,128)S(1)}, u32[]{:S(2)}, u32[]{:S(2)}) %all-to-all-start) | async-done | bytes 2162720 | tf_op jit(solution)/shard_map/all_to_all | solution.py:763
  44.2 2.5 %first_restrict.1 = (f32[16,32,128]{2,1,0:T(8,128)S(1)}, bf16[32,128,128]{2,1,0:T(8,128)(2,1)S(1)}, bf16[32,128,128]{2,1,0:T(8,128)(2,1)S(1)}, f32[32,1,128]{2,1,0:T(1,128)S(1)}, bf16[32,64,128]{2,1,0:T(8,128)(2,1)S(1)}) custom-call(f32[16,264,128]{2,1,0:T(8,128)S(1)} %all-to-all-done.arrived.x_peer, bf16[16,2,128,128]{3,2,1,0:T(8,128)(2,1)} %get-tuple-element.50.rs, ...), custom_call_target="tpu_custom_call" | custom-call | tf_op jit(solution)/shard_map/first_restrict/pallas_call | solution.py:400
  46.6 13.2 %all_to_all.30.arrived = f32[16,32,128]{2,1,0:T(8,128)S(1)} all-to-all(f32[16,32,128]{2,1,0:T(8,128)S(1)} %get-tuple-element.52), channel_id=1, replica_groups=mesh['grp'=8,'sub'=8,'chip'=2] {'sub','chip'}, dimensions={0} | all-to-all | bytes 524288 | tf_op jit(solution)/shard_map/all_to_all | solution.py:763
  59.9 0.4 lowest_part.2
  60.3 12.9 %all_to_all.31.arrived = f32[8,32,128]{2,1,0:T(8,128)S(1)} all-to-all(f32[8,32,128]{2,1,0:T(8,128)S(1)} %get-tuple-element.54), channel_id=1, replica_groups=mesh['grp'=8,'sub'=8,'chip'=2] {'grp'}, dimensions={0} | all-to-all | bytes 262144 | tf_op jit(solution)/shard_map/all_to_all | solution.py:763
  73.3 7.2 %forward_part.1 = (f32[2,32,64,128]{3,2,1,0:T(8,128)S(1)}, f32[2,32,64,128]{3,2,1,0:T(8,128)S(1)}, f32[32,64,128]{2,1,0:T(8,128)S(1)}, f32[16,40,128]{2,1,0:T(8,128)S(1)}, f32[64,64]{1,0:T(8,128)S(1)}) custom-call(s32[1]{0:T(128)} %bitcast.5.member, f32[8,32,128]{2,1,0:T(8,128)S(1)} %all_to_all.31.arrived, ...), custom_call_target="tpu_custom_call" | custom-call | tf_op jit(solution)/shard_map/forward_part/pallas_call | solution.py:597
  80.5 10.9 %all_to_all.32.arrived = f32[16,40,128]{2,1,0:T(8,128)S(1)} all-to-all(f32[16,40,128]{2,1,0:T(8,128)S(1)} %get-tuple-element.77), channel_id=1, replica_groups=mesh['grp'=8,'sub'=8,'chip'=2] {'sub','chip'}, dimensions={0} | all-to-all | bytes 655360 | tf_op jit(solution)/shard_map/all_to_all | solution.py:763
  91.4 0.4 lowest_part.3
  91.8 10.2 %all_to_all.33.arrived = f32[8,40,128]{2,1,0:T(8,128)S(1)} all-to-all(f32[8,40,128]{2,1,0:T(8,128)S(1)} %get-tuple-element.78), channel_id=1, replica_groups=mesh['grp'=8,'sub'=8,'chip'=2] {'grp'}, dimensions={0} | all-to-all | bytes 327680 | tf_op jit(solution)/shard_map/all_to_all | solution.py:763
  102.0 6.3 %second_part.1 = (f32[2,32,64,128]{3,2,1,0:T(8,128)S(1)}, f32[2,32,64,128]{3,2,1,0:T(8,128)S(1)}, f32[128,2,128]{2,1,0:T(2,128)S(1)}, f32[8,128]{1,0:T(8,128)S(1)}) custom-call(s32[1]{0:T(128)} %bitcast.5.member, f32[8,40,128]{2,1,0:T(8,128)S(1)} %all_to_all.33.arrived, f32[64,512]{1,0:T(8,128)S(1)} %constant_dynamic-slice_fusion.inverse_rows, ...), custom_call_target="tpu_custom_call" | custom-call | tf_op jit(solution)/shard_map/second_part/pallas_call | solution.py:697
  108.3 14.1 %all_to_all.34.arrived = f32[128,2,128]{2,1,0:T(2,128)S(1)} all-to-all(f32[128,2,128]{2,1,0:T(2,128)S(1)} %get-tuple-element.87), channel_id=1, replica_groups=mesh['grp'=8,'sub'=8,'chip'=2] {'grp','sub','chip'}, dimensions={0} | all-to-all | bytes 262144 | tf_op jit(solution)/shard_map/all_to_all | solution.py:763
  122.5 3.0 %combine.1 = (f32[64,8192]{1,0:T(8,128)}, f32[64,8192]{1,0:T(8,128)}) custom-call(s32[64]{0:T(128)S(1)} %select_reduce_fusion.where, f32[8,128]{1,0:T(8,128)S(1)} %get-tuple-element.86.dots, f32[128,2,128]{2,1,0:T(2,128)S(1)} %all_to_all.34.arrived, f32[64,8192]{1,0:T(8,128)S(1)} %copy-done.1, f32[2,32,64,128]{3,2,1,0:T(8,128)S(1)} %get-tuple-element.81.z_in.z, ...), custom_call_target="tpu_custom_call" | custom-call | tf_op jit(solution)/shard_map/combine/pallas_call | solution.py:747
  (51 shorter events, 0.1 us)
Async XLA Ops:
  0.6 33.3 %copy-start = (f32[512,512]{1,0:T(8,128)S(1)}, f32[512,512]{1,0:T(8,128)}, u32[]{:S(2)}) copy-start(f32[512,512]{1,0:T(8,128)} %param.17) | copy-start | bytes 3145732
  4.9 8.5 %copy-start.24 = (s32[1,16,2]{1,2,0:T(2,128)S(1)}, s32[1,16,2]{1,2,0:T(2,128)}, u32[]{:S(2)}) copy-start(s32[1,16,2]{1,2,0:T(2,128)} %param.13) | copy-start | bytes 388
  4.9 8.7 %copy-start.22 = (s32[1024]{0:T(1024)S(1)}, s32[1024]{0:T(1024)}, u32[]{:S(2)}) copy-start(s32[1024]{0:T(1024)} %param.15) | copy-start | bytes 12292
  4.9 39.2 %all-to-all-start = ((f32[16,264,128]{2,1,0:T(8,128)}), f32[16,264,128]{2,1,0:T(8,128)S(1)}, u32[]{:S(2)}, u32[]{:S(2)}) async-start(f32[16,264,128]{2,1,0:T(8,128)} %boundary_pack.1), calls=%async_computation | async-start | bytes 4325376 | tf_op jit(solution)/shard_map/all_to_all | solution.py:763
  15.8 3.2 %copy-start.23 = (s32[1,16]{1,0:T(1,128)S(1)}, s32[1,16]{1,0:T(1,128)}, u32[]{:S(2)}) copy-start(s32[1,16]{1,0:T(1,128)} %param.12) | copy-start | bytes 196
  18.6 15.3 %copy-start.14 = (f32[64,1024]{1,0:T(8,128)}, f32[64,1024]{1,0:T(8,128)S(1)}, u32[]{:S(2)}) copy-start(f32[64,1024]{1,0:T(8,128)S(1)} %get-tuple-element.53.g) | copy-start | bytes 786436
  44.1 15.7 %copy-start.15 = (f32[64,1024]{1,0:T(8,128)S(1)}, f32[64,1024]{1,0:T(8,128)}, u32[]{:S(2)}) copy-start(f32[64,1024]{1,0:T(8,128)} %copy-done.14) | copy-start | bytes 786436
  59.8 13.4 %copy-start.2 = (bf16[1024,1024]{1,0:T(8,128)(2,1)S(1)}, bf16[1024,1024]{1,0:T(8,128)(2,1)}, u32[]{:S(2)}) copy-start(bf16[1024,1024]{1,0:T(8,128)(2,1)} %get-tuple-element.58.op_hi) | copy-start | bytes 6291460
  59.8 13.4 %copy-start.3 = (bf16[1024,1024]{1,0:T(8,128)(2,1)S(1)}, bf16[1024,1024]{1,0:T(8,128)(2,1)}, u32[]{:S(2)}) copy-start(bf16[1024,1024]{1,0:T(8,128)(2,1)} %get-tuple-element.59.op_lo) | copy-start | bytes 6291460
  59.8 13.4 %copy-start.4 = (bf16[32,128,256]{2,1,0:T(8,128)(2,1)S(1)}, bf16[32,128,256]{2,1,0:T(8,128)(2,1)}, u32[]{:S(2)}) copy-start(bf16[32,128,256]{2,1,0:T(8,128)(2,1)} %get-tuple-element.66.hi_top) | copy-start | bytes 6291460
  59.8 13.4 %copy-start.5 = (bf16[32,128,256]{2,1,0:T(8,128)(2,1)S(1)}, bf16[32,128,256]{2,1,0:T(8,128)(2,1)}, u32[]{:S(2)}) copy-start(bf16[32,128,256]{2,1,0:T(8,128)(2,1)} %get-tuple-element.67.lo_top) | copy-start | bytes 6291460
  59.8 13.4 %copy-start.6 = (bf16[32,128,256]{2,1,0:T(8,128)(2,1)S(1)}, bf16[32,128,256]{2,1,0:T(8,128)(2,1)}, u32[]{:S(2)}) copy-start(bf16[32,128,256]{2,1,0:T(8,128)(2,1)} %get-tuple-element.74.hi_unit) | copy-start | bytes 6291460
  59.8 13.4 %copy-start.7 = (bf16[32,128,256]{2,1,0:T(8,128)(2,1)S(1)}, bf16[32,128,256]{2,1,0:T(8,128)(2,1)}, u32[]{:S(2)}) copy-start(bf16[32,128,256]{2,1,0:T(8,128)(2,1)} %get-tuple-element.75.lo_unit) | copy-start | bytes 6291460
  59.8 13.4 %copy-start.8 = (f32[32,64,128]{2,1,0:T(8,128)S(1)}, f32[32,64,128]{2,1,0:T(8,128)}, u32[]{:S(2)}) copy-start(f32[32,64,128]{2,1,0:T(8,128)} %get-tuple-element.60.b_slot) | copy-start | bytes 3145732
  59.9 13.4 %copy-start.9 = (f32[32,64,128]{2,1,0:T(8,128)S(1)}, f32[32,64,128]{2,1,0:T(8,128)}, u32[]{:S(2)}) copy-start(f32[32,64,128]{2,1,0:T(8,128)} %get-tuple-element.61.b_rest) | copy-start | bytes 3145732
  59.9 13.4 %copy-start.10 = (bf16[32,128,128]{2,1,0:T(8,128)(2,1)S(1)}, bf16[32,128,128]{2,1,0:T(8,128)(2,1)}, u32[]{:S(2)}) copy-start(bf16[32,128,128]{2,1,0:T(8,128)(2,1)} %get-tuple-element.68.hi_side) | copy-start | bytes 3145732
  59.9 13.4 %copy-start.11 = (bf16[32,128,128]{2,1,0:T(8,128)(2,1)S(1)}, bf16[32,128,128]{2,1,0:T(8,128)(2,1)}, u32[]{:S(2)}) copy-start(bf16[32,128,128]{2,1,0:T(8,128)(2,1)} %get-tuple-element.69.lo_side) | copy-start | bytes 3145732
  59.9 13.4 %copy-start.13 = (bf16[32,64,128]{2,1,0:T(8,128)(2,1)S(1)}, bf16[32,64,128]{2,1,0:T(8,128)(2,1)}, u32[]{:S(2)}) copy-start(bf16[32,64,128]{2,1,0:T(8,128)(2,1)} %get-tuple-element.64.s_slot) | copy-start | bytes 1572868
  59.9 13.4 %copy-start.18 = (f32[32,64,128]{2,1,0:T(8,128)S(1)}, f32[32,64,128]{2,1,0:T(8,128)}, u32[]{:S(2)}) copy-start(f32[32,64,128]{2,1,0:T(8,128)} %get-tuple-element.72.z_rest) | copy-start | bytes 3145732
  59.9 13.4 %copy-start.19 = (f32[32,64,128]{2,1,0:T(8,128)S(1)}, f32[32,64,128]{2,1,0:T(8,128)}, u32[]{:S(2)}) copy-start(f32[32,64,128]{2,1,0:T(8,128)} %get-tuple-element.73.w_rest) | copy-start | bytes 3145732
  59.9 13.4 %copy-start.21 = (f32[32,1,128]{2,1,0:T(1,128)S(1)}, f32[32,1,128]{2,1,0:T(1,128)}, u32[]{:S(2)}) copy-start(f32[32,1,128]{2,1,0:T(1,128)} %get-tuple-element.62.d_slot) | copy-start | bytes 49156
  91.4 10.6 %copy-start.16 = (f32[32,64,128]{2,1,0:T(8,128)S(1)}, f32[32,64,128]{2,1,0:T(8,128)}, u32[]{:S(2)}) copy-start(f32[32,64,128]{2,1,0:T(8,128)} %get-tuple-element.84.v_rest) | copy-start | bytes 3145732
  91.4 10.6 %copy-start.17 = (f32[32,64,128]{2,1,0:T(8,128)S(1)}, f32[32,64,128]{2,1,0:T(8,128)}, u32[]{:S(2)}) copy-start(f32[32,64,128]{2,1,0:T(8,128)} %get-tuple-element.85.u_rest) | copy-start | bytes 3145732
  102.0 20.5 %copy-start.1 = (f32[64,8192]{1,0:T(8,128)S(1)}, f32[64,8192]{1,0:T(8,128)}, u32[]{:S(2)}) copy-start(f32[64,8192]{1,0:T(8,128)} %b.1) | copy-start | bytes 6291460
  (2 other events, 5.4 us)
